TPU v7x, 32 devices: a whole 2x2x4 slice. The times are simulated.
32 devices in a mesh: groups: 2 (over x), tensor: 16 (over z, y, core).
Axes of the slice: x: 2, y: 2, z: 4, core: 2. Of those that a mesh axis runs over, the one named last changes fastest.
Arguments:
- tokens: bfloat16 [1536, 16384], P(('groups', 'tensor')), parts along dimension 0, may hold values from -6 to 6
- weight_codes: bfloat16 [16384, 16384], P(None, 'tensor'), may hold values from -127 to 127, as said below
- column_scale: float32 [16384], P('tensor'), may hold values from 4.6875e-05 to 0.0001875
- shrink_store: bfloat16 [32, 16384, 64], P(('groups', 'tensor')), parts along dimension 0, may hold values from -0.046875 to 0.046875
- expand_store: bfloat16 [32, 16384, 64], P('groups', 'tensor'), parts along dimension 0, may hold values from -0.75 to 0.75
- row_adapter: int32 [1536], P('groups'), parts along dimension 0, may hold values from 0 to 15, as said below
- placement: int32 [32], P('groups'), parts along dimension 0, may hold values from 0 to 15, each once
- document_lengths: int32 [16], P('groups'), parts along dimension 0, may hold values from 1 to 384, 768 in all
Outputs:
- queries: bfloat16 [1536, 16384], P('groups', 'tensor'), parts along dimension 0
There are 2 independent parts, one for each index of `groups`. A program takes and returns all parts, laid end to end along the dimension named above; an argument that names none is the same for every part. Nothing has to cross between parts.
Inputs may be any that keep to these rules, and one draw needn't show every extreme that they name: `weight_codes`: every entry is a whole number. `row_adapter`: constant on each aligned block of 128 rows and never falling from row to row.
All inputs are finite; a program needn't handle non-finite values.
Results may differ from a plain program's by a relative error of at most 0.0039.
Values may be sent and summed in bfloat16 or wider, within the bound.
No kernel may reach another device: no remote copies, remote signals or barrier semaphores. Data moves between devices by JAX's collectives and lax.ppermute only.
A program may use at most 192 MiB of HBM per device.

v0:
```python
import jax
import jax.numpy as jnp
from jax import lax
from jax.sharding import PartitionSpec as P

HD = 128
SEG = 128


def row_positions(document_lengths, total_rows):
    ends = jnp.cumsum(document_lengths)
    row_index = jnp.arange(total_rows, dtype=jnp.int32)
    passed = (row_index[:, None] >= ends[None, :]).astype(jnp.int32)
    return row_index - jnp.sum(passed * document_lengths[None, :], axis=1)


def rotary(values, positions, head_size):
    total_rows = values.shape[0]
    half_size = head_size // 2
    freq_index = jnp.arange(half_size, dtype=jnp.float32)
    inverse = jnp.exp(freq_index * (-2.0 / head_size) * jnp.log(jnp.float32(500000.0)))
    angles = positions.astype(jnp.float32)[:, None] * inverse[None, :]
    cosine = jnp.cos(angles)[:, None, :]
    sine_part = jnp.sin(angles)[:, None, :]
    shaped = values.reshape(total_rows, -1, head_size)
    first = shaped[..., :half_size]
    second = shaped[..., half_size:]
    turned = jnp.concatenate(
        [first * cosine - second * sine_part, second * cosine + first * sine_part], axis=-1
    )
    return turned.reshape(total_rows, -1)


def owned_term(rows_block, factor):
    return jnp.dot(rows_block, factor, preferred_element_type=jnp.float32)


def absent_term(rows_block, factor):
    return jnp.zeros((rows_block.shape[0], factor.shape[1]), jnp.float32)


def body(
    tokens,
    weight_codes,
    column_scale,
    shrink_store,
    expand_store,
    row_adapter,
    placement,
    document_lengths,
):
    gathered = lax.all_gather(tokens, "tensor", axis=0, tiled=True)
    shard_index = lax.axis_index("tensor")
    local_cols = weight_codes.shape[1]
    total_rows = gathered.shape[0]
    segment_count = total_rows // SEG
    segment_slot = placement[row_adapter[::SEG]]
    projected = (
        jnp.dot(gathered, weight_codes, preferred_element_type=jnp.float32) * column_scale[None, :]
    )
    blocks = gathered.reshape(segment_count, SEG, gathered.shape[1])
    held = shrink_store.shape[0]
    owner_index = segment_slot // held
    local_slot = segment_slot % held
    terms = []
    for segment in range(segment_count):
        shrink_full = shrink_store[local_slot[segment]]
        terms.append(
            lax.cond(
                owner_index[segment] == shard_index,
                owned_term,
                absent_term,
                blocks[segment],
                shrink_full,
            )
        )
    shrunk = lax.psum(jnp.stack(terms), "tensor").astype(jnp.bfloat16)
    expand = expand_store[segment_slot]
    update = jnp.einsum("sqr,scr->sqc", shrunk, expand, preferred_element_type=jnp.float32).reshape(
        total_rows, local_cols
    )
    positions = row_positions(document_lengths, total_rows)
    return rotary(projected + update, positions, HD).astype(jnp.bfloat16)


def solution(mesh):
    placed = (
        P(("groups", "tensor"), None),
        P(None, "tensor"),
        P("tensor"),
        P(("groups", "tensor"), None, None),
        P("groups", "tensor", None),
        P("groups"),
        P("groups"),
        P("groups"),
    )
    return jax.shard_map(
        body, mesh=mesh, in_specs=placed, out_specs=P("groups", "tensor"), check_vma=False
    )
```

profile of v0, /device:TPU:0, one launch (start us, length us, event | category | flops | bytes accessed | tf_op | source)
XLA Modules:
  0.0 256.3 jit_solution(14773031210217802687)
XLA Ops:
  6.5 0.0 copy-start
  6.5 0.0 all-gather.2.cloned.1.call-start
  6.5 0.7 all-gather.2.cloned.1.call-update
  7.3 0.8 slice.63
  8.0 1.3 gather_fusion
  9.3 0.7 fusion.34
  10.7 0.0 copy-start.3
  10.7 4.9 %copy.11 = bf16[1,16384,64]{2,1,0:T(8,128)(2,1)} copy(bf16[1,16384,64]{1,2,0:T(8,128)(2,1)} %param.23) | data formatting | bytes 4194304 | tf_op args[3]
  18.9 0.0 copy-done
  18.9 0.6 gather_fusion.1
  19.5 0.2 reduce-window.8
  19.7 0.1 select_reduce_fusion
  19.8 2.4 multiply_cosine_fusion
  22.2 118.1 %all-gather.2.cloned.1.call-done = bf16[768,16384]{1,0:T(8,128)(2,1)} async-done(((bf16[48,16384]{1,0:T(8,128)(2,1)}), bf16[768,16384]{1,0:T(8,128)(2,1)}) %all-gather.2.cloned.1.call-update) | async-done | bytes 25165840 | tf_op jit(solution)/shard_map/all_gather | solution.py:52
  140.5 0.0 copy-start.4
  140.5 70.9 %all-reduce.1 = bf16[6,128,64]{1,2,0:T(8,128)(2,1)S(1)} all-reduce(f32[6,128,64]{1,2,0:T(8,128)S(1)} %constant_dynamic-update-slice_fusion), channel_id=1, replica_groups=mesh['groups'=2,'tensor'=16] {'tensor'}, use_global_device_ids=true, to_apply=%region_12.13 | all-reduce | flops 49152 | bytes 294912 | tf_op jit(solution)/shard_map/psum | solution.py:77
  211.5 0.6 fusion.35
  212.1 32.4 %fusion.30 = f32[96,8,8,128]{3,1,2,0:T(8,128)S(1)} fusion(f32[6,128,1024]{2,1,0:T(8,128)S(1)} %fusion.35, bf16[768,16384]{1,0:T(8,128)(2,1)} %all-gather.2.cloned.1.call-done, bf16[16384,1024]{1,0:T(8,128)(2,1)} %param.21, f32[1024]{0:T(1024)S(1)} %copy-done.4), kind=kOutput, calls=%fused_computation.23 | convolution fusion | flops 25771376640 | bytes 65015808 | tf_op jit(solution)/shard_map/dot_general | solution.py:59
  244.5 0.0 copy-start.2
  244.5 0.7 copy.12
  245.3 0.2 copy-done.2
  245.5 1.4 subtract_convert_fusion
  247.0 0.9 pad_maximum_fusion
  247.8 1.6 copy.15
  (28 shorter events, 0.2 us)
Async XLA Ops:
  6.5 12.4 %copy-start = (bf16[16,1024,64]{1,2,0:T(8,128)(2,1)S(1)}, bf16[16,1024,64]{1,2,0:T(8,128)(2,1)}, u32[]{:S(2)}) copy-start(bf16[16,1024,64]{1,2,0:T(8,128)(2,1)} %param.24) | copy-start | bytes 6291460
  6.5 133.7 %all-gather.2.cloned.1.call-start = ((), (), s32[]{:S(2)}) async-start(), calls=%async_computation | async-start | bytes 26738688 | tf_op jit(solution)/shard_map/all_gather | solution.py:52
  10.7 8.8 %copy-start.3 = (s32[8]{0:T(128)S(1)}, s32[8]{0:T(128)}, u32[]{:S(2)}) copy-start(s32[8]{0:T(128)} %param.27) | copy-start | bytes 100
  140.5 71.6 %copy-start.4 = (f32[1024]{0:T(1024)S(1)}, f32[1024]{0:T(1024)}, u32[]{:S(2)}) copy-start(f32[1024]{0:T(1024)} %param.22) | copy-start | bytes 12292
  244.5 1.0 copy-start.2
  245.5 3.9 %copy-start.1 = (bf16[16,1024,64]{1,2,0:T(8,128)(2,1)S(1)}, bf16[16,1024,64]{1,2,0:T(8,128)(2,1)}, u32[]{:S(2)}) copy-start(bf16[16,1024,64]{1,2,0:T(8,128)(2,1)} %param.24) | copy-start | bytes 6291460
Sparse Core Ops, SparseCore 0:
  9.0 131.2 all-gather.1
where the time goes:
time: 255 us; the launch traced here: 256 us
  waiting for transfers between devices  119 us (47%)
  blocking collectives  70.9 us (28%)
  matrix products  33 us (13%)
  between operations  17.5 us (7%)
  local copies, waits for them, and re-layouts  10.9 us (4%)
  other arithmetic  4.99 us (2%)
    all_gather x1, waiting for transfers between devices, body(): gathered = lax.all_gather(tokens, 'tensor', axis=0, tiled=True)  118 us
    psum x1, blocking collectives, body(): shrunk = lax.psum(jnp.stack(terms), 'tensor').astype(jnp.bfloat16)  70.9 us
    dot_general x1, matrix products, body(): jnp.dot(gathered, weight_codes, preferred_element_type=jnp.float32)  32.4 us
    unnamed x18, local copies, waits for them, and re-layouts  7.51 us
  transfers between devices with their start and end apart: 1, of which 1 were waited for; matrix products, arithmetic and copies ran while one was open for 4% of the time, Pallas kernels for 0%

commit v1 on v0

v1 whole, which is shorter than its diff:
```python
import functools

import jax
import jax.numpy as jnp
from jax import lax
from jax.experimental import pallas as pl
from jax.experimental.pallas import tpu as pltpu
from jax.sharding import PartitionSpec as P

HD = 128
SEG = 128
VMEM = 48 * 1024 * 1024
F32 = jnp.float32
NT = (((1,), (1,)), ((), ()))


def row_positions(document_lengths, total_rows):
    ends = jnp.cumsum(document_lengths)
    row_index = jnp.arange(total_rows, dtype=jnp.int32)
    passed = (row_index[:, None] >= ends[None, :]).astype(jnp.int32)
    return row_index - jnp.sum(passed * document_lengths[None, :], axis=1)


def rotary_tables(positions):
    half_size = HD // 2
    freq_index = jnp.arange(half_size, dtype=F32)
    inverse = jnp.exp(freq_index * (-2.0 / HD) * jnp.log(F32(500000.0)))
    angles = positions.astype(F32)[:, None] * inverse[None, :]
    cosine, sine = jnp.cos(angles), jnp.sin(angles)
    return jnp.concatenate([cosine, cosine], 1), jnp.concatenate([-sine, sine], 1)


def shrink_kernel(x_ref, s_ref, h_in, h_out):
    @pl.when(pl.program_id(0) == 0)
    def _():
        h_out[...] = h_in[...]

    h_out[...] += lax.dot_general(x_ref[...], s_ref[...], NT, preferred_element_type=F32)


def shrink_chunk(x, shrink, offset, tile, h):
    rows, depth = x.shape
    rank = shrink.shape[0]
    whole = pl.BlockSpec((rows, rank), lambda k: (0, 0))
    return pl.pallas_call(
        shrink_kernel,
        grid=(depth // tile,),
        in_specs=[
            pl.BlockSpec((rows, tile), lambda k: (0, k)),
            pl.BlockSpec((rank, tile), lambda k: (0, k + offset // tile)),
            whole,
        ],
        out_specs=whole,
        out_shape=jax.ShapeDtypeStruct((rows, rank), F32),
        compiler_params=pltpu.CompilerParams(vmem_limit_bytes=VMEM),
        cost_estimate=pl.CostEstimate(
            flops=2 * rows * depth * 256, bytes_accessed=2 * rows * depth, transcendentals=0
        ),
        name="shrink",
    )(x, shrink, h)


def project_kernel(first, x_ref, w_ref, *refs):
    acc_out = refs[-1]

    @pl.when(pl.program_id(0) == 0)
    def _():
        acc_out[...] = jnp.zeros_like(acc_out) if first else refs[0][...]

    acc_out[...] += jnp.dot(x_ref[...], w_ref[...], preferred_element_type=F32)


def project_chunk(x, weights, offset, tile, acc):
    rows, depth = x.shape
    cols = weights.shape[1]
    whole = pl.BlockSpec((rows, cols), lambda k: (0, 0))
    first = acc is None
    return pl.pallas_call(
        functools.partial(project_kernel, first),
        grid=(depth // tile,),
        in_specs=[
            pl.BlockSpec((rows, tile), lambda k: (0, k)),
            pl.BlockSpec((tile, cols), lambda k: (k + offset // tile, 0)),
        ]
        + ([] if first else [whole]),
        out_specs=whole,
        out_shape=jax.ShapeDtypeStruct((rows, cols), F32),
        compiler_params=pltpu.CompilerParams(vmem_limit_bytes=VMEM),
        cost_estimate=pl.CostEstimate(
            flops=2 * rows * depth * cols, bytes_accessed=2 * depth * cols, transcendentals=0
        ),
        name="project",
    )(*((x, weights) if first else (x, weights, acc)))


def finish_kernel(acc_ref, scale_ref, h_ref, expand_ref, cos_ref, sin_ref, out_ref):
    update = jnp.dot(h_ref[...], expand_ref[0], preferred_element_type=F32)
    cosine, sine = cos_ref[...], sin_ref[...]
    for head in range(out_ref.shape[1] // HD):
        cut = slice(head * HD, (head + 1) * HD)
        value = acc_ref[:, cut] * scale_ref[:, cut] + update[:, cut]
        turned = value * cosine + pltpu.roll(value, HD // 2, 1) * sine
        out_ref[:, cut] = turned.astype(out_ref.dtype)


def finish(acc, scale, h, expand, cosine, sine):
    rows, cols = acc.shape
    rank = h.shape[1]
    return pl.pallas_call(
        finish_kernel,
        grid=(rows // SEG,),
        in_specs=[
            pl.BlockSpec((SEG, cols), lambda r: (r, 0)),
            pl.BlockSpec((1, cols), lambda r: (0, 0)),
            pl.BlockSpec((SEG, rank), lambda r: (r, 0)),
            pl.BlockSpec((1, rank, cols), lambda r: (r, 0, 0)),
            pl.BlockSpec((SEG, HD), lambda r: (r, 0)),
            pl.BlockSpec((SEG, HD), lambda r: (r, 0)),
        ],
        out_specs=pl.BlockSpec((SEG, cols), lambda r: (r, 0)),
        out_shape=jax.ShapeDtypeStruct((rows, cols), jnp.bfloat16),
        compiler_params=pltpu.CompilerParams(vmem_limit_bytes=VMEM),
        name="finish",
    )(acc, scale, h, expand, cosine, sine)


def spread(h, parts):
    step = 1
    while step < parts:
        pairs = [(i, i ^ step) for i in range(parts)]
        h = h + lax.ppermute(h, "tensor", pairs)
        step *= 2
    return h


def body(parts, tokens, weight_codes, column_scale, shrink_store, expand_store, row_adapter, placement, document_lengths):
    depth = tokens.shape[1]
    cuts = [0, 5 * depth // 16, 10 * depth // 16, 14 * depth // 16, depth]
    tile = depth // 16
    shard_index = lax.axis_index("tensor")
    total_rows = tokens.shape[0] * parts
    held = shrink_store.shape[0]
    rank = shrink_store.shape[2]
    segment_slot = placement[row_adapter[::SEG]]
    shrinks = jnp.swapaxes(shrink_store, 1, 2)
    expand = jnp.swapaxes(expand_store, 1, 2)[segment_slot]
    cosine, sine = rotary_tables(row_positions(document_lengths, total_rows))

    acc = None
    hs = [jnp.zeros((total_rows, rank), F32) for _ in range(held)]
    for low, high in zip(cuts[:-1], cuts[1:]):
        x = lax.all_gather(tokens[:, low:high], "tensor", axis=0, tiled=True)
        if acc is not None:
            x, acc = lax.optimization_barrier((x, acc))
        hs = [shrink_chunk(x, shrinks[i], low, tile, hs[i]) for i in range(held)]
        acc = project_chunk(x, weight_codes, low, tile, acc)
    row_slot = jnp.repeat(segment_slot, SEG, total_repeat_length=total_rows)
    h = jnp.zeros((total_rows, rank), jnp.bfloat16)
    for i in range(held):
        mine = (row_slot == shard_index * held + i)[:, None]
        h = jnp.where(mine, hs[i].astype(jnp.bfloat16), h)
    h = spread(h, parts)
    return finish(acc, column_scale[None, :], h, expand, cosine, sine)


def solution(mesh):
    placed = (
        P(("groups", "tensor"), None),
        P(None, "tensor"),
        P("tensor"),
        P(("groups", "tensor"), None, None),
        P("groups", "tensor", None),
        P("groups"),
        P("groups"),
        P("groups"),
    )
    return jax.shard_map(
        functools.partial(body, mesh.shape["tensor"]),
        mesh=mesh,
        in_specs=placed,
        out_specs=P("groups", "tensor"),
        check_vma=False,
    )
```

time: 255 us -> 308 us (1.21)
  waiting for transfers between devices: 119 us -> 196 us
  blocking collectives: 70.9 us -> 0 us
  Pallas kernels: 0 us -> 64.9 us
  matrix products: 33 us -> 0 us
  local copies, waits for them, and re-layouts: 10.9 us -> 18.5 us
  starting transfers between devices: 0.01 us -> 5.05 us
  other arithmetic: 4.99 us -> 9.61 us
  between operations: 17.5 us -> 13.3 us
    psum x1 -> x0, blocking collectives: 70.9 us -> none  [body(): shrunk = lax.psum(jnp.stack(terms), 'tensor').astype(jnp.bfloat16)]
    all_gather x1 -> x4, waiting for transfers between devices: 118 us -> 183 us  [body(): x = lax.all_gather(tokens[:, low:high], 'tensor', axis=0, tiled=True)]
    pallas_call x0 -> x9, Pallas kernels: none -> 64.9 us  [the longest x4 43.1 us: project_chunk(): pl.pallas_call(functools.partial(project_kernel, first), grid=(depth // t...]
    dot_general x2 -> x0, matrix products: 33 us -> none  [the longest x1 32.4 us: body(): jnp.dot(gathered, weight_codes, preferred_element_type=jnp.float32)]
    ppermute x0 -> x4, waiting for transfers between devices: none -> 12 us  [spread(): h = h + lax.ppermute(h, 'tensor', pairs)]
    slice x1 -> x3, local copies, waits for them, and re-layouts: 0.69 us -> 5.72 us  [body(): x = lax.all_gather(tokens[:, low:high], 'tensor', axis=0, tiled=True)]
    ppermute x0 -> x4, starting transfers between devices: none -> 4.93 us  [spread(): h = h + lax.ppermute(h, 'tensor', pairs)]
    gather x1 -> x2, other arithmetic: 0.01 us -> 3.83 us  [the longest x1 3.83 us: body(): row_slot = jnp.repeat(segment_slot, SEG, total_repeat_length=total_rows)]
  transfers between devices with their start and end apart: 1 -> 8, of which waited for: 1 -> 8; matrix products, arithmetic and copies ran while one was open for 4% -> 5% of each run, Pallas kernels for 0% -> 19%
where the time goes in v1:
time: 308 us; the launch traced here: 307 us
  waiting for transfers between devices  196 us (64%)
  Pallas kernels  64.9 us (21%)
  local copies, waits for them, and re-layouts  18.5 us (6%)
  between operations  13.3 us (4%)
  other arithmetic  9.61 us (3%)
  starting transfers between devices  5.05 us (2%)
    all_gather x4, waiting for transfers between devices, body(): x = lax.all_gather(tokens[:, low:high], 'tensor', axis=0, tiled=True)  183 us
    pallas_call x4, Pallas kernels, project_chunk(): pl.pallas_call(functools.partial(project_kernel, first), grid=(depth // t...  43.1 us
    pallas_call x4, Pallas kernels, shrink_chunk(): pl.pallas_call(shrink_kernel, grid=(depth // tile,), in_specs=[pl.BlockSp...  18.1 us
    ppermute x4, waiting for transfers between devices, spread(): h = h + lax.ppermute(h, 'tensor', pairs)  12 us
    unnamed x20, local copies, waits for them, and re-layouts  10.1 us
  transfers between devices with their start and end apart: 8, of which 8 were waited for; matrix products, arithmetic and copies ran while one was open for 5% of the time, Pallas kernels for 19%

profile of v1, /device:TPU:0, one launch (start us, length us, event | category | flops | bytes accessed | tf_op | source)
XLA Modules:
  0.0 307.1 jit_solution(13138996398342240137)
XLA Ops:
  6.5 2.3 fusion.10
  9.7 1.8 slice.32
  15.6 3.8 %fusion.8 = s32[768]{0:T(1024)S(1)} fusion(s32[1,1,6,128]{3,2,1,0:T(8,128)S(1)} %get-tuple-element.41, s32[1,1,6,128]{3,2,1,0:T(8,128)S(1)} %get-tuple-element.40, s32[]{:T(128)} %bitcast.3, s32[]{:T(128)} %bitcast.4, s32[]{:T(128)} %bitcast.5, s32[]{:T(128)} %bitcast.6, s32[]{:T(128)} %bitcast.8, s32[]{:T(128)} %bitcast.7), kind=kLoop, calls=%fused_computation.29 | loop fusion | flops 9216 | bytes 9240 | tf_op jit(solution)/shard_map/jit(_take)/gather | solution.py:157
  19.5 2.5 fusion
  22.0 62.0 %all-gather.11.cloned.1.call-done.x_ref = bf16[768,5120]{1,0:T(8,128)(2,1)} async-done(((bf16[48,5120]{1,0:T(8,128)(2,1)}), bf16[768,5120]{1,0:T(8,128)(2,1)}) %all-gather.11.cloned.1.call-update) | async-done | bytes 7864336 | tf_op jit(solution)/shard_map/all_gather | solution.py:152
  84.0 12.1 %project.4.refs_0_ = f32[768,1024]{1,0:T(8,128)S(1)} custom-call(bf16[768,5120]{1,0:T(8,128)(2,1)} %all-gather.11.cloned.1.call-done.x_ref, bf16[16384,1024]{1,0:T(8,128)(2,1)} %w_ref.7), custom_call_target="tpu_custom_call" | custom-call | flops 8053063680 | bytes 10485760 | tf_op jit(solution)/shard_map/project/pallas_call | solution.py:78
  96.1 1.7 copy-done.5
  97.7 58.5 %all-gather.9.cloned.1.call-done.x_ref = bf16[768,5120]{1,0:T(8,128)(2,1)} async-done(((bf16[48,5120]{1,0:T(8,128)(2,1)}), bf16[768,5120]{1,0:T(8,128)(2,1)}) %all-gather.9.cloned.1.call-update) | async-done | bytes 7864336 | tf_op jit(solution)/shard_map/all_gather | solution.py:152
  156.2 13.0 %project.5.refs_0_ = f32[768,1024]{1,0:T(8,128)S(1)} custom-call(bf16[768,5120]{1,0:T(8,128)(2,1)} %all-gather.9.cloned.1.call-done.x_ref, bf16[16384,1024]{1,0:T(8,128)(2,1)} %w_ref.7, f32[768,1024]{1,0:T(8,128)} %copy-done.5), custom_call_target="tpu_custom_call" | custom-call | flops 8053063680 | bytes 10485760 | tf_op jit(solution)/shard_map/project/pallas_call | solution.py:78
  169.2 1.7 copy-done.3
  170.9 47.8 %all-gather.7.cloned.1.call-done.x_ref = bf16[768,4096]{1,0:T(8,128)(2,1)} async-done(((bf16[48,4096]{1,0:T(8,128)(2,1)}), bf16[768,4096]{1,0:T(8,128)(2,1)}) %all-gather.7.cloned.1.call-update) | async-done | bytes 6291472 | tf_op jit(solution)/shard_map/all_gather | solution.py:152
  220.3 6.0 %shrink.4.h_in = f32[768,64]{1,0:T(8,128)S(1)} custom-call(bf16[768,5120]{1,0:T(8,128)(2,1)} %all-gather.11.cloned.1.call-done.x_ref, bf16[64,16384]{1,0:T(8,128)(2,1)S(1)} %bitcast.54, f32[768,64]{1,0:T(8,128)S(1)} %broadcast_in_dim.45.h_in), custom_call_target="tpu_custom_call" | custom-call | flops 2013265920 | bytes 7864320 | tf_op jit(solution)/shard_map/shrink/pallas_call | solution.py:45
  226.3 6.1 %shrink.5.h_in = f32[768,64]{1,0:T(8,128)S(1)} custom-call(bf16[768,5120]{1,0:T(8,128)(2,1)} %all-gather.9.cloned.1.call-done.x_ref, bf16[64,16384]{1,0:T(8,128)(2,1)S(1)} %bitcast.55, f32[768,64]{1,0:T(8,128)S(1)} %shrink.4.h_in), custom_call_target="tpu_custom_call" | custom-call | flops 2013265920 | bytes 7864320 | tf_op jit(solution)/shard_map/shrink/pallas_call | solution.py:45
  232.4 4.7 %shrink.6.h_in = f32[768,64]{1,0:T(8,128)S(1)} custom-call(bf16[768,4096]{1,0:T(8,128)(2,1)} %all-gather.7.cloned.1.call-done.x_ref, bf16[64,16384]{1,0:T(8,128)(2,1)S(1)} %bitcast.56, f32[768,64]{1,0:T(8,128)S(1)} %shrink.5.h_in), custom_call_target="tpu_custom_call" | custom-call | flops 1610612736 | bytes 6291456 | tf_op jit(solution)/shard_map/shrink/pallas_call | solution.py:45
  237.1 11.2 %project.6.refs_0_ = f32[768,1024]{1,0:T(8,128)S(1)} custom-call(bf16[768,4096]{1,0:T(8,128)(2,1)} %all-gather.7.cloned.1.call-done.x_ref, bf16[16384,1024]{1,0:T(8,128)(2,1)} %w_ref.7, f32[768,1024]{1,0:T(8,128)} %copy-done.3), custom_call_target="tpu_custom_call" | custom-call | flops 6442450944 | bytes 8388608 | tf_op jit(solution)/shard_map/project/pallas_call | solution.py:78
  249.9 14.7 %all-gather.5.cloned.1.call-done.x_ref = bf16[768,2048]{1,0:T(8,128)(2,1)} async-done(((bf16[48,2048]{1,0:T(8,128)(2,1)}), bf16[768,2048]{1,0:T(8,128)(2,1)}) %all-gather.5.cloned.1.call-update) | async-done | bytes 3145744 | tf_op jit(solution)/shard_map/all_gather | solution.py:152
  266.3 1.9 copy-done.6
  272.7 6.0 %collective-permute-done.1 = bf16[768,64]{1,0:T(8,128)(2,1)} collective-permute-done((bf16[768,64]{1,0:T(8,128)(2,1)S(1)}, bf16[768,64]{1,0:T(8,128)(2,1)}, u32[]{:S(2)}, u32[]{:S(2)}) %collective-permute-start.1) | collective-permute-done | bytes 98336 | tf_op jit(solution)/shard_map/ppermute | solution.py:131
  279.7 2.0 collective-permute-start.2
  283.1 3.0 collective-permute-done.2
  286.2 2.0 collective-permute-start.3
  288.2 6.9 %project.7.acc_ref = f32[768,1024]{1,0:T(8,128)S(1)} custom-call(bf16[768,2048]{1,0:T(8,128)(2,1)} %all-gather.5.cloned.1.call-done.x_ref, bf16[16384,1024]{1,0:T(8,128)(2,1)} %w_ref.7, f32[768,1024]{1,0:T(8,128)} %copy-done.4), custom_call_target="tpu_custom_call" | custom-call | flops 3221225472 | bytes 4194304 | tf_op jit(solution)/shard_map/project/pallas_call | solution.py:78
  295.1 1.8 collective-permute-done.3
  297.0 3.6 %finish.1 = bf16[768,1024]{1,0:T(8,128)(2,1)} custom-call(f32[768,1024]{1,0:T(8,128)S(1)} %project.7.acc_ref, f32[1,1024]{1,0:T(1,128)S(1)} %bitcast.58, bf16[768,64]{1,0:T(8,128)(2,1)S(1)} %add.86.h_ref, bf16[6,64,1024]{2,1,0:T(8,128)(2,1)S(1)} %gather_fusion.1, f32[768,128]{1,0:T(8,128)S(1)} %get-tuple-element.42.cos_ref, ...), custom_call_target="tpu_custom_call" | custom-call | tf_op jit(solution)/shard_map/finish/pallas_call | solution.py:109
  (51 shorter events, 16.8 us)
Async XLA Ops:
  6.5 265.5 %copy-start = (bf16[16,1024,64]{1,2,0:T(8,128)(2,1)S(1)}, bf16[16,1024,64]{1,2,0:T(8,128)(2,1)}, u32[]{:S(2)}) copy-start(bf16[16,1024,64]{1,2,0:T(8,128)(2,1)} %param.14) | copy-start | bytes 6291460
  6.5 7.5 %copy-start.8 = (s32[16]{0:T(128)S(1)}, s32[16]{0:T(128)}, u32[]{:S(2)}) copy-start(s32[16]{0:T(128)} %param.16) | copy-start | bytes 196
  6.5 8.1 %copy-start.9 = (s32[8]{0:T(128)S(1)}, s32[8]{0:T(128)}, u32[]{:S(2)}) copy-start(s32[8]{0:T(128)} %param.17) | copy-start | bytes 100
  6.5 77.4 %all-gather.11.cloned.1.call-start = ((), (), s32[]{:S(2)}) async-start(), calls=%async_computation.3 | async-start | bytes 8355840 | tf_op jit(solution)/shard_map/all_gather | solution.py:152
  8.9 147.3 %all-gather.9.cloned.1.call-start = ((), (), s32[]{:S(2)}) async-start(), calls=%async_computation.2 | async-start | bytes 8355840 | tf_op jit(solution)/shard_map/all_gather | solution.py:152
  9.7 209.1 %all-gather.7.cloned.1.call-start = ((), (), s32[]{:S(2)}) async-start(), calls=%async_computation.1 | async-start | bytes 6684672 | tf_op jit(solution)/shard_map/all_gather | solution.py:152
  11.5 253.2 %all-gather.5.cloned.1.call-start = ((), (), s32[]{:S(2)}) async-start(), calls=%async_computation | async-start | bytes 3342336 | tf_op jit(solution)/shard_map/all_gather | solution.py:152
  96.0 1.7 copy-start.5
  169.2 1.7 copy-start.3
  218.7 1.6 copy-start.1
  248.3 1.6 copy-start.4
  264.7 1.6 copy-start.2
  266.3 1.9 copy-start.6
  269.8 1.5 collective-permute-start
  271.4 7.2 %collective-permute-start.1 = (bf16[768,64]{1,0:T(8,128)(2,1)S(1)}, bf16[768,64]{1,0:T(8,128)(2,1)}, u32[]{:S(2)}, u32[]{:S(2)}) collective-permute-start(bf16[768,64]{1,0:T(8,128)(2,1)S(1)} %fusion.12), channel_id=1, source_target_pairs={{0,2},{1,3},{2,0},{3,1},{4,6},{5,7},{6,4},{7,5},{8,10},{9,11},{10,... | collective-permute-start | bytes 294920 | tf_op jit(solution)/shard_map/ppermute | solution.py:131
  279.7 6.5 %collective-permute-start.2 = (bf16[768,64]{1,0:T(8,128)(2,1)S(1)}, bf16[768,64]{1,0:T(8,128)(2,1)S(1)}, u32[]{:S(2)}, u32[]{:S(2)}) collective-permute-start(bf16[768,64]{1,0:T(8,128)(2,1)S(1)} %add.84), channel_id=1, source_target_pairs={{0,4},{1,5},{2,6},{3,7},{4,0},{5,1},{6,2},{7,3},{8,12},{9,13},{10,... | collective-permute-start | bytes 294920 | tf_op jit(solution)/shard_map/ppermute | solution.py:131
  286.2 10.8 %copy-start.7 = (f32[1024]{0:T(1024)S(1)}, f32[1024]{0:T(1024)}, u32[]{:S(2)}) copy-start(f32[1024]{0:T(1024)} %param.12) | copy-start | bytes 12292
  286.2 10.7 %collective-permute-start.3 = (bf16[768,64]{1,0:T(8,128)(2,1)S(1)}, bf16[768,64]{1,0:T(8,128)(2,1)S(1)}, u32[]{:S(2)}, u32[]{:S(2)}) collective-permute-start(bf16[768,64]{1,0:T(8,128)(2,1)S(1)} %add.85), channel_id=1, source_target_pairs={{0,8},{1,9},{2,10},{3,11},{4,12},{5,13},{6,14},{7,15},{8,0},{9,1},... | collective-permute-start | bytes 294920 | tf_op jit(solution)/shard_map/ppermute | solution.py:131
Sparse Core Ops, SparseCore 0:
  9.7 74.2 all-gather.10
  86.3 69.9 all-gather.8
  158.5 60.1 all-gather.6
  220.9 43.7 all-gather.4

commit v2 on v1

v2 whole, which is shorter than its diff:
```python
import functools

import jax
import jax.numpy as jnp
import numpy as np
from jax import lax
from jax.experimental import pallas as pl
from jax.experimental.pallas import tpu as pltpu
from jax.sharding import PartitionSpec as P

HD = 128
SEG = 128
VMEM = 40 * 1024 * 1024
F32 = jnp.float32
BF16 = jnp.bfloat16
NT = (((1,), (1,)), ((), ()))
PARAMS = pltpu.CompilerParams(vmem_limit_bytes=VMEM)
SNAKE = (0, 2, 4, 6, 7, 5, 3, 1)
ROUNDS = len(SNAKE) // 2


def row_positions(document_lengths, total_rows):
    ends = jnp.cumsum(document_lengths)
    row_index = jnp.arange(total_rows, dtype=jnp.int32)
    passed = (row_index[:, None] >= ends[None, :]).astype(jnp.int32)
    return row_index - jnp.sum(passed * document_lengths[None, :], axis=1)


def rotary_tables(positions):
    half_size = HD // 2
    freq_index = jnp.arange(half_size, dtype=F32)
    inverse = jnp.exp(freq_index * (-2.0 / HD) * jnp.log(F32(500000.0)))
    angles = positions.astype(F32)[:, None] * inverse[None, :]
    cosine, sine = jnp.cos(angles), jnp.sin(angles)
    return jnp.concatenate([cosine, cosine], 1), jnp.concatenate([-sine, sine], 1)


def rotate(value, cosine, sine):
    return value * cosine + pltpu.roll(value, HD // 2, 1) * sine


def shrink_kernel(x_ref, s_ref, h_out):
    @pl.when(pl.program_id(0) == 0)
    def _():
        h_out[...] = jnp.zeros_like(h_out)

    h_out[...] += lax.dot_general(x_ref[...], s_ref[...], NT, preferred_element_type=F32)


def shrink_all(x, shrink, tile):
    rows, depth = x.shape
    rank = shrink.shape[0]
    return pl.pallas_call(
        shrink_kernel,
        grid=(depth // tile,),
        in_specs=[
            pl.BlockSpec((rows, tile), lambda k: (0, k)),
            pl.BlockSpec((rank, tile), lambda k: (0, k)),
        ],
        out_specs=pl.BlockSpec((rows, rank), lambda k: (0, 0)),
        out_shape=jax.ShapeDtypeStruct((rows, rank), F32),
        compiler_params=PARAMS,
        name="shrink",
    )(x, shrink)


def project_kernel(x_ref, w_ref, acc_out):
    @pl.when(pl.program_id(0) == 0)
    def _():
        acc_out[...] = jnp.zeros_like(acc_out)

    acc_out[...] += jnp.dot(x_ref[...], w_ref[...], preferred_element_type=F32)


def project_all(x, weights, tile):
    rows, depth = x.shape
    cols = weights.shape[1]
    return pl.pallas_call(
        project_kernel,
        grid=(depth // tile,),
        in_specs=[
            pl.BlockSpec((rows, tile), lambda k: (0, k)),
            pl.BlockSpec((tile, cols), lambda k: (k, 0)),
        ],
        out_specs=pl.BlockSpec((rows, cols), lambda k: (0, 0)),
        out_shape=jax.ShapeDtypeStruct((rows, cols), F32),
        compiler_params=PARAMS,
        name="project",
    )(x, weights)


def segment_finish_kernel(acc_ref, scale_ref, h_ref, expand_ref, cos_ref, sin_ref, out_ref):
    update = jnp.dot(h_ref[...], expand_ref[0], preferred_element_type=F32)
    for head in range(out_ref.shape[1] // HD):
        cut = slice(head * HD, (head + 1) * HD)
        value = acc_ref[:, cut] * scale_ref[:, cut] + update[:, cut]
        out_ref[:, cut] = rotate(value, cos_ref[...], sin_ref[...]).astype(out_ref.dtype)


def segment_finish(acc, scale, h, expand, cosine, sine):
    rows, cols = acc.shape
    rank = h.shape[1]
    return pl.pallas_call(
        segment_finish_kernel,
        grid=(rows // SEG,),
        in_specs=[
            pl.BlockSpec((SEG, cols), lambda r: (r, 0)),
            pl.BlockSpec((1, cols), lambda r: (0, 0)),
            pl.BlockSpec((SEG, rank), lambda r: (r, 0)),
            pl.BlockSpec((1, rank, cols), lambda r: (r, 0, 0)),
            pl.BlockSpec((SEG, HD), lambda r: (r, 0)),
            pl.BlockSpec((SEG, HD), lambda r: (r, 0)),
        ],
        out_specs=pl.BlockSpec((SEG, cols), lambda r: (r, 0)),
        out_shape=jax.ShapeDtypeStruct((rows, cols), BF16),
        compiler_params=PARAMS,
        name="finish",
    )(acc, scale, h, expand, cosine, sine)


def spread(h, parts):
    step = 1
    while step < parts:
        h = h + lax.ppermute(h, "tensor", [(i, i ^ step) for i in range(parts)])
        step *= 2
    return h


def gather_plan(parts, tokens, weights, scale, shrinks, expands, segment_slot, cosine, sine):
    held, rank, depth = shrinks.shape
    tile = depth // 16
    x = lax.all_gather(tokens, "tensor", axis=0, tiled=True)
    row_slot = jnp.repeat(segment_slot, SEG, total_repeat_length=x.shape[0])
    h = jnp.zeros((x.shape[0], rank), BF16)
    for i in range(held):
        mine = (row_slot == lax.axis_index("tensor") * held + i)[:, None]
        h = jnp.where(mine, shrink_all(x, shrinks[i], tile).astype(BF16), h)
    h = spread(h, parts)
    acc = project_all(x, weights, tile)
    return segment_finish(acc, scale, h, expands[segment_slot], cosine, sine)


def block_owners():
    chips = len(SNAKE)
    owners = np.zeros((2 * chips, 2 * chips), np.int32)
    for place, chip in enumerate(SNAKE):
        for core in (0, 1):
            row = []
            for r in range(1, ROUNDS):
                before, after = SNAKE[place - r], SNAKE[(place + r) % chips]
                row += [2 * before + core, 2 * after + core, 2 * before + 1 - core, 2 * after + 1 - core]
            across = SNAKE[(place + ROUNDS) % chips]
            row += [2 * chip + core, 2 * chip + 1 - core, 2 * across + core, 2 * across + 1 - core]
            owners[2 * chip + core] = row
    return owners


def ring_pairs(ways):
    chips = len(SNAKE)
    pairs = []
    for place, chip in enumerate(SNAKE):
        for core in (0, 1):
            pairs.append((2 * chip + core, 2 * SNAKE[(place + ways[core]) % chips] + core))
    return pairs


def block_kernel(count, fresh, ranked, *refs):
    xs, refs = refs[:count], refs[count:]
    w_ref, refs = refs[0], refs[1:]
    if ranked:
        s_ref, refs = refs[0], refs[1:]
    acc_in, refs = refs[0], refs[1:]
    if ranked and not fresh:
        h_in, refs = refs[0], refs[1:]
    acc_out = refs[0]
    rows = xs[0].shape[0]

    @pl.when(pl.program_id(0) == 0)
    def _():
        acc_out[...] = jnp.zeros_like(acc_out) if fresh else acc_in[...]
        if ranked:
            refs[1][...] = jnp.zeros_like(refs[1]) if fresh else h_in[...]

    x = jnp.concatenate([ref[...] for ref in xs], 0)
    acc_out[...] += jnp.dot(x, w_ref[...], preferred_element_type=F32).reshape(acc_out.shape)
    if ranked:
        refs[1][...] += lax.dot_general(x, s_ref[...], NT, preferred_element_type=F32)


def block_product(xs, weights, shrink, low, tile, total, place, h, ranked):
    count = len(xs)
    rows, depth = xs[0].shape
    cols = weights.shape[1]
    rank = shrink.shape[0]
    fresh = low == 0
    skip = low // tile
    block = pl.BlockSpec((count, rows, cols), lambda k: (place // count, 0, 0))
    ranks = pl.BlockSpec((count * rows, rank), lambda k: (0, 0))
    operands = list(xs) + [weights]
    specs = [pl.BlockSpec((rows, tile), lambda k: (0, k))] * count
    specs += [pl.BlockSpec((tile, cols), lambda k: (k + skip, 0))]
    if ranked:
        operands.append(shrink)
        specs.append(pl.BlockSpec((rank, tile), lambda k: (0, k + skip)))
    aliases = {len(operands): 0}
    operands.append(total)
    specs.append(pl.BlockSpec(memory_space=pl.ANY) if fresh else block)
    if ranked and not fresh:
        operands.append(h)
        specs.append(ranks)
    outs = [jax.ShapeDtypeStruct(total.shape, F32)]
    out_specs = [block]
    if ranked:
        outs.append(jax.ShapeDtypeStruct((count * rows, rank), F32))
        out_specs.append(ranks)
    result = pl.pallas_call(
        functools.partial(block_kernel, count, fresh, ranked),
        grid=(depth // tile,),
        in_specs=specs,
        out_specs=out_specs,
        out_shape=outs,
        input_output_aliases=aliases,
        compiler_params=PARAMS,
        cost_estimate=pl.CostEstimate(
            flops=2 * count * rows * depth * cols, bytes_accessed=2 * depth * cols, transcendentals=0
        ),
        name="blocks",
    )(*operands)
    return result if ranked else (result[0], h)


def rank_kernel(counts, owners_ref, slot_ref, xa_ref, xb_ref, s_ref, *refs):
    h_refs, out_ref, grown, placed = refs[: len(counts)], refs[-3], refs[-2], refs[-1]
    step = pl.program_id(0)
    rows = xa_ref.shape[0]

    @pl.when(step == 0)
    def _():
        grown[...] = h_refs[-1][...]

    x = jnp.concatenate([xa_ref[...], xb_ref[...]], 0)
    grown[...] += lax.dot_general(x, s_ref[...], NT, preferred_element_type=F32)

    @pl.when(step == pl.num_programs(0) - 1)
    def _():
        block = 0
        for group, count in enumerate(counts):
            source = grown if group == len(counts) - 1 else h_refs[group]
            for i in range(count):
                to = pl.multiple_of(owners_ref[block] * rows, 16)
                placed[pl.ds(to, rows), :] = source[i * rows : (i + 1) * rows, :]
                block += 1
        pieces = []
        for segment in range(placed.shape[0] // SEG):
            piece = placed[segment * SEG : (segment + 1) * SEG, :]
            pieces.append(jnp.where(slot_ref[segment] == slot_ref[slot_ref.shape[0] - 1], piece, 0.0))
        half = len(pieces) // 2
        left, right = jnp.concatenate(pieces[:half], 0), jnp.concatenate(pieces[half:], 0)
        out_ref[...] = jnp.concatenate([left, right], 1).astype(out_ref.dtype)


def rank_terms(owners, slots, xs, shrink, low, tile, hs):
    rows, depth = xs[0].shape
    rank = shrink.shape[0]
    counts = [h.shape[0] // rows for h in hs]
    total_rows = sum(counts) * rows
    skip = low // tile
    whole = [pl.BlockSpec(h.shape, lambda k, *_: (0, 0)) for h in hs]
    return pl.pallas_call(
        functools.partial(rank_kernel, counts),
        grid_spec=pltpu.PrefetchScalarGridSpec(
            num_scalar_prefetch=2,
            grid=(depth // tile,),
            in_specs=[pl.BlockSpec((rows, tile), lambda k, *_: (0, k))] * 2
            + [pl.BlockSpec((rank, tile), lambda k, *_: (0, k + skip))]
            + whole,
            out_specs=pl.BlockSpec((total_rows // 2, 2 * rank), lambda k, *_: (0, 0)),
            scratch_shapes=[pltpu.VMEM(hs[-1].shape, F32), pltpu.VMEM((total_rows, rank), F32)],
        ),
        out_shape=jax.ShapeDtypeStruct((total_rows // 2, 2 * rank), BF16),
        compiler_params=PARAMS,
        name="ranks",
    )(owners, slots, *xs, shrink, *hs)


def block_finish_kernel(blocks, segments, places_ref, slot_ref, *refs):
    accs, refs = refs[:blocks], refs[blocks:]
    expands, refs = refs[:segments], refs[segments:]
    scale_ref, h_ref, cos_ref, sin_ref, out_ref, update = refs
    rank = h_ref.shape[1] // 2
    h = jnp.where(pl.program_id(0) == 0, h_ref[:, :rank], h_ref[:, rank:])
    for segment in range(segments):
        cut = slice(segment * SEG, (segment + 1) * SEG)
        update[cut, :] = jnp.dot(h[cut], expands[segment][0], preferred_element_type=F32)
    rows = accs[0].shape[1]
    for block in range(blocks):
        at = slice(block * rows, (block + 1) * rows)
        cosine, sine = cos_ref[at, :], sin_ref[at, :]
        for head in range(out_ref.shape[1] // HD):
            cut = slice(head * HD, (head + 1) * HD)
            value = accs[block][0, :, cut] * scale_ref[:, cut] + update[at, cut]
            out_ref[at, cut] = rotate(value, cosine, sine).astype(out_ref.dtype)


def block_finish(places, slots, total, expands, scale, h, cosine, sine):
    blocks, rows, cols = total.shape
    half = blocks // 2
    half_rows = half * rows
    segments = half_rows // SEG
    rank = expands.shape[1]

    def acc_at(i):
        return pl.BlockSpec((1, rows, cols), lambda g, places, slots: (places[g * half + i], 0, 0))

    def expand_at(i):
        return pl.BlockSpec((1, rank, cols), lambda g, places, slots: (slots[g * segments + i], 0, 0))

    half_of = lambda width: pl.BlockSpec((half_rows, width), lambda g, *_: (g, 0))
    return pl.pallas_call(
        functools.partial(block_finish_kernel, half, segments),
        grid_spec=pltpu.PrefetchScalarGridSpec(
            num_scalar_prefetch=2,
            grid=(2,),
            in_specs=[acc_at(i) for i in range(half)]
            + [expand_at(i) for i in range(segments)]
            + [
                pl.BlockSpec((1, cols), lambda g, *_: (0, 0)),
                pl.BlockSpec(h.shape, lambda g, *_: (0, 0)),
                half_of(HD),
                half_of(HD),
            ],
            out_specs=half_of(cols),
            scratch_shapes=[pltpu.VMEM((half_rows, cols), F32)],
        ),
        out_shape=jax.ShapeDtypeStruct((blocks * rows, cols), BF16),
        compiler_params=PARAMS,
        name="finish",
    )(places, slots, *([total] * half), *([expands] * segments), scale, h, cosine, sine)


def ring_plan(parts, tokens, weights, scale, shrinks, expands, segment_slot, cosine, sine):
    rows, depth = tokens.shape
    tile = depth // 16
    cuts = [0, depth // 2, depth]
    spans = list(zip(cuts[:-1], cuts[1:]))
    me = lax.axis_index("tensor")
    owners_table = block_owners()
    owners = jnp.asarray(owners_table)[me]
    places = jnp.asarray(np.argsort(owners_table, axis=1).astype(np.int32))[me]
    slots = jnp.concatenate([segment_slot, me[None].astype(jnp.int32)])
    shrink = shrinks[0]
    send = lambda value, pairs: lax.ppermute(value, "tensor", pairs)
    swap = lambda value: send(value, [(i, i ^ 1) for i in range(parts)])
    onward, back = ring_pairs((1, 1)), ring_pairs((-1, -1))
    across = ring_pairs((1, -1))

    own = [tokens[:, low:high] for low, high in spans]
    total = jnp.zeros((parts, rows, weights.shape[1]), F32)
    hs = {}

    def multiply(stage, xs, total):
        j, r = stage
        low = spans[j][0]
        last = r == ROUNDS and j == len(spans) - 1
        place = {0: 12, ROUNDS: 14}.get(r, 4 * (r - 1))
        h = None
        if last:
            order = [hs[i] for i in range(1, ROUNDS)] + [hs[0], hs[ROUNDS]]
            h = rank_terms(owners, slots, xs, shrink, low, tile, order)
        total, hs[r] = block_product(xs, weights, shrink, low, tile, total, place, hs.get(r), not last)
        return total, h

    arriving = {(j, 1): [send(part, onward), send(part, back)] for j, part in enumerate(own)}
    waiting = [((j, 0), [part, swap(part)]) for j, part in enumerate(own)]
    for r in range(1, ROUNDS + 1):
        for j in range(len(spans)):
            arrived = arriving.pop((j, r))
            arrived, total = lax.optimization_barrier((arrived, total))
            if r < ROUNDS - 1:
                arriving[j, r + 1] = [send(arrived[0], onward), send(arrived[1], back)]
            elif r == ROUNDS - 1:
                arriving[j, r + 1] = [send(jnp.where(me % 2 == 0, *arrived), across)]
            waiting.append(((j, r), arrived + [swap(part) for part in arrived]))
            stage, xs = waiting.pop(0)
            if r < ROUNDS:
                xs, _ = lax.optimization_barrier((xs, arrived))
            total, _ = multiply(stage, xs, total)
    for stage, xs in waiting:
        total, h = multiply(stage, xs, total)
    h = spread(h, parts)
    return block_finish(places, segment_slot, total, expands, scale, h, cosine, sine)


def body(parts, tokens, weight_codes, column_scale, shrink_store, expand_store, row_adapter, placement, document_lengths):
    rows = tokens.shape[0]
    total_rows = rows * parts
    segment_slot = placement[row_adapter[::SEG]]
    shrinks = jnp.swapaxes(shrink_store, 1, 2)
    expands = jnp.swapaxes(expand_store, 1, 2)
    cosine, sine = rotary_tables(row_positions(document_lengths, total_rows))
    ring = parts == 2 * len(SNAKE) and rows % 16 == 0 and shrinks.shape[0] == 1 and total_rows % (2 * SEG) == 0
    plan = ring_plan if ring else gather_plan
    return plan(parts, tokens, weight_codes, column_scale[None, :], shrinks, expands, segment_slot, cosine, sine)


def solution(mesh):
    placed = (
        P(("groups", "tensor"), None),
        P(None, "tensor"),
        P("tensor"),
        P(("groups", "tensor"), None, None),
        P("groups", "tensor", None),
        P("groups"),
        P("groups"),
        P("groups"),
    )
    return jax.shard_map(
        functools.partial(body, mesh.shape["tensor"]),
        mesh=mesh,
        in_specs=placed,
        out_specs=P("groups", "tensor"),
        check_vma=False,
    )
```

time: 308 us -> 209 us (0.68)
  waiting for transfers between devices: 196 us -> 51.7 us
  Pallas kernels: 64.9 us -> 110 us
  starting transfers between devices: 5.05 us -> 26.2 us
  between operations: 13.3 us -> 0.4 us
  other arithmetic: 9.61 us -> 4.63 us
  local copies, waits for them, and re-layouts: 18.5 us -> 14.3 us
    all_gather x4 -> x0, waiting for transfers between devices: 183 us -> none  [body(): x = lax.all_gather(tokens[:, low:high], 'tensor', axis=0, tiled=True)]
    pallas_call x9 -> x12, Pallas kernels: 64.9 us -> 110 us  [the longest x10 105 us: block_product(): pl.pallas_call(functools.partial(block_kernel, count, fresh, ranked), gri...]
    ppermute x4 -> x34, waiting for transfers between devices: 12 us -> 51.7 us  [the longest x30 45.3 us: ring_plan(): send = lambda value, pairs: lax.ppermute(value, 'tensor', pairs)]
    ppermute x4 -> x34, starting transfers between devices: 4.93 us -> 26.2 us  [the longest x30 21 us: ring_plan(): send = lambda value, pairs: lax.ppermute(value, 'tensor', pairs)]
    slice x3 -> x1, local copies, waits for them, and re-layouts: 5.72 us -> 1.62 us  [ring_plan(): own = [tokens[:, low:high] for low, high in spans]]
    gather x2 -> x0, other arithmetic: 3.83 us -> none  [the longest x1 3.83 us: body(): row_slot = jnp.repeat(segment_slot, SEG, total_repeat_length=total_rows)]
    unnamed x20 -> x36, local copies, waits for them, and re-layouts: 10.1 us -> 9.54 us
  transfers between devices with their start and end apart: 8 -> 34, of which waited for: 8 -> 10; matrix products, arithmetic and copies ran while one was open for 5% -> 4% of each run, Pallas kernels for 19% -> 50%
where the time goes in v2:
time: 209 us; the launch traced here: 207 us
  Pallas kernels  110 us (53%)
  waiting for transfers between devices  51.7 us (25%)
  starting transfers between devices  26.2 us (13%)
  local copies, waits for them, and re-layouts  14.3 us (7%)
  other arithmetic  4.63 us (2%)
    pallas_call x10, Pallas kernels, block_product(): pl.pallas_call(functools.partial(block_kernel, count, fresh, ranked), gri...  105 us
    ppermute x30, waiting for transfers between devices, ring_plan(): send = lambda value, pairs: lax.ppermute(value, 'tensor', pairs)  45.3 us
    ppermute x30, starting transfers between devices, ring_plan(): send = lambda value, pairs: lax.ppermute(value, 'tensor', pairs)  21 us
    unnamed x36, local copies, waits for them, and re-layouts  9.54 us
    ppermute x4, waiting for transfers between devices, spread(): h = h + lax.ppermute(h, 'tensor', [(i, i ^ step) for i in range(parts)])  6.46 us
    ppermute x4, starting transfers between devices, spread(): h = h + lax.ppermute(h, 'tensor', [(i, i ^ step) for i in range(parts)])  5.19 us
  transfers between devices with their start and end apart: 34, of which 10 were waited for; matrix products, arithmetic and copies ran while one was open for 4% of the time, Pallas kernels for 50%

profile of v2, /device:TPU:0, one launch (start us, length us, event | category | flops | bytes accessed | tf_op | source)
XLA Modules:
  0.0 207.4 jit_solution(5805185785743454568)
XLA Ops:
  1.6 3.1 %collective-permute-start.3 = (bf16[48,8192]{1,0:T(8,128)(2,1)S(1)}, bf16[48,8192]{1,0:T(8,128)(2,1)S(1)}, u32[]{:S(2)}, u32[]{:S(2)}) collective-permute-start(bf16[48,8192]{1,0:T(8,128)(2,1)S(1)} %get-tuple-element.67.refs_0_), channel_id=1, source_target_pairs={{0,4},{1,5},{4,8},{5,9},{8,12},{9,13},{12,14},{13,15},{14,10},{15,... | collective-permute-start | bytes 2359304 | tf_op jit(solution)/shard_map/ppermute | solution.py:352
  4.7 2.0 collective-permute-start
  6.7 16.3 %collective-permute-done.3.refs_0_ = bf16[48,8192]{1,0:T(8,128)(2,1)S(1)} collective-permute-done((bf16[48,8192]{1,0:T(8,128)(2,1)S(1)}, bf16[48,8192]{1,0:T(8,128)(2,1)S(1)}, u32[]{:S(2)}, u32[]{:S(2)}) %collective-permute-start.3) | collective-permute-done | bytes 786464 | tf_op jit(solution)/shard_map/ppermute | solution.py:352
  23.0 2.1 %collective-permute-done.4.refs_1_ = bf16[48,8192]{1,0:T(8,128)(2,1)S(1)} collective-permute-done((bf16[48,8192]{1,0:T(8,128)(2,1)S(1)}, bf16[48,8192]{1,0:T(8,128)(2,1)S(1)}, u32[]{:S(2)}, u32[]{:S(2)}) %collective-permute-start.4) | collective-permute-done | bytes 786464 | tf_op jit(solution)/shard_map/ppermute | solution.py:352
  25.2 2.0 collective-permute-start.9
  27.2 12.8 %collective-permute-done.refs_0_ = bf16[48,8192]{1,0:T(8,128)(2,1)} collective-permute-done((bf16[48,8192]{1,0:T(8,128)(2,1)S(1)}, bf16[48,8192]{1,0:T(8,128)(2,1)}, u32[]{:S(2)}, u32[]{:S(2)}) %collective-permute-start) | collective-permute-done | bytes 786464 | tf_op jit(solution)/shard_map/ppermute | solution.py:352
  40.0 2.1 %collective-permute-done.1.refs_1_ = bf16[48,8192]{1,0:T(8,128)(2,1)} collective-permute-done((bf16[48,8192]{1,0:T(8,128)(2,1)S(1)}, bf16[48,8192]{1,0:T(8,128)(2,1)}, u32[]{:S(2)}, u32[]{:S(2)}) %collective-permute-start.1) | collective-permute-done | bytes 786464 | tf_op jit(solution)/shard_map/ppermute | solution.py:352
  42.5 9.7 %blocks.10 = (f32[16,48,1024]{2,1,0:T(8,128)S(1)}, f32[96,64]{1,0:T(8,128)S(1)}) custom-call(bf16[48,8192]{1,0:T(8,128)(2,1)S(1)} %get-tuple-element.67.refs_0_, bf16[48,8192]{1,0:T(8,128)(2,1)S(1)} %collective-permute-done.2.refs_1_, bf16[16384,1024]{1,0:T(8,128)(2,1)} %refs_2_.7, bf16[64,16384]{1,0:T(8,128)(2,1)S(1)} %bitcast.12, ...), custom_call_target="tpu_custom_call", output_to_operand_aliasing={{0}: (4, {})} | custom-call | flops 1610612736 | bytes 16777216 | tf_op jit(solution)/shard_map/blocks/pallas_call | solution.py:216
  53.9 3.5 %collective-permute-done.10.refs_1_ = bf16[48,8192]{1,0:T(8,128)(2,1)S(1)} collective-permute-done((bf16[48,8192]{1,0:T(8,128)(2,1)S(1)}, bf16[48,8192]{1,0:T(8,128)(2,1)S(1)}, u32[]{:S(2)}, u32[]{:S(2)}) %collective-permute-start.10) | collective-permute-done | bytes 786464 | tf_op jit(solution)/shard_map/ppermute | solution.py:352
  57.7 9.8 %blocks.11 = (f32[16,48,1024]{2,1,0:T(8,128)S(1)}, f32[96,64]{1,0:T(8,128)S(1)}) custom-call(bf16[48,8192]{1,0:T(8,128)(2,1)S(1)} %get-tuple-element.73.refs_0_, bf16[48,8192]{1,0:T(8,128)(2,1)S(1)} %collective-permute-done.11.refs_1_, bf16[16384,1024]{1,0:T(8,128)(2,1)} %refs_2_.7, bf16[64,16384]{1,0:T(8,128)(2,1)S(1)} %bitcast.13, ...), custom_call_target="tpu_custom_call", output_to_operand_aliasing={{0}: (4, {})} | custom-call | flops 1610612736 | bytes 16777216 | tf_op jit(solution)/shard_map/blocks/pallas_call | solution.py:216
  82.8 10.6 %blocks.12 = (f32[16,48,1024]{2,1,0:T(8,128)S(1)}, f32[192,64]{1,0:T(8,128)S(1)}) custom-call(bf16[48,8192]{1,0:T(8,128)(2,1)S(1)} %copy-done.9, bf16[48,8192]{1,0:T(8,128)(2,1)S(1)} %copy-done.11, bf16[48,8192]{1,0:T(8,128)(2,1)S(1)} %copy-done.13, bf16[48,8192]{1,0:T(8,128)(2,1)S(1)} %copy-done.15, ...), custom_call_target="tpu_custom_call", output_to_operand_aliasing={{0}: (6, {})} | custom-call | flops 3221225472 | bytes 16777216 | tf_op jit(solution)/shard_map/blocks/pallas_call | solution.py:216
  97.8 11.4 %blocks.13 = (f32[16,48,1024]{2,1,0:T(8,128)S(1)}, f32[192,64]{1,0:T(8,128)S(1)}) custom-call(bf16[48,8192]{1,0:T(8,128)(2,1)} %collective-permute-done.refs_0_, bf16[48,8192]{1,0:T(8,128)(2,1)} %collective-permute-done.1.refs_1_, bf16[48,8192]{1,0:T(8,128)(2,1)} %collective-permute-done.18.refs_2_, ...), custom_call_target="tpu_custom_call", output_to_operand_aliasing={{0}: (6, {})} | custom-call | flops 3221225472 | bytes 16777216 | tf_op jit(solution)/shard_map/blocks/pallas_call | solution.py:216
  109.8 11.0 %blocks.14 = (f32[16,48,1024]{2,1,0:T(8,128)S(1)}, f32[192,64]{1,0:T(8,128)S(1)}) custom-call(bf16[48,8192]{1,0:T(8,128)(2,1)} %collective-permute-done.9.refs_0_, bf16[48,8192]{1,0:T(8,128)(2,1)S(1)} %copy-done.7, bf16[48,8192]{1,0:T(8,128)(2,1)} %collective-permute-done.14.refs_2_, ...), custom_call_target="tpu_custom_call", output_to_operand_aliasing={{0}: (6, {})} | custom-call | flops 3221225472 | bytes 16777216 | tf_op jit(solution)/shard_map/blocks/pallas_call | solution.py:216
  128.1 6.6 %collective-permute-done.23.refs_0_ = bf16[48,8192]{1,0:T(8,128)(2,1)S(1)} collective-permute-done((bf16[48,8192]{1,0:T(8,128)(2,1)S(1)}, bf16[48,8192]{1,0:T(8,128)(2,1)S(1)}, u32[]{:S(2)}, u32[]{:S(2)}) %collective-permute-start.23) | collective-permute-done | bytes 786464 | tf_op jit(solution)/shard_map/ppermute | solution.py:352
  134.6 10.9 %blocks.15 = (f32[16,48,1024]{2,1,0:T(8,128)S(1)}, f32[192,64]{1,0:T(8,128)S(1)}) custom-call(bf16[48,8192]{1,0:T(8,128)(2,1)} %collective-permute-done.5.refs_0_, bf16[48,8192]{1,0:T(8,128)(2,1)} %collective-permute-done.6.refs_1_, bf16[48,8192]{1,0:T(8,128)(2,1)S(1)} %collective-permute-done.24.refs_2_, ...), custom_call_target="tpu_custom_call", output_to_operand_aliasing={{0}: (6, {})} | custom-call | flops 3221225472 | bytes 16777216 | tf_op jit(solution)/shard_map/blocks/pallas_call | solution.py:216
  146.1 10.8 %blocks.16 = (f32[16,48,1024]{2,1,0:T(8,128)S(1)}, f32[192,64]{1,0:T(8,128)S(1)}) custom-call(bf16[48,8192]{1,0:T(8,128)(2,1)} %collective-permute-done.16.refs_0_, bf16[48,8192]{1,0:T(8,128)(2,1)} %collective-permute-done.17.refs_1_, bf16[48,8192]{1,0:T(8,128)(2,1)S(1)} %collective-permute-done.21.refs_2_, ...), custom_call_target="tpu_custom_call", output_to_operand_aliasing={{0}: (6, {})} | custom-call | flops 3221225472 | bytes 16777216 | tf_op jit(solution)/shard_map/blocks/pallas_call | solution.py:216
  157.2 10.9 %blocks.17 = (f32[16,48,1024]{2,1,0:T(8,128)S(1)}, f32[192,64]{1,0:T(8,128)S(1)}) custom-call(bf16[48,8192]{1,0:T(8,128)(2,1)} %collective-permute-done.12.refs_0_, bf16[48,8192]{1,0:T(8,128)(2,1)} %collective-permute-done.13.refs_1_, bf16[48,8192]{1,0:T(8,128)(2,1)S(1)} %collective-permute-done.28.refs_2_, ...), custom_call_target="tpu_custom_call", output_to_operand_aliasing={{0}: (6, {})} | custom-call | flops 3221225472 | bytes 16777216 | tf_op jit(solution)/shard_map/blocks/pallas_call | solution.py:216
  168.1 9.7 %blocks.18 = (f32[16,48,1024]{2,1,0:T(8,128)S(1)}, f32[96,64]{1,0:T(8,128)S(1)}) custom-call(bf16[48,8192]{1,0:T(8,128)(2,1)S(1)} %collective-permute-done.23.refs_0_, bf16[48,8192]{1,0:T(8,128)(2,1)S(1)} %collective-permute-done.27.refs_1_, bf16[16384,1024]{1,0:T(8,128)(2,1)} %refs_2_.7, ...), custom_call_target="tpu_custom_call", output_to_operand_aliasing={{0}: (4, {})} | custom-call | flops 1610612736 | bytes 16777216 | tf_op jit(solution)/shard_map/blocks/pallas_call | solution.py:216
  177.9 2.6 %ranks.1 = bf16[384,128]{1,0:T(8,128)(2,1)S(1)} custom-call(s32[16]{0:T(128)S(1)} %dynamic-slice_bitcast_fusion.owners_ref, s32[7]{0:T(128)S(1)} %pad_add_fusion.slot_ref, bf16[48,8192]{1,0:T(8,128)(2,1)S(1)} %collective-permute-done.20.refs_0_.xa_ref, bf16[48,8192]{1,0:T(8,128)(2,1)S(1)} %collective-permute-done.26.refs_1_.xb_ref, ...), custom_call_target="tpu_custom_call" | custom-call | tf_op jit(solution)/shard_map/ranks/pallas_call | solution.py:269
  183.3 4.1 %collective-permute-done.31 = bf16[384,128]{1,0:T(8,128)(2,1)S(1)} collective-permute-done((bf16[384,128]{1,0:T(8,128)(2,1)S(1)}, bf16[384,128]{1,0:T(8,128)(2,1)S(1)}, u32[]{:S(2)}, u32[]{:S(2)}) %collective-permute-start.31) | collective-permute-done | bytes 98336 | tf_op jit(solution)/shard_map/ppermute | solution.py:124
  189.6 2.4 %collective-permute-done.32 = bf16[384,128]{1,0:T(8,128)(2,1)S(1)} collective-permute-done((bf16[384,128]{1,0:T(8,128)(2,1)S(1)}, bf16[384,128]{1,0:T(8,128)(2,1)S(1)}, u32[]{:S(2)}, u32[]{:S(2)}) %collective-permute-start.32) | collective-permute-done | bytes 98336 | tf_op jit(solution)/shard_map/ppermute | solution.py:124
  192.1 2.6 %collective-permute-start.33 = (bf16[384,128]{1,0:T(8,128)(2,1)S(1)}, bf16[384,128]{1,0:T(8,128)(2,1)S(1)}, u32[]{:S(2)}, u32[]{:S(2)}) collective-permute-start(bf16[384,128]{1,0:T(8,128)(2,1)S(1)} %add.29), channel_id=1, source_target_pairs={{0,8},{1,9},{2,10},{3,11},{4,12},{5,13},{6,14},{7,15},{8,0},{9,1},... | collective-permute-start | bytes 294920 | tf_op jit(solution)/shard_map/ppermute | solution.py:124
  194.7 9.7 %blocks.19.refs_0_.refs_1_.refs_2_.refs_3_.refs_4_.refs_5_.refs_6_.refs_7_ = f32[16,48,1024]{2,1,0:T(8,128)S(1)} custom-call(bf16[48,8192]{1,0:T(8,128)(2,1)S(1)} %collective-permute-done.20.refs_0_.xa_ref, bf16[48,8192]{1,0:T(8,128)(2,1)S(1)} %collective-permute-done.26.refs_1_.xb_ref, bf16[16384,1024]{1,0:T(8,128)(2,1)} %refs_2_.7, ...), custom_call_target="tpu_custom_call", output_to_operand_aliasing={{}: (3, {})} | custom-call | flops 1610612736 | bytes 16777216 | tf_op jit(solution)/shard_map/blocks/pallas_call | solution.py:216
  204.4 3.0 %finish.1 = bf16[768,1024]{1,0:T(8,128)(2,1)} custom-call(s32[16]{0:T(128)S(1)} %dynamic-slice_bitcast_fusion.1.places_ref, s32[6]{0:T(128)S(1)} %gather_fusion, f32[16,48,1024]{2,1,0:T(8,128)S(1)} %blocks.19.refs_0_.refs_1_.refs_2_.refs_3_.refs_4_.refs_5_.refs_6_.refs_7_, ...), custom_call_target="tpu_custom_call" | custom-call | tf_op jit(solution)/shard_map/finish/pallas_call | solution.py:319
  (113 shorter events, 37.3 us)
Async XLA Ops:
  1.6 21.4 %collective-permute-start.3 = (bf16[48,8192]{1,0:T(8,128)(2,1)S(1)}, bf16[48,8192]{1,0:T(8,128)(2,1)S(1)}, u32[]{:S(2)}, u32[]{:S(2)}) collective-permute-start(bf16[48,8192]{1,0:T(8,128)(2,1)S(1)} %get-tuple-element.67.refs_0_), channel_id=1, source_target_pairs={{0,4},{1,5},{4,8},{5,9},{8,12},{9,13},{12,14},{13,15},{14,10},{15,... | collective-permute-start | bytes 2359304 | tf_op jit(solution)/shard_map/ppermute | solution.py:352
  4.7 20.5 %collective-permute-start.4 = (bf16[48,8192]{1,0:T(8,128)(2,1)S(1)}, bf16[48,8192]{1,0:T(8,128)(2,1)S(1)}, u32[]{:S(2)}, u32[]{:S(2)}) collective-permute-start(bf16[48,8192]{1,0:T(8,128)(2,1)S(1)} %get-tuple-element.67.refs_0_), channel_id=1, source_target_pairs={{0,2},{1,3},{4,0},{5,1},{8,4},{9,5},{12,8},{13,9},{14,12},{15,13},... | collective-permute-start | bytes 2359304 | tf_op jit(solution)/shard_map/ppermute | solution.py:352
  4.7 35.3 %collective-permute-start = (bf16[48,8192]{1,0:T(8,128)(2,1)S(1)}, bf16[48,8192]{1,0:T(8,128)(2,1)}, u32[]{:S(2)}, u32[]{:S(2)}) collective-permute-start(bf16[48,8192]{1,0:T(8,128)(2,1)S(1)} %get-tuple-element.73.refs_0_), channel_id=1, source_target_pairs={{0,4},{1,5},{4,8},{5,9},{8,12},{9,13},{12,14},{13,15},{14,10},{15,... | collective-permute-start | bytes 2359304 | tf_op jit(solution)/shard_map/ppermute | solution.py:352
  6.7 35.4 %collective-permute-start.1 = (bf16[48,8192]{1,0:T(8,128)(2,1)S(1)}, bf16[48,8192]{1,0:T(8,128)(2,1)}, u32[]{:S(2)}, u32[]{:S(2)}) collective-permute-start(bf16[48,8192]{1,0:T(8,128)(2,1)S(1)} %get-tuple-element.73.refs_0_), channel_id=1, source_target_pairs={{0,2},{1,3},{4,0},{5,1},{8,4},{9,5},{12,8},{13,9},{14,12},{15,13},... | collective-permute-start | bytes 2359304 | tf_op jit(solution)/shard_map/ppermute | solution.py:352
  23.0 29.3 %collective-permute-start.11 = (bf16[48,8192]{1,0:T(8,128)(2,1)S(1)}, bf16[48,8192]{1,0:T(8,128)(2,1)S(1)}, u32[]{:S(2)}, u32[]{:S(2)}) collective-permute-start(bf16[48,8192]{1,0:T(8,128)(2,1)S(1)} %get-tuple-element.73.refs_0_), channel_id=1, source_target_pairs={{0,1},{1,0},{2,3},{3,2},{4,5},{5,4},{6,7},{7,6},{8,9},{9,8},{10,11... | collective-permute-start | bytes 2359304 | tf_op jit(solution)/shard_map/ppermute | solution.py:352
  25.2 32.2 %collective-permute-start.10 = (bf16[48,8192]{1,0:T(8,128)(2,1)S(1)}, bf16[48,8192]{1,0:T(8,128)(2,1)S(1)}, u32[]{:S(2)}, u32[]{:S(2)}) collective-permute-start(bf16[48,8192]{1,0:T(8,128)(2,1)S(1)} %collective-permute-done.4.refs_1_), channel_id=1, source_target_pairs={{0,2},{1,3},{4,0},{5,1},{8,4},{9,5},{12,8},{13,9},{14,12},{15,13},... | collective-permute-start | bytes 2359304 | tf_op jit(solution)/shard_map/ppermute | solution.py:352
  25.2 32.5 %collective-permute-start.9 = (bf16[48,8192]{1,0:T(8,128)(2,1)S(1)}, bf16[48,8192]{1,0:T(8,128)(2,1)}, u32[]{:S(2)}, u32[]{:S(2)}) collective-permute-start(bf16[48,8192]{1,0:T(8,128)(2,1)S(1)} %collective-permute-done.3.refs_0_), channel_id=1, source_target_pairs={{0,4},{1,5},{4,8},{5,9},{8,12},{9,13},{12,14},{13,15},{14,10},{15,... | collective-permute-start | bytes 2359304 | tf_op jit(solution)/shard_map/ppermute | solution.py:352
  40.0 27.5 %collective-permute-start.7 = (bf16[48,8192]{1,0:T(8,128)(2,1)S(1)}, bf16[48,8192]{1,0:T(8,128)(2,1)S(1)}, u32[]{:S(2)}, u32[]{:S(2)}) collective-permute-start(bf16[48,8192]{1,0:T(8,128)(2,1)S(1)} %collective-permute-done.3.refs_0_), channel_id=1, source_target_pairs={{0,1},{1,0},{2,3},{3,2},{4,5},{5,4},{6,7},{7,6},{8,9},{9,8},{10,11... | collective-permute-start | bytes 2359304 | tf_op jit(solution)/shard_map/ppermute | solution.py:352
  42.1 26.8 %collective-permute-start.8 = (bf16[48,8192]{1,0:T(8,128)(2,1)S(1)}, bf16[48,8192]{1,0:T(8,128)(2,1)S(1)}, u32[]{:S(2)}, u32[]{:S(2)}) collective-permute-start(bf16[48,8192]{1,0:T(8,128)(2,1)S(1)} %collective-permute-done.4.refs_1_), channel_id=1, source_target_pairs={{0,1},{1,0},{2,3},{3,2},{4,5},{5,4},{6,7},{7,6},{8,9},{9,8},{10,11... | collective-permute-start | bytes 2359304 | tf_op jit(solution)/shard_map/ppermute | solution.py:352
  52.3 20.6 %collective-permute-start.5 = (bf16[48,8192]{1,0:T(8,128)(2,1)}, bf16[48,8192]{1,0:T(8,128)(2,1)}, u32[]{:S(2)}, u32[]{:S(2)}) collective-permute-start(bf16[48,8192]{1,0:T(8,128)(2,1)} %collective-permute-done.refs_0_), channel_id=1, source_target_pairs={{0,4},{1,5},{4,8},{5,9},{8,12},{9,13},{12,14},{13,15},{14,10},{15,... | collective-permute-start | bytes 2359304 | tf_op jit(solution)/shard_map/ppermute | solution.py:352
  68.4 25.0 %collective-permute-start.19 = (bf16[48,8192]{1,0:T(8,128)(2,1)}, bf16[48,8192]{1,0:T(8,128)(2,1)}, u32[]{:S(2)}, u32[]{:S(2)}) collective-permute-start(bf16[48,8192]{1,0:T(8,128)(2,1)} %collective-permute-done.1.refs_1_), channel_id=1, source_target_pairs={{0,1},{1,0},{2,3},{3,2},{4,5},{5,4},{6,7},{7,6},{8,9},{9,8},{10,11... | collective-permute-start | bytes 2359304 | tf_op jit(solution)/shard_map/ppermute | solution.py:352
  69.8 25.2 %collective-permute-start.16 = (bf16[48,8192]{1,0:T(8,128)(2,1)}, bf16[48,8192]{1,0:T(8,128)(2,1)}, u32[]{:S(2)}, u32[]{:S(2)}) collective-permute-start(bf16[48,8192]{1,0:T(8,128)(2,1)} %collective-permute-done.9.refs_0_), channel_id=1, source_target_pairs={{0,4},{1,5},{4,8},{5,9},{8,12},{9,13},{12,14},{13,15},{14,10},{15,... | collective-permute-start | bytes 2359304 | tf_op jit(solution)/shard_map/ppermute | solution.py:352
  72.9 36.3 %collective-permute-start.17 = (bf16[48,8192]{1,0:T(8,128)(2,1)}, bf16[48,8192]{1,0:T(8,128)(2,1)}, u32[]{:S(2)}, u32[]{:S(2)}) collective-permute-start(bf16[48,8192]{1,0:T(8,128)(2,1)} %copy-done.6), channel_id=1, source_target_pairs={{0,2},{1,3},{4,0},{5,1},{8,4},{9,5},{12,8},{13,9},{14,12},{15,13},... | collective-permute-start | bytes 2359304 | tf_op jit(solution)/shard_map/ppermute | solution.py:352
  76.1 33.1 %collective-permute-start.14 = (bf16[48,8192]{1,0:T(8,128)(2,1)}, bf16[48,8192]{1,0:T(8,128)(2,1)}, u32[]{:S(2)}, u32[]{:S(2)}) collective-permute-start(bf16[48,8192]{1,0:T(8,128)(2,1)} %collective-permute-done.9.refs_0_), channel_id=1, source_target_pairs={{0,1},{1,0},{2,3},{3,2},{4,5},{5,4},{6,7},{7,6},{8,9},{9,8},{10,11... | collective-permute-start | bytes 2359304 | tf_op jit(solution)/shard_map/ppermute | solution.py:352
  76.1 33.6 %collective-permute-start.15 = (bf16[48,8192]{1,0:T(8,128)(2,1)}, bf16[48,8192]{1,0:T(8,128)(2,1)}, u32[]{:S(2)}, u32[]{:S(2)}) collective-permute-start(bf16[48,8192]{1,0:T(8,128)(2,1)} %copy-done.6), channel_id=1, source_target_pairs={{0,1},{1,0},{2,3},{3,2},{4,5},{5,4},{6,7},{7,6},{8,9},{9,8},{10,11... | collective-permute-start | bytes 2359304 | tf_op jit(solution)/shard_map/ppermute | solution.py:352
  93.4 27.4 %collective-permute-start.12 = (bf16[48,8192]{1,0:T(8,128)(2,1)}, bf16[48,8192]{1,0:T(8,128)(2,1)}, u32[]{:S(2)}, u32[]{:S(2)}) collective-permute-start(bf16[48,8192]{1,0:T(8,128)(2,1)} %collective-permute-done.5.refs_0_), channel_id=1, source_target_pairs={{0,4},{1,5},{4,8},{5,9},{8,12},{9,13},{12,14},{13,15},{14,10},{15,... | collective-permute-start | bytes 2359304 | tf_op jit(solution)/shard_map/ppermute | solution.py:352
  95.0 26.3 %collective-permute-start.13 = (bf16[48,8192]{1,0:T(8,128)(2,1)}, bf16[48,8192]{1,0:T(8,128)(2,1)}, u32[]{:S(2)}, u32[]{:S(2)}) collective-permute-start(bf16[48,8192]{1,0:T(8,128)(2,1)} %collective-permute-done.6.refs_1_), channel_id=1, source_target_pairs={{0,2},{1,3},{4,0},{5,1},{8,4},{9,5},{12,8},{13,9},{14,12},{15,13},... | collective-permute-start | bytes 2359304 | tf_op jit(solution)/shard_map/ppermute | solution.py:352
  109.7 35.8 %collective-permute-start.21 = (bf16[48,8192]{1,0:T(8,128)(2,1)}, bf16[48,8192]{1,0:T(8,128)(2,1)S(1)}, u32[]{:S(2)}, u32[]{:S(2)}) collective-permute-start(bf16[48,8192]{1,0:T(8,128)(2,1)} %collective-permute-done.16.refs_0_), channel_id=1, source_target_pairs={{0,1},{1,0},{2,3},{3,2},{4,5},{5,4},{6,7},{7,6},{8,9},{9,8},{10,11... | collective-permute-start | bytes 2359304 | tf_op jit(solution)/shard_map/ppermute | solution.py:352
  120.9 25.3 %collective-permute-start.22 = (bf16[48,8192]{1,0:T(8,128)(2,1)}, bf16[48,8192]{1,0:T(8,128)(2,1)S(1)}, u32[]{:S(2)}, u32[]{:S(2)}) collective-permute-start(bf16[48,8192]{1,0:T(8,128)(2,1)} %collective-permute-done.17.refs_1_), channel_id=1, source_target_pairs={{0,1},{1,0},{2,3},{3,2},{4,5},{5,4},{6,7},{7,6},{8,9},{9,8},{10,11... | collective-permute-start | bytes 2359304 | tf_op jit(solution)/shard_map/ppermute | solution.py:352
  125.4 31.6 %collective-permute-start.20 = (bf16[48,8192]{1,0:T(8,128)(2,1)S(1)}, bf16[48,8192]{1,0:T(8,128)(2,1)S(1)}, u32[]{:S(2)}, u32[]{:S(2)}) collective-permute-start(bf16[48,8192]{1,0:T(8,128)(2,1)S(1)} %broadcast_select_fusion.1), channel_id=1, source_target_pairs={{0,4},{1,3},{4,8},{5,1},{8,12},{9,5},{12,14},{13,9},{14,10},{15,13... | collective-permute-start | bytes 2359304 | tf_op jit(solution)/shard_map/ppermute | solution.py:352
  128.0 29.2 %collective-permute-start.28 = (bf16[48,8192]{1,0:T(8,128)(2,1)}, bf16[48,8192]{1,0:T(8,128)(2,1)S(1)}, u32[]{:S(2)}, u32[]{:S(2)}) collective-permute-start(bf16[48,8192]{1,0:T(8,128)(2,1)} %collective-permute-done.12.refs_0_), channel_id=1, source_target_pairs={{0,1},{1,0},{2,3},{3,2},{4,5},{5,4},{6,7},{7,6},{8,9},{9,8},{10,11... | collective-permute-start | bytes 2359304 | tf_op jit(solution)/shard_map/ppermute | solution.py:352
  134.6 22.6 %collective-permute-start.29 = (bf16[48,8192]{1,0:T(8,128)(2,1)}, bf16[48,8192]{1,0:T(8,128)(2,1)S(1)}, u32[]{:S(2)}, u32[]{:S(2)}) collective-permute-start(bf16[48,8192]{1,0:T(8,128)(2,1)} %collective-permute-done.13.refs_1_), channel_id=1, source_target_pairs={{0,1},{1,0},{2,3},{3,2},{4,5},{5,4},{6,7},{7,6},{8,9},{9,8},{10,11... | collective-permute-start | bytes 2359304 | tf_op jit(solution)/shard_map/ppermute | solution.py:352
  145.5 22.6 %collective-permute-start.27 = (bf16[48,8192]{1,0:T(8,128)(2,1)S(1)}, bf16[48,8192]{1,0:T(8,128)(2,1)S(1)}, u32[]{:S(2)}, u32[]{:S(2)}) collective-permute-start(bf16[48,8192]{1,0:T(8,128)(2,1)S(1)} %collective-permute-done.23.refs_0_), channel_id=1, source_target_pairs={{0,1},{1,0},{2,3},{3,2},{4,5},{5,4},{6,7},{7,6},{8,9},{9,8},{10,11... | collective-permute-start | bytes 2359304 | tf_op jit(solution)/shard_map/ppermute | solution.py:352
  157.0 20.9 %collective-permute-start.26 = (bf16[48,8192]{1,0:T(8,128)(2,1)S(1)}, bf16[48,8192]{1,0:T(8,128)(2,1)S(1)}, u32[]{:S(2)}, u32[]{:S(2)}) collective-permute-start(bf16[48,8192]{1,0:T(8,128)(2,1)S(1)} %collective-permute-done.20.refs_0_.xa_ref), channel_id=1, source_target_pairs={{0,1},{1,0},{2,3},{3,2},{4,5},{5,4},{6,7},{7,6},{8,9},{9,8},{10,11... | collective-permute-start | bytes 2359304 | tf_op jit(solution)/shard_map/ppermute | solution.py:352
  (28 other events, 391.4 us)

commit v3 on v2

--- a/solution.py
+++ b/solution.py
@@ -10,10 +10,11 @@
 
 HD = 128
 SEG = 128
-VMEM = 40 * 1024 * 1024
+VMEM = 26 * 1024 * 1024
 F32 = jnp.float32
 BF16 = jnp.bfloat16
 NT = (((1,), (1,)), ((), ()))
+STREAMS = 4
 PARAMS = pltpu.CompilerParams(vmem_limit_bytes=VMEM)
 SNAKE = (0, 2, 4, 6, 7, 5, 3, 1)
 ROUNDS = len(SNAKE) // 2
@@ -145,12 +146,12 @@
     owners = np.zeros((2 * chips, 2 * chips), np.int32)
     for place, chip in enumerate(SNAKE):
         for core in (0, 1):
-            row = []
+            row = [2 * chip + core, 2 * chip + 1 - core]
             for r in range(1, ROUNDS):
                 before, after = SNAKE[place - r], SNAKE[(place + r) % chips]
                 row += [2 * before + core, 2 * after + core, 2 * before + 1 - core, 2 * after + 1 - core]
             across = SNAKE[(place + ROUNDS) % chips]
-            row += [2 * chip + core, 2 * chip + 1 - core, 2 * across + core, 2 * across + 1 - core]
+            row += [2 * across + core, 2 * across + 1 - core]
             owners[2 * chip + core] = row
     return owners
 
@@ -164,123 +165,159 @@
     return pairs
 
 
-def block_kernel(count, fresh, ranked, *refs):
+def block_kernel(count, first, base, fresh, ranked, *refs):
     xs, refs = refs[:count], refs[count:]
-    w_ref, refs = refs[0], refs[1:]
+    ws, refs = refs[:STREAMS], refs[STREAMS:]
     if ranked:
         s_ref, refs = refs[0], refs[1:]
-    acc_in, refs = refs[0], refs[1:]
+    if not first:
+        total_in, refs = refs[0], refs[1:]
     if ranked and not fresh:
         h_in, refs = refs[0], refs[1:]
-    acc_out = refs[0]
+    total_out, refs = refs[0], refs[1:]
+    if ranked:
+        h_out, refs = refs[0], refs[1:]
+    acc, before, sems = refs
+    step, last = pl.program_id(0), pl.num_programs(0) - 1
     rows = xs[0].shape[0]
 
-    @pl.when(pl.program_id(0) == 0)
+    def load():
+        return pltpu.make_async_copy(total_in.at[pl.ds(base, count)], before, sems.at[0])
+
+    @pl.when(step == 0)
     def _():
-        acc_out[...] = jnp.zeros_like(acc_out) if fresh else acc_in[...]
+        if not fresh:
+            load().start()
+        acc[...] = jnp.zeros_like(acc)
         if ranked:
-            refs[1][...] = jnp.zeros_like(refs[1]) if fresh else h_in[...]
+            h_out[...] = jnp.zeros_like(h_out) if fresh else h_in[...]
 
     x = jnp.concatenate([ref[...] for ref in xs], 0)
-    acc_out[...] += jnp.dot(x, w_ref[...], preferred_element_type=F32).reshape(acc_out.shape)
+    w = jnp.concatenate([ref[...] for ref in ws], 0)
+    acc[...] += jnp.dot(x, w, preferred_element_type=F32).reshape(acc.shape)
     if ranked:
-        refs[1][...] += lax.dot_general(x, s_ref[...], NT, preferred_element_type=F32)
-
-
-def block_product(xs, weights, shrink, low, tile, total, place, h, ranked):
+        h_out[...] += lax.dot_general(x, s_ref[...], NT, preferred_element_type=F32)
+
+    @pl.when(step == last)
+    def _():
+        if not fresh:
+            load().wait()
+            acc[...] += before[...]
+        store = pltpu.make_async_copy(acc, total_out.at[pl.ds(base, count)], sems.at[1])
+        store.start()
+        store.wait()
+
+
+def block_product(xs, weights, shrink, starts, low, high, tile, total, base, h, ranked):
     count = len(xs)
-    rows, depth = xs[0].shape
-    cols = weights.shape[1]
+    rows = xs[0].shape[0]
+    depth, cols = weights.shape
     rank = shrink.shape[0]
     fresh = low == 0
     skip = low // tile
-    block = pl.BlockSpec((count, rows, cols), lambda k: (place // count, 0, 0))
+    starts = starts or [0] * count
+    strip = tile // STREAMS
     ranks = pl.BlockSpec((count * rows, rank), lambda k: (0, 0))
-    operands = list(xs) + [weights]
-    specs = [pl.BlockSpec((rows, tile), lambda k: (0, k))] * count
-    specs += [pl.BlockSpec((tile, cols), lambda k: (k + skip, 0))]
+    operands = list(xs) + [weights] * STREAMS
+    specs = [pl.BlockSpec((rows, tile), lambda k, i=(low - start) // tile: (0, k + i)) for start in starts]
+    for i in range(STREAMS):
+        specs.append(pl.BlockSpec((strip, cols), lambda k, i=i: (STREAMS * (k + skip) + i, 0)))
     if ranked:
         operands.append(shrink)
         specs.append(pl.BlockSpec((rank, tile), lambda k: (0, k + skip)))
-    aliases = {len(operands): 0}
-    operands.append(total)
-    specs.append(pl.BlockSpec(memory_space=pl.ANY) if fresh else block)
+    aliases = {}
+    first = total is None
+    if not first:
+        aliases = {len(operands): 0}
+        operands.append(total)
+        specs.append(pl.BlockSpec(memory_space=pl.ANY))
     if ranked and not fresh:
         operands.append(h)
         specs.append(ranks)
-    outs = [jax.ShapeDtypeStruct(total.shape, F32)]
-    out_specs = [block]
+    outs = [jax.ShapeDtypeStruct(total_shape(rows, cols), F32)]
+    out_specs = [pl.BlockSpec(memory_space=pl.ANY)]
     if ranked:
         outs.append(jax.ShapeDtypeStruct((count * rows, rank), F32))
         out_specs.append(ranks)
     result = pl.pallas_call(
-        functools.partial(block_kernel, count, fresh, ranked),
-        grid=(depth // tile,),
+        functools.partial(block_kernel, count, first, base, fresh, ranked),
+        grid=((high - low) // tile,),
         in_specs=specs,
         out_specs=out_specs,
         out_shape=outs,
+        scratch_shapes=[
+            pltpu.VMEM((count, rows, cols), F32),
+            pltpu.VMEM((1, 8, 128) if fresh else (count, rows, cols), F32),
+            pltpu.SemaphoreType.DMA((2,)),
+        ],
         input_output_aliases=aliases,
         compiler_params=PARAMS,
         cost_estimate=pl.CostEstimate(
-            flops=2 * count * rows * depth * cols, bytes_accessed=2 * depth * cols, transcendentals=0
+            flops=2 * count * rows * (high - low) * cols,
+            bytes_accessed=2 * (high - low) * cols,
+            transcendentals=0,
         ),
         name="blocks",
     )(*operands)
     return result if ranked else (result[0], h)
 
 
-def rank_kernel(counts, owners_ref, slot_ref, xa_ref, xb_ref, s_ref, *refs):
-    h_refs, out_ref, grown, placed = refs[: len(counts)], refs[-3], refs[-2], refs[-1]
-    step = pl.program_id(0)
-    rows = xa_ref.shape[0]
-
-    @pl.when(step == 0)
-    def _():
-        grown[...] = h_refs[-1][...]
-
-    x = jnp.concatenate([xa_ref[...], xb_ref[...]], 0)
-    grown[...] += lax.dot_general(x, s_ref[...], NT, preferred_element_type=F32)
-
-    @pl.when(step == pl.num_programs(0) - 1)
-    def _():
-        block = 0
-        for group, count in enumerate(counts):
-            source = grown if group == len(counts) - 1 else h_refs[group]
-            for i in range(count):
-                to = pl.multiple_of(owners_ref[block] * rows, 16)
-                placed[pl.ds(to, rows), :] = source[i * rows : (i + 1) * rows, :]
-                block += 1
-        pieces = []
-        for segment in range(placed.shape[0] // SEG):
-            piece = placed[segment * SEG : (segment + 1) * SEG, :]
-            pieces.append(jnp.where(slot_ref[segment] == slot_ref[slot_ref.shape[0] - 1], piece, 0.0))
-        half = len(pieces) // 2
-        left, right = jnp.concatenate(pieces[:half], 0), jnp.concatenate(pieces[half:], 0)
-        out_ref[...] = jnp.concatenate([left, right], 1).astype(out_ref.dtype)
-
-
-def rank_terms(owners, slots, xs, shrink, low, tile, hs):
-    rows, depth = xs[0].shape
+def total_shape(rows, cols):
+    return (2 * len(SNAKE), rows, cols)
+
+
+def rank_kernel(counts, sides, pieces, owners_ref, slot_ref, *refs):
+    side, refs = refs[:sides], refs[sides:]
+    split, refs = refs[: 2 * pieces], refs[2 * pieces :]
+    s_ref, h_refs, out_ref, placed = refs[0], refs[1:-2], refs[-2], refs[-1]
+    rows, width = side[0].shape
+    x = jnp.concatenate([ref[...] for ref in side], 0)
+    grown = lax.dot_general(x, s_ref[...], NT, preferred_element_type=F32)
+    last = 0.0
+    for piece in range(pieces):
+        x = jnp.concatenate([split[2 * piece][...], split[2 * piece + 1][...]], 0)
+        cut = slice(piece * width // pieces, (piece + 1) * width // pieces)
+        last += lax.dot_general(x, s_ref[:, cut], NT, preferred_element_type=F32)
+    late = h_refs[-1][...] + jnp.concatenate([grown, last], 0)
+    block = 0
+    for count, source in zip(counts, h_refs[:-1] + (late,)):
+        for i in range(count):
+            to = pl.multiple_of(owners_ref[block] * rows, 16)
+            placed[pl.ds(to, rows), :] = source[i * rows : (i + 1) * rows, :]
+            block += 1
+    parts = []
+    for segment in range(placed.shape[0] // SEG):
+        part = placed[segment * SEG : (segment + 1) * SEG, :]
+        parts.append(jnp.where(slot_ref[segment] == slot_ref[slot_ref.shape[0] - 1], part, 0.0))
+    half = len(parts) // 2
+    left, right = jnp.concatenate(parts[:half], 0), jnp.concatenate(parts[half:], 0)
+    out_ref[...] = jnp.concatenate([left, right], 1).astype(out_ref.dtype)
+
+
+def rank_terms(owners, slots, side, pieces, shrink, low, hs):
+    rows, depth = side[0].shape
     rank = shrink.shape[0]
     counts = [h.shape[0] // rows for h in hs]
     total_rows = sum(counts) * rows
-    skip = low // tile
-    whole = [pl.BlockSpec(h.shape, lambda k, *_: (0, 0)) for h in hs]
+    whole = lambda shape: pl.BlockSpec(shape, lambda _, *rest: (0, 0))
+    upper = lambda height: pl.BlockSpec((height, depth - low), lambda _, *rest: (0, low // (depth - low)))
+    flat = [part for piece in pieces for part in piece]
     return pl.pallas_call(
-        functools.partial(rank_kernel, counts),
+        functools.partial(rank_kernel, counts, len(side), len(pieces)),
         grid_spec=pltpu.PrefetchScalarGridSpec(
             num_scalar_prefetch=2,
-            grid=(depth // tile,),
-            in_specs=[pl.BlockSpec((rows, tile), lambda k, *_: (0, k))] * 2
-            + [pl.BlockSpec((rank, tile), lambda k, *_: (0, k + skip))]
-            + whole,
-            out_specs=pl.BlockSpec((total_rows // 2, 2 * rank), lambda k, *_: (0, 0)),
-            scratch_shapes=[pltpu.VMEM(hs[-1].shape, F32), pltpu.VMEM((total_rows, rank), F32)],
+            grid=(1,),
+            in_specs=[upper(rows)] * len(side)
+            + [whole(part.shape) for part in flat]
+            + [upper(rank)]
+            + [whole(h.shape) for h in hs],
+            out_specs=whole((total_rows // 2, 2 * rank)),
+            scratch_shapes=[pltpu.VMEM((total_rows, rank), F32)],
         ),
         out_shape=jax.ShapeDtypeStruct((total_rows // 2, 2 * rank), BF16),
         compiler_params=PARAMS,
         name="ranks",
-    )(owners, slots, *xs, shrink, *hs)
+    )(owners, slots, *side, *flat, shrink, *hs)
 
 
 def block_finish_kernel(blocks, segments, places_ref, slot_ref, *refs):
@@ -341,8 +378,6 @@
 def ring_plan(parts, tokens, weights, scale, shrinks, expands, segment_slot, cosine, sine):
     rows, depth = tokens.shape
     tile = depth // 16
-    cuts = [0, depth // 2, depth]
-    spans = list(zip(cuts[:-1], cuts[1:]))
     me = lax.axis_index("tensor")
     owners_table = block_owners()
     owners = jnp.asarray(owners_table)[me]
@@ -354,40 +389,50 @@
     onward, back = ring_pairs((1, 1)), ring_pairs((-1, -1))
     across = ring_pairs((1, -1))
 
-    own = [tokens[:, low:high] for low, high in spans]
-    total = jnp.zeros((parts, rows, weights.shape[1]), F32)
-    hs = {}
-
-    def multiply(stage, xs, total):
-        j, r = stage
-        low = spans[j][0]
-        last = r == ROUNDS and j == len(spans) - 1
-        place = {0: 12, ROUNDS: 14}.get(r, 4 * (r - 1))
-        h = None
-        if last:
-            order = [hs[i] for i in range(1, ROUNDS)] + [hs[0], hs[ROUNDS]]
-            h = rank_terms(owners, slots, xs, shrink, low, tile, order)
-        total, hs[r] = block_product(xs, weights, shrink, low, tile, total, place, hs.get(r), not last)
-        return total, h
-
-    arriving = {(j, 1): [send(part, onward), send(part, back)] for j, part in enumerate(own)}
-    waiting = [((j, 0), [part, swap(part)]) for j, part in enumerate(own)]
-    for r in range(1, ROUNDS + 1):
-        for j in range(len(spans)):
-            arrived = arriving.pop((j, r))
-            arrived, total = lax.optimization_barrier((arrived, total))
-            if r < ROUNDS - 1:
-                arriving[j, r + 1] = [send(arrived[0], onward), send(arrived[1], back)]
-            elif r == ROUNDS - 1:
-                arriving[j, r + 1] = [send(jnp.where(me % 2 == 0, *arrived), across)]
-            waiting.append(((j, r), arrived + [swap(part) for part in arrived]))
-            stage, xs = waiting.pop(0)
-            if r < ROUNDS:
-                xs, _ = lax.optimization_barrier((xs, arrived))
-            total, _ = multiply(stage, xs, total)
-    for stage, xs in waiting:
-        total, h = multiply(stage, xs, total)
-    h = spread(h, parts)
+    total, hs, held = None, [], 0
+    blocks = [tokens, swap(tokens)]
+    ahead = [tokens, tokens]
+    for r in range(1, ROUNDS):
+        ahead = [send(ahead[0], onward), send(ahead[1], back)]
+        if total is not None:
+            ahead, total = lax.optimization_barrier((ahead, total))
+        if r == ROUNDS - 1:
+            break
+        blocks += ahead + [swap(part) for part in ahead]
+        total, h = block_product(blocks, weights, shrink, None, 0, depth, tile, total, held, None, True)
+        hs.append(h)
+        held += len(blocks)
+        blocks = []
+    side = ahead + [swap(part) for part in ahead]
+
+    picked = jnp.where(me % 2 == 0, *ahead)
+    quarter = depth // 4
+    cuts = [q * quarter for q in range(4)]
+    arriving = [send(picked[:, low : low + quarter], across) for low in cuts]
+    pieces = [[part, swap(part)] for part in arriving[:2]]
+
+    def late_product(q, total, h, ranked, tie=None):
+        xs = side + pieces[q]
+        if tie is not None:
+            xs, _ = lax.optimization_barrier((xs, tie))
+        starts = [0] * len(side) + [cuts[q]] * 2
+        return block_product(
+            xs, weights, shrink, starts, cuts[q], cuts[q] + quarter, tile, total, held, h, ranked
+        )
+
+    h_late = None
+    for q in (0, 1):
+        total, h_late = late_product(q, total, h_late, True)
+        part, total = lax.optimization_barrier((arriving[q + 2], total))
+        pieces.append([part, swap(part)])
+    h = rank_terms(owners, slots, side, pieces[2:], shrink, cuts[2], hs + [h_late])
+    for q, steps in zip((2, 3, None), ([1], [2, 4, 6], [8])):
+        more = [send(h, [(i, i ^ step) for i in range(parts)]) for step in steps]
+        if q is not None:
+            total, _ = late_product(q, total, None, False, h)
+        for part in more:
+            h = h + part
+        h, total = lax.optimization_barrier((h, total))
     return block_finish(places, segment_slot, total, expands, scale, h, cosine, sine)
 
 

time: 209 us -> 186 us (0.89)
  Pallas kernels: 110 us -> 78.4 us
  waiting for transfers between devices: 51.7 us -> 72 us
  starting transfers between devices: 26.2 us -> 19.1 us
  local copies, waits for them, and re-layouts: 14.3 us -> 10.7 us
    pallas_call x11 -> x7, Pallas kernels: 107 us -> 75.4 us  [the longest x6 71.5 us: block_product(): pl.pallas_call(functools.partial(block_kernel, count, first, base, fresh,...]
    ppermute x30 -> x26, waiting for transfers between devices: 45.3 us -> 72 us  [ring_plan(): send = lambda value, pairs: lax.ppermute(value, 'tensor', pairs)]
    ppermute x4 -> x0, waiting for transfers between devices: 6.46 us -> none  [spread(): h = h + lax.ppermute(h, 'tensor', [(i, i ^ step) for i in range(parts)])]
    ppermute x4 -> x0, starting transfers between devices: 5.19 us -> none  [spread(): h = h + lax.ppermute(h, 'tensor', [(i, i ^ step) for i in range(parts)])]
    unnamed x36 -> x28, local copies, waits for them, and re-layouts: 9.54 us -> 6.87 us
    ppermute x30 -> x26, starting transfers between devices: 21 us -> 19.1 us  [ring_plan(): send = lambda value, pairs: lax.ppermute(value, 'tensor', pairs)]
  transfers between devices with their start and end apart: 34 -> 26, of which waited for: 10 -> 12; matrix products, arithmetic and copies ran while one was open for 4% -> 4% of each run, Pallas kernels for 50% -> 39%
where the time goes in v3:
time: 186 us; the launch traced here: 185 us
  Pallas kernels  78.4 us (42%)
  waiting for transfers between devices  72 us (39%)
  starting transfers between devices  19.1 us (10%)
  local copies, waits for them, and re-layouts  10.7 us (6%)
  other arithmetic  4.25 us (2%)
    ppermute x26, waiting for transfers between devices, ring_plan(): send = lambda value, pairs: lax.ppermute(value, 'tensor', pairs)  72 us
    pallas_call x6, Pallas kernels, block_product(): pl.pallas_call(functools.partial(block_kernel, count, first, base, fresh,...  71.5 us
    ppermute x26, starting transfers between devices, ring_plan(): send = lambda value, pairs: lax.ppermute(value, 'tensor', pairs)  19.1 us
    unnamed x28, local copies, waits for them, and re-layouts  6.87 us
    pallas_call x1, Pallas kernels, rank_terms(): pl.pallas_call(functools.partial(rank_kernel, counts, len(side), len(piec...  3.87 us
  transfers between devices with their start and end apart: 26, of which 12 were waited for; matrix products, arithmetic and copies ran while one was open for 4% of the time, Pallas kernels for 39%

profile of v3, /device:TPU:0, one launch (start us, length us, event | category | flops | bytes accessed | tf_op | source)
XLA Modules:
  0.0 184.6 jit_solution(7646087565770853742)
XLA Ops:
  0.0 3.0 %collective-permute-start = (bf16[48,16384]{1,0:T(8,128)(2,1)}, bf16[48,16384]{1,0:T(8,128)(2,1)S(1)}, u32[]{:S(2)}, u32[]{:S(2)}) collective-permute-start(bf16[48,16384]{1,0:T(8,128)(2,1)} %refs_0_.1), channel_id=1, source_target_pairs={{0,4},{1,5},{4,8},{5,9},{8,12},{9,13},{12,14},{13,15},{14,10},{15,... | collective-permute-start | bytes 4718600 | tf_op jit(solution)/shard_map/ppermute | solution.py:387
  3.0 34.5 %collective-permute-done.refs_2_ = bf16[48,16384]{1,0:T(8,128)(2,1)S(1)} collective-permute-done((bf16[48,16384]{1,0:T(8,128)(2,1)}, bf16[48,16384]{1,0:T(8,128)(2,1)S(1)}, u32[]{:S(2)}, u32[]{:S(2)}) %collective-permute-start) | collective-permute-done | bytes 1572896 | tf_op jit(solution)/shard_map/ppermute | solution.py:387
  39.1 1.6 collective-permute-start.1
  41.1 2.1 %collective-permute-done.6.refs_5_ = bf16[48,16384]{1,0:T(8,128)(2,1)S(1)} collective-permute-done((bf16[48,16384]{1,0:T(8,128)(2,1)S(1)}, bf16[48,16384]{1,0:T(8,128)(2,1)S(1)}, u32[]{:S(2)}, u32[]{:S(2)}) %collective-permute-start.6) | collective-permute-done | bytes 1572896 | tf_op jit(solution)/shard_map/ppermute | solution.py:387
  43.2 1.6 copy-done.2
  46.2 22.4 %blocks.6 = (f32[16,48,1024]{2,1,0:T(8,128)S(1)}, f32[288,64]{1,0:T(8,128)S(1)}) custom-call(bf16[48,16384]{1,0:T(8,128)(2,1)S(1)} %copy-done.6, bf16[48,16384]{1,0:T(8,128)(2,1)S(1)} %collective-permute-done.4.refs_1_, bf16[48,16384]{1,0:T(8,128)(2,1)S(1)} %collective-permute-done.refs_2_, bf16[48,16384]{1,0:T(8,128)(2,1)S(1)} %collective-permute-done.2.refs_3_, ...), custom_call_target="tpu_custom_call" | custom-call | flops 9663676416 | bytes 33554432 | tf_op jit(solution)/shard_map/blocks/pallas_call | solution.py:242
  69.3 6.7 %collective-permute-done.1.refs_0_ = bf16[48,16384]{1,0:T(8,128)(2,1)} collective-permute-done((bf16[48,16384]{1,0:T(8,128)(2,1)S(1)}, bf16[48,16384]{1,0:T(8,128)(2,1)}, u32[]{:S(2)}, u32[]{:S(2)}) %collective-permute-start.1) | collective-permute-done | bytes 1572896 | tf_op jit(solution)/shard_map/ppermute | solution.py:387
  77.8 1.6 collective-permute-start.7
  81.1 2.2 %collective-permute-done.9.refs_2_ = bf16[48,16384]{1,0:T(8,128)(2,1)} collective-permute-done((bf16[48,16384]{1,0:T(8,128)(2,1)}, bf16[48,16384]{1,0:T(8,128)(2,1)}, u32[]{:S(2)}, u32[]{:S(2)}) %collective-permute-start.9) | collective-permute-done | bytes 1572896 | tf_op jit(solution)/shard_map/ppermute | solution.py:387
  83.3 1.6 copy-done.3
  84.9 20.9 %blocks.7 = (f32[16,48,1024]{2,1,0:T(8,128)S(1)}, f32[192,64]{1,0:T(8,128)S(1)}) custom-call(bf16[48,16384]{1,0:T(8,128)(2,1)} %collective-permute-done.1.refs_0_, bf16[48,16384]{1,0:T(8,128)(2,1)} %collective-permute-done.3.refs_1_, bf16[48,16384]{1,0:T(8,128)(2,1)} %collective-permute-done.9.refs_2_, ...), custom_call_target="tpu_custom_call", output_to_operand_aliasing={{0}: (9, {})} | custom-call | flops 6442450944 | bytes 33554432 | tf_op jit(solution)/shard_map/blocks/pallas_call | solution.py:242
  105.9 8.6 %collective-permute-done.7.refs_0_ = bf16[48,16384]{1,0:T(8,128)(2,1)} collective-permute-done((bf16[48,16384]{1,0:T(8,128)(2,1)}, bf16[48,16384]{1,0:T(8,128)(2,1)}, u32[]{:S(2)}, u32[]{:S(2)}) %collective-permute-start.7) | collective-permute-done | bytes 1572896 | tf_op jit(solution)/shard_map/ppermute | solution.py:387
  121.1 5.6 %collective-permute-done.14.refs_4_ = bf16[48,4096]{1,0:T(8,128)(2,1)} collective-permute-done((bf16[48,4096]{1,0:T(8,128)(2,1)S(1)}, bf16[48,4096]{1,0:T(8,128)(2,1)}, u32[]{:S(2)}, u32[]{:S(2)}) %collective-permute-start.14) | collective-permute-done | bytes 393248 | tf_op jit(solution)/shard_map/ppermute | solution.py:387
  128.3 2.7 %collective-permute-done.18.refs_4_ = bf16[48,4096]{1,0:T(8,128)(2,1)} collective-permute-done((bf16[48,4096]{1,0:T(8,128)(2,1)}, bf16[48,4096]{1,0:T(8,128)(2,1)}, u32[]{:S(2)}, u32[]{:S(2)}) %collective-permute-start.18) | collective-permute-done | bytes 393248 | tf_op jit(solution)/shard_map/ppermute | solution.py:387
  134.4 1.6 copy-done.4
  136.0 7.0 %blocks.8 = (f32[16,48,1024]{2,1,0:T(8,128)S(1)}, f32[288,64]{1,0:T(8,128)S(1)}) custom-call(bf16[48,16384]{1,0:T(8,128)(2,1)} %collective-permute-done.7.refs_0_, bf16[48,16384]{1,0:T(8,128)(2,1)} %collective-permute-done.8.refs_1_, bf16[48,16384]{1,0:T(8,128)(2,1)} %collective-permute-done.11.refs_2_, ...), custom_call_target="tpu_custom_call", output_to_operand_aliasing={{0}: (11, {})} | custom-call | flops 2415919104 | bytes 8388608 | tf_op jit(solution)/shard_map/blocks/pallas_call | solution.py:242
  143.0 7.5 %blocks.9 = (f32[16,48,1024]{2,1,0:T(8,128)S(1)}, f32[288,64]{1,0:T(8,128)S(1)}) custom-call(bf16[48,16384]{1,0:T(8,128)(2,1)} %collective-permute-done.7.refs_0_, bf16[48,16384]{1,0:T(8,128)(2,1)} %collective-permute-done.8.refs_1_, bf16[48,16384]{1,0:T(8,128)(2,1)} %collective-permute-done.11.refs_2_, ...), custom_call_target="tpu_custom_call", output_to_operand_aliasing={{0}: (11, {})} | custom-call | flops 2415919104 | bytes 8388608 | tf_op jit(solution)/shard_map/blocks/pallas_call | solution.py:242
  152.9 3.9 %ranks.1 = bf16[384,128]{1,0:T(8,128)(2,1)S(1)} custom-call(s32[16]{0:T(128)S(1)} %dynamic-slice_bitcast_fusion.owners_ref, s32[7]{0:T(128)S(1)} %pad_add_fusion.slot_ref, bf16[48,16384]{1,0:T(8,128)(2,1)} %collective-permute-done.7.refs_0_, bf16[48,16384]{1,0:T(8,128)(2,1)} %collective-permute-done.8.refs_1_, ...), custom_call_target="tpu_custom_call" | custom-call | tf_op jit(solution)/shard_map/ranks/pallas_call | solution.py:305
  156.9 6.8 %blocks.10.refs_10_ = f32[16,48,1024]{2,1,0:T(8,128)S(1)} custom-call(bf16[48,16384]{1,0:T(8,128)(2,1)} %collective-permute-done.7.refs_0_, bf16[48,16384]{1,0:T(8,128)(2,1)} %collective-permute-done.8.refs_1_, bf16[48,16384]{1,0:T(8,128)(2,1)} %collective-permute-done.11.refs_2_, ...), custom_call_target="tpu_custom_call", output_to_operand_aliasing={{}: (10, {})} | custom-call | flops 2415919104 | bytes 8388608 | tf_op jit(solution)/shard_map/blocks/pallas_call | solution.py:242
  164.8 2.5 %collective-permute-start.24 = (bf16[384,128]{1,0:T(8,128)(2,1)S(1)}, bf16[384,128]{1,0:T(8,128)(2,1)S(1)}, u32[]{:S(2)}, u32[]{:S(2)}) collective-permute-start(bf16[384,128]{1,0:T(8,128)(2,1)S(1)} %add.29), channel_id=1, source_target_pairs={{0,6},{1,7},{2,4},{3,5},{4,2},{5,3},{6,0},{7,1},{8,14},{9,15},{10,... | collective-permute-start | bytes 294920 | tf_op jit(solution)/shard_map/ppermute | solution.py:387
  167.3 6.9 %blocks.11.refs_0_.refs_1_.refs_2_.refs_3_.refs_4_.refs_5_.refs_6_.refs_7_ = f32[16,48,1024]{2,1,0:T(8,128)S(1)} custom-call(bf16[48,16384]{1,0:T(8,128)(2,1)} %collective-permute-done.7.refs_0_, bf16[48,16384]{1,0:T(8,128)(2,1)} %collective-permute-done.8.refs_1_, ...), custom_call_target="tpu_custom_call", output_to_operand_aliasing={{}: (10, {})} | custom-call | flops 2415919104 | bytes 8388608 | tf_op jit(solution)/shard_map/blocks/pallas_call | solution.py:242
  174.3 1.7 collective-permute-start.25
  176.7 4.9 %collective-permute-done.25 = bf16[384,128]{1,0:T(8,128)(2,1)S(1)} collective-permute-done((bf16[384,128]{1,0:T(8,128)(2,1)S(1)}, bf16[384,128]{1,0:T(8,128)(2,1)S(1)}, u32[]{:S(2)}, u32[]{:S(2)}) %collective-permute-start.25) | collective-permute-done | bytes 98336 | tf_op jit(solution)/shard_map/ppermute | solution.py:387
  181.7 3.0 %finish.1 = bf16[768,1024]{1,0:T(8,128)(2,1)} custom-call(s32[16]{0:T(128)S(1)} %dynamic-slice_bitcast_fusion.1.places_ref, s32[6]{0:T(128)S(1)} %gather_fusion, f32[16,48,1024]{2,1,0:T(8,128)S(1)} %blocks.11.refs_0_.refs_1_.refs_2_.refs_3_.refs_4_.refs_5_.refs_6_.refs_7_, ...), custom_call_target="tpu_custom_call" | custom-call | tf_op jit(solution)/shard_map/finish/pallas_call | solution.py:356
  (82 shorter events, 23.5 us)
Async XLA Ops:
  0.0 37.6 %collective-permute-start = (bf16[48,16384]{1,0:T(8,128)(2,1)}, bf16[48,16384]{1,0:T(8,128)(2,1)S(1)}, u32[]{:S(2)}, u32[]{:S(2)}) collective-permute-start(bf16[48,16384]{1,0:T(8,128)(2,1)} %refs_0_.1), channel_id=1, source_target_pairs={{0,4},{1,5},{4,8},{5,9},{8,12},{9,13},{12,14},{13,15},{14,10},{15,... | collective-permute-start | bytes 4718600 | tf_op jit(solution)/shard_map/ppermute | solution.py:387
  3.0 36.1 %collective-permute-start.2 = (bf16[48,16384]{1,0:T(8,128)(2,1)}, bf16[48,16384]{1,0:T(8,128)(2,1)S(1)}, u32[]{:S(2)}, u32[]{:S(2)}) collective-permute-start(bf16[48,16384]{1,0:T(8,128)(2,1)} %refs_0_.1), channel_id=1, source_target_pairs={{0,2},{1,3},{4,0},{5,1},{8,4},{9,5},{12,8},{13,9},{14,12},{15,13},... | collective-permute-start | bytes 4718600 | tf_op jit(solution)/shard_map/ppermute | solution.py:387
  3.0 38.1 %collective-permute-start.4 = (bf16[48,16384]{1,0:T(8,128)(2,1)}, bf16[48,16384]{1,0:T(8,128)(2,1)S(1)}, u32[]{:S(2)}, u32[]{:S(2)}) collective-permute-start(bf16[48,16384]{1,0:T(8,128)(2,1)} %refs_0_.1), channel_id=1, source_target_pairs={{0,1},{1,0},{2,3},{3,2},{4,5},{5,4},{6,7},{7,6},{8,9},{9,8},{10,11... | collective-permute-start | bytes 4718600 | tf_op jit(solution)/shard_map/ppermute | solution.py:387
  37.6 3.6 %collective-permute-start.5 = (bf16[48,16384]{1,0:T(8,128)(2,1)S(1)}, bf16[48,16384]{1,0:T(8,128)(2,1)S(1)}, u32[]{:S(2)}, u32[]{:S(2)}) collective-permute-start(bf16[48,16384]{1,0:T(8,128)(2,1)S(1)} %collective-permute-done.refs_2_), channel_id=1, source_target_pairs={{0,1},{1,0},{2,3},{3,2},{4,5},{5,4},{6,7},{7,6},{8,9},{9,8},{10,11... | collective-permute-start | bytes 4718600 | tf_op jit(solution)/shard_map/ppermute | solution.py:387
  39.1 4.1 %collective-permute-start.6 = (bf16[48,16384]{1,0:T(8,128)(2,1)S(1)}, bf16[48,16384]{1,0:T(8,128)(2,1)S(1)}, u32[]{:S(2)}, u32[]{:S(2)}) collective-permute-start(bf16[48,16384]{1,0:T(8,128)(2,1)S(1)} %collective-permute-done.2.refs_3_), channel_id=1, source_target_pairs={{0,1},{1,0},{2,3},{3,2},{4,5},{5,4},{6,7},{7,6},{8,9},{9,8},{10,11... | collective-permute-start | bytes 4718600 | tf_op jit(solution)/shard_map/ppermute | solution.py:387
  39.1 36.9 %collective-permute-start.1 = (bf16[48,16384]{1,0:T(8,128)(2,1)S(1)}, bf16[48,16384]{1,0:T(8,128)(2,1)}, u32[]{:S(2)}, u32[]{:S(2)}) collective-permute-start(bf16[48,16384]{1,0:T(8,128)(2,1)S(1)} %collective-permute-done.refs_2_), channel_id=1, source_target_pairs={{0,4},{1,5},{4,8},{5,9},{8,12},{9,13},{12,14},{13,15},{14,10},{15,... | collective-permute-start | bytes 4718600 | tf_op jit(solution)/shard_map/ppermute | solution.py:387
  40.7 36.6 %collective-permute-start.3 = (bf16[48,16384]{1,0:T(8,128)(2,1)S(1)}, bf16[48,16384]{1,0:T(8,128)(2,1)}, u32[]{:S(2)}, u32[]{:S(2)}) collective-permute-start(bf16[48,16384]{1,0:T(8,128)(2,1)S(1)} %collective-permute-done.2.refs_3_), channel_id=1, source_target_pairs={{0,2},{1,3},{4,0},{5,1},{8,4},{9,5},{12,8},{13,9},{14,12},{15,13},... | collective-permute-start | bytes 4718600 | tf_op jit(solution)/shard_map/ppermute | solution.py:387
  77.3 3.8 %collective-permute-start.10 = (bf16[48,16384]{1,0:T(8,128)(2,1)}, bf16[48,16384]{1,0:T(8,128)(2,1)}, u32[]{:S(2)}, u32[]{:S(2)}) collective-permute-start(bf16[48,16384]{1,0:T(8,128)(2,1)} %collective-permute-done.3.refs_1_), channel_id=1, source_target_pairs={{0,1},{1,0},{2,3},{3,2},{4,5},{5,4},{6,7},{7,6},{8,9},{9,8},{10,11... | collective-permute-start | bytes 4718600 | tf_op jit(solution)/shard_map/ppermute | solution.py:387
  77.3 6.0 %collective-permute-start.9 = (bf16[48,16384]{1,0:T(8,128)(2,1)}, bf16[48,16384]{1,0:T(8,128)(2,1)}, u32[]{:S(2)}, u32[]{:S(2)}) collective-permute-start(bf16[48,16384]{1,0:T(8,128)(2,1)} %collective-permute-done.1.refs_0_), channel_id=1, source_target_pairs={{0,1},{1,0},{2,3},{3,2},{4,5},{5,4},{6,7},{7,6},{8,9},{9,8},{10,11... | collective-permute-start | bytes 4718600 | tf_op jit(solution)/shard_map/ppermute | solution.py:387
  77.8 36.6 %collective-permute-start.7 = (bf16[48,16384]{1,0:T(8,128)(2,1)}, bf16[48,16384]{1,0:T(8,128)(2,1)}, u32[]{:S(2)}, u32[]{:S(2)}) collective-permute-start(bf16[48,16384]{1,0:T(8,128)(2,1)} %collective-permute-done.1.refs_0_), channel_id=1, source_target_pairs={{0,4},{1,5},{4,8},{5,9},{8,12},{9,13},{12,14},{13,15},{14,10},{15,... | collective-permute-start | bytes 4718600 | tf_op jit(solution)/shard_map/ppermute | solution.py:387
  79.4 36.3 %collective-permute-start.8 = (bf16[48,16384]{1,0:T(8,128)(2,1)}, bf16[48,16384]{1,0:T(8,128)(2,1)}, u32[]{:S(2)}, u32[]{:S(2)}) collective-permute-start(bf16[48,16384]{1,0:T(8,128)(2,1)} %collective-permute-done.3.refs_1_), channel_id=1, source_target_pairs={{0,2},{1,3},{4,0},{5,1},{8,4},{9,5},{12,8},{13,9},{14,12},{15,13},... | collective-permute-start | bytes 4718600 | tf_op jit(solution)/shard_map/ppermute | solution.py:387
  115.7 18.6 %collective-permute-start.11 = (bf16[48,16384]{1,0:T(8,128)(2,1)}, bf16[48,16384]{1,0:T(8,128)(2,1)}, u32[]{:S(2)}, u32[]{:S(2)}) collective-permute-start(bf16[48,16384]{1,0:T(8,128)(2,1)} %collective-permute-done.7.refs_0_), channel_id=1, source_target_pairs={{0,1},{1,0},{2,3},{3,2},{4,5},{5,4},{6,7},{7,6},{8,9},{9,8},{10,11... | collective-permute-start | bytes 4718600 | tf_op jit(solution)/shard_map/ppermute | solution.py:387
  115.7 18.6 %collective-permute-start.12 = (bf16[48,16384]{1,0:T(8,128)(2,1)}, bf16[48,16384]{1,0:T(8,128)(2,1)}, u32[]{:S(2)}, u32[]{:S(2)}) collective-permute-start(bf16[48,16384]{1,0:T(8,128)(2,1)} %collective-permute-done.8.refs_1_), channel_id=1, source_target_pairs={{0,1},{1,0},{2,3},{3,2},{4,5},{5,4},{6,7},{7,6},{8,9},{9,8},{10,11... | collective-permute-start | bytes 4718600 | tf_op jit(solution)/shard_map/ppermute | solution.py:387
  118.9 7.9 %collective-permute-start.14 = (bf16[48,4096]{1,0:T(8,128)(2,1)S(1)}, bf16[48,4096]{1,0:T(8,128)(2,1)}, u32[]{:S(2)}, u32[]{:S(2)}) collective-permute-start(bf16[48,4096]{1,0:T(8,128)(2,1)S(1)} %get-tuple-element.79), channel_id=1, source_target_pairs={{0,4},{1,3},{4,8},{5,1},{8,12},{9,5},{12,14},{13,9},{14,10},{15,13... | collective-permute-start | bytes 1179656 | tf_op jit(solution)/shard_map/ppermute | solution.py:387
  120.4 10.6 %collective-permute-start.18 = (bf16[48,4096]{1,0:T(8,128)(2,1)}, bf16[48,4096]{1,0:T(8,128)(2,1)}, u32[]{:S(2)}, u32[]{:S(2)}) collective-permute-start(bf16[48,4096]{1,0:T(8,128)(2,1)} %get-tuple-element.77), channel_id=1, source_target_pairs={{0,4},{1,3},{4,8},{5,1},{8,12},{9,5},{12,14},{13,9},{14,10},{15,13... | collective-permute-start | bytes 1179656 | tf_op jit(solution)/shard_map/ppermute | solution.py:387
  126.8 6.1 %collective-permute-start.15 = (bf16[48,4096]{1,0:T(8,128)(2,1)}, bf16[48,4096]{1,0:T(8,128)(2,1)}, u32[]{:S(2)}, u32[]{:S(2)}) collective-permute-start(bf16[48,4096]{1,0:T(8,128)(2,1)} %collective-permute-done.14.refs_4_), channel_id=1, source_target_pairs={{0,1},{1,0},{2,3},{3,2},{4,5},{5,4},{6,7},{7,6},{8,9},{9,8},{10,11... | collective-permute-start | bytes 1179656 | tf_op jit(solution)/shard_map/ppermute | solution.py:387
  126.8 16.2 %collective-permute-start.13 = (bf16[48,4096]{1,0:T(8,128)(2,1)}, bf16[48,4096]{1,0:T(8,128)(2,1)S(1)}, u32[]{:S(2)}, u32[]{:S(2)}) collective-permute-start(bf16[48,4096]{1,0:T(8,128)(2,1)} %get-tuple-element.80), channel_id=1, source_target_pairs={{0,4},{1,3},{4,8},{5,1},{8,12},{9,5},{12,14},{13,9},{14,10},{15,13... | collective-permute-start | bytes 1179656 | tf_op jit(solution)/shard_map/ppermute | solution.py:387
  131.0 12.0 %collective-permute-start.19 = (bf16[48,4096]{1,0:T(8,128)(2,1)}, bf16[48,4096]{1,0:T(8,128)(2,1)}, u32[]{:S(2)}, u32[]{:S(2)}) collective-permute-start(bf16[48,4096]{1,0:T(8,128)(2,1)} %collective-permute-done.18.refs_4_), channel_id=1, source_target_pairs={{0,1},{1,0},{2,3},{3,2},{4,5},{5,4},{6,7},{7,6},{8,9},{9,8},{10,11... | collective-permute-start | bytes 1179656 | tf_op jit(solution)/shard_map/ppermute | solution.py:387
  132.8 17.6 %collective-permute-start.17 = (bf16[48,4096]{1,0:T(8,128)(2,1)}, bf16[48,4096]{1,0:T(8,128)(2,1)S(1)}, u32[]{:S(2)}, u32[]{:S(2)}) collective-permute-start(bf16[48,4096]{1,0:T(8,128)(2,1)} %get-tuple-element.78), channel_id=1, source_target_pairs={{0,4},{1,3},{4,8},{5,1},{8,12},{9,5},{12,14},{13,9},{14,10},{15,13... | collective-permute-start | bytes 1179656 | tf_op jit(solution)/shard_map/ppermute | solution.py:387
  156.8 6.9 %collective-permute-start.21 = (bf16[384,128]{1,0:T(8,128)(2,1)S(1)}, bf16[384,128]{1,0:T(8,128)(2,1)S(1)}, u32[]{:S(2)}, u32[]{:S(2)}) collective-permute-start(bf16[384,128]{1,0:T(8,128)(2,1)S(1)} %ranks.1), channel_id=1, source_target_pairs={{0,1},{1,0},{2,3},{3,2},{4,5},{5,4},{6,7},{7,6},{8,9},{9,8},{10,11... | collective-permute-start | bytes 294920 | tf_op jit(solution)/shard_map/ppermute | solution.py:387
  163.8 10.5 %collective-permute-start.22 = (bf16[384,128]{1,0:T(8,128)(2,1)S(1)}, bf16[384,128]{1,0:T(8,128)(2,1)S(1)}, u32[]{:S(2)}, u32[]{:S(2)}) collective-permute-start(bf16[384,128]{1,0:T(8,128)(2,1)S(1)} %add.29), channel_id=1, source_target_pairs={{0,2},{1,3},{2,0},{3,1},{4,6},{5,7},{6,4},{7,5},{8,10},{9,11},{10,... | collective-permute-start | bytes 294920 | tf_op jit(solution)/shard_map/ppermute | solution.py:387
  164.4 9.9 %collective-permute-start.23 = (bf16[384,128]{1,0:T(8,128)(2,1)S(1)}, bf16[384,128]{1,0:T(8,128)(2,1)S(1)}, u32[]{:S(2)}, u32[]{:S(2)}) collective-permute-start(bf16[384,128]{1,0:T(8,128)(2,1)S(1)} %add.29), channel_id=1, source_target_pairs={{0,4},{1,5},{2,6},{3,7},{4,0},{5,1},{6,2},{7,3},{8,12},{9,13},{10,... | collective-permute-start | bytes 294920 | tf_op jit(solution)/shard_map/ppermute | solution.py:387
  164.8 9.5 %collective-permute-start.24 = (bf16[384,128]{1,0:T(8,128)(2,1)S(1)}, bf16[384,128]{1,0:T(8,128)(2,1)S(1)}, u32[]{:S(2)}, u32[]{:S(2)}) collective-permute-start(bf16[384,128]{1,0:T(8,128)(2,1)S(1)} %add.29), channel_id=1, source_target_pairs={{0,6},{1,7},{2,4},{3,5},{4,2},{5,3},{6,0},{7,1},{8,14},{9,15},{10,... | collective-permute-start | bytes 294920 | tf_op jit(solution)/shard_map/ppermute | solution.py:387
  174.3 7.3 %collective-permute-start.25 = (bf16[384,128]{1,0:T(8,128)(2,1)S(1)}, bf16[384,128]{1,0:T(8,128)(2,1)S(1)}, u32[]{:S(2)}, u32[]{:S(2)}) collective-permute-start(bf16[384,128]{1,0:T(8,128)(2,1)S(1)} %add_add_fusion), channel_id=1, source_target_pairs={{0,8},{1,9},{2,10},{3,11},{4,12},{5,13},{6,14},{7,15},{8,0},{9,1},... | collective-permute-start | bytes 294920 | tf_op jit(solution)/shard_map/ppermute | solution.py:387
  (16 other events, 204.9 us)

commit v4 on v3

--- a/solution.py
+++ b/solution.py
@@ -10,11 +10,12 @@
 
 HD = 128
 SEG = 128
-VMEM = 26 * 1024 * 1024
+VMEM = 20 * 1024 * 1024
 F32 = jnp.float32
 BF16 = jnp.bfloat16
 NT = (((1,), (1,)), ((), ()))
-STREAMS = 4
+SLOTS = 4
+BIG_VMEM = 24 * 1024 * 1024
 PARAMS = pltpu.CompilerParams(vmem_limit_bytes=VMEM)
 SNAKE = (0, 2, 4, 6, 7, 5, 3, 1)
 ROUNDS = len(SNAKE) // 2
@@ -165,9 +166,9 @@
     return pairs
 
 
-def block_kernel(count, first, base, fresh, ranked, *refs):
-    xs, refs = refs[:count], refs[count:]
-    ws, refs = refs[:STREAMS], refs[STREAMS:]
+def block_kernel(starts, low, tile, steps, first, base, fresh, ranked, *refs):
+    count = len(starts)
+    xs, w_ref, refs = refs[:count], refs[count], refs[count + 1 :]
     if ranked:
         s_ref, refs = refs[0], refs[1:]
     if not first:
@@ -177,81 +178,100 @@
     total_out, refs = refs[0], refs[1:]
     if ranked:
         h_out, refs = refs[0], refs[1:]
-    acc, before, sems = refs
-    step, last = pl.program_id(0), pl.num_programs(0) - 1
+    acc, before, x_slots, w_slots, s_slots, sems, total_sems = refs
     rows = xs[0].shape[0]
 
-    def load():
-        return pltpu.make_async_copy(total_in.at[pl.ds(base, count)], before, sems.at[0])
-
-    @pl.when(step == 0)
-    def _():
-        if not fresh:
-            load().start()
-        acc[...] = jnp.zeros_like(acc)
+    def copies(step):
+        slot = lax.rem(step, SLOTS)
+        at = pl.multiple_of(step * tile, tile)
+        sem = lambda i: sems.at[slot, i]
+        out = [pltpu.make_async_copy(w_ref.at[pl.ds(low + at, tile)], w_slots.at[slot], sem(count))]
+        for i, start in enumerate(starts):
+            cut = xs[i].at[:, pl.ds(low - start + at, tile)]
+            out.append(pltpu.make_async_copy(cut, x_slots.at[slot, pl.ds(i * rows, rows)], sem(i)))
         if ranked:
-            h_out[...] = jnp.zeros_like(h_out) if fresh else h_in[...]
-
-    x = jnp.concatenate([ref[...] for ref in xs], 0)
-    w = jnp.concatenate([ref[...] for ref in ws], 0)
-    acc[...] += jnp.dot(x, w, preferred_element_type=F32).reshape(acc.shape)
+            cut = s_ref.at[:, pl.ds(low + at, tile)]
+            out.append(pltpu.make_async_copy(cut, s_slots.at[slot], sem(count + 1)))
+        return out
+
+    def start(step):
+        for copy in copies(step):
+            copy.start()
+
+    for step in range(min(SLOTS, steps)):
+        start(jnp.int32(step))
+    if not fresh:
+        load = pltpu.make_async_copy(total_in.at[pl.ds(base, count)], before, total_sems.at[0])
+        load.start()
+    acc[...] = jnp.zeros_like(acc)
     if ranked:
-        h_out[...] += lax.dot_general(x, s_ref[...], NT, preferred_element_type=F32)
-
-    @pl.when(step == last)
-    def _():
-        if not fresh:
-            load().wait()
-            acc[...] += before[...]
-        store = pltpu.make_async_copy(acc, total_out.at[pl.ds(base, count)], sems.at[1])
-        store.start()
-        store.wait()
+        h_out[...] = jnp.zeros_like(h_out) if fresh else h_in[...]
+
+    @pl.loop(0, steps)
+    def _(step):
+        for copy in copies(step):
+            copy.wait()
+        slot = lax.rem(step, SLOTS)
+        x = x_slots[slot]
+        acc[...] += jnp.dot(x, w_slots[slot], preferred_element_type=F32).reshape(acc.shape)
+        if ranked:
+            h_out[...] += lax.dot_general(x, s_slots[slot], NT, preferred_element_type=F32)
+
+        @pl.when(step + SLOTS < steps)
+        def _():
+            start(step + SLOTS)
+
+    if not fresh:
+        load.wait()
+        acc[...] += before[...]
+    store = pltpu.make_async_copy(acc, total_out.at[pl.ds(base, count)], total_sems.at[1])
+    store.start()
+    store.wait()
 
 
 def block_product(xs, weights, shrink, starts, low, high, tile, total, base, h, ranked):
     count = len(xs)
     rows = xs[0].shape[0]
-    depth, cols = weights.shape
+    cols = weights.shape[1]
     rank = shrink.shape[0]
-    fresh = low == 0
-    skip = low // tile
-    starts = starts or [0] * count
-    strip = tile // STREAMS
-    ranks = pl.BlockSpec((count * rows, rank), lambda k: (0, 0))
-    operands = list(xs) + [weights] * STREAMS
-    specs = [pl.BlockSpec((rows, tile), lambda k, i=(low - start) // tile: (0, k + i)) for start in starts]
-    for i in range(STREAMS):
-        specs.append(pl.BlockSpec((strip, cols), lambda k, i=i: (STREAMS * (k + skip) + i, 0)))
+    fresh, first = low == 0, total is None
+    anywhere, whole = pl.BlockSpec(memory_space=pl.ANY), pl.BlockSpec(memory_space=pltpu.VMEM)
+    operands = list(xs) + [weights]
+    specs = [anywhere] * (count + 1)
     if ranked:
         operands.append(shrink)
-        specs.append(pl.BlockSpec((rank, tile), lambda k: (0, k + skip)))
+        specs.append(anywhere)
     aliases = {}
-    first = total is None
     if not first:
         aliases = {len(operands): 0}
         operands.append(total)
-        specs.append(pl.BlockSpec(memory_space=pl.ANY))
+        specs.append(anywhere)
     if ranked and not fresh:
         operands.append(h)
-        specs.append(ranks)
-    outs = [jax.ShapeDtypeStruct(total_shape(rows, cols), F32)]
-    out_specs = [pl.BlockSpec(memory_space=pl.ANY)]
+        specs.append(whole)
+    outs, out_specs = [jax.ShapeDtypeStruct(total_shape(rows, cols), F32)], [anywhere]
     if ranked:
         outs.append(jax.ShapeDtypeStruct((count * rows, rank), F32))
-        out_specs.append(ranks)
+        out_specs.append(whole)
+    steps = (high - low) // tile
     result = pl.pallas_call(
-        functools.partial(block_kernel, count, first, base, fresh, ranked),
-        grid=((high - low) // tile,),
+        functools.partial(
+            block_kernel, starts or [0] * count, low, tile, steps, first, base, fresh, ranked
+        ),
         in_specs=specs,
         out_specs=out_specs,
         out_shape=outs,
         scratch_shapes=[
             pltpu.VMEM((count, rows, cols), F32),
             pltpu.VMEM((1, 8, 128) if fresh else (count, rows, cols), F32),
+            pltpu.VMEM((SLOTS, count * rows, tile), BF16),
+            pltpu.VMEM((SLOTS, tile, cols), BF16),
+            pltpu.VMEM((SLOTS, rank, tile), BF16),
+            pltpu.SemaphoreType.DMA((SLOTS, count + 2)),
             pltpu.SemaphoreType.DMA((2,)),
         ],
         input_output_aliases=aliases,
-        compiler_params=PARAMS,
+        compiler_params=pltpu.CompilerParams(vmem_limit_bytes=BIG_VMEM),
         cost_estimate=pl.CostEstimate(
             flops=2 * count * rows * (high - low) * cols,
             bytes_accessed=2 * (high - low) * cols,
@@ -405,10 +425,10 @@
         blocks = []
     side = ahead + [swap(part) for part in ahead]
 
-    picked = jnp.where(me % 2 == 0, *ahead)
+    picked = lambda low: jnp.where(me % 2 == 0, *(part[:, low : low + quarter] for part in ahead))
     quarter = depth // 4
     cuts = [q * quarter for q in range(4)]
-    arriving = [send(picked[:, low : low + quarter], across) for low in cuts]
+    arriving = [send(picked(low), across) for low in cuts]
     pieces = [[part, swap(part)] for part in arriving[:2]]
 
     def late_product(q, total, h, ranked, tie=None):

time: 186 us -> 181 us (0.973)
  Pallas kernels: 78.4 us -> 63.5 us
  waiting for transfers between devices: 72 us -> 82 us
    pallas_call x6, Pallas kernels: 71.5 us -> 56.7 us  [block_product(): pl.pallas_call(functools.partial(block_kernel, starts or [0] * count, low...]
    ppermute x26, waiting for transfers between devices: 72 us -> 82 us  [ring_plan(): send = lambda value, pairs: lax.ppermute(value, 'tensor', pairs)]
    unnamed x28 -> x30, local copies, waits for them, and re-layouts: 6.87 us -> 6.88 us
  transfers between devices with their start and end apart: 26 -> 26, of which waited for: 12 -> 12; matrix products, arithmetic and copies ran while one was open for 4% -> 5% of each run, Pallas kernels for 39% -> 31%
where the time goes in v4:
time: 181 us; the launch traced here: 180 us
  waiting for transfers between devices  82 us (45%)
  Pallas kernels  63.5 us (35%)
  starting transfers between devices  19.1 us (11%)
  local copies, waits for them, and re-layouts  9.68 us (5%)
  other arithmetic  5.54 us (3%)
    ppermute x26, waiting for transfers between devices, ring_plan(): send = lambda value, pairs: lax.ppermute(value, 'tensor', pairs)  82 us
    pallas_call x6, Pallas kernels, block_product(): pl.pallas_call(functools.partial(block_kernel, starts or [0] * count, low...  56.7 us
    ppermute x26, starting transfers between devices, ring_plan(): send = lambda value, pairs: lax.ppermute(value, 'tensor', pairs)  19.1 us
    unnamed x30, local copies, waits for them, and re-layouts  6.88 us
    pallas_call x1, Pallas kernels, rank_terms(): pl.pallas_call(functools.partial(rank_kernel, counts, len(side), len(piec...  3.87 us
  transfers between devices with their start and end apart: 26, of which 12 were waited for; matrix products, arithmetic and copies ran while one was open for 5% of the time, Pallas kernels for 31%

profile of v4, /device:TPU:0, one launch (start us, length us, event | category | flops | bytes accessed | tf_op | source)
XLA Modules:
  0.0 180.1 jit_solution(15318633991114562488)
XLA Ops:
  0.0 3.0 %collective-permute-start = (bf16[48,16384]{1,0:T(8,128)(2,1)}, bf16[48,16384]{1,0:T(8,128)(2,1)S(1)}, u32[]{:S(2)}, u32[]{:S(2)}) collective-permute-start(bf16[48,16384]{1,0:T(8,128)(2,1)} %refs_0_.1), channel_id=1, source_target_pairs={{0,4},{1,5},{4,8},{5,9},{8,12},{9,13},{12,14},{13,15},{14,10},{15,... | collective-permute-start | bytes 4718600 | tf_op jit(solution)/shard_map/ppermute | solution.py:407
  3.0 34.5 %collective-permute-done.refs_2_ = bf16[48,16384]{1,0:T(8,128)(2,1)S(1)} collective-permute-done((bf16[48,16384]{1,0:T(8,128)(2,1)}, bf16[48,16384]{1,0:T(8,128)(2,1)S(1)}, u32[]{:S(2)}, u32[]{:S(2)}) %collective-permute-start) | collective-permute-done | bytes 1572896 | tf_op jit(solution)/shard_map/ppermute | solution.py:407
  39.1 1.6 collective-permute-start.1
  41.1 2.1 %collective-permute-done.6.refs_5_ = bf16[48,16384]{1,0:T(8,128)(2,1)S(1)} collective-permute-done((bf16[48,16384]{1,0:T(8,128)(2,1)S(1)}, bf16[48,16384]{1,0:T(8,128)(2,1)S(1)}, u32[]{:S(2)}, u32[]{:S(2)}) %collective-permute-start.6) | collective-permute-done | bytes 1572896 | tf_op jit(solution)/shard_map/ppermute | solution.py:407
  43.2 1.6 copy-done.2
  46.2 19.4 %blocks.6 = (f32[16,48,1024]{2,1,0:T(8,128)S(1)}, f32[288,64]{1,0:T(8,128)S(1)}) custom-call(bf16[48,16384]{1,0:T(8,128)(2,1)S(1)} %copy-done.7, bf16[48,16384]{1,0:T(8,128)(2,1)S(1)} %collective-permute-done.4.refs_1_, bf16[48,16384]{1,0:T(8,128)(2,1)S(1)} %collective-permute-done.refs_2_, bf16[48,16384]{1,0:T(8,128)(2,1)S(1)} %collective-permute-done.2.refs_3_, ...), custom_call_target="tpu_custom_call" | custom-call | flops 9663676416 | bytes 33554432 | tf_op jit(solution)/shard_map/blocks/pallas_call | solution.py:257
  66.3 9.7 %collective-permute-done.1.refs_0_ = bf16[48,16384]{1,0:T(8,128)(2,1)} collective-permute-done((bf16[48,16384]{1,0:T(8,128)(2,1)S(1)}, bf16[48,16384]{1,0:T(8,128)(2,1)}, u32[]{:S(2)}, u32[]{:S(2)}) %collective-permute-start.1) | collective-permute-done | bytes 1572896 | tf_op jit(solution)/shard_map/ppermute | solution.py:407
  81.1 2.2 %collective-permute-done.9.refs_2_ = bf16[48,16384]{1,0:T(8,128)(2,1)} collective-permute-done((bf16[48,16384]{1,0:T(8,128)(2,1)}, bf16[48,16384]{1,0:T(8,128)(2,1)}, u32[]{:S(2)}, u32[]{:S(2)}) %collective-permute-start.9) | collective-permute-done | bytes 1572896 | tf_op jit(solution)/shard_map/ppermute | solution.py:407
  83.3 1.6 copy-done.3
  84.9 13.9 %blocks.7 = (f32[16,48,1024]{2,1,0:T(8,128)S(1)}, f32[192,64]{1,0:T(8,128)S(1)}) custom-call(bf16[48,16384]{1,0:T(8,128)(2,1)} %collective-permute-done.1.refs_0_, bf16[48,16384]{1,0:T(8,128)(2,1)} %collective-permute-done.3.refs_1_, bf16[48,16384]{1,0:T(8,128)(2,1)} %collective-permute-done.9.refs_2_, ...), custom_call_target="tpu_custom_call", output_to_operand_aliasing={{0}: (6, {})} | custom-call | flops 6442450944 | bytes 33554432 | tf_op jit(solution)/shard_map/blocks/pallas_call | solution.py:257
  98.8 15.6 %collective-permute-done.7.refs_0_ = bf16[48,16384]{1,0:T(8,128)(2,1)} collective-permute-done((bf16[48,16384]{1,0:T(8,128)(2,1)}, bf16[48,16384]{1,0:T(8,128)(2,1)}, u32[]{:S(2)}, u32[]{:S(2)}) %collective-permute-start.7) | collective-permute-done | bytes 1572896 | tf_op jit(solution)/shard_map/ppermute | solution.py:407
  116.2 2.9 %slice_select_fusion = (bf16[48,4096]{1,0:T(8,128)(2,1)}, bf16[48,4096]{1,0:T(8,128)(2,1)}, bf16[48,4096]{1,0:T(8,128)(2,1)S(1)}, bf16[48,4096]{1,0:T(8,128)(2,1)}) fusion(bf16[48,16384]{1,0:T(8,128)(2,1)} %collective-permute-done.8.refs_1_, bf16[48,16384]{1,0:T(8,128)(2,1)} %collective-permute-done.7.refs_0_, pred[]{:T(512)S(6)} %eq.11), kind=kLoop, calls=%fused_computation.5 | loop fusion | flops 786432 | bytes 4718593 | tf_op jit(solution)/shard_map/jit(_where)/select_n | solution.py:428
  121.4 5.6 %collective-permute-done.14.refs_4_ = bf16[48,4096]{1,0:T(8,128)(2,1)} collective-permute-done((bf16[48,4096]{1,0:T(8,128)(2,1)S(1)}, bf16[48,4096]{1,0:T(8,128)(2,1)}, u32[]{:S(2)}, u32[]{:S(2)}) %collective-permute-start.14) | collective-permute-done | bytes 393248 | tf_op jit(solution)/shard_map/ppermute | solution.py:407
  128.5 2.7 %collective-permute-done.18.refs_4_ = bf16[48,4096]{1,0:T(8,128)(2,1)} collective-permute-done((bf16[48,4096]{1,0:T(8,128)(2,1)}, bf16[48,4096]{1,0:T(8,128)(2,1)}, u32[]{:S(2)}, u32[]{:S(2)}) %collective-permute-start.18) | collective-permute-done | bytes 393248 | tf_op jit(solution)/shard_map/ppermute | solution.py:407
  134.6 1.6 copy-done.4
  136.2 6.0 %blocks.8 = (f32[16,48,1024]{2,1,0:T(8,128)S(1)}, f32[288,64]{1,0:T(8,128)S(1)}) custom-call(bf16[48,16384]{1,0:T(8,128)(2,1)} %collective-permute-done.7.refs_0_, bf16[48,16384]{1,0:T(8,128)(2,1)} %collective-permute-done.8.refs_1_, bf16[48,16384]{1,0:T(8,128)(2,1)} %collective-permute-done.11.refs_2_, ...), custom_call_target="tpu_custom_call", output_to_operand_aliasing={{0}: (8, {})} | custom-call | flops 2415919104 | bytes 8388608 | tf_op jit(solution)/shard_map/blocks/pallas_call | solution.py:257
  142.3 6.2 %blocks.9 = (f32[16,48,1024]{2,1,0:T(8,128)S(1)}, f32[288,64]{1,0:T(8,128)S(1)}) custom-call(bf16[48,16384]{1,0:T(8,128)(2,1)} %collective-permute-done.7.refs_0_, bf16[48,16384]{1,0:T(8,128)(2,1)} %collective-permute-done.8.refs_1_, bf16[48,16384]{1,0:T(8,128)(2,1)} %collective-permute-done.11.refs_2_, ...), custom_call_target="tpu_custom_call", output_to_operand_aliasing={{0}: (8, {})} | custom-call | flops 2415919104 | bytes 8388608 | tf_op jit(solution)/shard_map/blocks/pallas_call | solution.py:257
  151.0 3.9 %ranks.1 = bf16[384,128]{1,0:T(8,128)(2,1)S(1)} custom-call(s32[16]{0:T(128)S(1)} %dynamic-slice_bitcast_fusion.owners_ref, s32[7]{0:T(128)S(1)} %pad_add_fusion.slot_ref, bf16[48,16384]{1,0:T(8,128)(2,1)} %collective-permute-done.7.refs_0_, bf16[48,16384]{1,0:T(8,128)(2,1)} %collective-permute-done.8.refs_1_, ...), custom_call_target="tpu_custom_call" | custom-call | tf_op jit(solution)/shard_map/ranks/pallas_call | solution.py:325
  155.0 5.5 %blocks.10.refs_7_ = f32[16,48,1024]{2,1,0:T(8,128)S(1)} custom-call(bf16[48,16384]{1,0:T(8,128)(2,1)} %collective-permute-done.7.refs_0_, bf16[48,16384]{1,0:T(8,128)(2,1)} %collective-permute-done.8.refs_1_, bf16[48,16384]{1,0:T(8,128)(2,1)} %collective-permute-done.11.refs_2_, ...), custom_call_target="tpu_custom_call", output_to_operand_aliasing={{}: (7, {})} | custom-call | flops 2415919104 | bytes 8388608 | tf_op jit(solution)/shard_map/blocks/pallas_call | solution.py:257
  161.6 2.5 %collective-permute-start.24 = (bf16[384,128]{1,0:T(8,128)(2,1)S(1)}, bf16[384,128]{1,0:T(8,128)(2,1)S(1)}, u32[]{:S(2)}, u32[]{:S(2)}) collective-permute-start(bf16[384,128]{1,0:T(8,128)(2,1)S(1)} %add.32), channel_id=1, source_target_pairs={{0,6},{1,7},{2,4},{3,5},{4,2},{5,3},{6,0},{7,1},{8,14},{9,15},{10,... | collective-permute-start | bytes 294920 | tf_op jit(solution)/shard_map/ppermute | solution.py:407
  164.1 5.6 %blocks.11.refs_0_.refs_1_.refs_2_.refs_3_.refs_4_.refs_5_.refs_6_.refs_7_ = f32[16,48,1024]{2,1,0:T(8,128)S(1)} custom-call(bf16[48,16384]{1,0:T(8,128)(2,1)} %collective-permute-done.7.refs_0_, bf16[48,16384]{1,0:T(8,128)(2,1)} %collective-permute-done.8.refs_1_, ...), custom_call_target="tpu_custom_call", output_to_operand_aliasing={{}: (7, {})} | custom-call | flops 2415919104 | bytes 8388608 | tf_op jit(solution)/shard_map/blocks/pallas_call | solution.py:257
  169.8 1.7 collective-permute-start.25
  172.2 4.9 %collective-permute-done.25 = bf16[384,128]{1,0:T(8,128)(2,1)S(1)} collective-permute-done((bf16[384,128]{1,0:T(8,128)(2,1)S(1)}, bf16[384,128]{1,0:T(8,128)(2,1)S(1)}, u32[]{:S(2)}, u32[]{:S(2)}) %collective-permute-start.25) | collective-permute-done | bytes 98336 | tf_op jit(solution)/shard_map/ppermute | solution.py:407
  177.2 3.0 %finish.1 = bf16[768,1024]{1,0:T(8,128)(2,1)} custom-call(s32[16]{0:T(128)S(1)} %dynamic-slice_bitcast_fusion.1.places_ref, s32[6]{0:T(128)S(1)} %gather_fusion, f32[16,48,1024]{2,1,0:T(8,128)S(1)} %blocks.11.refs_0_.refs_1_.refs_2_.refs_3_.refs_4_.refs_5_.refs_6_.refs_7_, ...), custom_call_target="tpu_custom_call" | custom-call | tf_op jit(solution)/shard_map/finish/pallas_call | solution.py:376
  (83 shorter events, 22.4 us)
Async XLA Ops:
  0.0 37.6 %collective-permute-start = (bf16[48,16384]{1,0:T(8,128)(2,1)}, bf16[48,16384]{1,0:T(8,128)(2,1)S(1)}, u32[]{:S(2)}, u32[]{:S(2)}) collective-permute-start(bf16[48,16384]{1,0:T(8,128)(2,1)} %refs_0_.1), channel_id=1, source_target_pairs={{0,4},{1,5},{4,8},{5,9},{8,12},{9,13},{12,14},{13,15},{14,10},{15,... | collective-permute-start | bytes 4718600 | tf_op jit(solution)/shard_map/ppermute | solution.py:407
  3.0 36.1 %collective-permute-start.2 = (bf16[48,16384]{1,0:T(8,128)(2,1)}, bf16[48,16384]{1,0:T(8,128)(2,1)S(1)}, u32[]{:S(2)}, u32[]{:S(2)}) collective-permute-start(bf16[48,16384]{1,0:T(8,128)(2,1)} %refs_0_.1), channel_id=1, source_target_pairs={{0,2},{1,3},{4,0},{5,1},{8,4},{9,5},{12,8},{13,9},{14,12},{15,13},... | collective-permute-start | bytes 4718600 | tf_op jit(solution)/shard_map/ppermute | solution.py:407
  3.0 38.1 %collective-permute-start.4 = (bf16[48,16384]{1,0:T(8,128)(2,1)}, bf16[48,16384]{1,0:T(8,128)(2,1)S(1)}, u32[]{:S(2)}, u32[]{:S(2)}) collective-permute-start(bf16[48,16384]{1,0:T(8,128)(2,1)} %refs_0_.1), channel_id=1, source_target_pairs={{0,1},{1,0},{2,3},{3,2},{4,5},{5,4},{6,7},{7,6},{8,9},{9,8},{10,11... | collective-permute-start | bytes 4718600 | tf_op jit(solution)/shard_map/ppermute | solution.py:407
  37.6 3.6 %collective-permute-start.5 = (bf16[48,16384]{1,0:T(8,128)(2,1)S(1)}, bf16[48,16384]{1,0:T(8,128)(2,1)S(1)}, u32[]{:S(2)}, u32[]{:S(2)}) collective-permute-start(bf16[48,16384]{1,0:T(8,128)(2,1)S(1)} %collective-permute-done.refs_2_), channel_id=1, source_target_pairs={{0,1},{1,0},{2,3},{3,2},{4,5},{5,4},{6,7},{7,6},{8,9},{9,8},{10,11... | collective-permute-start | bytes 4718600 | tf_op jit(solution)/shard_map/ppermute | solution.py:407
  39.1 4.1 %collective-permute-start.6 = (bf16[48,16384]{1,0:T(8,128)(2,1)S(1)}, bf16[48,16384]{1,0:T(8,128)(2,1)S(1)}, u32[]{:S(2)}, u32[]{:S(2)}) collective-permute-start(bf16[48,16384]{1,0:T(8,128)(2,1)S(1)} %collective-permute-done.2.refs_3_), channel_id=1, source_target_pairs={{0,1},{1,0},{2,3},{3,2},{4,5},{5,4},{6,7},{7,6},{8,9},{9,8},{10,11... | collective-permute-start | bytes 4718600 | tf_op jit(solution)/shard_map/ppermute | solution.py:407
  39.1 36.9 %collective-permute-start.1 = (bf16[48,16384]{1,0:T(8,128)(2,1)S(1)}, bf16[48,16384]{1,0:T(8,128)(2,1)}, u32[]{:S(2)}, u32[]{:S(2)}) collective-permute-start(bf16[48,16384]{1,0:T(8,128)(2,1)S(1)} %collective-permute-done.refs_2_), channel_id=1, source_target_pairs={{0,4},{1,5},{4,8},{5,9},{8,12},{9,13},{12,14},{13,15},{14,10},{15,... | collective-permute-start | bytes 4718600 | tf_op jit(solution)/shard_map/ppermute | solution.py:407
  40.7 36.6 %collective-permute-start.3 = (bf16[48,16384]{1,0:T(8,128)(2,1)S(1)}, bf16[48,16384]{1,0:T(8,128)(2,1)}, u32[]{:S(2)}, u32[]{:S(2)}) collective-permute-start(bf16[48,16384]{1,0:T(8,128)(2,1)S(1)} %collective-permute-done.2.refs_3_), channel_id=1, source_target_pairs={{0,2},{1,3},{4,0},{5,1},{8,4},{9,5},{12,8},{13,9},{14,12},{15,13},... | collective-permute-start | bytes 4718600 | tf_op jit(solution)/shard_map/ppermute | solution.py:407
  77.3 3.8 %collective-permute-start.10 = (bf16[48,16384]{1,0:T(8,128)(2,1)}, bf16[48,16384]{1,0:T(8,128)(2,1)}, u32[]{:S(2)}, u32[]{:S(2)}) collective-permute-start(bf16[48,16384]{1,0:T(8,128)(2,1)} %collective-permute-done.3.refs_1_), channel_id=1, source_target_pairs={{0,1},{1,0},{2,3},{3,2},{4,5},{5,4},{6,7},{7,6},{8,9},{9,8},{10,11... | collective-permute-start | bytes 4718600 | tf_op jit(solution)/shard_map/ppermute | solution.py:407
  77.3 6.0 %collective-permute-start.9 = (bf16[48,16384]{1,0:T(8,128)(2,1)}, bf16[48,16384]{1,0:T(8,128)(2,1)}, u32[]{:S(2)}, u32[]{:S(2)}) collective-permute-start(bf16[48,16384]{1,0:T(8,128)(2,1)} %collective-permute-done.1.refs_0_), channel_id=1, source_target_pairs={{0,1},{1,0},{2,3},{3,2},{4,5},{5,4},{6,7},{7,6},{8,9},{9,8},{10,11... | collective-permute-start | bytes 4718600 | tf_op jit(solution)/shard_map/ppermute | solution.py:407
  77.8 36.6 %collective-permute-start.7 = (bf16[48,16384]{1,0:T(8,128)(2,1)}, bf16[48,16384]{1,0:T(8,128)(2,1)}, u32[]{:S(2)}, u32[]{:S(2)}) collective-permute-start(bf16[48,16384]{1,0:T(8,128)(2,1)} %collective-permute-done.1.refs_0_), channel_id=1, source_target_pairs={{0,4},{1,5},{4,8},{5,9},{8,12},{9,13},{12,14},{13,15},{14,10},{15,... | collective-permute-start | bytes 4718600 | tf_op jit(solution)/shard_map/ppermute | solution.py:407
  79.4 36.3 %collective-permute-start.8 = (bf16[48,16384]{1,0:T(8,128)(2,1)}, bf16[48,16384]{1,0:T(8,128)(2,1)}, u32[]{:S(2)}, u32[]{:S(2)}) collective-permute-start(bf16[48,16384]{1,0:T(8,128)(2,1)} %collective-permute-done.3.refs_1_), channel_id=1, source_target_pairs={{0,2},{1,3},{4,0},{5,1},{8,4},{9,5},{12,8},{13,9},{14,12},{15,13},... | collective-permute-start | bytes 4718600 | tf_op jit(solution)/shard_map/ppermute | solution.py:407
  115.7 18.9 %collective-permute-start.11 = (bf16[48,16384]{1,0:T(8,128)(2,1)}, bf16[48,16384]{1,0:T(8,128)(2,1)}, u32[]{:S(2)}, u32[]{:S(2)}) collective-permute-start(bf16[48,16384]{1,0:T(8,128)(2,1)} %collective-permute-done.7.refs_0_), channel_id=1, source_target_pairs={{0,1},{1,0},{2,3},{3,2},{4,5},{5,4},{6,7},{7,6},{8,9},{9,8},{10,11... | collective-permute-start | bytes 4718600 | tf_op jit(solution)/shard_map/ppermute | solution.py:407
  115.7 18.9 %collective-permute-start.12 = (bf16[48,16384]{1,0:T(8,128)(2,1)}, bf16[48,16384]{1,0:T(8,128)(2,1)}, u32[]{:S(2)}, u32[]{:S(2)}) collective-permute-start(bf16[48,16384]{1,0:T(8,128)(2,1)} %collective-permute-done.8.refs_1_), channel_id=1, source_target_pairs={{0,1},{1,0},{2,3},{3,2},{4,5},{5,4},{6,7},{7,6},{8,9},{9,8},{10,11... | collective-permute-start | bytes 4718600 | tf_op jit(solution)/shard_map/ppermute | solution.py:407
  119.1 7.9 %collective-permute-start.14 = (bf16[48,4096]{1,0:T(8,128)(2,1)S(1)}, bf16[48,4096]{1,0:T(8,128)(2,1)}, u32[]{:S(2)}, u32[]{:S(2)}) collective-permute-start(bf16[48,4096]{1,0:T(8,128)(2,1)S(1)} %get-tuple-element.79), channel_id=1, source_target_pairs={{0,4},{1,3},{4,8},{5,1},{8,12},{9,5},{12,14},{13,9},{14,10},{15,13... | collective-permute-start | bytes 1179656 | tf_op jit(solution)/shard_map/ppermute | solution.py:407
  120.6 10.6 %collective-permute-start.18 = (bf16[48,4096]{1,0:T(8,128)(2,1)}, bf16[48,4096]{1,0:T(8,128)(2,1)}, u32[]{:S(2)}, u32[]{:S(2)}) collective-permute-start(bf16[48,4096]{1,0:T(8,128)(2,1)} %get-tuple-element.77), channel_id=1, source_target_pairs={{0,4},{1,3},{4,8},{5,1},{8,12},{9,5},{12,14},{13,9},{14,10},{15,13... | collective-permute-start | bytes 1179656 | tf_op jit(solution)/shard_map/ppermute | solution.py:407
  127.0 6.1 %collective-permute-start.15 = (bf16[48,4096]{1,0:T(8,128)(2,1)}, bf16[48,4096]{1,0:T(8,128)(2,1)}, u32[]{:S(2)}, u32[]{:S(2)}) collective-permute-start(bf16[48,4096]{1,0:T(8,128)(2,1)} %collective-permute-done.14.refs_4_), channel_id=1, source_target_pairs={{0,1},{1,0},{2,3},{3,2},{4,5},{5,4},{6,7},{7,6},{8,9},{9,8},{10,11... | collective-permute-start | bytes 1179656 | tf_op jit(solution)/shard_map/ppermute | solution.py:407
  127.0 15.3 %collective-permute-start.13 = (bf16[48,4096]{1,0:T(8,128)(2,1)}, bf16[48,4096]{1,0:T(8,128)(2,1)S(1)}, u32[]{:S(2)}, u32[]{:S(2)}) collective-permute-start(bf16[48,4096]{1,0:T(8,128)(2,1)} %get-tuple-element.80), channel_id=1, source_target_pairs={{0,4},{1,3},{4,8},{5,1},{8,12},{9,5},{12,14},{13,9},{14,10},{15,13... | collective-permute-start | bytes 1179656 | tf_op jit(solution)/shard_map/ppermute | solution.py:407
  131.2 11.1 %collective-permute-start.19 = (bf16[48,4096]{1,0:T(8,128)(2,1)}, bf16[48,4096]{1,0:T(8,128)(2,1)}, u32[]{:S(2)}, u32[]{:S(2)}) collective-permute-start(bf16[48,4096]{1,0:T(8,128)(2,1)} %collective-permute-done.18.refs_4_), channel_id=1, source_target_pairs={{0,1},{1,0},{2,3},{3,2},{4,5},{5,4},{6,7},{7,6},{8,9},{9,8},{10,11... | collective-permute-start | bytes 1179656 | tf_op jit(solution)/shard_map/ppermute | solution.py:407
  133.1 15.4 %collective-permute-start.17 = (bf16[48,4096]{1,0:T(8,128)(2,1)}, bf16[48,4096]{1,0:T(8,128)(2,1)S(1)}, u32[]{:S(2)}, u32[]{:S(2)}) collective-permute-start(bf16[48,4096]{1,0:T(8,128)(2,1)} %get-tuple-element.78), channel_id=1, source_target_pairs={{0,4},{1,3},{4,8},{5,1},{8,12},{9,5},{12,14},{13,9},{14,10},{15,13... | collective-permute-start | bytes 1179656 | tf_op jit(solution)/shard_map/ppermute | solution.py:407
  154.8 5.7 %collective-permute-start.21 = (bf16[384,128]{1,0:T(8,128)(2,1)S(1)}, bf16[384,128]{1,0:T(8,128)(2,1)S(1)}, u32[]{:S(2)}, u32[]{:S(2)}) collective-permute-start(bf16[384,128]{1,0:T(8,128)(2,1)S(1)} %ranks.1), channel_id=1, source_target_pairs={{0,1},{1,0},{2,3},{3,2},{4,5},{5,4},{6,7},{7,6},{8,9},{9,8},{10,11... | collective-permute-start | bytes 294920 | tf_op jit(solution)/shard_map/ppermute | solution.py:407
  160.6 9.2 %collective-permute-start.22 = (bf16[384,128]{1,0:T(8,128)(2,1)S(1)}, bf16[384,128]{1,0:T(8,128)(2,1)S(1)}, u32[]{:S(2)}, u32[]{:S(2)}) collective-permute-start(bf16[384,128]{1,0:T(8,128)(2,1)S(1)} %add.32), channel_id=1, source_target_pairs={{0,2},{1,3},{2,0},{3,1},{4,6},{5,7},{6,4},{7,5},{8,10},{9,11},{10,... | collective-permute-start | bytes 294920 | tf_op jit(solution)/shard_map/ppermute | solution.py:407
  161.1 8.7 %collective-permute-start.23 = (bf16[384,128]{1,0:T(8,128)(2,1)S(1)}, bf16[384,128]{1,0:T(8,128)(2,1)S(1)}, u32[]{:S(2)}, u32[]{:S(2)}) collective-permute-start(bf16[384,128]{1,0:T(8,128)(2,1)S(1)} %add.32), channel_id=1, source_target_pairs={{0,4},{1,5},{2,6},{3,7},{4,0},{5,1},{6,2},{7,3},{8,12},{9,13},{10,... | collective-permute-start | bytes 294920 | tf_op jit(solution)/shard_map/ppermute | solution.py:407
  161.6 8.2 %collective-permute-start.24 = (bf16[384,128]{1,0:T(8,128)(2,1)S(1)}, bf16[384,128]{1,0:T(8,128)(2,1)S(1)}, u32[]{:S(2)}, u32[]{:S(2)}) collective-permute-start(bf16[384,128]{1,0:T(8,128)(2,1)S(1)} %add.32), channel_id=1, source_target_pairs={{0,6},{1,7},{2,4},{3,5},{4,2},{5,3},{6,0},{7,1},{8,14},{9,15},{10,... | collective-permute-start | bytes 294920 | tf_op jit(solution)/shard_map/ppermute | solution.py:407
  169.8 7.3 %collective-permute-start.25 = (bf16[384,128]{1,0:T(8,128)(2,1)S(1)}, bf16[384,128]{1,0:T(8,128)(2,1)S(1)}, u32[]{:S(2)}, u32[]{:S(2)}) collective-permute-start(bf16[384,128]{1,0:T(8,128)(2,1)S(1)} %add_add_fusion), channel_id=1, source_target_pairs={{0,8},{1,9},{2,10},{3,11},{4,12},{5,13},{6,14},{7,15},{8,0},{9,1},... | collective-permute-start | bytes 294920 | tf_op jit(solution)/shard_map/ppermute | solution.py:407
  (17 other events, 213.8 us)

commit v5 on v4

--- a/solution.py
+++ b/solution.py
@@ -148,11 +148,13 @@
     for place, chip in enumerate(SNAKE):
         for core in (0, 1):
             row = [2 * chip + core, 2 * chip + 1 - core]
-            for r in range(1, ROUNDS):
-                before, after = SNAKE[place - r], SNAKE[(place + r) % chips]
-                row += [2 * before + core, 2 * after + core, 2 * before + 1 - core, 2 * after + 1 - core]
-            across = SNAKE[(place + ROUNDS) % chips]
-            row += [2 * across + core, 2 * across + 1 - core]
+            for r in range(1, ROUNDS + 1):
+                far, near = place - r * (1 - 2 * core), place + r * (1 - 2 * core)
+                far, near = SNAKE[far % chips], SNAKE[near % chips]
+                if r < ROUNDS:
+                    row += [2 * far + core, 2 * near + core, 2 * near + 1 - core, 2 * far + 1 - core]
+                else:
+                    row += [2 * far + core, 2 * near + 1 - core]
             owners[2 * chip + core] = row
     return owners
 
@@ -286,21 +288,13 @@
     return (2 * len(SNAKE), rows, cols)
 
 
-def rank_kernel(counts, sides, pieces, owners_ref, slot_ref, *refs):
-    side, refs = refs[:sides], refs[sides:]
-    split, refs = refs[: 2 * pieces], refs[2 * pieces :]
-    s_ref, h_refs, out_ref, placed = refs[0], refs[1:-2], refs[-2], refs[-1]
-    rows, width = side[0].shape
-    x = jnp.concatenate([ref[...] for ref in side], 0)
-    grown = lax.dot_general(x, s_ref[...], NT, preferred_element_type=F32)
-    last = 0.0
-    for piece in range(pieces):
-        x = jnp.concatenate([split[2 * piece][...], split[2 * piece + 1][...]], 0)
-        cut = slice(piece * width // pieces, (piece + 1) * width // pieces)
-        last += lax.dot_general(x, s_ref[:, cut], NT, preferred_element_type=F32)
-    late = h_refs[-1][...] + jnp.concatenate([grown, last], 0)
+def rank_kernel(counts, owners_ref, slot_ref, xa_ref, xb_ref, s_ref, *refs):
+    h_refs, out_ref, placed = refs[:-2], refs[-2], refs[-1]
+    rows = xa_ref.shape[0]
+    x = jnp.concatenate([xa_ref[...], xb_ref[...]], 0)
+    last = lax.dot_general(x, s_ref[...], NT, preferred_element_type=F32)
     block = 0
-    for count, source in zip(counts, h_refs[:-1] + (late,)):
+    for count, source in zip(counts, h_refs + (last,)):
         for i in range(count):
             to = pl.multiple_of(owners_ref[block] * rows, 16)
             placed[pl.ds(to, rows), :] = source[i * rows : (i + 1) * rows, :]
@@ -314,22 +308,19 @@
     out_ref[...] = jnp.concatenate([left, right], 1).astype(out_ref.dtype)
 
 
-def rank_terms(owners, slots, side, pieces, shrink, low, hs):
-    rows, depth = side[0].shape
+def rank_terms(owners, slots, xs, shrink, hs):
+    rows, depth = xs[0].shape
     rank = shrink.shape[0]
-    counts = [h.shape[0] // rows for h in hs]
+    counts = [h.shape[0] // rows for h in hs] + [len(xs)]
     total_rows = sum(counts) * rows
     whole = lambda shape: pl.BlockSpec(shape, lambda _, *rest: (0, 0))
-    upper = lambda height: pl.BlockSpec((height, depth - low), lambda _, *rest: (0, low // (depth - low)))
-    flat = [part for piece in pieces for part in piece]
     return pl.pallas_call(
-        functools.partial(rank_kernel, counts, len(side), len(pieces)),
+        functools.partial(rank_kernel, counts),
         grid_spec=pltpu.PrefetchScalarGridSpec(
             num_scalar_prefetch=2,
             grid=(1,),
-            in_specs=[upper(rows)] * len(side)
-            + [whole(part.shape) for part in flat]
-            + [upper(rank)]
+            in_specs=[whole((rows, depth))] * 2
+            + [whole((rank, depth))]
             + [whole(h.shape) for h in hs],
             out_specs=whole((total_rows // 2, 2 * rank)),
             scratch_shapes=[pltpu.VMEM((total_rows, rank), F32)],
@@ -337,7 +328,7 @@
         out_shape=jax.ShapeDtypeStruct((total_rows // 2, 2 * rank), BF16),
         compiler_params=PARAMS,
         name="ranks",
-    )(owners, slots, *side, *flat, shrink, *hs)
+    )(owners, slots, *xs, shrink, *hs)
 
 
 def block_finish_kernel(blocks, segments, places_ref, slot_ref, *refs):
@@ -406,50 +397,33 @@
     shrink = shrinks[0]
     send = lambda value, pairs: lax.ppermute(value, "tensor", pairs)
     swap = lambda value: send(value, [(i, i ^ 1) for i in range(parts)])
-    onward, back = ring_pairs((1, 1)), ring_pairs((-1, -1))
-    across = ring_pairs((1, -1))
+    out, home = ring_pairs((1, -1)), ring_pairs((-1, 1))
 
     total, hs, held = None, [], 0
     blocks = [tokens, swap(tokens)]
+    tables = (owners, places, slots, segment_slot, cosine, sine)
+    blocks, tables = lax.optimization_barrier((blocks, tables))
+    owners, places, slots, segment_slot, cosine, sine = tables
     ahead = [tokens, tokens]
     for r in range(1, ROUNDS):
-        ahead = [send(ahead[0], onward), send(ahead[1], back)]
+        ahead = [send(ahead[0], out), send(ahead[1], home)]
         if total is not None:
             ahead, total = lax.optimization_barrier((ahead, total))
-        if r == ROUNDS - 1:
-            break
         blocks += ahead + [swap(part) for part in ahead]
         total, h = block_product(blocks, weights, shrink, None, 0, depth, tile, total, held, None, True)
         hs.append(h)
         held += len(blocks)
         blocks = []
-    side = ahead + [swap(part) for part in ahead]
-
-    picked = lambda low: jnp.where(me % 2 == 0, *(part[:, low : low + quarter] for part in ahead))
-    quarter = depth // 4
-    cuts = [q * quarter for q in range(4)]
-    arriving = [send(picked(low), across) for low in cuts]
-    pieces = [[part, swap(part)] for part in arriving[:2]]
-
-    def late_product(q, total, h, ranked, tie=None):
-        xs = side + pieces[q]
-        if tie is not None:
-            xs, _ = lax.optimization_barrier((xs, tie))
-        starts = [0] * len(side) + [cuts[q]] * 2
-        return block_product(
-            xs, weights, shrink, starts, cuts[q], cuts[q] + quarter, tile, total, held, h, ranked
-        )
-
-    h_late = None
-    for q in (0, 1):
-        total, h_late = late_product(q, total, h_late, True)
-        part, total = lax.optimization_barrier((arriving[q + 2], total))
-        pieces.append([part, swap(part)])
-    h = rank_terms(owners, slots, side, pieces[2:], shrink, cuts[2], hs + [h_late])
-    for q, steps in zip((2, 3, None), ([1], [2, 4, 6], [8])):
+
+    across, total = lax.optimization_barrier((send(ahead[0], out), total))
+    across = [across, swap(across)]
+    h = rank_terms(owners, slots, across, shrink, hs)
+    half = depth // 2
+    for low, steps in ((0, [1]), (half, [2, 4, 6]), (None, [8])):
         more = [send(h, [(i, i ^ step) for i in range(parts)]) for step in steps]
-        if q is not None:
-            total, _ = late_product(q, total, None, False, h)
+        if low is not None:
+            xs, _ = lax.optimization_barrier((across, h))
+            total = block_product(xs, weights, shrink, None, low, low + half, tile, total, held, None, False)[0]
         for part in more:
             h = h + part
         h, total = lax.optimization_barrier((h, total))

time: 181 us -> 171 us (0.945)
  local copies, waits for them, and re-layouts: 9.68 us -> 2.16 us
  Pallas kernels: 63.5 us -> 66 us
  other arithmetic: 5.54 us -> 3.47 us
    unnamed x30 -> x12, local copies, waits for them, and re-layouts: 6.88 us -> 0.03 us
    pallas_call x6 -> x5, Pallas kernels: 56.7 us -> 61.5 us  [block_product(): pl.pallas_call(functools.partial(block_kernel, starts or [0] * count, low...]
    select_n x1 -> x0, other arithmetic: 2.87 us -> none  [ring_plan(): jnp.where(me % 2 == 0, *(part[:, low:low + quarter] for part in ahead))]
    pallas_call x1, Pallas kernels: 3.87 us -> 1.6 us  [rank_terms(): pl.pallas_call(functools.partial(rank_kernel, counts), grid_spec=pltpu.Pr...]
    ppermute x26 -> x20, waiting for transfers between devices: 82 us -> 81.1 us  [ring_plan(): send = lambda value, pairs: lax.ppermute(value, 'tensor', pairs)]
    ppermute x26 -> x20, starting transfers between devices: 19.1 us -> 18.2 us  [ring_plan(): send = lambda value, pairs: lax.ppermute(value, 'tensor', pairs)]
  transfers between devices with their start and end apart: 26 -> 20, of which waited for: 12 -> 11; matrix products, arithmetic and copies ran while one was open for 5% -> 3% of each run, Pallas kernels for 31% -> 36%
where the time goes in v5:
time: 171 us
  waiting for transfers between devices  81.1 us (47%)
  Pallas kernels  66 us (39%)
  starting transfers between devices  18.2 us (11%)
  other arithmetic  3.47 us (2%)
  local copies, waits for them, and re-layouts  2.16 us (1%)
    ppermute x20, waiting for transfers between devices, ring_plan(): send = lambda value, pairs: lax.ppermute(value, 'tensor', pairs)  81.1 us
    pallas_call x5, Pallas kernels, block_product(): pl.pallas_call(functools.partial(block_kernel, starts or [0] * count, low...  61.5 us
    ppermute x20, starting transfers between devices, ring_plan(): send = lambda value, pairs: lax.ppermute(value, 'tensor', pairs)  18.2 us
  transfers between devices with their start and end apart: 20, of which 11 were waited for; matrix products, arithmetic and copies ran while one was open for 3% of the time, Pallas kernels for 36%

profile of v5, /device:TPU:0, one launch (start us, length us, event | category | flops | bytes accessed | tf_op | source)
XLA Modules:
  0.0 171.1 jit_solution(10257232463600148296)
XLA Ops:
  0.0 3.0 %collective-permute-start.1 = (bf16[48,16384]{1,0:T(8,128)(2,1)}, bf16[48,16384]{1,0:T(8,128)(2,1)S(1)}, u32[]{:S(2)}, u32[]{:S(2)}) collective-permute-start(bf16[48,16384]{1,0:T(8,128)(2,1)} %refs_0_), channel_id=1, source_target_pairs={{0,4},{1,3},{4,8},{5,1},{8,12},{9,5},{12,14},{13,9},{14,10},{15,13... | collective-permute-start | bytes 4718600 | tf_op jit(solution)/shard_map/ppermute | solution.py:398
  3.0 34.8 %collective-permute-done.1.refs_2_ = bf16[48,16384]{1,0:T(8,128)(2,1)S(1)} collective-permute-done((bf16[48,16384]{1,0:T(8,128)(2,1)}, bf16[48,16384]{1,0:T(8,128)(2,1)S(1)}, u32[]{:S(2)}, u32[]{:S(2)}) %collective-permute-start.1) | collective-permute-done | bytes 1572896 | tf_op jit(solution)/shard_map/ppermute | solution.py:398
  42.1 1.6 collective-permute-start.2
  43.7 0.9 collective-permute-start.4
  44.7 1.4 fusion
  46.5 18.3 %blocks.5 = (f32[16,48,1024]{2,1,0:T(8,128)S(1)}, f32[288,64]{1,0:T(8,128)S(1)}) custom-call(bf16[48,16384]{1,0:T(8,128)(2,1)S(1)} %copy-done.4, bf16[48,16384]{1,0:T(8,128)(2,1)} %collective-permute-done.refs_1_, bf16[48,16384]{1,0:T(8,128)(2,1)S(1)} %collective-permute-done.1.refs_2_, bf16[48,16384]{1,0:T(8,128)(2,1)} %collective-permute-done.3.refs_3_, ...), custom_call_target="tpu_custom_call" | custom-call | flops 9663676416 | bytes 33554432 | tf_op jit(solution)/shard_map/blocks/pallas_call | solution.py:259
  64.8 14.0 %collective-permute-done.2.refs_0_ = bf16[48,16384]{1,0:T(8,128)(2,1)S(1)} collective-permute-done((bf16[48,16384]{1,0:T(8,128)(2,1)S(1)}, bf16[48,16384]{1,0:T(8,128)(2,1)S(1)}, u32[]{:S(2)}, u32[]{:S(2)}) %collective-permute-start.2) | collective-permute-done | bytes 1572896 | tf_op jit(solution)/shard_map/ppermute | solution.py:398
  79.7 1.8 %collective-permute-start.7 = (bf16[48,16384]{1,0:T(8,128)(2,1)S(1)}, bf16[48,16384]{1,0:T(8,128)(2,1)S(1)}, u32[]{:S(2)}, u32[]{:S(2)}) collective-permute-start(bf16[48,16384]{1,0:T(8,128)(2,1)S(1)} %collective-permute-done.2.refs_0_), channel_id=1, source_target_pairs={{0,4},{1,3},{4,8},{5,1},{8,12},{9,5},{12,14},{13,9},{14,10},{15,13... | collective-permute-start | bytes 4718600 | tf_op jit(solution)/shard_map/ppermute | solution.py:398
  82.7 2.2 %collective-permute-done.9.refs_2_ = bf16[48,16384]{1,0:T(8,128)(2,1)S(1)} collective-permute-done((bf16[48,16384]{1,0:T(8,128)(2,1)S(1)}, bf16[48,16384]{1,0:T(8,128)(2,1)S(1)}, u32[]{:S(2)}, u32[]{:S(2)}) %collective-permute-start.9) | collective-permute-done | bytes 1572896 | tf_op jit(solution)/shard_map/ppermute | solution.py:398
  85.0 14.6 %blocks.6 = (f32[16,48,1024]{2,1,0:T(8,128)S(1)}, f32[192,64]{1,0:T(8,128)S(1)}) custom-call(bf16[48,16384]{1,0:T(8,128)(2,1)S(1)} %collective-permute-done.2.refs_0_, bf16[48,16384]{1,0:T(8,128)(2,1)S(1)} %collective-permute-done.4.refs_1_, bf16[48,16384]{1,0:T(8,128)(2,1)S(1)} %collective-permute-done.9.refs_2_, ...), custom_call_target="tpu_custom_call", output_to_operand_aliasing={{0}: (6, {})} | custom-call | flops 6442450944 | bytes 33554432 | tf_op jit(solution)/shard_map/blocks/pallas_call | solution.py:259
  99.5 16.5 %collective-permute-done.7.refs_0_ = bf16[48,16384]{1,0:T(8,128)(2,1)S(1)} collective-permute-done((bf16[48,16384]{1,0:T(8,128)(2,1)S(1)}, bf16[48,16384]{1,0:T(8,128)(2,1)S(1)}, u32[]{:S(2)}, u32[]{:S(2)}) %collective-permute-start.7) | collective-permute-done | bytes 1572896 | tf_op jit(solution)/shard_map/ppermute | solution.py:398
  117.0 2.0 %collective-permute-start.11 = (bf16[48,16384]{1,0:T(8,128)(2,1)S(1)}, bf16[48,16384]{1,0:T(8,128)(2,1)S(1)}, u32[]{:S(2)}, u32[]{:S(2)}) collective-permute-start(bf16[48,16384]{1,0:T(8,128)(2,1)S(1)} %collective-permute-done.7.refs_0_), channel_id=1, source_target_pairs={{0,4},{1,3},{4,8},{5,1},{8,12},{9,5},{12,14},{13,9},{14,10},{15,13... | collective-permute-start | bytes 4718600 | tf_op jit(solution)/shard_map/ppermute | solution.py:398
  119.0 1.0 collective-permute-done.12.refs_2_
  120.0 2.2 %collective-permute-done.13.refs_3_ = bf16[48,16384]{1,0:T(8,128)(2,1)S(1)} collective-permute-done((bf16[48,16384]{1,0:T(8,128)(2,1)S(1)}, bf16[48,16384]{1,0:T(8,128)(2,1)S(1)}, u32[]{:S(2)}, u32[]{:S(2)}) %collective-permute-start.13) | collective-permute-done | bytes 1572896 | tf_op jit(solution)/shard_map/ppermute | solution.py:398
  122.3 14.6 %blocks.7 = (f32[16,48,1024]{2,1,0:T(8,128)S(1)}, f32[192,64]{1,0:T(8,128)S(1)}) custom-call(bf16[48,16384]{1,0:T(8,128)(2,1)S(1)} %collective-permute-done.7.refs_0_, bf16[48,16384]{1,0:T(8,128)(2,1)S(1)} %collective-permute-done.8.refs_1_, bf16[48,16384]{1,0:T(8,128)(2,1)S(1)} %collective-permute-done.12.refs_2_, ...), custom_call_target="tpu_custom_call", output_to_operand_aliasing={{0}: (6, {})} | custom-call | flops 6442450944 | bytes 33554432 | tf_op jit(solution)/shard_map/blocks/pallas_call | solution.py:259
  137.5 3.4 %collective-permute-done.14.xb_ref.refs_1_ = bf16[48,16384]{1,0:T(8,128)(2,1)S(1)} collective-permute-done((bf16[48,16384]{1,0:T(8,128)(2,1)S(1)}, bf16[48,16384]{1,0:T(8,128)(2,1)S(1)}, u32[]{:S(2)}, u32[]{:S(2)}) %collective-permute-start.14) | collective-permute-done | bytes 1572896 | tf_op jit(solution)/shard_map/ppermute | solution.py:398
  140.9 1.6 ranks.1
  142.7 6.9 %blocks.8.refs_3_ = f32[16,48,1024]{2,1,0:T(8,128)S(1)} custom-call(bf16[48,16384]{1,0:T(8,128)(2,1)S(1)} %collective-permute-done.11.xa_ref.refs_0_, bf16[48,16384]{1,0:T(8,128)(2,1)S(1)} %collective-permute-done.14.xb_ref.refs_1_, bf16[16384,1024]{1,0:T(8,128)(2,1)} %refs_2_.3, ...), custom_call_target="tpu_custom_call", output_to_operand_aliasing={{}: (3, {})} | custom-call | flops 1610612736 | bytes 16777216 | tf_op jit(solution)/shard_map/blocks/pallas_call | solution.py:259
  149.7 2.1 %collective-permute-start.16 = (bf16[384,128]{1,0:T(8,128)(2,1)S(1)}, bf16[384,128]{1,0:T(8,128)(2,1)S(1)}, u32[]{:S(2)}, u32[]{:S(2)}) collective-permute-start(bf16[384,128]{1,0:T(8,128)(2,1)S(1)} %add.24), channel_id=1, source_target_pairs={{0,2},{1,3},{2,0},{3,1},{4,6},{5,7},{6,4},{7,5},{8,10},{9,11},{10,... | collective-permute-start | bytes 294920 | tf_op jit(solution)/shard_map/ppermute | solution.py:398
  151.8 1.6 collective-permute-start.17
  153.4 7.1 %blocks.9.refs_0_.refs_1_.refs_2_.refs_3_.refs_4_.refs_5_.refs_6_.refs_7_ = f32[16,48,1024]{2,1,0:T(8,128)S(1)} custom-call(bf16[48,16384]{1,0:T(8,128)(2,1)S(1)} %collective-permute-done.11.xa_ref.refs_0_, bf16[48,16384]{1,0:T(8,128)(2,1)S(1)} %collective-permute-done.14.xb_ref.refs_1_, ...), custom_call_target="tpu_custom_call", output_to_operand_aliasing={{}: (3, {})} | custom-call | flops 1610612736 | bytes 16777216 | tf_op jit(solution)/shard_map/blocks/pallas_call | solution.py:259
  160.6 2.7 %collective-permute-start.19 = (bf16[384,128]{1,0:T(8,128)(2,1)S(1)}, bf16[384,128]{1,0:T(8,128)(2,1)S(1)}, u32[]{:S(2)}, u32[]{:S(2)}) collective-permute-start(bf16[384,128]{1,0:T(8,128)(2,1)S(1)} %add_add_fusion), channel_id=1, source_target_pairs={{0,8},{1,9},{2,10},{3,11},{4,12},{5,13},{6,14},{7,15},{8,0},{9,1},... | collective-permute-start | bytes 294920 | tf_op jit(solution)/shard_map/ppermute | solution.py:398
  163.2 4.9 %collective-permute-done.19 = bf16[384,128]{1,0:T(8,128)(2,1)S(1)} collective-permute-done((bf16[384,128]{1,0:T(8,128)(2,1)S(1)}, bf16[384,128]{1,0:T(8,128)(2,1)S(1)}, u32[]{:S(2)}, u32[]{:S(2)}) %collective-permute-start.19) | collective-permute-done | bytes 98336 | tf_op jit(solution)/shard_map/ppermute | solution.py:398
  168.2 2.9 %finish.1 = bf16[768,1024]{1,0:T(8,128)(2,1)} custom-call(s32[16]{0:T(128)S(1)} %get-tuple-element.37.places_ref, s32[6]{0:T(128)S(1)} %gather_fusion, f32[16,48,1024]{2,1,0:T(8,128)S(1)} %blocks.9.refs_0_.refs_1_.refs_2_.refs_3_.refs_4_.refs_5_.refs_6_.refs_7_, f32[16,48,1024]{2,1,0:T(8,128)S(1)} %blocks.9.refs_0_.refs_1_.refs_2_.refs_3_.refs_4_.refs_5_.refs_6_.refs_7_, ...), custom_call_target="tpu_custom_call" | custom-call | tf_op jit(solution)/shard_map/finish/pallas_call | solution.py:367
  (50 shorter events, 8.6 us)
Async XLA Ops:
  0.0 40.0 %copy-start = (s32[16]{0:T(128)S(1)}, s32[16]{0:T(128)}, u32[]{:S(2)}) copy-start(s32[16]{0:T(128)} %param.16) | copy-start | bytes 196
  0.0 37.9 %collective-permute-start.1 = (bf16[48,16384]{1,0:T(8,128)(2,1)}, bf16[48,16384]{1,0:T(8,128)(2,1)S(1)}, u32[]{:S(2)}, u32[]{:S(2)}) collective-permute-start(bf16[48,16384]{1,0:T(8,128)(2,1)} %refs_0_), channel_id=1, source_target_pairs={{0,4},{1,3},{4,8},{5,1},{8,12},{9,5},{12,14},{13,9},{14,10},{15,13... | collective-permute-start | bytes 4718600 | tf_op jit(solution)/shard_map/ppermute | solution.py:398
  3.0 34.9 %collective-permute-start.3 = (bf16[48,16384]{1,0:T(8,128)(2,1)}, bf16[48,16384]{1,0:T(8,128)(2,1)}, u32[]{:S(2)}, u32[]{:S(2)}) collective-permute-start(bf16[48,16384]{1,0:T(8,128)(2,1)} %refs_0_), channel_id=1, source_target_pairs={{0,2},{1,5},{4,0},{5,9},{8,4},{9,13},{12,8},{13,15},{14,12},{15,11... | collective-permute-start | bytes 4718600 | tf_op jit(solution)/shard_map/ppermute | solution.py:398
  3.0 43.4 %collective-permute-start = (bf16[48,16384]{1,0:T(8,128)(2,1)}, bf16[48,16384]{1,0:T(8,128)(2,1)}, u32[]{:S(2)}, u32[]{:S(2)}) collective-permute-start(bf16[48,16384]{1,0:T(8,128)(2,1)} %refs_0_), channel_id=1, source_target_pairs={{0,1},{1,0},{2,3},{3,2},{4,5},{5,4},{6,7},{7,6},{8,9},{9,8},{10,11... | collective-permute-start | bytes 4718600 | tf_op jit(solution)/shard_map/ppermute | solution.py:398
  37.9 8.6 %collective-permute-start.5 = (bf16[48,16384]{1,0:T(8,128)(2,1)S(1)}, bf16[48,16384]{1,0:T(8,128)(2,1)}, u32[]{:S(2)}, u32[]{:S(2)}) collective-permute-start(bf16[48,16384]{1,0:T(8,128)(2,1)S(1)} %collective-permute-done.1.refs_2_), channel_id=1, source_target_pairs={{0,1},{1,0},{2,3},{3,2},{4,5},{5,4},{6,7},{7,6},{8,9},{9,8},{10,11... | collective-permute-start | bytes 4718600 | tf_op jit(solution)/shard_map/ppermute | solution.py:398
  37.9 8.6 %collective-permute-start.6 = (bf16[48,16384]{1,0:T(8,128)(2,1)}, bf16[48,16384]{1,0:T(8,128)(2,1)}, u32[]{:S(2)}, u32[]{:S(2)}) collective-permute-start(bf16[48,16384]{1,0:T(8,128)(2,1)} %collective-permute-done.3.refs_3_), channel_id=1, source_target_pairs={{0,1},{1,0},{2,3},{3,2},{4,5},{5,4},{6,7},{7,6},{8,9},{9,8},{10,11... | collective-permute-start | bytes 4718600 | tf_op jit(solution)/shard_map/ppermute | solution.py:398
  40.0 6.5 %copy-start.4 = (bf16[48,16384]{1,0:T(8,128)(2,1)S(1)}, bf16[48,16384]{1,0:T(8,128)(2,1)}, u32[]{:S(2)}) copy-start(bf16[48,16384]{1,0:T(8,128)(2,1)} %refs_0_) | copy-start | bytes 4718596
  42.1 36.7 %collective-permute-start.2 = (bf16[48,16384]{1,0:T(8,128)(2,1)S(1)}, bf16[48,16384]{1,0:T(8,128)(2,1)S(1)}, u32[]{:S(2)}, u32[]{:S(2)}) collective-permute-start(bf16[48,16384]{1,0:T(8,128)(2,1)S(1)} %collective-permute-done.1.refs_2_), channel_id=1, source_target_pairs={{0,4},{1,3},{4,8},{5,1},{8,12},{9,5},{12,14},{13,9},{14,10},{15,13... | collective-permute-start | bytes 4718600 | tf_op jit(solution)/shard_map/ppermute | solution.py:398
  43.7 35.1 %collective-permute-start.4 = (bf16[48,16384]{1,0:T(8,128)(2,1)}, bf16[48,16384]{1,0:T(8,128)(2,1)S(1)}, u32[]{:S(2)}, u32[]{:S(2)}) collective-permute-start(bf16[48,16384]{1,0:T(8,128)(2,1)} %collective-permute-done.3.refs_3_), channel_id=1, source_target_pairs={{0,2},{1,5},{4,0},{5,9},{8,4},{9,13},{12,8},{13,15},{14,12},{15,11... | collective-permute-start | bytes 4718600 | tf_op jit(solution)/shard_map/ppermute | solution.py:398
  78.9 3.8 %collective-permute-start.10 = (bf16[48,16384]{1,0:T(8,128)(2,1)S(1)}, bf16[48,16384]{1,0:T(8,128)(2,1)S(1)}, u32[]{:S(2)}, u32[]{:S(2)}) collective-permute-start(bf16[48,16384]{1,0:T(8,128)(2,1)S(1)} %collective-permute-done.4.refs_1_), channel_id=1, source_target_pairs={{0,1},{1,0},{2,3},{3,2},{4,5},{5,4},{6,7},{7,6},{8,9},{9,8},{10,11... | collective-permute-start | bytes 4718600 | tf_op jit(solution)/shard_map/ppermute | solution.py:398
  79.7 5.3 %collective-permute-start.9 = (bf16[48,16384]{1,0:T(8,128)(2,1)S(1)}, bf16[48,16384]{1,0:T(8,128)(2,1)S(1)}, u32[]{:S(2)}, u32[]{:S(2)}) collective-permute-start(bf16[48,16384]{1,0:T(8,128)(2,1)S(1)} %collective-permute-done.2.refs_0_), channel_id=1, source_target_pairs={{0,1},{1,0},{2,3},{3,2},{4,5},{5,4},{6,7},{7,6},{8,9},{9,8},{10,11... | collective-permute-start | bytes 4718600 | tf_op jit(solution)/shard_map/ppermute | solution.py:398
  79.7 36.4 %collective-permute-start.7 = (bf16[48,16384]{1,0:T(8,128)(2,1)S(1)}, bf16[48,16384]{1,0:T(8,128)(2,1)S(1)}, u32[]{:S(2)}, u32[]{:S(2)}) collective-permute-start(bf16[48,16384]{1,0:T(8,128)(2,1)S(1)} %collective-permute-done.2.refs_0_), channel_id=1, source_target_pairs={{0,4},{1,3},{4,8},{5,1},{8,12},{9,5},{12,14},{13,9},{14,10},{15,13... | collective-permute-start | bytes 4718600 | tf_op jit(solution)/shard_map/ppermute | solution.py:398
  81.4 35.1 %collective-permute-start.8 = (bf16[48,16384]{1,0:T(8,128)(2,1)S(1)}, bf16[48,16384]{1,0:T(8,128)(2,1)S(1)}, u32[]{:S(2)}, u32[]{:S(2)}) collective-permute-start(bf16[48,16384]{1,0:T(8,128)(2,1)S(1)} %collective-permute-done.4.refs_1_), channel_id=1, source_target_pairs={{0,2},{1,5},{4,0},{5,9},{8,4},{9,13},{12,8},{13,15},{14,12},{15,11... | collective-permute-start | bytes 4718600 | tf_op jit(solution)/shard_map/ppermute | solution.py:398
  116.5 3.5 %collective-permute-start.12 = (bf16[48,16384]{1,0:T(8,128)(2,1)S(1)}, bf16[48,16384]{1,0:T(8,128)(2,1)S(1)}, u32[]{:S(2)}, u32[]{:S(2)}) collective-permute-start(bf16[48,16384]{1,0:T(8,128)(2,1)S(1)} %collective-permute-done.7.refs_0_), channel_id=1, source_target_pairs={{0,1},{1,0},{2,3},{3,2},{4,5},{5,4},{6,7},{7,6},{8,9},{9,8},{10,11... | collective-permute-start | bytes 4718600 | tf_op jit(solution)/shard_map/ppermute | solution.py:398
  117.0 5.3 %collective-permute-start.13 = (bf16[48,16384]{1,0:T(8,128)(2,1)S(1)}, bf16[48,16384]{1,0:T(8,128)(2,1)S(1)}, u32[]{:S(2)}, u32[]{:S(2)}) collective-permute-start(bf16[48,16384]{1,0:T(8,128)(2,1)S(1)} %collective-permute-done.8.refs_1_), channel_id=1, source_target_pairs={{0,1},{1,0},{2,3},{3,2},{4,5},{5,4},{6,7},{7,6},{8,9},{9,8},{10,11... | collective-permute-start | bytes 4718600 | tf_op jit(solution)/shard_map/ppermute | solution.py:398
  117.0 20.5 %collective-permute-start.11 = (bf16[48,16384]{1,0:T(8,128)(2,1)S(1)}, bf16[48,16384]{1,0:T(8,128)(2,1)S(1)}, u32[]{:S(2)}, u32[]{:S(2)}) collective-permute-start(bf16[48,16384]{1,0:T(8,128)(2,1)S(1)} %collective-permute-done.7.refs_0_), channel_id=1, source_target_pairs={{0,4},{1,3},{4,8},{5,1},{8,12},{9,5},{12,14},{13,9},{14,10},{15,13... | collective-permute-start | bytes 4718600 | tf_op jit(solution)/shard_map/ppermute | solution.py:398
  137.5 3.4 %collective-permute-start.14 = (bf16[48,16384]{1,0:T(8,128)(2,1)S(1)}, bf16[48,16384]{1,0:T(8,128)(2,1)S(1)}, u32[]{:S(2)}, u32[]{:S(2)}) collective-permute-start(bf16[48,16384]{1,0:T(8,128)(2,1)S(1)} %collective-permute-done.11.xa_ref.refs_0_), channel_id=1, source_target_pairs={{0,1},{1,0},{2,3},{3,2},{4,5},{5,4},{6,7},{7,6},{8,9},{9,8},{10,11... | collective-permute-start | bytes 4718600 | tf_op jit(solution)/shard_map/ppermute | solution.py:398
  142.5 7.1 %collective-permute-start.15 = (bf16[384,128]{1,0:T(8,128)(2,1)S(1)}, bf16[384,128]{1,0:T(8,128)(2,1)S(1)}, u32[]{:S(2)}, u32[]{:S(2)}) collective-permute-start(bf16[384,128]{1,0:T(8,128)(2,1)S(1)} %ranks.1), channel_id=1, source_target_pairs={{0,1},{1,0},{2,3},{3,2},{4,5},{5,4},{6,7},{7,6},{8,9},{9,8},{10,11... | collective-permute-start | bytes 294920 | tf_op jit(solution)/shard_map/ppermute | solution.py:398
  149.7 18.5 %copy-start.5 = (f32[1024]{0:T(1024)S(1)}, f32[1024]{0:T(1024)}, u32[]{:S(2)}) copy-start(f32[1024]{0:T(1024)} %param.12) | copy-start | bytes 12292
  149.7 10.8 %collective-permute-start.16 = (bf16[384,128]{1,0:T(8,128)(2,1)S(1)}, bf16[384,128]{1,0:T(8,128)(2,1)S(1)}, u32[]{:S(2)}, u32[]{:S(2)}) collective-permute-start(bf16[384,128]{1,0:T(8,128)(2,1)S(1)} %add.24), channel_id=1, source_target_pairs={{0,2},{1,3},{2,0},{3,1},{4,6},{5,7},{6,4},{7,5},{8,10},{9,11},{10,... | collective-permute-start | bytes 294920 | tf_op jit(solution)/shard_map/ppermute | solution.py:398
  151.8 8.7 %collective-permute-start.17 = (bf16[384,128]{1,0:T(8,128)(2,1)S(1)}, bf16[384,128]{1,0:T(8,128)(2,1)S(1)}, u32[]{:S(2)}, u32[]{:S(2)}) collective-permute-start(bf16[384,128]{1,0:T(8,128)(2,1)S(1)} %add.24), channel_id=1, source_target_pairs={{0,4},{1,5},{2,6},{3,7},{4,0},{5,1},{6,2},{7,3},{8,12},{9,13},{10,... | collective-permute-start | bytes 294920 | tf_op jit(solution)/shard_map/ppermute | solution.py:398
  153.4 7.1 %collective-permute-start.18 = (bf16[384,128]{1,0:T(8,128)(2,1)S(1)}, bf16[384,128]{1,0:T(8,128)(2,1)S(1)}, u32[]{:S(2)}, u32[]{:S(2)}) collective-permute-start(bf16[384,128]{1,0:T(8,128)(2,1)S(1)} %add.24), channel_id=1, source_target_pairs={{0,6},{1,7},{2,4},{3,5},{4,2},{5,3},{6,0},{7,1},{8,14},{9,15},{10,... | collective-permute-start | bytes 294920 | tf_op jit(solution)/shard_map/ppermute | solution.py:398
  153.4 14.8 %copy-start.3 = (bf16[16,1024,64]{1,2,0:T(8,128)(2,1)S(1)}, bf16[16,1024,64]{1,2,0:T(8,128)(2,1)}, u32[]{:S(2)}) copy-start(bf16[16,1024,64]{1,2,0:T(8,128)(2,1)} %param.14) | copy-start | bytes 6291460
  160.6 7.6 %collective-permute-start.19 = (bf16[384,128]{1,0:T(8,128)(2,1)S(1)}, bf16[384,128]{1,0:T(8,128)(2,1)S(1)}, u32[]{:S(2)}, u32[]{:S(2)}) collective-permute-start(bf16[384,128]{1,0:T(8,128)(2,1)S(1)} %add_add_fusion), channel_id=1, source_target_pairs={{0,8},{1,9},{2,10},{3,11},{4,12},{5,13},{6,14},{7,15},{8,0},{9,1},... | collective-permute-start | bytes 294920 | tf_op jit(solution)/shard_map/ppermute | solution.py:398
  (2 other events, 4.7 us)

commit v6 on v5

--- a/solution.py
+++ b/solution.py
@@ -150,11 +150,10 @@
             row = [2 * chip + core, 2 * chip + 1 - core]
             for r in range(1, ROUNDS + 1):
                 far, near = place - r * (1 - 2 * core), place + r * (1 - 2 * core)
-                far, near = SNAKE[far % chips], SNAKE[near % chips]
+                far, near = 2 * SNAKE[far % chips], 2 * SNAKE[near % chips]
+                row += [far + core, near + 1 - core]
                 if r < ROUNDS:
-                    row += [2 * far + core, 2 * near + core, 2 * near + 1 - core, 2 * far + 1 - core]
-                else:
-                    row += [2 * far + core, 2 * near + 1 - core]
+                    row += [near + core, far + 1 - core]
             owners[2 * chip + core] = row
     return owners
 
@@ -288,6 +287,27 @@
     return (2 * len(SNAKE), rows, cols)
 
 
+def some_ranks_kernel(*refs):
+    xs, s_ref, out_ref = refs[:-2], refs[-2], refs[-1]
+    x = jnp.concatenate([ref[...] for ref in xs], 0)
+    out_ref[...] = lax.dot_general(x, s_ref[...], NT, preferred_element_type=F32)
+
+
+def some_ranks(xs, shrink):
+    rows, depth = xs[0].shape
+    rank = shrink.shape[0]
+    whole = lambda shape: pl.BlockSpec(shape, lambda _: (0, 0))
+    return pl.pallas_call(
+        some_ranks_kernel,
+        grid=(1,),
+        in_specs=[whole((rows, depth))] * len(xs) + [whole((rank, depth))],
+        out_specs=whole((len(xs) * rows, rank)),
+        out_shape=jax.ShapeDtypeStruct((len(xs) * rows, rank), F32),
+        compiler_params=PARAMS,
+        name="some_ranks",
+    )(*xs, shrink)
+
+
 def rank_kernel(counts, owners_ref, slot_ref, xa_ref, xb_ref, s_ref, *refs):
     h_refs, out_ref, placed = refs[:-2], refs[-2], refs[-1]
     rows = xa_ref.shape[0]
@@ -399,34 +419,52 @@
     swap = lambda value: send(value, [(i, i ^ 1) for i in range(parts)])
     out, home = ring_pairs((1, -1)), ring_pairs((-1, 1))
 
-    total, hs, held = None, [], 0
-    blocks = [tokens, swap(tokens)]
+    half = depth // 2
+    hs, counts = [], []
+
+    def multiply(xs, total, low=0, high=depth):
+        if low == 0:
+            hs.append(None)
+            counts.append(len(xs))
+        held = sum(counts[:-1])
+        total, hs[-1] = block_product(xs, weights, shrink, None, low, high, tile, total, held, hs[-1], True)
+        return total
+
+    streams = [send(tokens, out), None]
+    own = [tokens, swap(tokens)]
+    total = multiply(own, None, 0, half)
+    second, total = lax.optimization_barrier((tokens, total))
+    streams[1] = send(second, home)
     tables = (owners, places, slots, segment_slot, cosine, sine)
-    blocks, tables = lax.optimization_barrier((blocks, tables))
+    total, tables = lax.optimization_barrier((total, tables))
     owners, places, slots, segment_slot, cosine, sine = tables
-    ahead = [tokens, tokens]
-    for r in range(1, ROUNDS):
-        ahead = [send(ahead[0], out), send(ahead[1], home)]
-        if total is not None:
-            ahead, total = lax.optimization_barrier((ahead, total))
-        blocks += ahead + [swap(part) for part in ahead]
-        total, h = block_product(blocks, weights, shrink, None, 0, depth, tile, total, held, None, True)
-        hs.append(h)
-        held += len(blocks)
-        blocks = []
-
-    across, total = lax.optimization_barrier((send(ahead[0], out), total))
-    across = [across, swap(across)]
-    h = rank_terms(owners, slots, across, shrink, hs)
-    half = depth // 2
-    for low, steps in ((0, [1]), (half, [2, 4, 6]), (None, [8])):
+    total = multiply(own, total, half, depth)
+
+    blocks, hops = [], 2 * ROUNDS - 1
+    totals = [total] * 2
+    for hop in range(hops):
+        arrived, _ = lax.optimization_barrier((streams[hop % 2], totals[min(hop, hops - 2)]))
+        if hop + 2 < hops:
+            streams[hop % 2] = send(arrived, home if hop % 2 else out)
+        blocks += [arrived, swap(arrived)]
+        if hop < hops - 3:
+            total = multiply(blocks, total)
+            totals.append(total)
+            blocks = []
+    early = some_ranks(blocks[:-2], shrink)
+    hs.append(early)
+    held = sum(counts)
+
+    h = rank_terms(owners, slots, blocks[-2:], shrink, hs)
+    low = 0
+    for high, steps in ((4, [1]), (10, [2, 4, 6]), (16, [8])):
         more = [send(h, [(i, i ^ step) for i in range(parts)]) for step in steps]
-        if low is not None:
-            xs, _ = lax.optimization_barrier((across, h))
-            total = block_product(xs, weights, shrink, None, low, low + half, tile, total, held, None, False)[0]
+        xs, _ = lax.optimization_barrier((blocks, h))
+        total = block_product(xs, weights, shrink, None, low * tile, high * tile, tile, total, held, None, False)[0]
         for part in more:
             h = h + part
         h, total = lax.optimization_barrier((h, total))
+        low = high
     return block_finish(places, segment_slot, total, expands, scale, h, cosine, sine)
 
 

time: 171 us -> 158 us (0.924)
  waiting for transfers between devices: 81.1 us -> 42.8 us
  Pallas kernels: 66 us -> 87.8 us
  starting transfers between devices: 18.2 us -> 21.4 us
    ppermute x20, waiting for transfers between devices: 81.1 us -> 42.8 us  [ring_plan(): send = lambda value, pairs: lax.ppermute(value, 'tensor', pairs)]
    pallas_call x5 -> x9, Pallas kernels: 61.5 us -> 81.5 us  [block_product(): pl.pallas_call(functools.partial(block_kernel, starts or [0] * count, low...]
    ppermute x20, starting transfers between devices: 18.2 us -> 21.4 us  [ring_plan(): send = lambda value, pairs: lax.ppermute(value, 'tensor', pairs)]
    pallas_call x0 -> x1, Pallas kernels: none -> 1.76 us  [some_ranks(): pl.pallas_call(some_ranks_kernel, grid=(1,), in_specs=[whole((rows, depth...]
  transfers between devices with their start and end apart: 20 -> 20, of which waited for: 11 -> 7; matrix products, arithmetic and copies ran while one was open for 3% -> 3% of each run, Pallas kernels for 36% -> 53%
where the time goes in v6:
time: 158 us
  Pallas kernels  87.8 us (56%)
  waiting for transfers between devices  42.8 us (27%)
  starting transfers between devices  21.4 us (14%)
  other arithmetic  3.47 us (2%)
  local copies, waits for them, and re-layouts  2.16 us (1%)
    pallas_call x9, Pallas kernels, block_product(): pl.pallas_call(functools.partial(block_kernel, starts or [0] * count, low...  81.5 us
    ppermute x20, waiting for transfers between devices, ring_plan(): send = lambda value, pairs: lax.ppermute(value, 'tensor', pairs)  42.8 us
    ppermute x20, starting transfers between devices, ring_plan(): send = lambda value, pairs: lax.ppermute(value, 'tensor', pairs)  21.4 us
  transfers between devices with their start and end apart: 20, of which 7 were waited for; matrix products, arithmetic and copies ran while one was open for 3% of the time, Pallas kernels for 53%

profile of v6, /device:TPU:0, one launch (start us, length us, event | category | flops | bytes accessed | tf_op | source)
XLA Modules:
  0.0 157.9 jit_solution(13553922628871733029)
XLA Ops:
  0.5 2.6 %collective-permute-start.1 = (bf16[48,16384]{1,0:T(8,128)(2,1)}, bf16[48,16384]{1,0:T(8,128)(2,1)}, u32[]{:S(2)}, u32[]{:S(2)}) collective-permute-start(bf16[48,16384]{1,0:T(8,128)(2,1)} %refs_0_.3), channel_id=1, source_target_pairs={{0,4},{1,3},{4,8},{5,1},{8,12},{9,5},{12,14},{13,9},{14,10},{15,13... | collective-permute-start | bytes 4718600 | tf_op jit(solution)/shard_map/ppermute | solution.py:418
  8.7 7.0 %blocks.9 = (f32[16,48,1024]{2,1,0:T(8,128)S(1)}, f32[96,64]{1,0:T(8,128)S(1)}) custom-call(bf16[48,16384]{1,0:T(8,128)(2,1)S(1)} %copy-done.4, bf16[48,16384]{1,0:T(8,128)(2,1)S(1)} %collective-permute-done.refs_1_, bf16[16384,1024]{1,0:T(8,128)(2,1)} %refs_6_.5, bf16[64,16384]{1,0:T(8,128)(2,1)S(1)} %bitcast.12), custom_call_target="tpu_custom_call" | custom-call | flops 1610612736 | bytes 16777216 | tf_op jit(solution)/shard_map/blocks/pallas_call | solution.py:258
  15.7 7.0 %blocks.10 = (f32[16,48,1024]{2,1,0:T(8,128)S(1)}, f32[96,64]{1,0:T(8,128)S(1)}) custom-call(bf16[48,16384]{1,0:T(8,128)(2,1)S(1)} %copy-done.4, bf16[48,16384]{1,0:T(8,128)(2,1)S(1)} %collective-permute-done.refs_1_, bf16[16384,1024]{1,0:T(8,128)(2,1)} %refs_6_.5, bf16[64,16384]{1,0:T(8,128)(2,1)S(1)} %bitcast.13, ...), custom_call_target="tpu_custom_call", output_to_operand_aliasing={{0}: (4, {})} | custom-call | flops 1610612736 | bytes 16777216 | tf_op jit(solution)/shard_map/blocks/pallas_call | solution.py:258
  22.8 3.4 %collective-permute-done.1.refs_0_ = bf16[48,16384]{1,0:T(8,128)(2,1)} collective-permute-done((bf16[48,16384]{1,0:T(8,128)(2,1)}, bf16[48,16384]{1,0:T(8,128)(2,1)}, u32[]{:S(2)}, u32[]{:S(2)}) %collective-permute-start.1) | collective-permute-done | bytes 1572896 | tf_op jit(solution)/shard_map/ppermute | solution.py:418
  26.2 2.5 %collective-permute-start.2 = (bf16[48,16384]{1,0:T(8,128)(2,1)}, bf16[48,16384]{1,0:T(8,128)(2,1)S(1)}, u32[]{:S(2)}, u32[]{:S(2)}) collective-permute-start(bf16[48,16384]{1,0:T(8,128)(2,1)} %collective-permute-done.1.refs_0_), channel_id=1, source_target_pairs={{0,4},{1,3},{4,8},{5,1},{8,12},{9,5},{12,14},{13,9},{14,10},{15,13... | collective-permute-start | bytes 4718600 | tf_op jit(solution)/shard_map/ppermute | solution.py:418
  28.7 18.1 %collective-permute-done.6.refs_0_ = bf16[48,16384]{1,0:T(8,128)(2,1)S(1)} collective-permute-done((bf16[48,16384]{1,0:T(8,128)(2,1)S(1)}, bf16[48,16384]{1,0:T(8,128)(2,1)S(1)}, u32[]{:S(2)}, u32[]{:S(2)}) %collective-permute-start.6) | collective-permute-done | bytes 1572896 | tf_op jit(solution)/shard_map/ppermute | solution.py:418
  47.0 2.9 %collective-permute-start.9 = (bf16[48,16384]{1,0:T(8,128)(2,1)S(1)}, bf16[48,16384]{1,0:T(8,128)(2,1)S(1)}, u32[]{:S(2)}, u32[]{:S(2)}) collective-permute-start(bf16[48,16384]{1,0:T(8,128)(2,1)S(1)} %collective-permute-done.6.refs_0_), channel_id=1, source_target_pairs={{0,2},{1,5},{4,0},{5,9},{8,4},{9,13},{12,8},{13,15},{14,12},{15,11... | collective-permute-start | bytes 4718600 | tf_op jit(solution)/shard_map/ppermute | solution.py:418
  50.0 12.2 %blocks.11 = (f32[16,48,1024]{2,1,0:T(8,128)S(1)}, f32[96,64]{1,0:T(8,128)S(1)}) custom-call(bf16[48,16384]{1,0:T(8,128)(2,1)} %collective-permute-done.1.refs_0_, bf16[48,16384]{1,0:T(8,128)(2,1)S(1)} %collective-permute-done.3.refs_1_, bf16[16384,1024]{1,0:T(8,128)(2,1)} %refs_6_.5, ...), custom_call_target="tpu_custom_call", output_to_operand_aliasing={{0}: (4, {})} | custom-call | flops 3221225472 | bytes 33554432 | tf_op jit(solution)/shard_map/blocks/pallas_call | solution.py:258
  63.5 11.8 %blocks.12 = (f32[16,48,1024]{2,1,0:T(8,128)S(1)}, f32[96,64]{1,0:T(8,128)S(1)}) custom-call(bf16[48,16384]{1,0:T(8,128)(2,1)S(1)} %collective-permute-done.6.refs_0_, bf16[48,16384]{1,0:T(8,128)(2,1)S(1)} %collective-permute-done.7.refs_1_, bf16[16384,1024]{1,0:T(8,128)(2,1)} %refs_6_.5, ...), custom_call_target="tpu_custom_call", output_to_operand_aliasing={{0}: (4, {})} | custom-call | flops 3221225472 | bytes 33554432 | tf_op jit(solution)/shard_map/blocks/pallas_call | solution.py:258
  75.2 3.4 %collective-permute-done.9.refs_0_ = bf16[48,16384]{1,0:T(8,128)(2,1)S(1)} collective-permute-done((bf16[48,16384]{1,0:T(8,128)(2,1)S(1)}, bf16[48,16384]{1,0:T(8,128)(2,1)S(1)}, u32[]{:S(2)}, u32[]{:S(2)}) %collective-permute-start.9) | collective-permute-done | bytes 1572896 | tf_op jit(solution)/shard_map/ppermute | solution.py:418
  79.1 2.0 %collective-permute-start.13 = (bf16[48,16384]{1,0:T(8,128)(2,1)S(1)}, bf16[48,16384]{1,0:T(8,128)(2,1)S(1)}, u32[]{:S(2)}, u32[]{:S(2)}) collective-permute-start(bf16[48,16384]{1,0:T(8,128)(2,1)S(1)} %collective-permute-done.9.refs_0_), channel_id=1, source_target_pairs={{0,2},{1,5},{4,0},{5,9},{8,4},{9,13},{12,8},{13,15},{14,12},{15,11... | collective-permute-start | bytes 4718600 | tf_op jit(solution)/shard_map/ppermute | solution.py:418
  81.1 11.8 %blocks.13 = (f32[16,48,1024]{2,1,0:T(8,128)S(1)}, f32[96,64]{1,0:T(8,128)S(1)}) custom-call(bf16[48,16384]{1,0:T(8,128)(2,1)S(1)} %collective-permute-done.2.refs_0_, bf16[48,16384]{1,0:T(8,128)(2,1)S(1)} %collective-permute-done.5.refs_1_, bf16[16384,1024]{1,0:T(8,128)(2,1)} %refs_6_.5, ...), custom_call_target="tpu_custom_call", output_to_operand_aliasing={{0}: (4, {})} | custom-call | flops 3221225472 | bytes 33554432 | tf_op jit(solution)/shard_map/blocks/pallas_call | solution.py:258
  92.9 3.2 %collective-permute-done.4.refs_0_ = bf16[48,16384]{1,0:T(8,128)(2,1)S(1)} collective-permute-done((bf16[48,16384]{1,0:T(8,128)(2,1)S(1)}, bf16[48,16384]{1,0:T(8,128)(2,1)S(1)}, u32[]{:S(2)}, u32[]{:S(2)}) %collective-permute-start.4) | collective-permute-done | bytes 1572896 | tf_op jit(solution)/shard_map/ppermute | solution.py:418
  96.1 1.9 %collective-permute-start.8 = (bf16[48,16384]{1,0:T(8,128)(2,1)S(1)}, bf16[48,16384]{1,0:T(8,128)(2,1)S(1)}, u32[]{:S(2)}, u32[]{:S(2)}) collective-permute-start(bf16[48,16384]{1,0:T(8,128)(2,1)S(1)} %collective-permute-done.4.refs_0_), channel_id=1, source_target_pairs={{0,4},{1,3},{4,8},{5,1},{8,12},{9,5},{12,14},{13,9},{14,10},{15,13... | collective-permute-start | bytes 4718600 | tf_op jit(solution)/shard_map/ppermute | solution.py:418
  98.0 11.8 %blocks.14 = (f32[16,48,1024]{2,1,0:T(8,128)S(1)}, f32[96,64]{1,0:T(8,128)S(1)}) custom-call(bf16[48,16384]{1,0:T(8,128)(2,1)S(1)} %collective-permute-done.9.refs_0_, bf16[48,16384]{1,0:T(8,128)(2,1)S(1)} %collective-permute-done.10.refs_1_, bf16[16384,1024]{1,0:T(8,128)(2,1)} %refs_6_.5, ...), custom_call_target="tpu_custom_call", output_to_operand_aliasing={{0}: (4, {})} | custom-call | flops 3221225472 | bytes 33554432 | tf_op jit(solution)/shard_map/blocks/pallas_call | solution.py:258
  109.8 4.3 %collective-permute-done.13.refs_2_ = bf16[48,16384]{1,0:T(8,128)(2,1)S(1)} collective-permute-done((bf16[48,16384]{1,0:T(8,128)(2,1)S(1)}, bf16[48,16384]{1,0:T(8,128)(2,1)S(1)}, u32[]{:S(2)}, u32[]{:S(2)}) %collective-permute-start.13) | collective-permute-done | bytes 1572896 | tf_op jit(solution)/shard_map/ppermute | solution.py:418
  114.1 8.6 %collective-permute-done.8.xa_ref.refs_4_ = bf16[48,16384]{1,0:T(8,128)(2,1)S(1)} collective-permute-done((bf16[48,16384]{1,0:T(8,128)(2,1)S(1)}, bf16[48,16384]{1,0:T(8,128)(2,1)S(1)}, u32[]{:S(2)}, u32[]{:S(2)}) %collective-permute-start.8) | collective-permute-done | bytes 1572896 | tf_op jit(solution)/shard_map/ppermute | solution.py:418
  122.8 1.8 %some_ranks.1.refs_5_ = f32[192,64]{1,0:T(8,128)S(1)} custom-call(bf16[48,16384]{1,0:T(8,128)(2,1)S(1)} %collective-permute-done.4.refs_0_, bf16[48,16384]{1,0:T(8,128)(2,1)S(1)} %collective-permute-done.12.refs_1_, bf16[48,16384]{1,0:T(8,128)(2,1)S(1)} %collective-permute-done.13.refs_2_, bf16[48,16384]{1,0:T(8,128)(2,1)S(1)} %collective-permute-done.14.refs_3_, ...), custom_call_target="tpu_custom_call" | custom-call | tf_op jit(solution)/shard_map/some_ranks/pallas_call | solution.py:300
  128.0 5.3 %blocks.15.refs_7_ = f32[16,48,1024]{2,1,0:T(8,128)S(1)} custom-call(bf16[48,16384]{1,0:T(8,128)(2,1)S(1)} %collective-permute-done.4.refs_0_, bf16[48,16384]{1,0:T(8,128)(2,1)S(1)} %collective-permute-done.12.refs_1_, bf16[48,16384]{1,0:T(8,128)(2,1)S(1)} %collective-permute-done.13.refs_2_, ...), custom_call_target="tpu_custom_call", output_to_operand_aliasing={{}: (7, {})} | custom-call | flops 2415919104 | bytes 8388608 | tf_op jit(solution)/shard_map/blocks/pallas_call | solution.py:258
  133.3 2.1 %collective-permute-start.16 = (bf16[384,128]{1,0:T(8,128)(2,1)S(1)}, bf16[384,128]{1,0:T(8,128)(2,1)S(1)}, u32[]{:S(2)}, u32[]{:S(2)}) collective-permute-start(bf16[384,128]{1,0:T(8,128)(2,1)S(1)} %add.24), channel_id=1, source_target_pairs={{0,2},{1,3},{2,0},{3,1},{4,6},{5,7},{6,4},{7,5},{8,10},{9,11},{10,... | collective-permute-start | bytes 294920 | tf_op jit(solution)/shard_map/ppermute | solution.py:418
  137.0 7.3 %blocks.16.refs_7_ = f32[16,48,1024]{2,1,0:T(8,128)S(1)} custom-call(bf16[48,16384]{1,0:T(8,128)(2,1)S(1)} %collective-permute-done.4.refs_0_, bf16[48,16384]{1,0:T(8,128)(2,1)S(1)} %collective-permute-done.12.refs_1_, bf16[48,16384]{1,0:T(8,128)(2,1)S(1)} %collective-permute-done.13.refs_2_, ...), custom_call_target="tpu_custom_call", output_to_operand_aliasing={{}: (7, {})} | custom-call | flops 3623878656 | bytes 12582912 | tf_op jit(solution)/shard_map/blocks/pallas_call | solution.py:258
  144.4 3.0 %collective-permute-start.19 = (bf16[384,128]{1,0:T(8,128)(2,1)S(1)}, bf16[384,128]{1,0:T(8,128)(2,1)S(1)}, u32[]{:S(2)}, u32[]{:S(2)}) collective-permute-start(bf16[384,128]{1,0:T(8,128)(2,1)S(1)} %add_add_fusion), channel_id=1, source_target_pairs={{0,8},{1,9},{2,10},{3,11},{4,12},{5,13},{6,14},{7,15},{8,0},{9,1},... | collective-permute-start | bytes 294920 | tf_op jit(solution)/shard_map/ppermute | solution.py:418
  147.4 7.5 %blocks.17.refs_0_.refs_1_.refs_2_.refs_3_.refs_4_.refs_5_.refs_6_.refs_7_ = f32[16,48,1024]{2,1,0:T(8,128)S(1)} custom-call(bf16[48,16384]{1,0:T(8,128)(2,1)S(1)} %collective-permute-done.4.refs_0_, bf16[48,16384]{1,0:T(8,128)(2,1)S(1)} %collective-permute-done.12.refs_1_, ...), custom_call_target="tpu_custom_call", output_to_operand_aliasing={{}: (7, {})} | custom-call | flops 3623878656 | bytes 12582912 | tf_op jit(solution)/shard_map/blocks/pallas_call | solution.py:258
  155.0 2.9 %finish.1 = bf16[768,1024]{1,0:T(8,128)(2,1)} custom-call(s32[16]{0:T(128)S(1)} %get-tuple-element.59.places_ref, s32[6]{0:T(128)S(1)} %gather_fusion, f32[16,48,1024]{2,1,0:T(8,128)S(1)} %blocks.17.refs_0_.refs_1_.refs_2_.refs_3_.refs_4_.refs_5_.refs_6_.refs_7_, f32[16,48,1024]{2,1,0:T(8,128)S(1)} %blocks.17.refs_0_.refs_1_.refs_2_.refs_3_.refs_4_.refs_5_.refs_6_.refs_7_, ...), custom_call_target="tpu_custom_call" | custom-call | tf_op jit(solution)/shard_map/finish/pallas_call | solution.py:387
  (55 shorter events, 13.2 us)
Async XLA Ops:
  0.0 4.7 %copy-start = (s32[16]{0:T(128)S(1)}, s32[16]{0:T(128)}, u32[]{:S(2)}) copy-start(s32[16]{0:T(128)} %param.16) | copy-start | bytes 196
  0.0 8.7 %collective-permute-start = (bf16[48,16384]{1,0:T(8,128)(2,1)}, bf16[48,16384]{1,0:T(8,128)(2,1)S(1)}, u32[]{:S(2)}, u32[]{:S(2)}) collective-permute-start(bf16[48,16384]{1,0:T(8,128)(2,1)} %refs_0_.3), channel_id=1, source_target_pairs={{0,1},{1,0},{2,3},{3,2},{4,5},{5,4},{6,7},{7,6},{8,9},{9,8},{10,11... | collective-permute-start | bytes 4718600 | tf_op jit(solution)/shard_map/ppermute | solution.py:418
  0.5 25.8 %collective-permute-start.1 = (bf16[48,16384]{1,0:T(8,128)(2,1)}, bf16[48,16384]{1,0:T(8,128)(2,1)}, u32[]{:S(2)}, u32[]{:S(2)}) collective-permute-start(bf16[48,16384]{1,0:T(8,128)(2,1)} %refs_0_.3), channel_id=1, source_target_pairs={{0,4},{1,3},{4,8},{5,1},{8,12},{9,5},{12,14},{13,9},{14,10},{15,13... | collective-permute-start | bytes 4718600 | tf_op jit(solution)/shard_map/ppermute | solution.py:418
  4.7 4.0 %copy-start.4 = (bf16[48,16384]{1,0:T(8,128)(2,1)S(1)}, bf16[48,16384]{1,0:T(8,128)(2,1)}, u32[]{:S(2)}) copy-start(bf16[48,16384]{1,0:T(8,128)(2,1)} %refs_0_.3) | copy-start | bytes 4718596
  15.7 31.1 %collective-permute-start.6 = (bf16[48,16384]{1,0:T(8,128)(2,1)S(1)}, bf16[48,16384]{1,0:T(8,128)(2,1)S(1)}, u32[]{:S(2)}, u32[]{:S(2)}) collective-permute-start(bf16[48,16384]{1,0:T(8,128)(2,1)S(1)} %copy-done.4), channel_id=1, source_target_pairs={{0,2},{1,5},{4,0},{5,9},{8,4},{9,13},{12,8},{13,15},{14,12},{15,11... | collective-permute-start | bytes 4718600 | tf_op jit(solution)/shard_map/ppermute | solution.py:418
  26.2 23.7 %collective-permute-start.3 = (bf16[48,16384]{1,0:T(8,128)(2,1)}, bf16[48,16384]{1,0:T(8,128)(2,1)S(1)}, u32[]{:S(2)}, u32[]{:S(2)}) collective-permute-start(bf16[48,16384]{1,0:T(8,128)(2,1)} %collective-permute-done.1.refs_0_), channel_id=1, source_target_pairs={{0,1},{1,0},{2,3},{3,2},{4,5},{5,4},{6,7},{7,6},{8,9},{9,8},{10,11... | collective-permute-start | bytes 4718600 | tf_op jit(solution)/shard_map/ppermute | solution.py:418
  26.2 35.9 %collective-permute-start.2 = (bf16[48,16384]{1,0:T(8,128)(2,1)}, bf16[48,16384]{1,0:T(8,128)(2,1)S(1)}, u32[]{:S(2)}, u32[]{:S(2)}) collective-permute-start(bf16[48,16384]{1,0:T(8,128)(2,1)} %collective-permute-done.1.refs_0_), channel_id=1, source_target_pairs={{0,4},{1,3},{4,8},{5,1},{8,12},{9,5},{12,14},{13,9},{14,10},{15,13... | collective-permute-start | bytes 4718600 | tf_op jit(solution)/shard_map/ppermute | solution.py:418
  46.8 16.7 %collective-permute-start.7 = (bf16[48,16384]{1,0:T(8,128)(2,1)S(1)}, bf16[48,16384]{1,0:T(8,128)(2,1)S(1)}, u32[]{:S(2)}, u32[]{:S(2)}) collective-permute-start(bf16[48,16384]{1,0:T(8,128)(2,1)S(1)} %collective-permute-done.6.refs_0_), channel_id=1, source_target_pairs={{0,1},{1,0},{2,3},{3,2},{4,5},{5,4},{6,7},{7,6},{8,9},{9,8},{10,11... | collective-permute-start | bytes 4718600 | tf_op jit(solution)/shard_map/ppermute | solution.py:418
  47.0 31.6 %collective-permute-start.9 = (bf16[48,16384]{1,0:T(8,128)(2,1)S(1)}, bf16[48,16384]{1,0:T(8,128)(2,1)S(1)}, u32[]{:S(2)}, u32[]{:S(2)}) collective-permute-start(bf16[48,16384]{1,0:T(8,128)(2,1)S(1)} %collective-permute-done.6.refs_0_), channel_id=1, source_target_pairs={{0,2},{1,5},{4,0},{5,9},{8,4},{9,13},{12,8},{13,15},{14,12},{15,11... | collective-permute-start | bytes 4718600 | tf_op jit(solution)/shard_map/ppermute | solution.py:418
  62.1 18.9 %collective-permute-start.5 = (bf16[48,16384]{1,0:T(8,128)(2,1)S(1)}, bf16[48,16384]{1,0:T(8,128)(2,1)S(1)}, u32[]{:S(2)}, u32[]{:S(2)}) collective-permute-start(bf16[48,16384]{1,0:T(8,128)(2,1)S(1)} %collective-permute-done.2.refs_0_), channel_id=1, source_target_pairs={{0,1},{1,0},{2,3},{3,2},{4,5},{5,4},{6,7},{7,6},{8,9},{9,8},{10,11... | collective-permute-start | bytes 4718600 | tf_op jit(solution)/shard_map/ppermute | solution.py:418
  62.2 33.9 %collective-permute-start.4 = (bf16[48,16384]{1,0:T(8,128)(2,1)S(1)}, bf16[48,16384]{1,0:T(8,128)(2,1)S(1)}, u32[]{:S(2)}, u32[]{:S(2)}) collective-permute-start(bf16[48,16384]{1,0:T(8,128)(2,1)S(1)} %collective-permute-done.2.refs_0_), channel_id=1, source_target_pairs={{0,4},{1,3},{4,8},{5,1},{8,12},{9,5},{12,14},{13,9},{14,10},{15,13... | collective-permute-start | bytes 4718600 | tf_op jit(solution)/shard_map/ppermute | solution.py:418
  78.6 19.4 %collective-permute-start.10 = (bf16[48,16384]{1,0:T(8,128)(2,1)S(1)}, bf16[48,16384]{1,0:T(8,128)(2,1)S(1)}, u32[]{:S(2)}, u32[]{:S(2)}) collective-permute-start(bf16[48,16384]{1,0:T(8,128)(2,1)S(1)} %collective-permute-done.9.refs_0_), channel_id=1, source_target_pairs={{0,1},{1,0},{2,3},{3,2},{4,5},{5,4},{6,7},{7,6},{8,9},{9,8},{10,11... | collective-permute-start | bytes 4718600 | tf_op jit(solution)/shard_map/ppermute | solution.py:418
  79.1 35.0 %collective-permute-start.13 = (bf16[48,16384]{1,0:T(8,128)(2,1)S(1)}, bf16[48,16384]{1,0:T(8,128)(2,1)S(1)}, u32[]{:S(2)}, u32[]{:S(2)}) collective-permute-start(bf16[48,16384]{1,0:T(8,128)(2,1)S(1)} %collective-permute-done.9.refs_0_), channel_id=1, source_target_pairs={{0,2},{1,5},{4,0},{5,9},{8,4},{9,13},{12,8},{13,15},{14,12},{15,11... | collective-permute-start | bytes 4718600 | tf_op jit(solution)/shard_map/ppermute | solution.py:418
  96.1 26.7 %collective-permute-start.8 = (bf16[48,16384]{1,0:T(8,128)(2,1)S(1)}, bf16[48,16384]{1,0:T(8,128)(2,1)S(1)}, u32[]{:S(2)}, u32[]{:S(2)}) collective-permute-start(bf16[48,16384]{1,0:T(8,128)(2,1)S(1)} %collective-permute-done.4.refs_0_), channel_id=1, source_target_pairs={{0,4},{1,3},{4,8},{5,1},{8,12},{9,5},{12,14},{13,9},{14,10},{15,13... | collective-permute-start | bytes 4718600 | tf_op jit(solution)/shard_map/ppermute | solution.py:418
  98.0 24.7 %collective-permute-start.12 = (bf16[48,16384]{1,0:T(8,128)(2,1)S(1)}, bf16[48,16384]{1,0:T(8,128)(2,1)S(1)}, u32[]{:S(2)}, u32[]{:S(2)}) collective-permute-start(bf16[48,16384]{1,0:T(8,128)(2,1)S(1)} %collective-permute-done.4.refs_0_), channel_id=1, source_target_pairs={{0,1},{1,0},{2,3},{3,2},{4,5},{5,4},{6,7},{7,6},{8,9},{9,8},{10,11... | collective-permute-start | bytes 4718600 | tf_op jit(solution)/shard_map/ppermute | solution.py:418
  114.1 8.7 %collective-permute-start.14 = (bf16[48,16384]{1,0:T(8,128)(2,1)S(1)}, bf16[48,16384]{1,0:T(8,128)(2,1)S(1)}, u32[]{:S(2)}, u32[]{:S(2)}) collective-permute-start(bf16[48,16384]{1,0:T(8,128)(2,1)S(1)} %collective-permute-done.13.refs_2_), channel_id=1, source_target_pairs={{0,1},{1,0},{2,3},{3,2},{4,5},{5,4},{6,7},{7,6},{8,9},{9,8},{10,11... | collective-permute-start | bytes 4718600 | tf_op jit(solution)/shard_map/ppermute | solution.py:418
  122.8 3.4 %collective-permute-start.11 = (bf16[48,16384]{1,0:T(8,128)(2,1)S(1)}, bf16[48,16384]{1,0:T(8,128)(2,1)S(1)}, u32[]{:S(2)}, u32[]{:S(2)}) collective-permute-start(bf16[48,16384]{1,0:T(8,128)(2,1)S(1)} %collective-permute-done.8.xa_ref.refs_4_), channel_id=1, source_target_pairs={{0,1},{1,0},{2,3},{3,2},{4,5},{5,4},{6,7},{7,6},{8,9},{9,8},{10,11... | collective-permute-start | bytes 4718600 | tf_op jit(solution)/shard_map/ppermute | solution.py:418
  127.8 5.5 %collective-permute-start.15 = (bf16[384,128]{1,0:T(8,128)(2,1)S(1)}, bf16[384,128]{1,0:T(8,128)(2,1)S(1)}, u32[]{:S(2)}, u32[]{:S(2)}) collective-permute-start(bf16[384,128]{1,0:T(8,128)(2,1)S(1)} %ranks.1), channel_id=1, source_target_pairs={{0,1},{1,0},{2,3},{3,2},{4,5},{5,4},{6,7},{7,6},{8,9},{9,8},{10,11... | collective-permute-start | bytes 294920 | tf_op jit(solution)/shard_map/ppermute | solution.py:418
  133.3 11.0 %collective-permute-start.16 = (bf16[384,128]{1,0:T(8,128)(2,1)S(1)}, bf16[384,128]{1,0:T(8,128)(2,1)S(1)}, u32[]{:S(2)}, u32[]{:S(2)}) collective-permute-start(bf16[384,128]{1,0:T(8,128)(2,1)S(1)} %add.24), channel_id=1, source_target_pairs={{0,2},{1,3},{2,0},{3,1},{4,6},{5,7},{6,4},{7,5},{8,10},{9,11},{10,... | collective-permute-start | bytes 294920 | tf_op jit(solution)/shard_map/ppermute | solution.py:418
  135.4 8.9 %collective-permute-start.17 = (bf16[384,128]{1,0:T(8,128)(2,1)S(1)}, bf16[384,128]{1,0:T(8,128)(2,1)S(1)}, u32[]{:S(2)}, u32[]{:S(2)}) collective-permute-start(bf16[384,128]{1,0:T(8,128)(2,1)S(1)} %add.24), channel_id=1, source_target_pairs={{0,4},{1,5},{2,6},{3,7},{4,0},{5,1},{6,2},{7,3},{8,12},{9,13},{10,... | collective-permute-start | bytes 294920 | tf_op jit(solution)/shard_map/ppermute | solution.py:418
  137.0 7.3 %collective-permute-start.18 = (bf16[384,128]{1,0:T(8,128)(2,1)S(1)}, bf16[384,128]{1,0:T(8,128)(2,1)S(1)}, u32[]{:S(2)}, u32[]{:S(2)}) collective-permute-start(bf16[384,128]{1,0:T(8,128)(2,1)S(1)} %add.24), channel_id=1, source_target_pairs={{0,6},{1,7},{2,4},{3,5},{4,2},{5,3},{6,0},{7,1},{8,14},{9,15},{10,... | collective-permute-start | bytes 294920 | tf_op jit(solution)/shard_map/ppermute | solution.py:418
  144.4 10.6 %copy-start.5 = (f32[1024]{0:T(1024)S(1)}, f32[1024]{0:T(1024)}, u32[]{:S(2)}) copy-start(f32[1024]{0:T(1024)} %param.12) | copy-start | bytes 12292
  144.4 10.5 %collective-permute-start.19 = (bf16[384,128]{1,0:T(8,128)(2,1)S(1)}, bf16[384,128]{1,0:T(8,128)(2,1)S(1)}, u32[]{:S(2)}, u32[]{:S(2)}) collective-permute-start(bf16[384,128]{1,0:T(8,128)(2,1)S(1)} %add_add_fusion), channel_id=1, source_target_pairs={{0,8},{1,9},{2,10},{3,11},{4,12},{5,13},{6,14},{7,15},{8,0},{9,1},... | collective-permute-start | bytes 294920 | tf_op jit(solution)/shard_map/ppermute | solution.py:418
  147.4 7.5 %copy-start.3 = (bf16[16,1024,64]{1,2,0:T(8,128)(2,1)S(1)}, bf16[16,1024,64]{1,2,0:T(8,128)(2,1)}, u32[]{:S(2)}) copy-start(bf16[16,1024,64]{1,2,0:T(8,128)(2,1)} %param.14) | copy-start | bytes 6291460
  (2 other events, 4.7 us)

commit v7 on v6

--- a/solution.py
+++ b/solution.py
@@ -15,6 +15,7 @@
 BF16 = jnp.bfloat16
 NT = (((1,), (1,)), ((), ()))
 SLOTS = 4
+CHUNK = 256
 BIG_VMEM = 24 * 1024 * 1024
 PARAMS = pltpu.CompilerParams(vmem_limit_bytes=VMEM)
 SNAKE = (0, 2, 4, 6, 7, 5, 3, 1)
@@ -167,11 +168,10 @@
     return pairs
 
 
-def block_kernel(starts, low, tile, steps, first, base, fresh, ranked, *refs):
-    count = len(starts)
+def block_kernel(count, low, tile, steps, first, base, fresh, ranked, *refs):
     xs, w_ref, refs = refs[:count], refs[count], refs[count + 1 :]
     if ranked:
-        s_ref, refs = refs[0], refs[1:]
+        s_refs, refs = refs[:2], refs[2:]
     if not first:
         total_in, refs = refs[0], refs[1:]
     if ranked and not fresh:
@@ -187,12 +187,14 @@
         at = pl.multiple_of(step * tile, tile)
         sem = lambda i: sems.at[slot, i]
         out = [pltpu.make_async_copy(w_ref.at[pl.ds(low + at, tile)], w_slots.at[slot], sem(count))]
-        for i, start in enumerate(starts):
-            cut = xs[i].at[:, pl.ds(low - start + at, tile)]
+        for i in range(count):
+            cut = xs[i].at[:, pl.ds(low + at, tile)]
             out.append(pltpu.make_async_copy(cut, x_slots.at[slot, pl.ds(i * rows, rows)], sem(i)))
         if ranked:
-            cut = s_ref.at[:, pl.ds(low + at, tile)]
-            out.append(pltpu.make_async_copy(cut, s_slots.at[slot], sem(count + 1)))
+            for i, s_ref in enumerate(s_refs):
+                cut, rank = s_ref.at[:, pl.ds(low + at, tile)], s_ref.shape[0]
+                to = s_slots.at[slot, pl.ds(i * rank, rank)]
+                out.append(pltpu.make_async_copy(cut, to, sem(count + 1 + i)))
         return out
 
     def start(step):
@@ -214,9 +216,12 @@
             copy.wait()
         slot = lax.rem(step, SLOTS)
         x = x_slots[slot]
-        acc[...] += jnp.dot(x, w_slots[slot], preferred_element_type=F32).reshape(acc.shape)
+        for left in range(0, acc.shape[2], CHUNK):
+            cut = slice(left, left + CHUNK)
+            product = jnp.dot(x, w_slots[slot, :, cut], preferred_element_type=F32)
+            acc[:, :, cut] += product.reshape(count, rows, CHUNK)
         if ranked:
-            h_out[...] += lax.dot_general(x, s_slots[slot], NT, preferred_element_type=F32)
+            h_out[...] += lax.dot_general(x[:rows], s_slots[slot], NT, preferred_element_type=F32)
 
         @pl.when(step + SLOTS < steps)
         def _():
@@ -230,18 +235,18 @@
     store.wait()
 
 
-def block_product(xs, weights, shrink, starts, low, high, tile, total, base, h, ranked):
+def block_product(xs, weights, factors, low, high, tile, total, base, h, ranked):
     count = len(xs)
     rows = xs[0].shape[0]
     cols = weights.shape[1]
-    rank = shrink.shape[0]
+    rank = 2 * factors[0].shape[0]
     fresh, first = low == 0, total is None
     anywhere, whole = pl.BlockSpec(memory_space=pl.ANY), pl.BlockSpec(memory_space=pltpu.VMEM)
     operands = list(xs) + [weights]
     specs = [anywhere] * (count + 1)
     if ranked:
-        operands.append(shrink)
-        specs.append(anywhere)
+        operands += factors
+        specs += [anywhere] * 2
     aliases = {}
     if not first:
         aliases = {len(operands): 0}
@@ -252,13 +257,11 @@
         specs.append(whole)
     outs, out_specs = [jax.ShapeDtypeStruct(total_shape(rows, cols), F32)], [anywhere]
     if ranked:
-        outs.append(jax.ShapeDtypeStruct((count * rows, rank), F32))
+        outs.append(jax.ShapeDtypeStruct((rows, rank), F32))
         out_specs.append(whole)
     steps = (high - low) // tile
     result = pl.pallas_call(
-        functools.partial(
-            block_kernel, starts or [0] * count, low, tile, steps, first, base, fresh, ranked
-        ),
+        functools.partial(block_kernel, count, low, tile, steps, first, base, fresh, ranked),
         in_specs=specs,
         out_specs=out_specs,
         out_shape=outs,
@@ -268,7 +271,7 @@
             pltpu.VMEM((SLOTS, count * rows, tile), BF16),
             pltpu.VMEM((SLOTS, tile, cols), BF16),
             pltpu.VMEM((SLOTS, rank, tile), BF16),
-            pltpu.SemaphoreType.DMA((SLOTS, count + 2)),
+            pltpu.SemaphoreType.DMA((SLOTS, count + 3)),
             pltpu.SemaphoreType.DMA((2,)),
         ],
         input_output_aliases=aliases,
@@ -287,68 +290,64 @@
     return (2 * len(SNAKE), rows, cols)
 
 
-def some_ranks_kernel(*refs):
-    xs, s_ref, out_ref = refs[:-2], refs[-2], refs[-1]
-    x = jnp.concatenate([ref[...] for ref in xs], 0)
-    out_ref[...] = lax.dot_general(x, s_ref[...], NT, preferred_element_type=F32)
-
-
-def some_ranks(xs, shrink):
-    rows, depth = xs[0].shape
-    rank = shrink.shape[0]
+def both_ranks(x, factors):
+    return jnp.concatenate([lax.dot_general(x, s, NT, preferred_element_type=F32) for s in factors], 1)
+
+
+def some_ranks_kernel(x_ref, sa_ref, sb_ref, out_ref):
+    out_ref[...] = both_ranks(x_ref[...], (sa_ref[...], sb_ref[...]))
+
+
+def some_ranks(x, factors):
     whole = lambda shape: pl.BlockSpec(shape, lambda _: (0, 0))
+    shape = (x.shape[0], 2 * factors[0].shape[0])
     return pl.pallas_call(
         some_ranks_kernel,
         grid=(1,),
-        in_specs=[whole((rows, depth))] * len(xs) + [whole((rank, depth))],
-        out_specs=whole((len(xs) * rows, rank)),
-        out_shape=jax.ShapeDtypeStruct((len(xs) * rows, rank), F32),
+        in_specs=[whole(value.shape) for value in (x, *factors)],
+        out_specs=whole(shape),
+        out_shape=jax.ShapeDtypeStruct(shape, F32),
         compiler_params=PARAMS,
         name="some_ranks",
-    )(*xs, shrink)
-
-
-def rank_kernel(counts, owners_ref, slot_ref, xa_ref, xb_ref, s_ref, *refs):
+    )(x, *factors)
+
+
+def rank_kernel(owners_ref, slot_ref, x_ref, sa_ref, sb_ref, *refs):
     h_refs, out_ref, placed = refs[:-2], refs[-2], refs[-1]
-    rows = xa_ref.shape[0]
-    x = jnp.concatenate([xa_ref[...], xb_ref[...]], 0)
-    last = lax.dot_general(x, s_ref[...], NT, preferred_element_type=F32)
-    block = 0
-    for count, source in zip(counts, h_refs + (last,)):
-        for i in range(count):
-            to = pl.multiple_of(owners_ref[block] * rows, 16)
-            placed[pl.ds(to, rows), :] = source[i * rows : (i + 1) * rows, :]
-            block += 1
+    rows, rank = x_ref.shape[0], sa_ref.shape[0]
+    last = both_ranks(x_ref[...], (sa_ref[...], sb_ref[...]))
+    placed[...] = jnp.zeros_like(placed)
+    for i, source in enumerate(h_refs + (last,)):
+        to = pl.multiple_of(owners_ref[2 * i] * rows, 16)
+        placed[pl.ds(to, rows), :] = source[...]
     parts = []
-    for segment in range(placed.shape[0] // SEG):
+    segments = placed.shape[0] // SEG
+    for segment in range(segments):
         part = placed[segment * SEG : (segment + 1) * SEG, :]
-        parts.append(jnp.where(slot_ref[segment] == slot_ref[slot_ref.shape[0] - 1], part, 0.0))
+        mine, other = (slot_ref[segment] == slot_ref[segments + i] for i in (0, 1))
+        parts.append(jnp.where(mine, part[:, :rank], jnp.where(other, part[:, rank:], 0.0)))
     half = len(parts) // 2
     left, right = jnp.concatenate(parts[:half], 0), jnp.concatenate(parts[half:], 0)
     out_ref[...] = jnp.concatenate([left, right], 1).astype(out_ref.dtype)
 
 
-def rank_terms(owners, slots, xs, shrink, hs):
-    rows, depth = xs[0].shape
-    rank = shrink.shape[0]
-    counts = [h.shape[0] // rows for h in hs] + [len(xs)]
-    total_rows = sum(counts) * rows
+def rank_terms(owners, slots, x, factors, hs):
+    rank = factors[0].shape[0]
+    total_rows = owners.shape[0] * x.shape[0]
     whole = lambda shape: pl.BlockSpec(shape, lambda _, *rest: (0, 0))
     return pl.pallas_call(
-        functools.partial(rank_kernel, counts),
+        rank_kernel,
         grid_spec=pltpu.PrefetchScalarGridSpec(
             num_scalar_prefetch=2,
             grid=(1,),
-            in_specs=[whole((rows, depth))] * 2
-            + [whole((rank, depth))]
-            + [whole(h.shape) for h in hs],
+            in_specs=[whole(value.shape) for value in (x, *factors, *hs)],
             out_specs=whole((total_rows // 2, 2 * rank)),
-            scratch_shapes=[pltpu.VMEM((total_rows, rank), F32)],
+            scratch_shapes=[pltpu.VMEM((total_rows, 2 * rank), F32)],
         ),
         out_shape=jax.ShapeDtypeStruct((total_rows // 2, 2 * rank), BF16),
         compiler_params=PARAMS,
         name="ranks",
-    )(owners, slots, *xs, shrink, *hs)
+    )(owners, slots, x, *factors, *hs)
 
 
 def block_finish_kernel(blocks, segments, places_ref, slot_ref, *refs):
@@ -413,13 +412,12 @@
     owners_table = block_owners()
     owners = jnp.asarray(owners_table)[me]
     places = jnp.asarray(np.argsort(owners_table, axis=1).astype(np.int32))[me]
-    slots = jnp.concatenate([segment_slot, me[None].astype(jnp.int32)])
-    shrink = shrinks[0]
+    slots = jnp.concatenate([segment_slot, jnp.stack([me, me ^ 1]).astype(jnp.int32)])
     send = lambda value, pairs: lax.ppermute(value, "tensor", pairs)
     swap = lambda value: send(value, [(i, i ^ 1) for i in range(parts)])
     out, home = ring_pairs((1, -1)), ring_pairs((-1, 1))
 
-    half = depth // 2
+    half, cut = depth // 2, 10 * tile
     hs, counts = [], []
 
     def multiply(xs, total, low=0, high=depth):
@@ -427,11 +425,12 @@
             hs.append(None)
             counts.append(len(xs))
         held = sum(counts[:-1])
-        total, hs[-1] = block_product(xs, weights, shrink, None, low, high, tile, total, held, hs[-1], True)
+        total, hs[-1] = block_product(xs, weights, factors, low, high, tile, total, held, hs[-1], True)
         return total
 
     streams = [send(tokens, out), None]
     own = [tokens, swap(tokens)]
+    factors = [shrinks[0], swap(shrinks[0])]
     total = multiply(own, None, 0, half)
     second, total = lax.optimization_barrier((tokens, total))
     streams[1] = send(second, home)
@@ -441,9 +440,9 @@
     total = multiply(own, total, half, depth)
 
     blocks, hops = [], 2 * ROUNDS - 1
-    totals = [total] * 2
+    totals, waits = [total] * 2, [0, 1, 2, 3, 4, 6, 7]
     for hop in range(hops):
-        arrived, _ = lax.optimization_barrier((streams[hop % 2], totals[min(hop, hops - 2)]))
+        arrived, _ = lax.optimization_barrier((streams[hop % 2], totals[waits[hop]]))
         if hop + 2 < hops:
             streams[hop % 2] = send(arrived, home if hop % 2 else out)
         blocks += [arrived, swap(arrived)]
@@ -451,20 +450,22 @@
             total = multiply(blocks, total)
             totals.append(total)
             blocks = []
-    early = some_ranks(blocks[:-2], shrink)
-    hs.append(early)
-    held = sum(counts)
-
-    h = rank_terms(owners, slots, blocks[-2:], shrink, hs)
-    low = 0
-    for high, steps in ((4, [1]), (10, [2, 4, 6]), (16, [8])):
+        elif hop == hops - 2:
+            hs += [some_ranks(part, factors) for part in blocks[::2]]
+            held = sum(counts)
+            total = block_product(blocks[:2], weights, factors, 0, cut, tile, total, held, None, False)[0]
+            totals.append((total, hs))
+        else:
+            totals.append(total)
+    h = rank_terms(owners, slots, blocks[4], factors, hs)
+    for steps, start, low, high in (([1], None, None, None), ([2, 4, 6], 2, 0, cut), ([8], 0, cut, depth)):
         more = [send(h, [(i, i ^ step) for i in range(parts)]) for step in steps]
-        xs, _ = lax.optimization_barrier((blocks, h))
-        total = block_product(xs, weights, shrink, None, low * tile, high * tile, tile, total, held, None, False)[0]
+        if start is not None:
+            xs, _ = lax.optimization_barrier((blocks[start:], h))
+            total = block_product(xs, weights, factors, low, high, tile, total, held + start, None, False)[0]
         for part in more:
             h = h + part
         h, total = lax.optimization_barrier((h, total))
-        low = high
     return block_finish(places, segment_slot, total, expands, scale, h, cosine, sine)
 
 

time: 158 us -> 160 us (1.013)
  waiting for transfers between devices: 42.8 us -> 35.3 us
  Pallas kernels: 87.8 us -> 94.6 us
    ppermute x20 -> x21, waiting for transfers between devices: 42.8 us -> 35.3 us  [ring_plan(): send = lambda value, pairs: lax.ppermute(value, 'tensor', pairs)]
    pallas_call x11 -> x12, Pallas kernels: 84.9 us -> 91.6 us  [the longest x9 86.9 us: block_product(): pl.pallas_call(functools.partial(block_kernel, count, low, tile, steps, f...]
    ppermute x20 -> x21, starting transfers between devices: 21.4 us -> 22.8 us  [ring_plan(): send = lambda value, pairs: lax.ppermute(value, 'tensor', pairs)]
  transfers between devices with their start and end apart: 20 -> 21, of which waited for: 7 -> 8; matrix products, arithmetic and copies ran while one was open for 3% -> 3% of each run, Pallas kernels for 53% -> 52%
where the time goes in v7:
time: 160 us
  Pallas kernels  94.6 us (59%)
  waiting for transfers between devices  35.3 us (22%)
  starting transfers between devices  22.8 us (14%)
  local copies, waits for them, and re-layouts  3.56 us (2%)
  other arithmetic  3.47 us (2%)
    pallas_call x9, Pallas kernels, block_product(): pl.pallas_call(functools.partial(block_kernel, count, low, tile, steps, f...  86.9 us
    ppermute x21, waiting for transfers between devices, ring_plan(): send = lambda value, pairs: lax.ppermute(value, 'tensor', pairs)  35.3 us
    ppermute x21, starting transfers between devices, ring_plan(): send = lambda value, pairs: lax.ppermute(value, 'tensor', pairs)  22.8 us
  transfers between devices with their start and end apart: 21, of which 8 were waited for; matrix products, arithmetic and copies ran while one was open for 3% of the time, Pallas kernels for 52%

profile of v7, /device:TPU:0, one launch (start us, length us, event | category | flops | bytes accessed | tf_op | source)
XLA Modules:
  0.0 160.0 jit_solution(12742602099732796608)
XLA Ops:
  0.5 3.0 %collective-permute-start.2 = (bf16[48,16384]{1,0:T(8,128)(2,1)}, bf16[48,16384]{1,0:T(8,128)(2,1)}, u32[]{:S(2)}, u32[]{:S(2)}) collective-permute-start(bf16[48,16384]{1,0:T(8,128)(2,1)} %refs_0_.3), channel_id=1, source_target_pairs={{0,4},{1,3},{4,8},{5,1},{8,12},{9,5},{12,14},{13,9},{14,10},{15,13... | collective-permute-start | bytes 4718600 | tf_op jit(solution)/shard_map/ppermute | solution.py:416
  10.5 7.2 %blocks.9 = (f32[16,48,1024]{2,1,0:T(8,128)S(1)}, f32[48,128]{1,0:T(8,128)S(1)}) custom-call(bf16[48,16384]{1,0:T(8,128)(2,1)S(1)} %copy-done.4, bf16[48,16384]{1,0:T(8,128)(2,1)} %collective-permute-done.refs_1_, bf16[16384,1024]{1,0:T(8,128)(2,1)} %refs_6_.1, bf16[64,16384]{1,0:T(8,128)(2,1)S(1)} %bitcast.14, ...), custom_call_target="tpu_custom_call" | custom-call | flops 1610612736 | bytes 16777216 | tf_op jit(solution)/shard_map/blocks/pallas_call | solution.py:263
  18.4 7.3 %blocks.10 = (f32[16,48,1024]{2,1,0:T(8,128)S(1)}, f32[48,128]{1,0:T(8,128)S(1)}) custom-call(bf16[48,16384]{1,0:T(8,128)(2,1)S(1)} %copy-done.4, bf16[48,16384]{1,0:T(8,128)(2,1)} %collective-permute-done.refs_1_, bf16[16384,1024]{1,0:T(8,128)(2,1)} %refs_6_.1, bf16[64,16384]{1,0:T(8,128)(2,1)S(1)} %bitcast.15, ...), custom_call_target="tpu_custom_call", output_to_operand_aliasing={{0}: (5, {})} | custom-call | flops 1610612736 | bytes 16777216 | tf_op jit(solution)/shard_map/blocks/pallas_call | solution.py:263
  25.7 1.5 collective-permute-start.3
  27.3 20.4 %collective-permute-done.7.refs_0_ = bf16[48,16384]{1,0:T(8,128)(2,1)S(1)} collective-permute-done((bf16[48,16384]{1,0:T(8,128)(2,1)S(1)}, bf16[48,16384]{1,0:T(8,128)(2,1)S(1)}, u32[]{:S(2)}, u32[]{:S(2)}) %collective-permute-start.7) | collective-permute-done | bytes 1572896 | tf_op jit(solution)/shard_map/ppermute | solution.py:416
  48.6 2.3 %collective-permute-start.11 = (bf16[48,16384]{1,0:T(8,128)(2,1)S(1)}, bf16[48,16384]{1,0:T(8,128)(2,1)S(1)}, u32[]{:S(2)}, u32[]{:S(2)}) collective-permute-start(bf16[48,16384]{1,0:T(8,128)(2,1)S(1)} %collective-permute-done.7.refs_0_), channel_id=1, source_target_pairs={{0,2},{1,5},{4,0},{5,9},{8,4},{9,13},{12,8},{13,15},{14,12},{15,11... | collective-permute-start | bytes 4718600 | tf_op jit(solution)/shard_map/ppermute | solution.py:416
  50.8 12.2 %blocks.11 = (f32[16,48,1024]{2,1,0:T(8,128)S(1)}, f32[48,128]{1,0:T(8,128)S(1)}) custom-call(bf16[48,16384]{1,0:T(8,128)(2,1)} %collective-permute-done.2.refs_0_, bf16[48,16384]{1,0:T(8,128)(2,1)S(1)} %collective-permute-done.4.refs_1_, bf16[16384,1024]{1,0:T(8,128)(2,1)} %refs_6_.1, ...), custom_call_target="tpu_custom_call", output_to_operand_aliasing={{0}: (5, {})} | custom-call | flops 3221225472 | bytes 33554432 | tf_op jit(solution)/shard_map/blocks/pallas_call | solution.py:263
  64.6 12.1 %blocks.12 = (f32[16,48,1024]{2,1,0:T(8,128)S(1)}, f32[48,128]{1,0:T(8,128)S(1)}) custom-call(bf16[48,16384]{1,0:T(8,128)(2,1)S(1)} %collective-permute-done.7.refs_0_, bf16[48,16384]{1,0:T(8,128)(2,1)S(1)} %collective-permute-done.8.refs_1_, bf16[16384,1024]{1,0:T(8,128)(2,1)} %refs_6_.1, ...), custom_call_target="tpu_custom_call", output_to_operand_aliasing={{0}: (5, {})} | custom-call | flops 3221225472 | bytes 33554432 | tf_op jit(solution)/shard_map/blocks/pallas_call | solution.py:263
  78.8 2.2 %collective-permute-start.13 = (bf16[48,16384]{1,0:T(8,128)(2,1)S(1)}, bf16[48,16384]{1,0:T(8,128)(2,1)S(1)}, u32[]{:S(2)}, u32[]{:S(2)}) collective-permute-start(bf16[48,16384]{1,0:T(8,128)(2,1)S(1)} %collective-permute-done.11.refs_0_), channel_id=1, source_target_pairs={{0,2},{1,5},{4,0},{5,9},{8,4},{9,13},{12,8},{13,15},{14,12},{15,11... | collective-permute-start | bytes 4718600 | tf_op jit(solution)/shard_map/ppermute | solution.py:416
  81.1 12.1 %blocks.13 = (f32[16,48,1024]{2,1,0:T(8,128)S(1)}, f32[48,128]{1,0:T(8,128)S(1)}) custom-call(bf16[48,16384]{1,0:T(8,128)(2,1)S(1)} %collective-permute-done.3.refs_0_, bf16[48,16384]{1,0:T(8,128)(2,1)S(1)} %collective-permute-done.6.refs_1_, bf16[16384,1024]{1,0:T(8,128)(2,1)} %refs_6_.1, ...), custom_call_target="tpu_custom_call", output_to_operand_aliasing={{0}: (5, {})} | custom-call | flops 3221225472 | bytes 33554432 | tf_op jit(solution)/shard_map/blocks/pallas_call | solution.py:263
  93.1 3.9 %collective-permute-done.5.refs_0_.x_ref = bf16[48,16384]{1,0:T(8,128)(2,1)S(1)} collective-permute-done((bf16[48,16384]{1,0:T(8,128)(2,1)S(1)}, bf16[48,16384]{1,0:T(8,128)(2,1)S(1)}, u32[]{:S(2)}, u32[]{:S(2)}) %collective-permute-start.5) | collective-permute-done | bytes 1572896 | tf_op jit(solution)/shard_map/ppermute | solution.py:416
  97.0 2.2 %collective-permute-start.9 = (bf16[48,16384]{1,0:T(8,128)(2,1)S(1)}, bf16[48,16384]{1,0:T(8,128)(2,1)S(1)}, u32[]{:S(2)}, u32[]{:S(2)}) collective-permute-start(bf16[48,16384]{1,0:T(8,128)(2,1)S(1)} %collective-permute-done.5.refs_0_.x_ref), channel_id=1, source_target_pairs={{0,4},{1,3},{4,8},{5,1},{8,12},{9,5},{12,14},{13,9},{14,10},{15,13... | collective-permute-start | bytes 4718600 | tf_op jit(solution)/shard_map/ppermute | solution.py:416
  100.5 12.1 %blocks.14 = (f32[16,48,1024]{2,1,0:T(8,128)S(1)}, f32[48,128]{1,0:T(8,128)S(1)}) custom-call(bf16[48,16384]{1,0:T(8,128)(2,1)S(1)} %collective-permute-done.11.refs_0_, bf16[48,16384]{1,0:T(8,128)(2,1)S(1)} %collective-permute-done.12.refs_1_, bf16[16384,1024]{1,0:T(8,128)(2,1)} %refs_6_.1, ...), custom_call_target="tpu_custom_call", output_to_operand_aliasing={{0}: (5, {})} | custom-call | flops 3221225472 | bytes 33554432 | tf_op jit(solution)/shard_map/blocks/pallas_call | solution.py:263
  113.9 8.1 %blocks.15.refs_5_ = f32[16,48,1024]{2,1,0:T(8,128)S(1)} custom-call(bf16[48,16384]{1,0:T(8,128)(2,1)S(1)} %collective-permute-done.5.refs_0_.x_ref, bf16[48,16384]{1,0:T(8,128)(2,1)S(1)} %collective-permute-done.10.refs_1_, bf16[16384,1024]{1,0:T(8,128)(2,1)} %refs_6_.1, f32[16,48,1024]{2,1,0:T(8,128)S(1)} %get-tuple-element.67.refs_3_), custom_call_target="tpu_custom_call", output_to_operand_aliasing={{}: (3, {})} | custom-call | flops 2013265920 | bytes 20971520 | tf_op jit(solution)/shard_map/blocks/pallas_call | solution.py:263
  123.7 2.1 %ranks.1 = bf16[384,128]{1,0:T(8,128)(2,1)S(1)} custom-call(s32[16]{0:T(128)S(1)} %get-tuple-element.53.owners_ref, s32[8]{0:T(128)S(1)} %pad_add_fusion.slot_ref, bf16[48,16384]{1,0:T(8,128)(2,1)S(1)} %collective-permute-done.9.x_ref.refs_2_.refs_4_, bf16[64,16384]{1,0:T(8,128)(2,1)S(1)} %bitcast.22, ...), custom_call_target="tpu_custom_call" | custom-call | tf_op jit(solution)/shard_map/ranks/pallas_call | solution.py:338
  125.9 3.2 %collective-permute-done.14 = bf16[384,128]{1,0:T(8,128)(2,1)S(1)} collective-permute-done((bf16[384,128]{1,0:T(8,128)(2,1)S(1)}, bf16[384,128]{1,0:T(8,128)(2,1)S(1)}, u32[]{:S(2)}, u32[]{:S(2)}) %collective-permute-start.14) | collective-permute-done | bytes 98336 | tf_op jit(solution)/shard_map/ppermute | solution.py:416
  129.0 2.1 %collective-permute-start.15 = (bf16[384,128]{1,0:T(8,128)(2,1)S(1)}, bf16[384,128]{1,0:T(8,128)(2,1)S(1)}, u32[]{:S(2)}, u32[]{:S(2)}) collective-permute-start(bf16[384,128]{1,0:T(8,128)(2,1)S(1)} %add.24), channel_id=1, source_target_pairs={{0,2},{1,3},{2,0},{3,1},{4,6},{5,7},{6,4},{7,5},{8,10},{9,11},{10,... | collective-permute-start | bytes 294920 | tf_op jit(solution)/shard_map/ppermute | solution.py:416
  131.1 1.6 collective-permute-start.16
  134.2 2.4 %collective-permute-done.16 = bf16[384,128]{1,0:T(8,128)(2,1)S(1)} collective-permute-done((bf16[384,128]{1,0:T(8,128)(2,1)S(1)}, bf16[384,128]{1,0:T(8,128)(2,1)S(1)}, u32[]{:S(2)}, u32[]{:S(2)}) %collective-permute-start.16) | collective-permute-done | bytes 98336 | tf_op jit(solution)/shard_map/ppermute | solution.py:416
  136.7 1.5 collective-permute-done.17
  138.3 8.5 %blocks.16.refs_7_ = f32[16,48,1024]{2,1,0:T(8,128)S(1)} custom-call(bf16[48,16384]{1,0:T(8,128)(2,1)S(1)} %collective-permute-done.13.x_ref.refs_0_.refs_2_, bf16[48,16384]{1,0:T(8,128)(2,1)S(1)} %collective-permute-done.18.refs_1_.refs_3_, bf16[48,16384]{1,0:T(8,128)(2,1)S(1)} %collective-permute-done.9.x_ref.refs_2_.refs_4_, ...), custom_call_target="tpu_custom_call", output_to_operand_aliasing={{}: (5, {})} | custom-call | flops 4026531840 | bytes 20971520 | tf_op jit(solution)/shard_map/blocks/pallas_call | solution.py:263
  146.8 2.7 %collective-permute-start.20 = (bf16[384,128]{1,0:T(8,128)(2,1)S(1)}, bf16[384,128]{1,0:T(8,128)(2,1)S(1)}, u32[]{:S(2)}, u32[]{:S(2)}) collective-permute-start(bf16[384,128]{1,0:T(8,128)(2,1)S(1)} %add_add_fusion), channel_id=1, source_target_pairs={{0,8},{1,9},{2,10},{3,11},{4,12},{5,13},{6,14},{7,15},{8,0},{9,1},... | collective-permute-start | bytes 294920 | tf_op jit(solution)/shard_map/ppermute | solution.py:416
  149.5 7.5 %blocks.17.refs_0_.refs_1_.refs_2_.refs_3_.refs_4_.refs_5_.refs_6_.refs_7_ = f32[16,48,1024]{2,1,0:T(8,128)S(1)} custom-call(bf16[48,16384]{1,0:T(8,128)(2,1)S(1)} %collective-permute-done.5.refs_0_.x_ref, bf16[48,16384]{1,0:T(8,128)(2,1)S(1)} %collective-permute-done.10.refs_1_, ...), custom_call_target="tpu_custom_call", output_to_operand_aliasing={{}: (7, {})} | custom-call | flops 3623878656 | bytes 12582912 | tf_op jit(solution)/shard_map/blocks/pallas_call | solution.py:263
  157.0 2.9 %finish.1 = bf16[768,1024]{1,0:T(8,128)(2,1)} custom-call(s32[16]{0:T(128)S(1)} %get-tuple-element.51.places_ref, s32[6]{0:T(128)S(1)} %gather_fusion, f32[16,48,1024]{2,1,0:T(8,128)S(1)} %blocks.17.refs_0_.refs_1_.refs_2_.refs_3_.refs_4_.refs_5_.refs_6_.refs_7_, f32[16,48,1024]{2,1,0:T(8,128)S(1)} %blocks.17.refs_0_.refs_1_.refs_2_.refs_3_.refs_4_.refs_5_.refs_6_.refs_7_, ...), custom_call_target="tpu_custom_call" | custom-call | tf_op jit(solution)/shard_map/finish/pallas_call | solution.py:386
  (58 shorter events, 18.7 us)
Async XLA Ops:
  0.0 5.2 %copy-start = (s32[16]{0:T(128)S(1)}, s32[16]{0:T(128)}, u32[]{:S(2)}) copy-start(s32[16]{0:T(128)} %param.16) | copy-start | bytes 196
  0.0 9.1 %collective-permute-start.1 = (bf16[64,16384]{1,0:T(8,128)(2,1)}, bf16[64,16384]{1,0:T(8,128)(2,1)S(1)}, u32[]{:S(2)}, u32[]{:S(2)}) collective-permute-start(bf16[64,16384]{1,0:T(8,128)(2,1)} %bitcast.13), channel_id=1, source_target_pairs={{0,1},{1,0},{2,3},{3,2},{4,5},{5,4},{6,7},{7,6},{8,9},{9,8},{10,11... | collective-permute-start | bytes 6291464 | tf_op jit(solution)/shard_map/ppermute | solution.py:416
  0.5 8.6 %collective-permute-start = (bf16[48,16384]{1,0:T(8,128)(2,1)}, bf16[48,16384]{1,0:T(8,128)(2,1)}, u32[]{:S(2)}, u32[]{:S(2)}) collective-permute-start(bf16[48,16384]{1,0:T(8,128)(2,1)} %refs_0_.3), channel_id=1, source_target_pairs={{0,1},{1,0},{2,3},{3,2},{4,5},{5,4},{6,7},{7,6},{8,9},{9,8},{10,11... | collective-permute-start | bytes 4718600 | tf_op jit(solution)/shard_map/ppermute | solution.py:416
  0.5 25.1 %collective-permute-start.2 = (bf16[48,16384]{1,0:T(8,128)(2,1)}, bf16[48,16384]{1,0:T(8,128)(2,1)}, u32[]{:S(2)}, u32[]{:S(2)}) collective-permute-start(bf16[48,16384]{1,0:T(8,128)(2,1)} %refs_0_.3), channel_id=1, source_target_pairs={{0,4},{1,3},{4,8},{5,1},{8,12},{9,5},{12,14},{13,9},{14,10},{15,13... | collective-permute-start | bytes 4718600 | tf_op jit(solution)/shard_map/ppermute | solution.py:416
  17.8 29.9 %collective-permute-start.7 = (bf16[48,16384]{1,0:T(8,128)(2,1)S(1)}, bf16[48,16384]{1,0:T(8,128)(2,1)S(1)}, u32[]{:S(2)}, u32[]{:S(2)}) collective-permute-start(bf16[48,16384]{1,0:T(8,128)(2,1)S(1)} %copy-done.4), channel_id=1, source_target_pairs={{0,2},{1,5},{4,0},{5,9},{8,4},{9,13},{12,8},{13,15},{14,12},{15,11... | collective-permute-start | bytes 4718600 | tf_op jit(solution)/shard_map/ppermute | solution.py:416
  25.7 25.2 %collective-permute-start.4 = (bf16[48,16384]{1,0:T(8,128)(2,1)}, bf16[48,16384]{1,0:T(8,128)(2,1)S(1)}, u32[]{:S(2)}, u32[]{:S(2)}) collective-permute-start(bf16[48,16384]{1,0:T(8,128)(2,1)} %collective-permute-done.2.refs_0_), channel_id=1, source_target_pairs={{0,1},{1,0},{2,3},{3,2},{4,5},{5,4},{6,7},{7,6},{8,9},{9,8},{10,11... | collective-permute-start | bytes 4718600 | tf_op jit(solution)/shard_map/ppermute | solution.py:416
  25.7 37.3 %collective-permute-start.3 = (bf16[48,16384]{1,0:T(8,128)(2,1)}, bf16[48,16384]{1,0:T(8,128)(2,1)S(1)}, u32[]{:S(2)}, u32[]{:S(2)}) collective-permute-start(bf16[48,16384]{1,0:T(8,128)(2,1)} %collective-permute-done.2.refs_0_), channel_id=1, source_target_pairs={{0,4},{1,3},{4,8},{5,1},{8,12},{9,5},{12,14},{13,9},{14,10},{15,13... | collective-permute-start | bytes 4718600 | tf_op jit(solution)/shard_map/ppermute | solution.py:416
  47.6 17.0 %collective-permute-start.8 = (bf16[48,16384]{1,0:T(8,128)(2,1)S(1)}, bf16[48,16384]{1,0:T(8,128)(2,1)S(1)}, u32[]{:S(2)}, u32[]{:S(2)}) collective-permute-start(bf16[48,16384]{1,0:T(8,128)(2,1)S(1)} %collective-permute-done.7.refs_0_), channel_id=1, source_target_pairs={{0,1},{1,0},{2,3},{3,2},{4,5},{5,4},{6,7},{7,6},{8,9},{9,8},{10,11... | collective-permute-start | bytes 4718600 | tf_op jit(solution)/shard_map/ppermute | solution.py:416
  48.6 29.3 %collective-permute-start.11 = (bf16[48,16384]{1,0:T(8,128)(2,1)S(1)}, bf16[48,16384]{1,0:T(8,128)(2,1)S(1)}, u32[]{:S(2)}, u32[]{:S(2)}) collective-permute-start(bf16[48,16384]{1,0:T(8,128)(2,1)S(1)} %collective-permute-done.7.refs_0_), channel_id=1, source_target_pairs={{0,2},{1,5},{4,0},{5,9},{8,4},{9,13},{12,8},{13,15},{14,12},{15,11... | collective-permute-start | bytes 4718600 | tf_op jit(solution)/shard_map/ppermute | solution.py:416
  63.0 18.0 %collective-permute-start.6 = (bf16[48,16384]{1,0:T(8,128)(2,1)S(1)}, bf16[48,16384]{1,0:T(8,128)(2,1)S(1)}, u32[]{:S(2)}, u32[]{:S(2)}) collective-permute-start(bf16[48,16384]{1,0:T(8,128)(2,1)S(1)} %collective-permute-done.3.refs_0_), channel_id=1, source_target_pairs={{0,1},{1,0},{2,3},{3,2},{4,5},{5,4},{6,7},{7,6},{8,9},{9,8},{10,11... | collective-permute-start | bytes 4718600 | tf_op jit(solution)/shard_map/ppermute | solution.py:416
  63.1 33.9 %collective-permute-start.5 = (bf16[48,16384]{1,0:T(8,128)(2,1)S(1)}, bf16[48,16384]{1,0:T(8,128)(2,1)S(1)}, u32[]{:S(2)}, u32[]{:S(2)}) collective-permute-start(bf16[48,16384]{1,0:T(8,128)(2,1)S(1)} %collective-permute-done.3.refs_0_), channel_id=1, source_target_pairs={{0,4},{1,3},{4,8},{5,1},{8,12},{9,5},{12,14},{13,9},{14,10},{15,13... | collective-permute-start | bytes 4718600 | tf_op jit(solution)/shard_map/ppermute | solution.py:416
  77.9 22.6 %collective-permute-start.12 = (bf16[48,16384]{1,0:T(8,128)(2,1)S(1)}, bf16[48,16384]{1,0:T(8,128)(2,1)S(1)}, u32[]{:S(2)}, u32[]{:S(2)}) collective-permute-start(bf16[48,16384]{1,0:T(8,128)(2,1)S(1)} %collective-permute-done.11.refs_0_), channel_id=1, source_target_pairs={{0,1},{1,0},{2,3},{3,2},{4,5},{5,4},{6,7},{7,6},{8,9},{9,8},{10,11... | collective-permute-start | bytes 4718600 | tf_op jit(solution)/shard_map/ppermute | solution.py:416
  78.8 33.8 %collective-permute-start.13 = (bf16[48,16384]{1,0:T(8,128)(2,1)S(1)}, bf16[48,16384]{1,0:T(8,128)(2,1)S(1)}, u32[]{:S(2)}, u32[]{:S(2)}) collective-permute-start(bf16[48,16384]{1,0:T(8,128)(2,1)S(1)} %collective-permute-done.11.refs_0_), channel_id=1, source_target_pairs={{0,2},{1,5},{4,0},{5,9},{8,4},{9,13},{12,8},{13,15},{14,12},{15,11... | collective-permute-start | bytes 4718600 | tf_op jit(solution)/shard_map/ppermute | solution.py:416
  97.0 16.9 %collective-permute-start.10 = (bf16[48,16384]{1,0:T(8,128)(2,1)S(1)}, bf16[48,16384]{1,0:T(8,128)(2,1)S(1)}, u32[]{:S(2)}, u32[]{:S(2)}) collective-permute-start(bf16[48,16384]{1,0:T(8,128)(2,1)S(1)} %collective-permute-done.5.refs_0_.x_ref), channel_id=1, source_target_pairs={{0,1},{1,0},{2,3},{3,2},{4,5},{5,4},{6,7},{7,6},{8,9},{9,8},{10,11... | collective-permute-start | bytes 4718600 | tf_op jit(solution)/shard_map/ppermute | solution.py:416
  97.0 26.2 %collective-permute-start.9 = (bf16[48,16384]{1,0:T(8,128)(2,1)S(1)}, bf16[48,16384]{1,0:T(8,128)(2,1)S(1)}, u32[]{:S(2)}, u32[]{:S(2)}) collective-permute-start(bf16[48,16384]{1,0:T(8,128)(2,1)S(1)} %collective-permute-done.5.refs_0_.x_ref), channel_id=1, source_target_pairs={{0,4},{1,3},{4,8},{5,1},{8,12},{9,5},{12,14},{13,9},{14,10},{15,13... | collective-permute-start | bytes 4718600 | tf_op jit(solution)/shard_map/ppermute | solution.py:416
  123.2 15.0 %collective-permute-start.19 = (bf16[48,16384]{1,0:T(8,128)(2,1)S(1)}, bf16[48,16384]{1,0:T(8,128)(2,1)S(1)}, u32[]{:S(2)}, u32[]{:S(2)}) collective-permute-start(bf16[48,16384]{1,0:T(8,128)(2,1)S(1)} %collective-permute-done.9.x_ref.refs_2_.refs_4_), channel_id=1, source_target_pairs={{0,1},{1,0},{2,3},{3,2},{4,5},{5,4},{6,7},{7,6},{8,9},{9,8},{10,11... | collective-permute-start | bytes 4718600 | tf_op jit(solution)/shard_map/ppermute | solution.py:416
  123.2 15.1 %collective-permute-start.18 = (bf16[48,16384]{1,0:T(8,128)(2,1)S(1)}, bf16[48,16384]{1,0:T(8,128)(2,1)S(1)}, u32[]{:S(2)}, u32[]{:S(2)}) collective-permute-start(bf16[48,16384]{1,0:T(8,128)(2,1)S(1)} %collective-permute-done.13.x_ref.refs_0_.refs_2_), channel_id=1, source_target_pairs={{0,1},{1,0},{2,3},{3,2},{4,5},{5,4},{6,7},{7,6},{8,9},{9,8},{10,11... | collective-permute-start | bytes 4718600 | tf_op jit(solution)/shard_map/ppermute | solution.py:416
  125.8 3.2 %collective-permute-start.14 = (bf16[384,128]{1,0:T(8,128)(2,1)S(1)}, bf16[384,128]{1,0:T(8,128)(2,1)S(1)}, u32[]{:S(2)}, u32[]{:S(2)}) collective-permute-start(bf16[384,128]{1,0:T(8,128)(2,1)S(1)} %ranks.1), channel_id=1, source_target_pairs={{0,1},{1,0},{2,3},{3,2},{4,5},{5,4},{6,7},{7,6},{8,9},{9,8},{10,11... | collective-permute-start | bytes 294920 | tf_op jit(solution)/shard_map/ppermute | solution.py:416
  129.0 5.2 %collective-permute-start.15 = (bf16[384,128]{1,0:T(8,128)(2,1)S(1)}, bf16[384,128]{1,0:T(8,128)(2,1)S(1)}, u32[]{:S(2)}, u32[]{:S(2)}) collective-permute-start(bf16[384,128]{1,0:T(8,128)(2,1)S(1)} %add.24), channel_id=1, source_target_pairs={{0,2},{1,3},{2,0},{3,1},{4,6},{5,7},{6,4},{7,5},{8,10},{9,11},{10,... | collective-permute-start | bytes 294920 | tf_op jit(solution)/shard_map/ppermute | solution.py:416
  131.1 5.5 %collective-permute-start.16 = (bf16[384,128]{1,0:T(8,128)(2,1)S(1)}, bf16[384,128]{1,0:T(8,128)(2,1)S(1)}, u32[]{:S(2)}, u32[]{:S(2)}) collective-permute-start(bf16[384,128]{1,0:T(8,128)(2,1)S(1)} %add.24), channel_id=1, source_target_pairs={{0,4},{1,5},{2,6},{3,7},{4,0},{5,1},{6,2},{7,3},{8,12},{9,13},{10,... | collective-permute-start | bytes 294920 | tf_op jit(solution)/shard_map/ppermute | solution.py:416
  132.7 5.5 %collective-permute-start.17 = (bf16[384,128]{1,0:T(8,128)(2,1)S(1)}, bf16[384,128]{1,0:T(8,128)(2,1)S(1)}, u32[]{:S(2)}, u32[]{:S(2)}) collective-permute-start(bf16[384,128]{1,0:T(8,128)(2,1)S(1)} %add.24), channel_id=1, source_target_pairs={{0,6},{1,7},{2,4},{3,5},{4,2},{5,3},{6,0},{7,1},{8,14},{9,15},{10,... | collective-permute-start | bytes 294920 | tf_op jit(solution)/shard_map/ppermute | solution.py:416
  146.8 10.2 %copy-start.5 = (f32[1024]{0:T(1024)S(1)}, f32[1024]{0:T(1024)}, u32[]{:S(2)}) copy-start(f32[1024]{0:T(1024)} %param.12) | copy-start | bytes 12292
  146.8 10.2 %collective-permute-start.20 = (bf16[384,128]{1,0:T(8,128)(2,1)S(1)}, bf16[384,128]{1,0:T(8,128)(2,1)S(1)}, u32[]{:S(2)}, u32[]{:S(2)}) collective-permute-start(bf16[384,128]{1,0:T(8,128)(2,1)S(1)} %add_add_fusion), channel_id=1, source_target_pairs={{0,8},{1,9},{2,10},{3,11},{4,12},{5,13},{6,14},{7,15},{8,0},{9,1},... | collective-permute-start | bytes 294920 | tf_op jit(solution)/shard_map/ppermute | solution.py:416
  149.5 7.5 %copy-start.3 = (bf16[16,1024,64]{1,2,0:T(8,128)(2,1)S(1)}, bf16[16,1024,64]{1,2,0:T(8,128)(2,1)}, u32[]{:S(2)}) copy-start(bf16[16,1024,64]{1,2,0:T(8,128)(2,1)} %param.14) | copy-start | bytes 6291460
  (3 other events, 6.1 us)

commit v8 on v7

--- a/solution.py
+++ b/solution.py
@@ -316,24 +316,23 @@
     h_refs, out_ref, placed = refs[:-2], refs[-2], refs[-1]
     rows, rank = x_ref.shape[0], sa_ref.shape[0]
     last = both_ranks(x_ref[...], (sa_ref[...], sb_ref[...]))
-    placed[...] = jnp.zeros_like(placed)
+    segments = slot_ref.shape[0] - 2
     for i, source in enumerate(h_refs + (last,)):
-        to = pl.multiple_of(owners_ref[2 * i] * rows, 16)
-        placed[pl.ds(to, rows), :] = source[...]
-    parts = []
-    segments = placed.shape[0] // SEG
-    for segment in range(segments):
-        part = placed[segment * SEG : (segment + 1) * SEG, :]
-        mine, other = (slot_ref[segment] == slot_ref[segments + i] for i in (0, 1))
-        parts.append(jnp.where(mine, part[:, :rank], jnp.where(other, part[:, rank:], 0.0)))
-    half = len(parts) // 2
-    left, right = jnp.concatenate(parts[:half], 0), jnp.concatenate(parts[half:], 0)
-    out_ref[...] = jnp.concatenate([left, right], 1).astype(out_ref.dtype)
+        owner = owners_ref[2 * i]
+        segment = owner * rows // SEG
+        after = jnp.minimum(segment + 1, segments - 1)
+        row = owner * rows + lax.broadcasted_iota(jnp.int32, (rows, rank), 0)
+        slot = jnp.where(row < (segment + 1) * SEG, slot_ref[segment], slot_ref[after])
+        terms = jnp.where(slot == slot_ref[segments + 1], source[:, rank:], 0.0)
+        terms = jnp.where(slot == slot_ref[segments], source[:, :rank], terms)
+        placed[pl.ds(pl.multiple_of(owner // 2 * rows, 16), rows), :] = terms
+    half = placed.shape[0] // 2
+    out_ref[...] = jnp.concatenate([placed[:half, :], placed[half:, :]], 1).astype(out_ref.dtype)
 
 
 def rank_terms(owners, slots, x, factors, hs):
     rank = factors[0].shape[0]
-    total_rows = owners.shape[0] * x.shape[0]
+    core_rows = owners.shape[0] // 2 * x.shape[0]
     whole = lambda shape: pl.BlockSpec(shape, lambda _, *rest: (0, 0))
     return pl.pallas_call(
         rank_kernel,
@@ -341,25 +340,31 @@
             num_scalar_prefetch=2,
             grid=(1,),
             in_specs=[whole(value.shape) for value in (x, *factors, *hs)],
-            out_specs=whole((total_rows // 2, 2 * rank)),
-            scratch_shapes=[pltpu.VMEM((total_rows, 2 * rank), F32)],
+            out_specs=whole((core_rows // 2, 2 * rank)),
+            scratch_shapes=[pltpu.VMEM((core_rows, rank), F32)],
         ),
-        out_shape=jax.ShapeDtypeStruct((total_rows // 2, 2 * rank), BF16),
+        out_shape=jax.ShapeDtypeStruct((core_rows // 2, 2 * rank), BF16),
         compiler_params=PARAMS,
         name="ranks",
     )(owners, slots, x, *factors, *hs)
 
 
-def block_finish_kernel(blocks, segments, places_ref, slot_ref, *refs):
+def block_finish_kernel(blocks, segments, places_ref, slot_ref, core_ref, *refs):
     accs, refs = refs[:blocks], refs[blocks:]
     expands, refs = refs[:segments], refs[segments:]
-    scale_ref, h_ref, cos_ref, sin_ref, out_ref, update = refs
-    rank = h_ref.shape[1] // 2
-    h = jnp.where(pl.program_id(0) == 0, h_ref[:, :rank], h_ref[:, rank:])
+    scale_ref, mine_ref, other_ref, cos_ref, sin_ref, out_ref, h, update = refs
+    rank = mine_ref.shape[1] // 2
+    rows = accs[0].shape[1]
+    first = pl.program_id(0) == 0
+    even = core_ref[0] == 0
+    mine, other = (jnp.where(first, ref[:, :rank], ref[:, rank:]) for ref in (mine_ref, other_ref))
+    for core, terms in enumerate((jnp.where(even, mine, other), jnp.where(even, other, mine))):
+        for i in range(blocks // 2):
+            at = (2 * i + core) * rows
+            h[at : at + rows, :] = terms[i * rows : (i + 1) * rows]
     for segment in range(segments):
         cut = slice(segment * SEG, (segment + 1) * SEG)
-        update[cut, :] = jnp.dot(h[cut], expands[segment][0], preferred_element_type=F32)
-    rows = accs[0].shape[1]
+        update[cut, :] = jnp.dot(h[cut, :], expands[segment][0], preferred_element_type=F32)
     for block in range(blocks):
         at = slice(block * rows, (block + 1) * rows)
         cosine, sine = cos_ref[at, :], sin_ref[at, :]
@@ -369,7 +374,7 @@
             out_ref[at, cut] = rotate(value, cosine, sine).astype(out_ref.dtype)
 
 
-def block_finish(places, slots, total, expands, scale, h, cosine, sine):
+def block_finish(places, slots, core, total, expands, scale, mine, other, cosine, sine):
     blocks, rows, cols = total.shape
     half = blocks // 2
     half_rows = half * rows
@@ -377,32 +382,33 @@
     rank = expands.shape[1]
 
     def acc_at(i):
-        return pl.BlockSpec((1, rows, cols), lambda g, places, slots: (places[g * half + i], 0, 0))
+        return pl.BlockSpec((1, rows, cols), lambda g, places, *_: (places[g * half + i], 0, 0))
 
     def expand_at(i):
-        return pl.BlockSpec((1, rank, cols), lambda g, places, slots: (slots[g * segments + i], 0, 0))
+        return pl.BlockSpec((1, rank, cols), lambda g, places, slots, _: (slots[g * segments + i], 0, 0))
 
     half_of = lambda width: pl.BlockSpec((half_rows, width), lambda g, *_: (g, 0))
     return pl.pallas_call(
         functools.partial(block_finish_kernel, half, segments),
         grid_spec=pltpu.PrefetchScalarGridSpec(
-            num_scalar_prefetch=2,
+            num_scalar_prefetch=3,
             grid=(2,),
             in_specs=[acc_at(i) for i in range(half)]
             + [expand_at(i) for i in range(segments)]
             + [
                 pl.BlockSpec((1, cols), lambda g, *_: (0, 0)),
-                pl.BlockSpec(h.shape, lambda g, *_: (0, 0)),
+                pl.BlockSpec(mine.shape, lambda g, *_: (0, 0)),
+                pl.BlockSpec(other.shape, lambda g, *_: (0, 0)),
                 half_of(HD),
                 half_of(HD),
             ],
             out_specs=half_of(cols),
-            scratch_shapes=[pltpu.VMEM((half_rows, cols), F32)],
+            scratch_shapes=[pltpu.VMEM((half_rows, rank), BF16), pltpu.VMEM((half_rows, cols), F32)],
         ),
         out_shape=jax.ShapeDtypeStruct((blocks * rows, cols), BF16),
         compiler_params=PARAMS,
         name="finish",
-    )(places, slots, *([total] * half), *([expands] * segments), scale, h, cosine, sine)
+    )(places, slots, core, *([total] * half), *([expands] * segments), scale, mine, other, cosine, sine)
 
 
 def ring_plan(parts, tokens, weights, scale, shrinks, expands, segment_slot, cosine, sine):
@@ -434,9 +440,10 @@
     total = multiply(own, None, 0, half)
     second, total = lax.optimization_barrier((tokens, total))
     streams[1] = send(second, home)
-    tables = (owners, places, slots, segment_slot, cosine, sine)
+    core = (me % 2)[None].astype(jnp.int32)
+    tables = (owners, places, slots, core, segment_slot, cosine, sine)
     total, tables = lax.optimization_barrier((total, tables))
-    owners, places, slots, segment_slot, cosine, sine = tables
+    owners, places, slots, core, segment_slot, cosine, sine = tables
     total = multiply(own, total, half, depth)
 
     blocks, hops = [], 2 * ROUNDS - 1
@@ -458,15 +465,19 @@
         else:
             totals.append(total)
     h = rank_terms(owners, slots, blocks[4], factors, hs)
-    for steps, start, low, high in (([1], None, None, None), ([2, 4, 6], 2, 0, cut), ([8], 0, cut, depth)):
-        more = [send(h, [(i, i ^ step) for i in range(parts)]) for step in steps]
-        if start is not None:
-            xs, _ = lax.optimization_barrier((blocks[start:], h))
-            total = block_product(xs, weights, factors, low, high, tile, total, held + start, None, False)[0]
-        for part in more:
-            h = h + part
-        h, total = lax.optimization_barrier((h, total))
-    return block_finish(places, segment_slot, total, expands, scale, h, cosine, sine)
+    beside = lambda step: send(h, [(i, i ^ step) for i in range(parts)])
+
+    def last_product(start, low, high, total):
+        xs, _ = lax.optimization_barrier((blocks[start:], h))
+        return block_product(xs, weights, factors, low, high, tile, total, held + start, None, False)[0]
+
+    near = [beside(step) for step in (2, 4, 6)]
+    near, total = lax.optimization_barrier((near, last_product(2, 0, cut, total)))
+    h = h + near[0] + near[1] + near[2]
+    far = [beside(step) for step in (8, 1, 9)]
+    far, total = lax.optimization_barrier((far, last_product(0, cut, depth, total)))
+    mine, other = h + far[0], far[1] + far[2]
+    return block_finish(places, segment_slot, core, total, expands, scale, mine, other, cosine, sine)
 
 
 def body(parts, tokens, weight_codes, column_scale, shrink_store, expand_store, row_adapter, placement, document_lengths):

time: 160 us -> 152 us (0.950)
  waiting for transfers between devices: 35.3 us -> 26.6 us
    ppermute x21 -> x22, waiting for transfers between devices: 35.3 us -> 26.6 us  [ring_plan(): send = lambda value, pairs: lax.ppermute(value, 'tensor', pairs)]
    ppermute x21 -> x22, starting transfers between devices: 22.8 us -> 23.3 us  [ring_plan(): send = lambda value, pairs: lax.ppermute(value, 'tensor', pairs)]
  transfers between devices with their start and end apart: 21 -> 22, of which waited for: 8 -> 4; matrix products, arithmetic and copies ran while one was open for 3% -> 4% of each run, Pallas kernels for 52% -> 60%
where the time goes in v8:
time: 152 us
  Pallas kernels  94.6 us (62%)
  waiting for transfers between devices  26.6 us (18%)
  starting transfers between devices  23.3 us (15%)
  local copies, waits for them, and re-layouts  3.56 us (2%)
  other arithmetic  3.44 us (2%)
    pallas_call x9, Pallas kernels, block_product(): pl.pallas_call(functools.partial(block_kernel, count, low, tile, steps, f...  87 us
    ppermute x22, waiting for transfers between devices, ring_plan(): send = lambda value, pairs: lax.ppermute(value, 'tensor', pairs)  26.6 us
    ppermute x22, starting transfers between devices, ring_plan(): send = lambda value, pairs: lax.ppermute(value, 'tensor', pairs)  23.3 us
  transfers between devices with their start and end apart: 22, of which 4 were waited for; matrix products, arithmetic and copies ran while one was open for 4% of the time, Pallas kernels for 60%

profile of v8, /device:TPU:0, one launch (start us, length us, event | category | flops | bytes accessed | tf_op | source)
XLA Modules:
  0.0 151.8 jit_solution(18384119028660191986)
XLA Ops:
  0.5 3.0 %collective-permute-start.2 = (bf16[48,16384]{1,0:T(8,128)(2,1)}, bf16[48,16384]{1,0:T(8,128)(2,1)}, u32[]{:S(2)}, u32[]{:S(2)}) collective-permute-start(bf16[48,16384]{1,0:T(8,128)(2,1)} %refs_0_.3), channel_id=1, source_target_pairs={{0,4},{1,3},{4,8},{5,1},{8,12},{9,5},{12,14},{13,9},{14,10},{15,13... | collective-permute-start | bytes 4718600 | tf_op jit(solution)/shard_map/ppermute | solution.py:422
  7.4 1.4 fusion
  9.1 1.4 copy-done.4
  10.5 7.2 %blocks.9 = (f32[16,48,1024]{2,1,0:T(8,128)S(1)}, f32[48,128]{1,0:T(8,128)S(1)}) custom-call(bf16[48,16384]{1,0:T(8,128)(2,1)S(1)} %copy-done.4, bf16[48,16384]{1,0:T(8,128)(2,1)} %collective-permute-done.refs_1_, bf16[16384,1024]{1,0:T(8,128)(2,1)} %refs_6_.1, bf16[64,16384]{1,0:T(8,128)(2,1)S(1)} %bitcast.15, ...), custom_call_target="tpu_custom_call" | custom-call | flops 1610612736 | bytes 16777216 | tf_op jit(solution)/shard_map/blocks/pallas_call | solution.py:263
  18.4 7.3 %blocks.10 = (f32[16,48,1024]{2,1,0:T(8,128)S(1)}, f32[48,128]{1,0:T(8,128)S(1)}) custom-call(bf16[48,16384]{1,0:T(8,128)(2,1)S(1)} %copy-done.4, bf16[48,16384]{1,0:T(8,128)(2,1)} %collective-permute-done.refs_1_, bf16[16384,1024]{1,0:T(8,128)(2,1)} %refs_6_.1, bf16[64,16384]{1,0:T(8,128)(2,1)S(1)} %bitcast.16, ...), custom_call_target="tpu_custom_call", output_to_operand_aliasing={{0}: (5, {})} | custom-call | flops 1610612736 | bytes 16777216 | tf_op jit(solution)/shard_map/blocks/pallas_call | solution.py:263
  25.7 1.5 %collective-permute-start.3 = (bf16[48,16384]{1,0:T(8,128)(2,1)}, bf16[48,16384]{1,0:T(8,128)(2,1)S(1)}, u32[]{:S(2)}, u32[]{:S(2)}) collective-permute-start(bf16[48,16384]{1,0:T(8,128)(2,1)} %collective-permute-done.2.refs_0_), channel_id=1, source_target_pairs={{0,4},{1,3},{4,8},{5,1},{8,12},{9,5},{12,14},{13,9},{14,10},{15,13... | collective-permute-start | bytes 4718600 | tf_op jit(solution)/shard_map/ppermute | solution.py:422
  27.3 20.4 %collective-permute-done.7.refs_0_ = bf16[48,16384]{1,0:T(8,128)(2,1)S(1)} collective-permute-done((bf16[48,16384]{1,0:T(8,128)(2,1)S(1)}, bf16[48,16384]{1,0:T(8,128)(2,1)S(1)}, u32[]{:S(2)}, u32[]{:S(2)}) %collective-permute-start.7) | collective-permute-done | bytes 1572896 | tf_op jit(solution)/shard_map/ppermute | solution.py:422
  48.6 2.3 %collective-permute-start.11 = (bf16[48,16384]{1,0:T(8,128)(2,1)S(1)}, bf16[48,16384]{1,0:T(8,128)(2,1)S(1)}, u32[]{:S(2)}, u32[]{:S(2)}) collective-permute-start(bf16[48,16384]{1,0:T(8,128)(2,1)S(1)} %collective-permute-done.7.refs_0_), channel_id=1, source_target_pairs={{0,2},{1,5},{4,0},{5,9},{8,4},{9,13},{12,8},{13,15},{14,12},{15,11... | collective-permute-start | bytes 4718600 | tf_op jit(solution)/shard_map/ppermute | solution.py:422
  50.8 12.2 %blocks.11 = (f32[16,48,1024]{2,1,0:T(8,128)S(1)}, f32[48,128]{1,0:T(8,128)S(1)}) custom-call(bf16[48,16384]{1,0:T(8,128)(2,1)} %collective-permute-done.2.refs_0_, bf16[48,16384]{1,0:T(8,128)(2,1)S(1)} %collective-permute-done.4.refs_1_, bf16[16384,1024]{1,0:T(8,128)(2,1)} %refs_6_.1, ...), custom_call_target="tpu_custom_call", output_to_operand_aliasing={{0}: (5, {})} | custom-call | flops 3221225472 | bytes 33554432 | tf_op jit(solution)/shard_map/blocks/pallas_call | solution.py:263
  63.1 1.5 collective-permute-start.5
  64.6 12.1 %blocks.12 = (f32[16,48,1024]{2,1,0:T(8,128)S(1)}, f32[48,128]{1,0:T(8,128)S(1)}) custom-call(bf16[48,16384]{1,0:T(8,128)(2,1)S(1)} %collective-permute-done.7.refs_0_, bf16[48,16384]{1,0:T(8,128)(2,1)S(1)} %collective-permute-done.8.refs_1_, bf16[16384,1024]{1,0:T(8,128)(2,1)} %refs_6_.1, ...), custom_call_target="tpu_custom_call", output_to_operand_aliasing={{0}: (5, {})} | custom-call | flops 3221225472 | bytes 33554432 | tf_op jit(solution)/shard_map/blocks/pallas_call | solution.py:263
  78.8 2.2 %collective-permute-start.13 = (bf16[48,16384]{1,0:T(8,128)(2,1)S(1)}, bf16[48,16384]{1,0:T(8,128)(2,1)S(1)}, u32[]{:S(2)}, u32[]{:S(2)}) collective-permute-start(bf16[48,16384]{1,0:T(8,128)(2,1)S(1)} %collective-permute-done.11.refs_0_), channel_id=1, source_target_pairs={{0,2},{1,5},{4,0},{5,9},{8,4},{9,13},{12,8},{13,15},{14,12},{15,11... | collective-permute-start | bytes 4718600 | tf_op jit(solution)/shard_map/ppermute | solution.py:422
  81.1 12.1 %blocks.13 = (f32[16,48,1024]{2,1,0:T(8,128)S(1)}, f32[48,128]{1,0:T(8,128)S(1)}) custom-call(bf16[48,16384]{1,0:T(8,128)(2,1)S(1)} %collective-permute-done.3.refs_0_, bf16[48,16384]{1,0:T(8,128)(2,1)S(1)} %collective-permute-done.6.refs_1_, bf16[16384,1024]{1,0:T(8,128)(2,1)} %refs_6_.1, ...), custom_call_target="tpu_custom_call", output_to_operand_aliasing={{0}: (5, {})} | custom-call | flops 3221225472 | bytes 33554432 | tf_op jit(solution)/shard_map/blocks/pallas_call | solution.py:263
  93.1 3.9 %collective-permute-done.5.refs_0_.x_ref = bf16[48,16384]{1,0:T(8,128)(2,1)S(1)} collective-permute-done((bf16[48,16384]{1,0:T(8,128)(2,1)S(1)}, bf16[48,16384]{1,0:T(8,128)(2,1)S(1)}, u32[]{:S(2)}, u32[]{:S(2)}) %collective-permute-start.5) | collective-permute-done | bytes 1572896 | tf_op jit(solution)/shard_map/ppermute | solution.py:422
  97.0 2.2 %collective-permute-start.9 = (bf16[48,16384]{1,0:T(8,128)(2,1)S(1)}, bf16[48,16384]{1,0:T(8,128)(2,1)S(1)}, u32[]{:S(2)}, u32[]{:S(2)}) collective-permute-start(bf16[48,16384]{1,0:T(8,128)(2,1)S(1)} %collective-permute-done.5.refs_0_.x_ref), channel_id=1, source_target_pairs={{0,4},{1,3},{4,8},{5,1},{8,12},{9,5},{12,14},{13,9},{14,10},{15,13... | collective-permute-start | bytes 4718600 | tf_op jit(solution)/shard_map/ppermute | solution.py:422
  100.5 12.1 %blocks.14 = (f32[16,48,1024]{2,1,0:T(8,128)S(1)}, f32[48,128]{1,0:T(8,128)S(1)}) custom-call(bf16[48,16384]{1,0:T(8,128)(2,1)S(1)} %collective-permute-done.11.refs_0_, bf16[48,16384]{1,0:T(8,128)(2,1)S(1)} %collective-permute-done.12.refs_1_, bf16[16384,1024]{1,0:T(8,128)(2,1)} %refs_6_.1, ...), custom_call_target="tpu_custom_call", output_to_operand_aliasing={{0}: (5, {})} | custom-call | flops 3221225472 | bytes 33554432 | tf_op jit(solution)/shard_map/blocks/pallas_call | solution.py:263
  113.9 8.1 %blocks.15.refs_5_ = f32[16,48,1024]{2,1,0:T(8,128)S(1)} custom-call(bf16[48,16384]{1,0:T(8,128)(2,1)S(1)} %collective-permute-done.5.refs_0_.x_ref, bf16[48,16384]{1,0:T(8,128)(2,1)S(1)} %collective-permute-done.10.refs_1_, bf16[16384,1024]{1,0:T(8,128)(2,1)} %refs_6_.1, f32[16,48,1024]{2,1,0:T(8,128)S(1)} %get-tuple-element.71.refs_3_), custom_call_target="tpu_custom_call", output_to_operand_aliasing={{}: (3, {})} | custom-call | flops 2013265920 | bytes 20971520 | tf_op jit(solution)/shard_map/blocks/pallas_call | solution.py:263
  123.7 2.0 %ranks.1 = bf16[192,128]{1,0:T(8,128)(2,1)S(1)} custom-call(s32[16]{0:T(128)S(1)} %get-tuple-element.57.owners_ref, s32[8]{0:T(128)S(1)} %pad_add_fusion.slot_ref, bf16[48,16384]{1,0:T(8,128)(2,1)S(1)} %collective-permute-done.9.x_ref.refs_2_.refs_4_, bf16[64,16384]{1,0:T(8,128)(2,1)S(1)} %bitcast.23, ...), custom_call_target="tpu_custom_call" | custom-call | tf_op jit(solution)/shard_map/ranks/pallas_call | solution.py:337
  125.7 2.1 %collective-permute-start.14 = (bf16[192,128]{1,0:T(8,128)(2,1)S(1)}, bf16[192,128]{1,0:T(8,128)(2,1)S(1)}, u32[]{:S(2)}, u32[]{:S(2)}) collective-permute-start(bf16[192,128]{1,0:T(8,128)(2,1)S(1)} %ranks.1), channel_id=1, source_target_pairs={{0,2},{1,3},{2,0},{3,1},{4,6},{5,7},{6,4},{7,5},{8,10},{9,11},{10,... | collective-permute-start | bytes 147464 | tf_op jit(solution)/shard_map/ppermute | solution.py:422
  127.8 1.6 %collective-permute-start.15 = (bf16[192,128]{1,0:T(8,128)(2,1)S(1)}, bf16[192,128]{1,0:T(8,128)(2,1)S(1)}, u32[]{:S(2)}, u32[]{:S(2)}) collective-permute-start(bf16[192,128]{1,0:T(8,128)(2,1)S(1)} %ranks.1), channel_id=1, source_target_pairs={{0,4},{1,5},{2,6},{3,7},{4,0},{5,1},{6,2},{7,3},{8,12},{9,13},{10,... | collective-permute-start | bytes 147464 | tf_op jit(solution)/shard_map/ppermute | solution.py:422
  129.4 8.5 %blocks.16.refs_7_ = f32[16,48,1024]{2,1,0:T(8,128)S(1)} custom-call(bf16[48,16384]{1,0:T(8,128)(2,1)S(1)} %collective-permute-done.13.x_ref.refs_0_.refs_2_, bf16[48,16384]{1,0:T(8,128)(2,1)S(1)} %collective-permute-done.17.refs_1_.refs_3_, bf16[48,16384]{1,0:T(8,128)(2,1)S(1)} %collective-permute-done.9.x_ref.refs_2_.refs_4_, ...), custom_call_target="tpu_custom_call", output_to_operand_aliasing={{}: (5, {})} | custom-call | flops 4026531840 | bytes 20971520 | tf_op jit(solution)/shard_map/blocks/pallas_call | solution.py:263
  138.0 3.0 %collective-permute-start.19 = (bf16[192,128]{1,0:T(8,128)(2,1)S(1)}, bf16[192,128]{1,0:T(8,128)(2,1)S(1)}, u32[]{:S(2)}, u32[]{:S(2)}) collective-permute-start(bf16[192,128]{1,0:T(8,128)(2,1)S(1)} %add_add_fusion), channel_id=1, source_target_pairs={{0,8},{1,9},{2,10},{3,11},{4,12},{5,13},{6,14},{7,15},{8,0},{9,1},... | collective-permute-start | bytes 147464 | tf_op jit(solution)/shard_map/ppermute | solution.py:422
  141.2 7.5 %blocks.17.refs_0_.refs_1_.refs_2_.refs_3_.refs_4_.refs_5_.refs_6_.refs_7_ = f32[16,48,1024]{2,1,0:T(8,128)S(1)} custom-call(bf16[48,16384]{1,0:T(8,128)(2,1)S(1)} %collective-permute-done.5.refs_0_.x_ref, bf16[48,16384]{1,0:T(8,128)(2,1)S(1)} %collective-permute-done.10.refs_1_, ...), custom_call_target="tpu_custom_call", output_to_operand_aliasing={{}: (7, {})} | custom-call | flops 3623878656 | bytes 12582912 | tf_op jit(solution)/shard_map/blocks/pallas_call | solution.py:263
  148.9 2.9 %finish.1 = bf16[768,1024]{1,0:T(8,128)(2,1)} custom-call(s32[16]{0:T(128)S(1)} %get-tuple-element.54.places_ref, s32[6]{0:T(128)S(1)} %gather_fusion, s32[1]{0:T(128)} %bitcast.7.core_ref, f32[16,48,1024]{2,1,0:T(8,128)S(1)} %blocks.17.refs_0_.refs_1_.refs_2_.refs_3_.refs_4_.refs_5_.refs_6_.refs_7_, ...), custom_call_target="tpu_custom_call" | custom-call | tf_op jit(solution)/shard_map/finish/pallas_call | solution.py:391
  (60 shorter events, 13.0 us)
Async XLA Ops:
  0.0 9.1 %collective-permute-start.1 = (bf16[64,16384]{1,0:T(8,128)(2,1)}, bf16[64,16384]{1,0:T(8,128)(2,1)S(1)}, u32[]{:S(2)}, u32[]{:S(2)}) collective-permute-start(bf16[64,16384]{1,0:T(8,128)(2,1)} %bitcast.14), channel_id=1, source_target_pairs={{0,1},{1,0},{2,3},{3,2},{4,5},{5,4},{6,7},{7,6},{8,9},{9,8},{10,11... | collective-permute-start | bytes 6291464 | tf_op jit(solution)/shard_map/ppermute | solution.py:422
  0.5 8.6 %collective-permute-start = (bf16[48,16384]{1,0:T(8,128)(2,1)}, bf16[48,16384]{1,0:T(8,128)(2,1)}, u32[]{:S(2)}, u32[]{:S(2)}) collective-permute-start(bf16[48,16384]{1,0:T(8,128)(2,1)} %refs_0_.3), channel_id=1, source_target_pairs={{0,1},{1,0},{2,3},{3,2},{4,5},{5,4},{6,7},{7,6},{8,9},{9,8},{10,11... | collective-permute-start | bytes 4718600 | tf_op jit(solution)/shard_map/ppermute | solution.py:422
  0.5 25.1 %collective-permute-start.2 = (bf16[48,16384]{1,0:T(8,128)(2,1)}, bf16[48,16384]{1,0:T(8,128)(2,1)}, u32[]{:S(2)}, u32[]{:S(2)}) collective-permute-start(bf16[48,16384]{1,0:T(8,128)(2,1)} %refs_0_.3), channel_id=1, source_target_pairs={{0,4},{1,3},{4,8},{5,1},{8,12},{9,5},{12,14},{13,9},{14,10},{15,13... | collective-permute-start | bytes 4718600 | tf_op jit(solution)/shard_map/ppermute | solution.py:422
  17.8 29.9 %collective-permute-start.7 = (bf16[48,16384]{1,0:T(8,128)(2,1)S(1)}, bf16[48,16384]{1,0:T(8,128)(2,1)S(1)}, u32[]{:S(2)}, u32[]{:S(2)}) collective-permute-start(bf16[48,16384]{1,0:T(8,128)(2,1)S(1)} %copy-done.4), channel_id=1, source_target_pairs={{0,2},{1,5},{4,0},{5,9},{8,4},{9,13},{12,8},{13,15},{14,12},{15,11... | collective-permute-start | bytes 4718600 | tf_op jit(solution)/shard_map/ppermute | solution.py:422
  25.7 25.2 %collective-permute-start.4 = (bf16[48,16384]{1,0:T(8,128)(2,1)}, bf16[48,16384]{1,0:T(8,128)(2,1)S(1)}, u32[]{:S(2)}, u32[]{:S(2)}) collective-permute-start(bf16[48,16384]{1,0:T(8,128)(2,1)} %collective-permute-done.2.refs_0_), channel_id=1, source_target_pairs={{0,1},{1,0},{2,3},{3,2},{4,5},{5,4},{6,7},{7,6},{8,9},{9,8},{10,11... | collective-permute-start | bytes 4718600 | tf_op jit(solution)/shard_map/ppermute | solution.py:422
  25.7 37.3 %collective-permute-start.3 = (bf16[48,16384]{1,0:T(8,128)(2,1)}, bf16[48,16384]{1,0:T(8,128)(2,1)S(1)}, u32[]{:S(2)}, u32[]{:S(2)}) collective-permute-start(bf16[48,16384]{1,0:T(8,128)(2,1)} %collective-permute-done.2.refs_0_), channel_id=1, source_target_pairs={{0,4},{1,3},{4,8},{5,1},{8,12},{9,5},{12,14},{13,9},{14,10},{15,13... | collective-permute-start | bytes 4718600 | tf_op jit(solution)/shard_map/ppermute | solution.py:422
  47.6 17.0 %collective-permute-start.8 = (bf16[48,16384]{1,0:T(8,128)(2,1)S(1)}, bf16[48,16384]{1,0:T(8,128)(2,1)S(1)}, u32[]{:S(2)}, u32[]{:S(2)}) collective-permute-start(bf16[48,16384]{1,0:T(8,128)(2,1)S(1)} %collective-permute-done.7.refs_0_), channel_id=1, source_target_pairs={{0,1},{1,0},{2,3},{3,2},{4,5},{5,4},{6,7},{7,6},{8,9},{9,8},{10,11... | collective-permute-start | bytes 4718600 | tf_op jit(solution)/shard_map/ppermute | solution.py:422
  48.6 29.3 %collective-permute-start.11 = (bf16[48,16384]{1,0:T(8,128)(2,1)S(1)}, bf16[48,16384]{1,0:T(8,128)(2,1)S(1)}, u32[]{:S(2)}, u32[]{:S(2)}) collective-permute-start(bf16[48,16384]{1,0:T(8,128)(2,1)S(1)} %collective-permute-done.7.refs_0_), channel_id=1, source_target_pairs={{0,2},{1,5},{4,0},{5,9},{8,4},{9,13},{12,8},{13,15},{14,12},{15,11... | collective-permute-start | bytes 4718600 | tf_op jit(solution)/shard_map/ppermute | solution.py:422
  63.0 18.0 %collective-permute-start.6 = (bf16[48,16384]{1,0:T(8,128)(2,1)S(1)}, bf16[48,16384]{1,0:T(8,128)(2,1)S(1)}, u32[]{:S(2)}, u32[]{:S(2)}) collective-permute-start(bf16[48,16384]{1,0:T(8,128)(2,1)S(1)} %collective-permute-done.3.refs_0_), channel_id=1, source_target_pairs={{0,1},{1,0},{2,3},{3,2},{4,5},{5,4},{6,7},{7,6},{8,9},{9,8},{10,11... | collective-permute-start | bytes 4718600 | tf_op jit(solution)/shard_map/ppermute | solution.py:422
  63.1 33.9 %collective-permute-start.5 = (bf16[48,16384]{1,0:T(8,128)(2,1)S(1)}, bf16[48,16384]{1,0:T(8,128)(2,1)S(1)}, u32[]{:S(2)}, u32[]{:S(2)}) collective-permute-start(bf16[48,16384]{1,0:T(8,128)(2,1)S(1)} %collective-permute-done.3.refs_0_), channel_id=1, source_target_pairs={{0,4},{1,3},{4,8},{5,1},{8,12},{9,5},{12,14},{13,9},{14,10},{15,13... | collective-permute-start | bytes 4718600 | tf_op jit(solution)/shard_map/ppermute | solution.py:422
  77.9 22.6 %collective-permute-start.12 = (bf16[48,16384]{1,0:T(8,128)(2,1)S(1)}, bf16[48,16384]{1,0:T(8,128)(2,1)S(1)}, u32[]{:S(2)}, u32[]{:S(2)}) collective-permute-start(bf16[48,16384]{1,0:T(8,128)(2,1)S(1)} %collective-permute-done.11.refs_0_), channel_id=1, source_target_pairs={{0,1},{1,0},{2,3},{3,2},{4,5},{5,4},{6,7},{7,6},{8,9},{9,8},{10,11... | collective-permute-start | bytes 4718600 | tf_op jit(solution)/shard_map/ppermute | solution.py:422
  78.8 33.8 %collective-permute-start.13 = (bf16[48,16384]{1,0:T(8,128)(2,1)S(1)}, bf16[48,16384]{1,0:T(8,128)(2,1)S(1)}, u32[]{:S(2)}, u32[]{:S(2)}) collective-permute-start(bf16[48,16384]{1,0:T(8,128)(2,1)S(1)} %collective-permute-done.11.refs_0_), channel_id=1, source_target_pairs={{0,2},{1,5},{4,0},{5,9},{8,4},{9,13},{12,8},{13,15},{14,12},{15,11... | collective-permute-start | bytes 4718600 | tf_op jit(solution)/shard_map/ppermute | solution.py:422
  97.0 16.9 %collective-permute-start.10 = (bf16[48,16384]{1,0:T(8,128)(2,1)S(1)}, bf16[48,16384]{1,0:T(8,128)(2,1)S(1)}, u32[]{:S(2)}, u32[]{:S(2)}) collective-permute-start(bf16[48,16384]{1,0:T(8,128)(2,1)S(1)} %collective-permute-done.5.refs_0_.x_ref), channel_id=1, source_target_pairs={{0,1},{1,0},{2,3},{3,2},{4,5},{5,4},{6,7},{7,6},{8,9},{9,8},{10,11... | collective-permute-start | bytes 4718600 | tf_op jit(solution)/shard_map/ppermute | solution.py:422
  97.0 26.2 %collective-permute-start.9 = (bf16[48,16384]{1,0:T(8,128)(2,1)S(1)}, bf16[48,16384]{1,0:T(8,128)(2,1)S(1)}, u32[]{:S(2)}, u32[]{:S(2)}) collective-permute-start(bf16[48,16384]{1,0:T(8,128)(2,1)S(1)} %collective-permute-done.5.refs_0_.x_ref), channel_id=1, source_target_pairs={{0,4},{1,3},{4,8},{5,1},{8,12},{9,5},{12,14},{13,9},{14,10},{15,13... | collective-permute-start | bytes 4718600 | tf_op jit(solution)/shard_map/ppermute | solution.py:422
  123.2 6.2 %collective-permute-start.18 = (bf16[48,16384]{1,0:T(8,128)(2,1)S(1)}, bf16[48,16384]{1,0:T(8,128)(2,1)S(1)}, u32[]{:S(2)}, u32[]{:S(2)}) collective-permute-start(bf16[48,16384]{1,0:T(8,128)(2,1)S(1)} %collective-permute-done.9.x_ref.refs_2_.refs_4_), channel_id=1, source_target_pairs={{0,1},{1,0},{2,3},{3,2},{4,5},{5,4},{6,7},{7,6},{8,9},{9,8},{10,11... | collective-permute-start | bytes 4718600 | tf_op jit(solution)/shard_map/ppermute | solution.py:422
  123.2 6.2 %collective-permute-start.17 = (bf16[48,16384]{1,0:T(8,128)(2,1)S(1)}, bf16[48,16384]{1,0:T(8,128)(2,1)S(1)}, u32[]{:S(2)}, u32[]{:S(2)}) collective-permute-start(bf16[48,16384]{1,0:T(8,128)(2,1)S(1)} %collective-permute-done.13.x_ref.refs_0_.refs_2_), channel_id=1, source_target_pairs={{0,1},{1,0},{2,3},{3,2},{4,5},{5,4},{6,7},{7,6},{8,9},{9,8},{10,11... | collective-permute-start | bytes 4718600 | tf_op jit(solution)/shard_map/ppermute | solution.py:422
  125.7 12.2 %collective-permute-start.14 = (bf16[192,128]{1,0:T(8,128)(2,1)S(1)}, bf16[192,128]{1,0:T(8,128)(2,1)S(1)}, u32[]{:S(2)}, u32[]{:S(2)}) collective-permute-start(bf16[192,128]{1,0:T(8,128)(2,1)S(1)} %ranks.1), channel_id=1, source_target_pairs={{0,2},{1,3},{2,0},{3,1},{4,6},{5,7},{6,4},{7,5},{8,10},{9,11},{10,... | collective-permute-start | bytes 147464 | tf_op jit(solution)/shard_map/ppermute | solution.py:422
  127.8 10.1 %collective-permute-start.15 = (bf16[192,128]{1,0:T(8,128)(2,1)S(1)}, bf16[192,128]{1,0:T(8,128)(2,1)S(1)}, u32[]{:S(2)}, u32[]{:S(2)}) collective-permute-start(bf16[192,128]{1,0:T(8,128)(2,1)S(1)} %ranks.1), channel_id=1, source_target_pairs={{0,4},{1,5},{2,6},{3,7},{4,0},{5,1},{6,2},{7,3},{8,12},{9,13},{10,... | collective-permute-start | bytes 147464 | tf_op jit(solution)/shard_map/ppermute | solution.py:422
  129.4 8.6 %collective-permute-start.16 = (bf16[192,128]{1,0:T(8,128)(2,1)S(1)}, bf16[192,128]{1,0:T(8,128)(2,1)S(1)}, u32[]{:S(2)}, u32[]{:S(2)}) collective-permute-start(bf16[192,128]{1,0:T(8,128)(2,1)S(1)} %ranks.1), channel_id=1, source_target_pairs={{0,6},{1,7},{2,4},{3,5},{4,2},{5,3},{6,0},{7,1},{8,14},{9,15},{10,... | collective-permute-start | bytes 147464 | tf_op jit(solution)/shard_map/ppermute | solution.py:422
  138.0 10.8 %copy-start.5 = (f32[1024]{0:T(1024)S(1)}, f32[1024]{0:T(1024)}, u32[]{:S(2)}) copy-start(f32[1024]{0:T(1024)} %param.12) | copy-start | bytes 12292
  138.0 10.7 %collective-permute-start.19 = (bf16[192,128]{1,0:T(8,128)(2,1)S(1)}, bf16[192,128]{1,0:T(8,128)(2,1)S(1)}, u32[]{:S(2)}, u32[]{:S(2)}) collective-permute-start(bf16[192,128]{1,0:T(8,128)(2,1)S(1)} %add_add_fusion), channel_id=1, source_target_pairs={{0,8},{1,9},{2,10},{3,11},{4,12},{5,13},{6,14},{7,15},{8,0},{9,1},... | collective-permute-start | bytes 147464 | tf_op jit(solution)/shard_map/ppermute | solution.py:422
  141.0 7.7 %collective-permute-start.20 = (bf16[192,128]{1,0:T(8,128)(2,1)S(1)}, bf16[192,128]{1,0:T(8,128)(2,1)S(1)}, u32[]{:S(2)}, u32[]{:S(2)}) collective-permute-start(bf16[192,128]{1,0:T(8,128)(2,1)S(1)} %add_add_fusion), channel_id=1, source_target_pairs={{0,1},{1,0},{2,3},{3,2},{4,5},{5,4},{6,7},{7,6},{8,9},{9,8},{10,11... | collective-permute-start | bytes 147464 | tf_op jit(solution)/shard_map/ppermute | solution.py:422
  141.0 7.7 %collective-permute-start.21 = (bf16[192,128]{1,0:T(8,128)(2,1)S(1)}, bf16[192,128]{1,0:T(8,128)(2,1)S(1)}, u32[]{:S(2)}, u32[]{:S(2)}) collective-permute-start(bf16[192,128]{1,0:T(8,128)(2,1)S(1)} %add_add_fusion), channel_id=1, source_target_pairs={{0,9},{1,8},{2,11},{3,10},{4,13},{5,12},{6,15},{7,14},{8,1},{9,0},... | collective-permute-start | bytes 147464 | tf_op jit(solution)/shard_map/ppermute | solution.py:422
  141.2 7.6 %copy-start.3 = (bf16[16,1024,64]{1,2,0:T(8,128)(2,1)S(1)}, bf16[16,1024,64]{1,2,0:T(8,128)(2,1)}, u32[]{:S(2)}) copy-start(bf16[16,1024,64]{1,2,0:T(8,128)(2,1)} %param.14) | copy-start | bytes 6291460
  (4 other events, 11.3 us)

commit v9 on v8

--- a/solution.py
+++ b/solution.py
@@ -36,6 +36,11 @@
     angles = positions.astype(F32)[:, None] * inverse[None, :]
     cosine, sine = jnp.cos(angles), jnp.sin(angles)
     return jnp.concatenate([cosine, cosine], 1), jnp.concatenate([-sine, sine], 1)
+
+
+def small_tables(row_adapter, placement, document_lengths, total_rows):
+    segment_slot = placement[row_adapter[::SEG]]
+    return segment_slot, *rotary_tables(row_positions(document_lengths, total_rows))
 
 
 def rotate(value, cosine, sine):
@@ -129,7 +134,8 @@
     return h
 
 
-def gather_plan(parts, tokens, weights, scale, shrinks, expands, segment_slot, cosine, sine):
+def gather_plan(parts, tokens, weights, scale, shrinks, expands, indices):
+    segment_slot, cosine, sine = small_tables(*indices, tokens.shape[0] * parts)
     held, rank, depth = shrinks.shape
     tile = depth // 16
     x = lax.all_gather(tokens, "tensor", axis=0, tiled=True)
@@ -174,8 +180,6 @@
         s_refs, refs = refs[:2], refs[2:]
     if not first:
         total_in, refs = refs[0], refs[1:]
-    if ranked and not fresh:
-        h_in, refs = refs[0], refs[1:]
     total_out, refs = refs[0], refs[1:]
     if ranked:
         h_out, refs = refs[0], refs[1:]
@@ -208,7 +212,7 @@
         load.start()
     acc[...] = jnp.zeros_like(acc)
     if ranked:
-        h_out[...] = jnp.zeros_like(h_out) if fresh else h_in[...]
+        h_out[...] = jnp.zeros_like(h_out)
 
     @pl.loop(0, steps)
     def _(step):
@@ -221,7 +225,8 @@
             product = jnp.dot(x, w_slots[slot, :, cut], preferred_element_type=F32)
             acc[:, :, cut] += product.reshape(count, rows, CHUNK)
         if ranked:
-            h_out[...] += lax.dot_general(x[:rows], s_slots[slot], NT, preferred_element_type=F32)
+            mine = jnp.concatenate([x[i * rows : (i + 1) * rows] for i in range(0, count, 2)], 0)
+            h_out[...] += lax.dot_general(mine, s_slots[slot], NT, preferred_element_type=F32)
 
         @pl.when(step + SLOTS < steps)
         def _():
@@ -235,7 +240,7 @@
     store.wait()
 
 
-def block_product(xs, weights, factors, low, high, tile, total, base, h, ranked):
+def block_product(xs, weights, factors, low, high, tile, total, base, ranked):
     count = len(xs)
     rows = xs[0].shape[0]
     cols = weights.shape[1]
@@ -252,12 +257,9 @@
         aliases = {len(operands): 0}
         operands.append(total)
         specs.append(anywhere)
-    if ranked and not fresh:
-        operands.append(h)
-        specs.append(whole)
     outs, out_specs = [jax.ShapeDtypeStruct(total_shape(rows, cols), F32)], [anywhere]
     if ranked:
-        outs.append(jax.ShapeDtypeStruct((rows, rank), F32))
+        outs.append(jax.ShapeDtypeStruct((count // 2 * rows, rank), F32))
         out_specs.append(whole)
     steps = (high - low) // tile
     result = pl.pallas_call(
@@ -283,7 +285,7 @@
         ),
         name="blocks",
     )(*operands)
-    return result if ranked else (result[0], h)
+    return result[0], result[1:]
 
 
 def total_shape(rows, cols):
@@ -317,15 +319,18 @@
     rows, rank = x_ref.shape[0], sa_ref.shape[0]
     last = both_ranks(x_ref[...], (sa_ref[...], sb_ref[...]))
     segments = slot_ref.shape[0] - 2
-    for i, source in enumerate(h_refs + (last,)):
-        owner = owners_ref[2 * i]
-        segment = owner * rows // SEG
-        after = jnp.minimum(segment + 1, segments - 1)
-        row = owner * rows + lax.broadcasted_iota(jnp.int32, (rows, rank), 0)
-        slot = jnp.where(row < (segment + 1) * SEG, slot_ref[segment], slot_ref[after])
-        terms = jnp.where(slot == slot_ref[segments + 1], source[:, rank:], 0.0)
-        terms = jnp.where(slot == slot_ref[segments], source[:, :rank], terms)
-        placed[pl.ds(pl.multiple_of(owner // 2 * rows, 16), rows), :] = terms
+    block = 0
+    for source in h_refs + (last,):
+        for low in range(0, source.shape[0], rows):
+            owner = owners_ref[2 * block]
+            segment = owner * rows // SEG
+            after = jnp.minimum(segment + 1, segments - 1)
+            row = owner * rows + lax.broadcasted_iota(jnp.int32, (rows, rank), 0)
+            slot = jnp.where(row < (segment + 1) * SEG, slot_ref[segment], slot_ref[after])
+            terms = jnp.where(slot == slot_ref[segments + 1], source[low : low + rows, rank:], 0.0)
+            terms = jnp.where(slot == slot_ref[segments], source[low : low + rows, :rank], terms)
+            placed[pl.ds(pl.multiple_of(owner // 2 * rows, 16), rows), :] = terms
+            block += 1
     half = placed.shape[0] // 2
     out_ref[...] = jnp.concatenate([placed[:half, :], placed[half:, :]], 1).astype(out_ref.dtype)
 
@@ -411,71 +416,75 @@
     )(places, slots, core, *([total] * half), *([expands] * segments), scale, mine, other, cosine, sine)
 
 
-def ring_plan(parts, tokens, weights, scale, shrinks, expands, segment_slot, cosine, sine):
+def ring_plan(parts, tokens, weights, scale, shrinks, expands, indices):
     rows, depth = tokens.shape
     tile = depth // 16
     me = lax.axis_index("tensor")
     owners_table = block_owners()
-    owners = jnp.asarray(owners_table)[me]
-    places = jnp.asarray(np.argsort(owners_table, axis=1).astype(np.int32))[me]
-    slots = jnp.concatenate([segment_slot, jnp.stack([me, me ^ 1]).astype(jnp.int32)])
     send = lambda value, pairs: lax.ppermute(value, "tensor", pairs)
     swap = lambda value: send(value, [(i, i ^ 1) for i in range(parts)])
     out, home = ring_pairs((1, -1)), ring_pairs((-1, 1))
 
-    half, cut = depth // 2, 10 * tile
+    half = depth // 2
     hs, counts = [], []
 
-    def multiply(xs, total, low=0, high=depth):
-        if low == 0:
-            hs.append(None)
-            counts.append(len(xs))
-        held = sum(counts[:-1])
-        total, hs[-1] = block_product(xs, weights, factors, low, high, tile, total, held, hs[-1], True)
+    def multiply(xs, total):
+        total, h = block_product(xs, weights, factors, 0, depth, tile, total, sum(counts), True)
+        hs.extend(h)
+        counts.append(len(xs))
         return total
 
     streams = [send(tokens, out), None]
-    own = [tokens, swap(tokens)]
+    own, part = [tokens, swap(tokens)], 2 * tile
     factors = [shrinks[0], swap(shrinks[0])]
-    total = multiply(own, None, 0, half)
+    total, _ = block_product(own, weights, factors, 0, part, tile, None, 0, False)
     second, total = lax.optimization_barrier((tokens, total))
     streams[1] = send(second, home)
-    core = (me % 2)[None].astype(jnp.int32)
-    tables = (owners, places, slots, core, segment_slot, cosine, sine)
-    total, tables = lax.optimization_barrier((total, tables))
-    owners, places, slots, core, segment_slot, cosine, sine = tables
-    total = multiply(own, total, half, depth)
+    total, _ = block_product(own, weights, factors, part, depth, tile, total, 0, False)
+    hs, total = lax.optimization_barrier(([some_ranks(tokens, factors)], total))
+    counts.append(len(own))
+
+    def make_tables(me, indices):
+        segment_slot, cosine, sine = small_tables(*indices, parts * rows)
+        owners = jnp.asarray(owners_table)[me]
+        places = jnp.asarray(np.argsort(owners_table, axis=1).astype(np.int32))[me]
+        slots = jnp.concatenate([segment_slot, jnp.stack([me, me ^ 1]).astype(jnp.int32)])
+        core = (me % 2)[None].astype(jnp.int32)
+        return owners, places, slots, core, segment_slot, cosine, sine
 
     blocks, hops = [], 2 * ROUNDS - 1
-    totals, waits = [total] * 2, [0, 1, 2, 3, 4, 6, 7]
+    totals = [total] * 2
     for hop in range(hops):
-        arrived, _ = lax.optimization_barrier((streams[hop % 2], totals[waits[hop]]))
+        arrived, _ = lax.optimization_barrier((streams[hop % 2], totals[hop if hop % 2 else hop + 1]))
         if hop + 2 < hops:
             streams[hop % 2] = send(arrived, home if hop % 2 else out)
-        blocks += [arrived, swap(arrived)]
-        if hop < hops - 3:
+        if hop % 2:
+            late = [arrived, swap(arrived)]
+            if hop == hops - 2:
+                early = some_ranks(arrived, factors)
             total = multiply(blocks, total)
-            totals.append(total)
-            blocks = []
-        elif hop == hops - 2:
-            hs += [some_ranks(part, factors) for part in blocks[::2]]
-            held = sum(counts)
-            total = block_product(blocks[:2], weights, factors, 0, cut, tile, total, held, None, False)[0]
-            totals.append((total, hs))
+            blocks = late
         else:
-            totals.append(total)
-    h = rank_terms(owners, slots, blocks[4], factors, hs)
+            blocks += [arrived, swap(arrived)]
+        if hop == 1:
+            known, total = lax.optimization_barrier(((me, indices), total))
+            tables, total = lax.optimization_barrier((make_tables(*known), total))
+        totals.append((total, early) if hop == hops - 2 else total)
+    held = sum(counts)
+    hs.append(early)
+    owners, places, slots, core, segment_slot, cosine, sine = tables
+    h = rank_terms(owners, slots, blocks[2], factors, hs)
     beside = lambda step: send(h, [(i, i ^ step) for i in range(parts)])
 
-    def last_product(start, low, high, total):
-        xs, _ = lax.optimization_barrier((blocks[start:], h))
-        return block_product(xs, weights, factors, low, high, tile, total, held + start, None, False)[0]
+    def last_product(low, high, total):
+        xs, _ = lax.optimization_barrier((blocks, h))
+        return block_product(xs, weights, factors, low, high, tile, total, held, False)[0]
 
     near = [beside(step) for step in (2, 4, 6)]
-    near, total = lax.optimization_barrier((near, last_product(2, 0, cut, total)))
+    near, total = lax.optimization_barrier((near, last_product(0, half, total)))
     h = h + near[0] + near[1] + near[2]
     far = [beside(step) for step in (8, 1, 9)]
-    far, total = lax.optimization_barrier((far, last_product(0, cut, depth, total)))
+    far, total = lax.optimization_barrier((far, last_product(half, depth, total)))
     mine, other = h + far[0], far[1] + far[2]
     return block_finish(places, segment_slot, core, total, expands, scale, mine, other, cosine, sine)
 
@@ -483,13 +492,12 @@
 def body(parts, tokens, weight_codes, column_scale, shrink_store, expand_store, row_adapter, placement, document_lengths):
     rows = tokens.shape[0]
     total_rows = rows * parts
-    segment_slot = placement[row_adapter[::SEG]]
     shrinks = jnp.swapaxes(shrink_store, 1, 2)
     expands = jnp.swapaxes(expand_store, 1, 2)
-    cosine, sine = rotary_tables(row_positions(document_lengths, total_rows))
     ring = parts == 2 * len(SNAKE) and rows % 16 == 0 and shrinks.shape[0] == 1 and total_rows % (2 * SEG) == 0
     plan = ring_plan if ring else gather_plan
-    return plan(parts, tokens, weight_codes, column_scale[None, :], shrinks, expands, segment_slot, cosine, sine)
+    indices = (row_adapter, placement, document_lengths)
+    return plan(parts, tokens, weight_codes, column_scale[None, :], shrinks, expands, indices)
 
 
 def solution(mesh):

time: 152 us -> 152 us (level)
  Pallas kernels: 94.6 us -> 78.7 us
  waiting for transfers between devices: 26.6 us -> 36.5 us
  starting transfers between devices: 23.3 us -> 26.9 us
  local copies, waits for them, and re-layouts: 3.56 us -> 6.94 us
    pallas_call x9 -> x7, Pallas kernels: 87 us -> 69 us  [block_product(): pl.pallas_call(functools.partial(block_kernel, count, low, tile, steps, f...]
    ppermute x22, waiting for transfers between devices: 26.6 us -> 36.5 us  [ring_plan(): send = lambda value, pairs: lax.ppermute(value, 'tensor', pairs)]
    ppermute x22, starting transfers between devices: 23.3 us -> 26.9 us  [ring_plan(): send = lambda value, pairs: lax.ppermute(value, 'tensor', pairs)]
    unnamed x12 -> x24, local copies, waits for them, and re-layouts: 1.43 us -> 4.81 us
    pallas_call x2, Pallas kernels: 2.64 us -> 4.74 us  [some_ranks(): pl.pallas_call(some_ranks_kernel, grid=(1,), in_specs=[whole(value.shape)...]
  transfers between devices with their start and end apart: 22 -> 22, of which waited for: 4 -> 6; matrix products, arithmetic and copies ran while one was open for 4% -> 3% of each run, Pallas kernels for 60% -> 50%
where the time goes in v9:
time: 152 us; the launch traced here: 151 us
  Pallas kernels  78.7 us (52%)
  waiting for transfers between devices  36.5 us (24%)
  starting transfers between devices  26.9 us (18%)
  local copies, waits for them, and re-layouts  6.94 us (5%)
  other arithmetic  2.14 us (1%)
    pallas_call x7, Pallas kernels, block_product(): pl.pallas_call(functools.partial(block_kernel, count, low, tile, steps, f...  69 us
    ppermute x22, waiting for transfers between devices, ring_plan(): send = lambda value, pairs: lax.ppermute(value, 'tensor', pairs)  36.5 us
    ppermute x22, starting transfers between devices, ring_plan(): send = lambda value, pairs: lax.ppermute(value, 'tensor', pairs)  26.9 us
    unnamed x24, local copies, waits for them, and re-layouts  4.81 us
    pallas_call x2, Pallas kernels, some_ranks(): pl.pallas_call(some_ranks_kernel, grid=(1,), in_specs=[whole(value.shape)...  4.74 us
  transfers between devices with their start and end apart: 22, of which 6 were waited for; matrix products, arithmetic and copies ran while one was open for 3% of the time, Pallas kernels for 50%

profile of v9, /device:TPU:0, one launch (start us, length us, event | category | flops | bytes accessed | tf_op | source)
XLA Modules:
  0.0 151.5 jit_solution(2469455971527324947)
XLA Ops:
  0.5 3.0 %collective-permute-start = (bf16[48,16384]{1,0:T(8,128)(2,1)}, bf16[48,16384]{1,0:T(8,128)(2,1)}, u32[]{:S(2)}, u32[]{:S(2)}) collective-permute-start(bf16[48,16384]{1,0:T(8,128)(2,1)} %refs_0_.3), channel_id=1, source_target_pairs={{0,4},{1,3},{4,8},{5,1},{8,12},{9,5},{12,14},{13,9},{14,10},{15,13... | collective-permute-start | bytes 4718600 | tf_op jit(solution)/shard_map/ppermute | solution.py:424
  3.5 3.2 %collective-permute-done.2.refs_1_ = bf16[48,16384]{1,0:T(8,128)(2,1)S(1)} collective-permute-done((bf16[48,16384]{1,0:T(8,128)(2,1)}, bf16[48,16384]{1,0:T(8,128)(2,1)S(1)}, u32[]{:S(2)}, u32[]{:S(2)}) %collective-permute-start.2) | collective-permute-done | bytes 1572896 | tf_op jit(solution)/shard_map/ppermute | solution.py:424
  6.7 3.1 %blocks.7.refs_3_ = f32[16,48,1024]{2,1,0:T(8,128)S(1)} custom-call(bf16[48,16384]{1,0:T(8,128)(2,1)} %refs_0_.3, bf16[48,16384]{1,0:T(8,128)(2,1)S(1)} %collective-permute-done.2.refs_1_, bf16[16384,1024]{1,0:T(8,128)(2,1)} %refs_4_.7), custom_call_target="tpu_custom_call" | custom-call | flops 402653184 | bytes 4194304 | tf_op jit(solution)/shard_map/blocks/pallas_call | solution.py:265
  9.8 2.9 %collective-permute-start.6 = (bf16[48,16384]{1,0:T(8,128)(2,1)}, bf16[48,16384]{1,0:T(8,128)(2,1)}, u32[]{:S(2)}, u32[]{:S(2)}) collective-permute-start(bf16[48,16384]{1,0:T(8,128)(2,1)} %refs_0_.3), channel_id=1, source_target_pairs={{0,2},{1,5},{4,0},{5,9},{8,4},{9,13},{12,8},{13,15},{14,12},{15,11... | collective-permute-start | bytes 4718600 | tf_op jit(solution)/shard_map/ppermute | solution.py:424
  12.8 10.9 %blocks.8.refs_5_ = f32[16,48,1024]{2,1,0:T(8,128)S(1)} custom-call(bf16[48,16384]{1,0:T(8,128)(2,1)} %refs_0_.3, bf16[48,16384]{1,0:T(8,128)(2,1)S(1)} %collective-permute-done.2.refs_1_, bf16[16384,1024]{1,0:T(8,128)(2,1)} %refs_4_.7, f32[16,48,1024]{2,1,0:T(8,128)S(1)} %blocks.7.refs_3_), custom_call_target="tpu_custom_call", output_to_operand_aliasing={{}: (3, {})} | custom-call | flops 2818572288 | bytes 29360128 | tf_op jit(solution)/shard_map/blocks/pallas_call | solution.py:265
  23.7 3.5 %some_ranks.2.refs_0_ = f32[48,128]{1,0:T(8,128)S(1)} custom-call(bf16[48,16384]{1,0:T(8,128)(2,1)} %refs_0_.3, bf16[64,16384]{1,0:T(8,128)(2,1)S(1)} %bitcast.15, bf16[64,16384]{1,0:T(8,128)(2,1)S(1)} %collective-permute-done.1.sb_ref.refs_4_.refs_6_), custom_call_target="tpu_custom_call" | custom-call | tf_op jit(solution)/shard_map/some_ranks/pallas_call | solution.py:306
  27.2 3.0 %collective-permute-done.refs_0_ = bf16[48,16384]{1,0:T(8,128)(2,1)} collective-permute-done((bf16[48,16384]{1,0:T(8,128)(2,1)}, bf16[48,16384]{1,0:T(8,128)(2,1)}, u32[]{:S(2)}, u32[]{:S(2)}) %collective-permute-start) | collective-permute-done | bytes 1572896 | tf_op jit(solution)/shard_map/ppermute | solution.py:424
  30.2 2.4 %collective-permute-start.4 = (bf16[48,16384]{1,0:T(8,128)(2,1)}, bf16[48,16384]{1,0:T(8,128)(2,1)}, u32[]{:S(2)}, u32[]{:S(2)}) collective-permute-start(bf16[48,16384]{1,0:T(8,128)(2,1)} %collective-permute-done.refs_0_), channel_id=1, source_target_pairs={{0,4},{1,3},{4,8},{5,1},{8,12},{9,5},{12,14},{13,9},{14,10},{15,13... | collective-permute-start | bytes 4718600 | tf_op jit(solution)/shard_map/ppermute | solution.py:424
  32.7 9.9 %collective-permute-done.6.refs_0_ = bf16[48,16384]{1,0:T(8,128)(2,1)} collective-permute-done((bf16[48,16384]{1,0:T(8,128)(2,1)}, bf16[48,16384]{1,0:T(8,128)(2,1)}, u32[]{:S(2)}, u32[]{:S(2)}) %collective-permute-start.6) | collective-permute-done | bytes 1572896 | tf_op jit(solution)/shard_map/ppermute | solution.py:424
  42.6 1.7 %collective-permute-start.10 = (bf16[48,16384]{1,0:T(8,128)(2,1)}, bf16[48,16384]{1,0:T(8,128)(2,1)}, u32[]{:S(2)}, u32[]{:S(2)}) collective-permute-start(bf16[48,16384]{1,0:T(8,128)(2,1)} %collective-permute-done.6.refs_0_), channel_id=1, source_target_pairs={{0,2},{1,5},{4,0},{5,9},{8,4},{9,13},{12,8},{13,15},{14,12},{15,11... | collective-permute-start | bytes 4718600 | tf_op jit(solution)/shard_map/ppermute | solution.py:424
  48.7 12.6 %blocks.9 = (f32[16,48,1024]{2,1,0:T(8,128)S(1)}, f32[48,128]{1,0:T(8,128)S(1)}) custom-call(bf16[48,16384]{1,0:T(8,128)(2,1)} %collective-permute-done.refs_0_, bf16[48,16384]{1,0:T(8,128)(2,1)} %collective-permute-done.3.refs_1_, bf16[16384,1024]{1,0:T(8,128)(2,1)} %refs_4_.7, bf16[64,16384]{1,0:T(8,128)(2,1)S(1)} %bitcast.16, ...), custom_call_target="tpu_custom_call", output_to_operand_aliasing={{0}: (5, {})} | custom-call | flops 3221225472 | bytes 33554432 | tf_op jit(solution)/shard_map/blocks/pallas_call | solution.py:265
  67.3 8.0 %collective-permute-done.10.refs_0_ = bf16[48,16384]{1,0:T(8,128)(2,1)} collective-permute-done((bf16[48,16384]{1,0:T(8,128)(2,1)}, bf16[48,16384]{1,0:T(8,128)(2,1)}, u32[]{:S(2)}, u32[]{:S(2)}) %collective-permute-start.10) | collective-permute-done | bytes 1572896 | tf_op jit(solution)/shard_map/ppermute | solution.py:424
  75.3 1.8 %collective-permute-start.13 = (bf16[48,16384]{1,0:T(8,128)(2,1)}, bf16[48,16384]{1,0:T(8,128)(2,1)S(1)}, u32[]{:S(2)}, u32[]{:S(2)}) collective-permute-start(bf16[48,16384]{1,0:T(8,128)(2,1)} %collective-permute-done.10.refs_0_), channel_id=1, source_target_pairs={{0,2},{1,5},{4,0},{5,9},{8,4},{9,13},{12,8},{13,15},{14,12},{15,11... | collective-permute-start | bytes 4718600 | tf_op jit(solution)/shard_map/ppermute | solution.py:424
  79.8 13.8 %blocks.10 = (f32[16,48,1024]{2,1,0:T(8,128)S(1)}, f32[96,128]{1,0:T(8,128)S(1)}) custom-call(bf16[48,16384]{1,0:T(8,128)(2,1)} %collective-permute-done.6.refs_0_, bf16[48,16384]{1,0:T(8,128)(2,1)} %collective-permute-done.7.refs_1_, bf16[48,16384]{1,0:T(8,128)(2,1)} %collective-permute-done.4.refs_2_, ...), custom_call_target="tpu_custom_call", output_to_operand_aliasing={{0}: (7, {})} | custom-call | flops 6442450944 | bytes 33554432 | tf_op jit(solution)/shard_map/blocks/pallas_call | solution.py:265
  93.6 5.9 %collective-permute-done.5.refs_2_ = bf16[48,16384]{1,0:T(8,128)(2,1)S(1)} collective-permute-done((bf16[48,16384]{1,0:T(8,128)(2,1)}, bf16[48,16384]{1,0:T(8,128)(2,1)S(1)}, u32[]{:S(2)}, u32[]{:S(2)}) %collective-permute-start.5) | collective-permute-done | bytes 1572896 | tf_op jit(solution)/shard_map/ppermute | solution.py:424
  99.5 2.4 %collective-permute-start.9 = (bf16[48,16384]{1,0:T(8,128)(2,1)S(1)}, bf16[48,16384]{1,0:T(8,128)(2,1)S(1)}, u32[]{:S(2)}, u32[]{:S(2)}) collective-permute-start(bf16[48,16384]{1,0:T(8,128)(2,1)S(1)} %collective-permute-done.5.refs_2_), channel_id=1, source_target_pairs={{0,4},{1,3},{4,8},{5,1},{8,12},{9,5},{12,14},{13,9},{14,10},{15,13... | collective-permute-start | bytes 4718600 | tf_op jit(solution)/shard_map/ppermute | solution.py:424
  101.8 6.5 %collective-permute-done.13.x_ref.refs_0_ = bf16[48,16384]{1,0:T(8,128)(2,1)S(1)} collective-permute-done((bf16[48,16384]{1,0:T(8,128)(2,1)}, bf16[48,16384]{1,0:T(8,128)(2,1)S(1)}, u32[]{:S(2)}, u32[]{:S(2)}) %collective-permute-start.13) | collective-permute-done | bytes 1572896 | tf_op jit(solution)/shard_map/ppermute | solution.py:424
  110.8 14.0 %blocks.11 = (f32[16,48,1024]{2,1,0:T(8,128)S(1)}, f32[96,128]{1,0:T(8,128)S(1)}) custom-call(bf16[48,16384]{1,0:T(8,128)(2,1)} %collective-permute-done.10.refs_0_, bf16[48,16384]{1,0:T(8,128)(2,1)S(1)} %collective-permute-done.11.refs_1_, bf16[48,16384]{1,0:T(8,128)(2,1)S(1)} %collective-permute-done.5.refs_2_, ...), custom_call_target="tpu_custom_call", output_to_operand_aliasing={{0}: (7, {})} | custom-call | flops 6442450944 | bytes 33554432 | tf_op jit(solution)/shard_map/blocks/pallas_call | solution.py:265
  124.9 2.0 %ranks.1 = bf16[192,128]{1,0:T(8,128)(2,1)S(1)} custom-call(s32[16]{0:T(128)S(1)} %get-tuple-element.63.owners_ref, s32[8]{0:T(128)S(1)} %pad_add_fusion.slot_ref, bf16[48,16384]{1,0:T(8,128)(2,1)S(1)} %collective-permute-done.9.x_ref.refs_2_, bf16[64,16384]{1,0:T(8,128)(2,1)S(1)} %bitcast.20, bf16[64,16384]{1,0:T(8,128)(2,1)S(1)} %copy-done.8, ...), custom_call_target="tpu_custom_call" | custom-call | tf_op jit(solution)/shard_map/ranks/pallas_call | solution.py:342
  126.9 2.0 %collective-permute-start.14 = (bf16[192,128]{1,0:T(8,128)(2,1)S(1)}, bf16[192,128]{1,0:T(8,128)(2,1)S(1)}, u32[]{:S(2)}, u32[]{:S(2)}) collective-permute-start(bf16[192,128]{1,0:T(8,128)(2,1)S(1)} %ranks.1), channel_id=1, source_target_pairs={{0,2},{1,3},{2,0},{3,1},{4,6},{5,7},{6,4},{7,5},{8,10},{9,11},{10,... | collective-permute-start | bytes 147464 | tf_op jit(solution)/shard_map/ppermute | solution.py:424
  130.6 7.1 %blocks.12.refs_5_ = f32[16,48,1024]{2,1,0:T(8,128)S(1)} custom-call(bf16[48,16384]{1,0:T(8,128)(2,1)S(1)} %collective-permute-done.13.x_ref.refs_0_, bf16[48,16384]{1,0:T(8,128)(2,1)S(1)} %collective-permute-done.17.refs_1_, bf16[48,16384]{1,0:T(8,128)(2,1)S(1)} %collective-permute-done.9.x_ref.refs_2_, ...), custom_call_target="tpu_custom_call", output_to_operand_aliasing={{}: (5, {})} | custom-call | flops 3221225472 | bytes 16777216 | tf_op jit(solution)/shard_map/blocks/pallas_call | solution.py:265
  137.8 3.0 %collective-permute-start.19 = (bf16[192,128]{1,0:T(8,128)(2,1)S(1)}, bf16[192,128]{1,0:T(8,128)(2,1)S(1)}, u32[]{:S(2)}, u32[]{:S(2)}) collective-permute-start(bf16[192,128]{1,0:T(8,128)(2,1)S(1)} %add_add_fusion), channel_id=1, source_target_pairs={{0,8},{1,9},{2,10},{3,11},{4,12},{5,13},{6,14},{7,15},{8,0},{9,1},... | collective-permute-start | bytes 147464 | tf_op jit(solution)/shard_map/ppermute | solution.py:424
  141.0 7.4 %blocks.13.refs_0_.refs_1_.refs_2_.refs_3_.refs_4_.refs_5_.refs_6_.refs_7_ = f32[16,48,1024]{2,1,0:T(8,128)S(1)} custom-call(bf16[48,16384]{1,0:T(8,128)(2,1)S(1)} %collective-permute-done.13.x_ref.refs_0_, bf16[48,16384]{1,0:T(8,128)(2,1)S(1)} %collective-permute-done.17.refs_1_, ...), custom_call_target="tpu_custom_call", output_to_operand_aliasing={{}: (5, {})} | custom-call | flops 3221225472 | bytes 16777216 | tf_op jit(solution)/shard_map/blocks/pallas_call | solution.py:265
  148.5 3.0 %finish.1 = bf16[768,1024]{1,0:T(8,128)(2,1)} custom-call(s32[16]{0:T(128)S(1)} %get-tuple-element.60.places_ref, s32[6]{0:T(128)S(1)} %gather_fusion, s32[1]{0:T(128)} %bitcast.7.core_ref, f32[16,48,1024]{2,1,0:T(8,128)S(1)} %blocks.13.refs_0_.refs_1_.refs_2_.refs_3_.refs_4_.refs_5_.refs_6_.refs_7_, ...), custom_call_target="tpu_custom_call" | custom-call | tf_op jit(solution)/shard_map/finish/pallas_call | solution.py:396
  (70 shorter events, 18.0 us)
Async XLA Ops:
  0.0 62.3 %copy-start = (s32[16]{0:T(128)S(1)}, s32[16]{0:T(128)}, u32[]{:S(2)}) copy-start(s32[16]{0:T(128)} %param.16) | copy-start | bytes 196
  0.0 23.7 %collective-permute-start.1 = (bf16[64,16384]{1,0:T(8,128)(2,1)}, bf16[64,16384]{1,0:T(8,128)(2,1)S(1)}, u32[]{:S(2)}, u32[]{:S(2)}) collective-permute-start(bf16[64,16384]{1,0:T(8,128)(2,1)} %bitcast.14), channel_id=1, source_target_pairs={{0,1},{1,0},{2,3},{3,2},{4,5},{5,4},{6,7},{7,6},{8,9},{9,8},{10,11... | collective-permute-start | bytes 6291464 | tf_op jit(solution)/shard_map/ppermute | solution.py:424
  0.5 6.2 %collective-permute-start.2 = (bf16[48,16384]{1,0:T(8,128)(2,1)}, bf16[48,16384]{1,0:T(8,128)(2,1)S(1)}, u32[]{:S(2)}, u32[]{:S(2)}) collective-permute-start(bf16[48,16384]{1,0:T(8,128)(2,1)} %refs_0_.3), channel_id=1, source_target_pairs={{0,1},{1,0},{2,3},{3,2},{4,5},{5,4},{6,7},{7,6},{8,9},{9,8},{10,11... | collective-permute-start | bytes 4718600 | tf_op jit(solution)/shard_map/ppermute | solution.py:424
  0.5 29.7 %collective-permute-start = (bf16[48,16384]{1,0:T(8,128)(2,1)}, bf16[48,16384]{1,0:T(8,128)(2,1)}, u32[]{:S(2)}, u32[]{:S(2)}) collective-permute-start(bf16[48,16384]{1,0:T(8,128)(2,1)} %refs_0_.3), channel_id=1, source_target_pairs={{0,4},{1,3},{4,8},{5,1},{8,12},{9,5},{12,14},{13,9},{14,10},{15,13... | collective-permute-start | bytes 4718600 | tf_op jit(solution)/shard_map/ppermute | solution.py:424
  9.8 32.7 %collective-permute-start.6 = (bf16[48,16384]{1,0:T(8,128)(2,1)}, bf16[48,16384]{1,0:T(8,128)(2,1)}, u32[]{:S(2)}, u32[]{:S(2)}) collective-permute-start(bf16[48,16384]{1,0:T(8,128)(2,1)} %refs_0_.3), channel_id=1, source_target_pairs={{0,2},{1,5},{4,0},{5,9},{8,4},{9,13},{12,8},{13,15},{14,12},{15,11... | collective-permute-start | bytes 4718600 | tf_op jit(solution)/shard_map/ppermute | solution.py:424
  30.2 15.2 %collective-permute-start.3 = (bf16[48,16384]{1,0:T(8,128)(2,1)}, bf16[48,16384]{1,0:T(8,128)(2,1)}, u32[]{:S(2)}, u32[]{:S(2)}) collective-permute-start(bf16[48,16384]{1,0:T(8,128)(2,1)} %collective-permute-done.refs_0_), channel_id=1, source_target_pairs={{0,1},{1,0},{2,3},{3,2},{4,5},{5,4},{6,7},{7,6},{8,9},{9,8},{10,11... | collective-permute-start | bytes 4718600 | tf_op jit(solution)/shard_map/ppermute | solution.py:424
  30.2 31.1 %copy-start.11 = (s32[8]{0:T(128)S(1)}, s32[8]{0:T(128)}, u32[]{:S(2)}) copy-start(s32[8]{0:T(128)} %param.17) | copy-start | bytes 100
  30.2 35.3 %collective-permute-start.4 = (bf16[48,16384]{1,0:T(8,128)(2,1)}, bf16[48,16384]{1,0:T(8,128)(2,1)}, u32[]{:S(2)}, u32[]{:S(2)}) collective-permute-start(bf16[48,16384]{1,0:T(8,128)(2,1)} %collective-permute-done.refs_0_), channel_id=1, source_target_pairs={{0,4},{1,3},{4,8},{5,1},{8,12},{9,5},{12,14},{13,9},{14,10},{15,13... | collective-permute-start | bytes 4718600 | tf_op jit(solution)/shard_map/ppermute | solution.py:424
  42.6 32.7 %collective-permute-start.10 = (bf16[48,16384]{1,0:T(8,128)(2,1)}, bf16[48,16384]{1,0:T(8,128)(2,1)}, u32[]{:S(2)}, u32[]{:S(2)}) collective-permute-start(bf16[48,16384]{1,0:T(8,128)(2,1)} %collective-permute-done.6.refs_0_), channel_id=1, source_target_pairs={{0,2},{1,5},{4,0},{5,9},{8,4},{9,13},{12,8},{13,15},{14,12},{15,11... | collective-permute-start | bytes 4718600 | tf_op jit(solution)/shard_map/ppermute | solution.py:424
  44.2 33.9 %collective-permute-start.7 = (bf16[48,16384]{1,0:T(8,128)(2,1)}, bf16[48,16384]{1,0:T(8,128)(2,1)}, u32[]{:S(2)}, u32[]{:S(2)}) collective-permute-start(bf16[48,16384]{1,0:T(8,128)(2,1)} %collective-permute-done.6.refs_0_), channel_id=1, source_target_pairs={{0,1},{1,0},{2,3},{3,2},{4,5},{5,4},{6,7},{7,6},{8,9},{9,8},{10,11... | collective-permute-start | bytes 4718600 | tf_op jit(solution)/shard_map/ppermute | solution.py:424
  65.6 12.6 %collective-permute-start.8 = (bf16[48,16384]{1,0:T(8,128)(2,1)}, bf16[48,16384]{1,0:T(8,128)(2,1)S(1)}, u32[]{:S(2)}, u32[]{:S(2)}) collective-permute-start(bf16[48,16384]{1,0:T(8,128)(2,1)} %collective-permute-done.4.refs_2_), channel_id=1, source_target_pairs={{0,1},{1,0},{2,3},{3,2},{4,5},{5,4},{6,7},{7,6},{8,9},{9,8},{10,11... | collective-permute-start | bytes 4718600 | tf_op jit(solution)/shard_map/ppermute | solution.py:424
  65.6 33.8 %collective-permute-start.5 = (bf16[48,16384]{1,0:T(8,128)(2,1)}, bf16[48,16384]{1,0:T(8,128)(2,1)S(1)}, u32[]{:S(2)}, u32[]{:S(2)}) collective-permute-start(bf16[48,16384]{1,0:T(8,128)(2,1)} %collective-permute-done.4.refs_2_), channel_id=1, source_target_pairs={{0,4},{1,3},{4,8},{5,1},{8,12},{9,5},{12,14},{13,9},{14,10},{15,13... | collective-permute-start | bytes 4718600 | tf_op jit(solution)/shard_map/ppermute | solution.py:424
  75.3 33.1 %collective-permute-start.13 = (bf16[48,16384]{1,0:T(8,128)(2,1)}, bf16[48,16384]{1,0:T(8,128)(2,1)S(1)}, u32[]{:S(2)}, u32[]{:S(2)}) collective-permute-start(bf16[48,16384]{1,0:T(8,128)(2,1)} %collective-permute-done.10.refs_0_), channel_id=1, source_target_pairs={{0,2},{1,5},{4,0},{5,9},{8,4},{9,13},{12,8},{13,15},{14,12},{15,11... | collective-permute-start | bytes 4718600 | tf_op jit(solution)/shard_map/ppermute | solution.py:424
  77.1 33.7 %collective-permute-start.11 = (bf16[48,16384]{1,0:T(8,128)(2,1)}, bf16[48,16384]{1,0:T(8,128)(2,1)S(1)}, u32[]{:S(2)}, u32[]{:S(2)}) collective-permute-start(bf16[48,16384]{1,0:T(8,128)(2,1)} %collective-permute-done.10.refs_0_), channel_id=1, source_target_pairs={{0,1},{1,0},{2,3},{3,2},{4,5},{5,4},{6,7},{7,6},{8,9},{9,8},{10,11... | collective-permute-start | bytes 4718600 | tf_op jit(solution)/shard_map/ppermute | solution.py:424
  99.5 11.3 %collective-permute-start.12 = (bf16[48,16384]{1,0:T(8,128)(2,1)S(1)}, bf16[48,16384]{1,0:T(8,128)(2,1)S(1)}, u32[]{:S(2)}, u32[]{:S(2)}) collective-permute-start(bf16[48,16384]{1,0:T(8,128)(2,1)S(1)} %collective-permute-done.5.refs_2_), channel_id=1, source_target_pairs={{0,1},{1,0},{2,3},{3,2},{4,5},{5,4},{6,7},{7,6},{8,9},{9,8},{10,11... | collective-permute-start | bytes 4718600 | tf_op jit(solution)/shard_map/ppermute | solution.py:424
  99.5 25.4 %collective-permute-start.9 = (bf16[48,16384]{1,0:T(8,128)(2,1)S(1)}, bf16[48,16384]{1,0:T(8,128)(2,1)S(1)}, u32[]{:S(2)}, u32[]{:S(2)}) collective-permute-start(bf16[48,16384]{1,0:T(8,128)(2,1)S(1)} %collective-permute-done.5.refs_2_), channel_id=1, source_target_pairs={{0,4},{1,3},{4,8},{5,1},{8,12},{9,5},{12,14},{13,9},{14,10},{15,13... | collective-permute-start | bytes 4718600 | tf_op jit(solution)/shard_map/ppermute | solution.py:424
  108.3 22.2 %collective-permute-start.17 = (bf16[48,16384]{1,0:T(8,128)(2,1)S(1)}, bf16[48,16384]{1,0:T(8,128)(2,1)S(1)}, u32[]{:S(2)}, u32[]{:S(2)}) collective-permute-start(bf16[48,16384]{1,0:T(8,128)(2,1)S(1)} %collective-permute-done.13.x_ref.refs_0_), channel_id=1, source_target_pairs={{0,1},{1,0},{2,3},{3,2},{4,5},{5,4},{6,7},{7,6},{8,9},{9,8},{10,11... | collective-permute-start | bytes 4718600 | tf_op jit(solution)/shard_map/ppermute | solution.py:424
  124.8 5.7 %collective-permute-start.18 = (bf16[48,16384]{1,0:T(8,128)(2,1)S(1)}, bf16[48,16384]{1,0:T(8,128)(2,1)S(1)}, u32[]{:S(2)}, u32[]{:S(2)}) collective-permute-start(bf16[48,16384]{1,0:T(8,128)(2,1)S(1)} %collective-permute-done.9.x_ref.refs_2_), channel_id=1, source_target_pairs={{0,1},{1,0},{2,3},{3,2},{4,5},{5,4},{6,7},{7,6},{8,9},{9,8},{10,11... | collective-permute-start | bytes 4718600 | tf_op jit(solution)/shard_map/ppermute | solution.py:424
  126.9 10.8 %collective-permute-start.14 = (bf16[192,128]{1,0:T(8,128)(2,1)S(1)}, bf16[192,128]{1,0:T(8,128)(2,1)S(1)}, u32[]{:S(2)}, u32[]{:S(2)}) collective-permute-start(bf16[192,128]{1,0:T(8,128)(2,1)S(1)} %ranks.1), channel_id=1, source_target_pairs={{0,2},{1,3},{2,0},{3,1},{4,6},{5,7},{6,4},{7,5},{8,10},{9,11},{10,... | collective-permute-start | bytes 147464 | tf_op jit(solution)/shard_map/ppermute | solution.py:424
  129.0 8.7 %collective-permute-start.15 = (bf16[192,128]{1,0:T(8,128)(2,1)S(1)}, bf16[192,128]{1,0:T(8,128)(2,1)S(1)}, u32[]{:S(2)}, u32[]{:S(2)}) collective-permute-start(bf16[192,128]{1,0:T(8,128)(2,1)S(1)} %ranks.1), channel_id=1, source_target_pairs={{0,4},{1,5},{2,6},{3,7},{4,0},{5,1},{6,2},{7,3},{8,12},{9,13},{10,... | collective-permute-start | bytes 147464 | tf_op jit(solution)/shard_map/ppermute | solution.py:424
  130.5 7.2 %collective-permute-start.16 = (bf16[192,128]{1,0:T(8,128)(2,1)S(1)}, bf16[192,128]{1,0:T(8,128)(2,1)S(1)}, u32[]{:S(2)}, u32[]{:S(2)}) collective-permute-start(bf16[192,128]{1,0:T(8,128)(2,1)S(1)} %ranks.1), channel_id=1, source_target_pairs={{0,6},{1,7},{2,4},{3,5},{4,2},{5,3},{6,0},{7,1},{8,14},{9,15},{10,... | collective-permute-start | bytes 147464 | tf_op jit(solution)/shard_map/ppermute | solution.py:424
  137.8 10.6 %collective-permute-start.19 = (bf16[192,128]{1,0:T(8,128)(2,1)S(1)}, bf16[192,128]{1,0:T(8,128)(2,1)S(1)}, u32[]{:S(2)}, u32[]{:S(2)}) collective-permute-start(bf16[192,128]{1,0:T(8,128)(2,1)S(1)} %add_add_fusion), channel_id=1, source_target_pairs={{0,8},{1,9},{2,10},{3,11},{4,12},{5,13},{6,14},{7,15},{8,0},{9,1},... | collective-permute-start | bytes 147464 | tf_op jit(solution)/shard_map/ppermute | solution.py:424
  140.8 7.6 %collective-permute-start.20 = (bf16[192,128]{1,0:T(8,128)(2,1)S(1)}, bf16[192,128]{1,0:T(8,128)(2,1)S(1)}, u32[]{:S(2)}, u32[]{:S(2)}) collective-permute-start(bf16[192,128]{1,0:T(8,128)(2,1)S(1)} %add_add_fusion), channel_id=1, source_target_pairs={{0,1},{1,0},{2,3},{3,2},{4,5},{5,4},{6,7},{7,6},{8,9},{9,8},{10,11... | collective-permute-start | bytes 147464 | tf_op jit(solution)/shard_map/ppermute | solution.py:424
  140.8 7.6 %collective-permute-start.21 = (bf16[192,128]{1,0:T(8,128)(2,1)S(1)}, bf16[192,128]{1,0:T(8,128)(2,1)S(1)}, u32[]{:S(2)}, u32[]{:S(2)}) collective-permute-start(bf16[192,128]{1,0:T(8,128)(2,1)S(1)} %add_add_fusion), channel_id=1, source_target_pairs={{0,9},{1,8},{2,11},{3,10},{4,13},{5,12},{6,15},{7,14},{8,1},{9,0},... | collective-permute-start | bytes 147464 | tf_op jit(solution)/shard_map/ppermute | solution.py:424
  (10 other events, 87.4 us)

commit v10 on v9

--- a/solution.py
+++ b/solution.py
@@ -292,32 +292,31 @@
     return (2 * len(SNAKE), rows, cols)
 
 
-def both_ranks(x, factors):
-    return jnp.concatenate([lax.dot_general(x, s, NT, preferred_element_type=F32) for s in factors], 1)
-
-
-def some_ranks_kernel(x_ref, sa_ref, sb_ref, out_ref):
-    out_ref[...] = both_ranks(x_ref[...], (sa_ref[...], sb_ref[...]))
-
-
-def some_ranks(x, factors):
+def some_ranks_kernel(x_ref, s_ref, out_ref):
+    out_ref[...] = lax.dot_general(x_ref[...], s_ref[...], NT, preferred_element_type=F32)
+
+
+def some_ranks(x, factor):
     whole = lambda shape: pl.BlockSpec(shape, lambda _: (0, 0))
-    shape = (x.shape[0], 2 * factors[0].shape[0])
+    shape = (x.shape[0], factor.shape[0])
     return pl.pallas_call(
         some_ranks_kernel,
         grid=(1,),
-        in_specs=[whole(value.shape) for value in (x, *factors)],
+        in_specs=[whole(x.shape), whole(factor.shape)],
         out_specs=whole(shape),
         out_shape=jax.ShapeDtypeStruct(shape, F32),
         compiler_params=PARAMS,
         name="some_ranks",
-    )(x, *factors)
-
-
-def rank_kernel(owners_ref, slot_ref, x_ref, sa_ref, sb_ref, *refs):
-    h_refs, out_ref, placed = refs[:-2], refs[-2], refs[-1]
-    rows, rank = x_ref.shape[0], sa_ref.shape[0]
-    last = both_ranks(x_ref[...], (sa_ref[...], sb_ref[...]))
+    )(x, factor)
+
+
+def rank_kernel(count, owners_ref, slot_ref, *refs):
+    xs, refs = refs[:count], refs[count:]
+    sa_ref, sb_ref, h_refs, out_ref, placed = refs[0], refs[1], refs[2:-2], refs[-2], refs[-1]
+    rows, rank = xs[0].shape[0], sa_ref.shape[0]
+    x = jnp.concatenate([ref[...] for ref in xs], 0)
+    last = [lax.dot_general(x, ref[...], NT, preferred_element_type=F32) for ref in (sa_ref, sb_ref)]
+    last = jnp.concatenate(last, 1)
     segments = slot_ref.shape[0] - 2
     block = 0
     for source in h_refs + (last,):
@@ -335,23 +334,23 @@
     out_ref[...] = jnp.concatenate([placed[:half, :], placed[half:, :]], 1).astype(out_ref.dtype)
 
 
-def rank_terms(owners, slots, x, factors, hs):
+def rank_terms(owners, slots, xs, factors, hs):
     rank = factors[0].shape[0]
-    core_rows = owners.shape[0] // 2 * x.shape[0]
+    core_rows = owners.shape[0] // 2 * xs[0].shape[0]
     whole = lambda shape: pl.BlockSpec(shape, lambda _, *rest: (0, 0))
     return pl.pallas_call(
-        rank_kernel,
+        functools.partial(rank_kernel, len(xs)),
         grid_spec=pltpu.PrefetchScalarGridSpec(
             num_scalar_prefetch=2,
             grid=(1,),
-            in_specs=[whole(value.shape) for value in (x, *factors, *hs)],
+            in_specs=[whole(value.shape) for value in (*xs, *factors, *hs)],
             out_specs=whole((core_rows // 2, 2 * rank)),
             scratch_shapes=[pltpu.VMEM((core_rows, rank), F32)],
         ),
         out_shape=jax.ShapeDtypeStruct((core_rows // 2, 2 * rank), BF16),
         compiler_params=PARAMS,
         name="ranks",
-    )(owners, slots, x, *factors, *hs)
+    )(owners, slots, *xs, *factors, *hs)
 
 
 def block_finish_kernel(blocks, segments, places_ref, slot_ref, core_ref, *refs):
@@ -435,13 +434,13 @@
         return total
 
     streams = [send(tokens, out), None]
-    own, part = [tokens, swap(tokens)], 2 * tile
-    factors = [shrinks[0], swap(shrinks[0])]
-    total, _ = block_product(own, weights, factors, 0, part, tile, None, 0, False)
-    second, total = lax.optimization_barrier((tokens, total))
+    own, factors = [tokens, swap(tokens)], [shrinks[0], swap(shrinks[0])]
+    mine = some_ranks(tokens, factors[0])
+    second, mine = lax.optimization_barrier((tokens, mine))
     streams[1] = send(second, home)
-    total, _ = block_product(own, weights, factors, part, depth, tile, total, 0, False)
-    hs, total = lax.optimization_barrier(([some_ranks(tokens, factors)], total))
+    total, _ = block_product(own, weights, factors, 0, depth, tile, None, 0, False)
+    mine = jnp.concatenate([mine, some_ranks(tokens, factors[1])], 1)
+    hs, total = lax.optimization_barrier(([mine], total))
     counts.append(len(own))
 
     def make_tables(me, indices):
@@ -460,8 +459,6 @@
             streams[hop % 2] = send(arrived, home if hop % 2 else out)
         if hop % 2:
             late = [arrived, swap(arrived)]
-            if hop == hops - 2:
-                early = some_ranks(arrived, factors)
             total = multiply(blocks, total)
             blocks = late
         else:
@@ -469,11 +466,10 @@
         if hop == 1:
             known, total = lax.optimization_barrier(((me, indices), total))
             tables, total = lax.optimization_barrier((make_tables(*known), total))
-        totals.append((total, early) if hop == hops - 2 else total)
+        totals.append(total)
     held = sum(counts)
-    hs.append(early)
     owners, places, slots, core, segment_slot, cosine, sine = tables
-    h = rank_terms(owners, slots, blocks[2], factors, hs)
+    h = rank_terms(owners, slots, blocks[::2], factors, hs)
     beside = lambda step: send(h, [(i, i ^ step) for i in range(parts)])
 
     def last_product(low, high, total):

time: 152 us -> 157 us (1.033)
  waiting for transfers between devices: 36.5 us -> 46.4 us
  starting transfers between devices: 26.9 us -> 21.5 us
  local copies, waits for them, and re-layouts: 6.94 us -> 8.52 us
    ppermute x22, waiting for transfers between devices: 36.5 us -> 46.4 us  [ring_plan(): send = lambda value, pairs: lax.ppermute(value, 'tensor', pairs)]
    ppermute x22, starting transfers between devices: 26.9 us -> 21.5 us  [ring_plan(): send = lambda value, pairs: lax.ppermute(value, 'tensor', pairs)]
    pallas_call x7 -> x6, Pallas kernels: 69 us -> 66.9 us  [block_product(): pl.pallas_call(functools.partial(block_kernel, count, low, tile, steps, f...]
    unnamed x24, local copies, waits for them, and re-layouts: 4.81 us -> 6.4 us
  transfers between devices with their start and end apart: 22 -> 22, of which waited for: 6 -> 6; matrix products, arithmetic and copies ran while one was open for 3% -> 3% of each run, Pallas kernels for 50% -> 48%
where the time goes in v10:
time: 157 us; the launch traced here: 156 us
  Pallas kernels  77.4 us (49%)
  waiting for transfers between devices  46.4 us (30%)
  starting transfers between devices  21.5 us (14%)
  local copies, waits for them, and re-layouts  8.52 us (5%)
  other arithmetic  2.22 us (1%)
    pallas_call x6, Pallas kernels, block_product(): pl.pallas_call(functools.partial(block_kernel, count, low, tile, steps, f...  66.9 us
    ppermute x22, waiting for transfers between devices, ring_plan(): send = lambda value, pairs: lax.ppermute(value, 'tensor', pairs)  46.4 us
    ppermute x22, starting transfers between devices, ring_plan(): send = lambda value, pairs: lax.ppermute(value, 'tensor', pairs)  21.5 us
    unnamed x24, local copies, waits for them, and re-layouts  6.4 us
    pallas_call x2, Pallas kernels, some_ranks(): pl.pallas_call(some_ranks_kernel, grid=(1,), in_specs=[whole(x.shape), wh...  4.93 us
  transfers between devices with their start and end apart: 22, of which 6 were waited for; matrix products, arithmetic and copies ran while one was open for 3% of the time, Pallas kernels for 48%

profile of v10, /device:TPU:0, one launch (start us, length us, event | category | flops | bytes accessed | tf_op | source)
XLA Modules:
  0.0 156.3 jit_solution(13277976934745054803)
XLA Ops:
  0.5 3.0 %collective-permute-start = (bf16[48,16384]{1,0:T(8,128)(2,1)}, bf16[48,16384]{1,0:T(8,128)(2,1)}, u32[]{:S(2)}, u32[]{:S(2)}) collective-permute-start(bf16[48,16384]{1,0:T(8,128)(2,1)} %refs_0_.1), channel_id=1, source_target_pairs={{0,4},{1,3},{4,8},{5,1},{8,12},{9,5},{12,14},{13,9},{14,10},{15,13... | collective-permute-start | bytes 4718600 | tf_op jit(solution)/shard_map/ppermute | solution.py:423
  3.5 1.6 %copy-done.2 = bf16[1,16384,64]{1,2,0:T(8,128)(2,1)S(1)} copy-done((bf16[1,16384,64]{1,2,0:T(8,128)(2,1)S(1)}, bf16[1,16384,64]{1,2,0:T(8,128)(2,1)}, u32[]{:S(2)}) %copy-start.2) | copy-done | bytes 2097176
  5.1 2.1 %some_ranks.2 = f32[48,64]{1,0:T(8,128)S(1)} custom-call(bf16[48,16384]{1,0:T(8,128)(2,1)} %refs_0_.1, bf16[64,16384]{1,0:T(8,128)(2,1)S(1)} %bitcast.15), custom_call_target="tpu_custom_call" | custom-call | tf_op jit(solution)/shard_map/some_ranks/pallas_call | solution.py:302
  7.3 12.1 %blocks.6.refs_5_ = f32[16,48,1024]{2,1,0:T(8,128)S(1)} custom-call(bf16[48,16384]{1,0:T(8,128)(2,1)} %refs_0_.1, bf16[48,16384]{1,0:T(8,128)(2,1)S(1)} %collective-permute-done.2.refs_1_, bf16[16384,1024]{1,0:T(8,128)(2,1)} %refs_4_.7), custom_call_target="tpu_custom_call" | custom-call | flops 3221225472 | bytes 33554432 | tf_op jit(solution)/shard_map/blocks/pallas_call | solution.py:265
  19.5 2.8 %some_ranks.3 = f32[48,64]{1,0:T(8,128)S(1)} custom-call(bf16[48,16384]{1,0:T(8,128)(2,1)} %refs_0_.1, bf16[64,16384]{1,0:T(8,128)(2,1)S(1)} %collective-permute-done.1.s_ref.refs_4_.refs_6_.refs_3_), custom_call_target="tpu_custom_call" | custom-call | tf_op jit(solution)/shard_map/some_ranks/pallas_call | solution.py:302
  22.4 13.3 %collective-permute-done.refs_0_ = bf16[48,16384]{1,0:T(8,128)(2,1)} collective-permute-done((bf16[48,16384]{1,0:T(8,128)(2,1)}, bf16[48,16384]{1,0:T(8,128)(2,1)}, u32[]{:S(2)}, u32[]{:S(2)}) %collective-permute-start) | collective-permute-done | bytes 1572896 | tf_op jit(solution)/shard_map/ppermute | solution.py:423
  35.8 2.5 %collective-permute-start.8 = (bf16[48,16384]{1,0:T(8,128)(2,1)}, bf16[48,16384]{1,0:T(8,128)(2,1)}, u32[]{:S(2)}, u32[]{:S(2)}) collective-permute-start(bf16[48,16384]{1,0:T(8,128)(2,1)} %collective-permute-done.refs_0_), channel_id=1, source_target_pairs={{0,4},{1,3},{4,8},{5,1},{8,12},{9,5},{12,14},{13,9},{14,10},{15,13... | collective-permute-start | bytes 4718600 | tf_op jit(solution)/shard_map/ppermute | solution.py:423
  38.5 1.7 %collective-permute-start.5 = (bf16[48,16384]{1,0:T(8,128)(2,1)}, bf16[48,16384]{1,0:T(8,128)(2,1)}, u32[]{:S(2)}, u32[]{:S(2)}) collective-permute-start(bf16[48,16384]{1,0:T(8,128)(2,1)} %collective-permute-done.4.refs_0_), channel_id=1, source_target_pairs={{0,2},{1,5},{4,0},{5,9},{8,4},{9,13},{12,8},{13,15},{14,12},{15,11... | collective-permute-start | bytes 4718600 | tf_op jit(solution)/shard_map/ppermute | solution.py:423
  40.7 1.6 %copy-done.3 = bf16[1,16384,64]{1,2,0:T(8,128)(2,1)S(1)} copy-done((bf16[1,16384,64]{1,2,0:T(8,128)(2,1)S(1)}, bf16[1,16384,64]{1,2,0:T(8,128)(2,1)}, u32[]{:S(2)}) %copy-start.3) | copy-done | bytes 2097176
  42.3 1.6 %copy-done.6 = bf16[64,16384]{1,0:T(8,128)(2,1)S(1)} copy-done((bf16[64,16384]{1,0:T(8,128)(2,1)S(1)}, bf16[64,16384]{1,0:T(8,128)(2,1)}, u32[]{:S(2)}) %copy-start.6) | copy-done | bytes 2097176
  43.9 12.6 %blocks.7 = (f32[16,48,1024]{2,1,0:T(8,128)S(1)}, f32[48,128]{1,0:T(8,128)S(1)}) custom-call(bf16[48,16384]{1,0:T(8,128)(2,1)} %collective-permute-done.refs_0_, bf16[48,16384]{1,0:T(8,128)(2,1)} %collective-permute-done.3.refs_1_, bf16[16384,1024]{1,0:T(8,128)(2,1)} %refs_4_.7, bf16[64,16384]{1,0:T(8,128)(2,1)S(1)} %bitcast.16, ...), custom_call_target="tpu_custom_call", output_to_operand_aliasing={{0}: (5, {})} | custom-call | flops 3221225472 | bytes 33554432 | tf_op jit(solution)/shard_map/blocks/pallas_call | solution.py:265
  60.8 10.9 %collective-permute-done.8.refs_2_ = bf16[48,16384]{1,0:T(8,128)(2,1)} collective-permute-done((bf16[48,16384]{1,0:T(8,128)(2,1)}, bf16[48,16384]{1,0:T(8,128)(2,1)}, u32[]{:S(2)}, u32[]{:S(2)}) %collective-permute-start.8) | collective-permute-done | bytes 1572896 | tf_op jit(solution)/shard_map/ppermute | solution.py:423
  71.6 2.5 %collective-permute-start.10 = (bf16[48,16384]{1,0:T(8,128)(2,1)}, bf16[48,16384]{1,0:T(8,128)(2,1)S(1)}, u32[]{:S(2)}, u32[]{:S(2)}) collective-permute-start(bf16[48,16384]{1,0:T(8,128)(2,1)} %collective-permute-done.8.refs_2_), channel_id=1, source_target_pairs={{0,4},{1,3},{4,8},{5,1},{8,12},{9,5},{12,14},{13,9},{14,10},{15,13... | collective-permute-start | bytes 4718600 | tf_op jit(solution)/shard_map/ppermute | solution.py:423
  77.0 13.6 %blocks.8 = (f32[16,48,1024]{2,1,0:T(8,128)S(1)}, f32[96,128]{1,0:T(8,128)S(1)}) custom-call(bf16[48,16384]{1,0:T(8,128)(2,1)} %collective-permute-done.4.refs_0_, bf16[48,16384]{1,0:T(8,128)(2,1)} %collective-permute-done.7.refs_1_, bf16[48,16384]{1,0:T(8,128)(2,1)} %collective-permute-done.8.refs_2_, ...), custom_call_target="tpu_custom_call", output_to_operand_aliasing={{0}: (7, {})} | custom-call | flops 6442450944 | bytes 33554432 | tf_op jit(solution)/shard_map/blocks/pallas_call | solution.py:265
  90.6 18.0 %collective-permute-done.10.refs_2_ = bf16[48,16384]{1,0:T(8,128)(2,1)S(1)} collective-permute-done((bf16[48,16384]{1,0:T(8,128)(2,1)}, bf16[48,16384]{1,0:T(8,128)(2,1)S(1)}, u32[]{:S(2)}, u32[]{:S(2)}) %collective-permute-start.10) | collective-permute-done | bytes 1572896 | tf_op jit(solution)/shard_map/ppermute | solution.py:423
  108.7 2.4 %collective-permute-start.11 = (bf16[48,16384]{1,0:T(8,128)(2,1)S(1)}, bf16[48,16384]{1,0:T(8,128)(2,1)S(1)}, u32[]{:S(2)}, u32[]{:S(2)}) collective-permute-start(bf16[48,16384]{1,0:T(8,128)(2,1)S(1)} %collective-permute-done.10.refs_2_), channel_id=1, source_target_pairs={{0,4},{1,3},{4,8},{5,1},{8,12},{9,5},{12,14},{13,9},{14,10},{15,13... | collective-permute-start | bytes 4718600 | tf_op jit(solution)/shard_map/ppermute | solution.py:423
  112.1 14.1 %blocks.9 = (f32[16,48,1024]{2,1,0:T(8,128)S(1)}, f32[96,128]{1,0:T(8,128)S(1)}) custom-call(bf16[48,16384]{1,0:T(8,128)(2,1)} %collective-permute-done.5.refs_0_, bf16[48,16384]{1,0:T(8,128)(2,1)S(1)} %collective-permute-done.12.refs_1_, bf16[48,16384]{1,0:T(8,128)(2,1)S(1)} %collective-permute-done.10.refs_2_, ...), custom_call_target="tpu_custom_call", output_to_operand_aliasing={{0}: (7, {})} | custom-call | flops 6442450944 | bytes 33554432 | tf_op jit(solution)/shard_map/blocks/pallas_call | solution.py:265
  126.2 2.9 %collective-permute-done.11.refs_1_.refs_2_ = bf16[48,16384]{1,0:T(8,128)(2,1)S(1)} collective-permute-done((bf16[48,16384]{1,0:T(8,128)(2,1)S(1)}, bf16[48,16384]{1,0:T(8,128)(2,1)S(1)}, u32[]{:S(2)}, u32[]{:S(2)}) %collective-permute-start.11) | collective-permute-done | bytes 1572896 | tf_op jit(solution)/shard_map/ppermute | solution.py:423
  129.2 2.5 %ranks.1 = bf16[192,128]{1,0:T(8,128)(2,1)S(1)} custom-call(s32[16]{0:T(128)S(1)} %get-tuple-element.63.owners_ref, s32[8]{0:T(128)S(1)} %pad_add_fusion.slot_ref, bf16[48,16384]{1,0:T(8,128)(2,1)S(1)} %collective-permute-done.6.refs_0_, bf16[48,16384]{1,0:T(8,128)(2,1)S(1)} %collective-permute-done.11.refs_1_.refs_2_, bf16[64,16384]{1,0:T(8,128)(2,1)S(1)} %bitcast.19, ...), custom_call_target="tpu_custom_call" | custom-call | tf_op jit(solution)/shard_map/ranks/pallas_call | solution.py:341
  131.8 2.3 %collective-permute-start.15 = (bf16[192,128]{1,0:T(8,128)(2,1)S(1)}, bf16[192,128]{1,0:T(8,128)(2,1)S(1)}, u32[]{:S(2)}, u32[]{:S(2)}) collective-permute-start(bf16[192,128]{1,0:T(8,128)(2,1)S(1)} %ranks.1), channel_id=1, source_target_pairs={{0,4},{1,5},{2,6},{3,7},{4,0},{5,1},{6,2},{7,3},{8,12},{9,13},{10,... | collective-permute-start | bytes 147464 | tf_op jit(solution)/shard_map/ppermute | solution.py:423
  135.5 7.1 %blocks.10.refs_5_ = f32[16,48,1024]{2,1,0:T(8,128)S(1)} custom-call(bf16[48,16384]{1,0:T(8,128)(2,1)S(1)} %collective-permute-done.6.refs_0_, bf16[48,16384]{1,0:T(8,128)(2,1)S(1)} %collective-permute-done.17.refs_1_, bf16[48,16384]{1,0:T(8,128)(2,1)S(1)} %collective-permute-done.11.refs_1_.refs_2_, ...), custom_call_target="tpu_custom_call", output_to_operand_aliasing={{}: (5, {})} | custom-call | flops 3221225472 | bytes 16777216 | tf_op jit(solution)/shard_map/blocks/pallas_call | solution.py:265
  142.7 2.5 %collective-permute-start.19 = (bf16[192,128]{1,0:T(8,128)(2,1)S(1)}, bf16[192,128]{1,0:T(8,128)(2,1)S(1)}, u32[]{:S(2)}, u32[]{:S(2)}) collective-permute-start(bf16[192,128]{1,0:T(8,128)(2,1)S(1)} %add_add_fusion), channel_id=1, source_target_pairs={{0,8},{1,9},{2,10},{3,11},{4,12},{5,13},{6,14},{7,15},{8,0},{9,1},... | collective-permute-start | bytes 147464 | tf_op jit(solution)/shard_map/ppermute | solution.py:423
  145.9 7.4 %blocks.11.refs_0_.refs_1_.refs_2_.refs_3_.refs_4_.refs_5_.refs_6_.refs_7_ = f32[16,48,1024]{2,1,0:T(8,128)S(1)} custom-call(bf16[48,16384]{1,0:T(8,128)(2,1)S(1)} %collective-permute-done.6.refs_0_, bf16[48,16384]{1,0:T(8,128)(2,1)S(1)} %collective-permute-done.17.refs_1_, ...), custom_call_target="tpu_custom_call", output_to_operand_aliasing={{}: (5, {})} | custom-call | flops 3221225472 | bytes 16777216 | tf_op jit(solution)/shard_map/blocks/pallas_call | solution.py:265
  153.3 3.0 %finish.1 = bf16[768,1024]{1,0:T(8,128)(2,1)} custom-call(s32[16]{0:T(128)S(1)} %get-tuple-element.60.places_ref, s32[6]{0:T(128)S(1)} %gather_fusion, s32[1]{0:T(128)} %bitcast.7.core_ref, f32[16,48,1024]{2,1,0:T(8,128)S(1)} %blocks.11.refs_0_.refs_1_.refs_2_.refs_3_.refs_4_.refs_5_.refs_6_.refs_7_, ...), custom_call_target="tpu_custom_call" | custom-call | tf_op jit(solution)/shard_map/finish/pallas_call | solution.py:395
  (70 shorter events, 11.8 us)
Async XLA Ops:
  0.0 57.5 %copy-start = (s32[16]{0:T(128)S(1)}, s32[16]{0:T(128)}, u32[]{:S(2)}) copy-start(s32[16]{0:T(128)} %param.16) | copy-start | bytes 196
  0.0 19.5 %collective-permute-start.1 = (bf16[64,16384]{1,0:T(8,128)(2,1)}, bf16[64,16384]{1,0:T(8,128)(2,1)S(1)}, u32[]{:S(2)}, u32[]{:S(2)}) collective-permute-start(bf16[64,16384]{1,0:T(8,128)(2,1)} %bitcast.14), channel_id=1, source_target_pairs={{0,1},{1,0},{2,3},{3,2},{4,5},{5,4},{6,7},{7,6},{8,9},{9,8},{10,11... | collective-permute-start | bytes 6291464 | tf_op jit(solution)/shard_map/ppermute | solution.py:423
  0.5 6.8 %collective-permute-start.2 = (bf16[48,16384]{1,0:T(8,128)(2,1)}, bf16[48,16384]{1,0:T(8,128)(2,1)S(1)}, u32[]{:S(2)}, u32[]{:S(2)}) collective-permute-start(bf16[48,16384]{1,0:T(8,128)(2,1)} %refs_0_.1), channel_id=1, source_target_pairs={{0,1},{1,0},{2,3},{3,2},{4,5},{5,4},{6,7},{7,6},{8,9},{9,8},{10,11... | collective-permute-start | bytes 4718600 | tf_op jit(solution)/shard_map/ppermute | solution.py:423
  0.5 35.2 %collective-permute-start = (bf16[48,16384]{1,0:T(8,128)(2,1)}, bf16[48,16384]{1,0:T(8,128)(2,1)}, u32[]{:S(2)}, u32[]{:S(2)}) collective-permute-start(bf16[48,16384]{1,0:T(8,128)(2,1)} %refs_0_.1), channel_id=1, source_target_pairs={{0,4},{1,3},{4,8},{5,1},{8,12},{9,5},{12,14},{13,9},{14,10},{15,13... | collective-permute-start | bytes 4718600 | tf_op jit(solution)/shard_map/ppermute | solution.py:423
  7.2 31.3 %collective-permute-start.4 = (bf16[48,16384]{1,0:T(8,128)(2,1)}, bf16[48,16384]{1,0:T(8,128)(2,1)}, u32[]{:S(2)}, u32[]{:S(2)}) collective-permute-start(bf16[48,16384]{1,0:T(8,128)(2,1)} %refs_0_.1), channel_id=1, source_target_pairs={{0,2},{1,5},{4,0},{5,9},{8,4},{9,13},{12,8},{13,15},{14,12},{15,11... | collective-permute-start | bytes 4718600 | tf_op jit(solution)/shard_map/ppermute | solution.py:423
  35.7 4.9 %collective-permute-start.3 = (bf16[48,16384]{1,0:T(8,128)(2,1)}, bf16[48,16384]{1,0:T(8,128)(2,1)}, u32[]{:S(2)}, u32[]{:S(2)}) collective-permute-start(bf16[48,16384]{1,0:T(8,128)(2,1)} %collective-permute-done.refs_0_), channel_id=1, source_target_pairs={{0,1},{1,0},{2,3},{3,2},{4,5},{5,4},{6,7},{7,6},{8,9},{9,8},{10,11... | collective-permute-start | bytes 4718600 | tf_op jit(solution)/shard_map/ppermute | solution.py:423
  35.7 20.8 %copy-start.11 = (s32[8]{0:T(128)S(1)}, s32[8]{0:T(128)}, u32[]{:S(2)}) copy-start(s32[8]{0:T(128)} %param.17) | copy-start | bytes 100
  35.8 35.9 %collective-permute-start.8 = (bf16[48,16384]{1,0:T(8,128)(2,1)}, bf16[48,16384]{1,0:T(8,128)(2,1)}, u32[]{:S(2)}, u32[]{:S(2)}) collective-permute-start(bf16[48,16384]{1,0:T(8,128)(2,1)} %collective-permute-done.refs_0_), channel_id=1, source_target_pairs={{0,4},{1,3},{4,8},{5,1},{8,12},{9,5},{12,14},{13,9},{14,10},{15,13... | collective-permute-start | bytes 4718600 | tf_op jit(solution)/shard_map/ppermute | solution.py:423
  38.5 35.6 %collective-permute-start.5 = (bf16[48,16384]{1,0:T(8,128)(2,1)}, bf16[48,16384]{1,0:T(8,128)(2,1)}, u32[]{:S(2)}, u32[]{:S(2)}) collective-permute-start(bf16[48,16384]{1,0:T(8,128)(2,1)} %collective-permute-done.4.refs_0_), channel_id=1, source_target_pairs={{0,2},{1,5},{4,0},{5,9},{8,4},{9,13},{12,8},{13,15},{14,12},{15,11... | collective-permute-start | bytes 4718600 | tf_op jit(solution)/shard_map/ppermute | solution.py:423
  40.2 35.2 %collective-permute-start.7 = (bf16[48,16384]{1,0:T(8,128)(2,1)}, bf16[48,16384]{1,0:T(8,128)(2,1)}, u32[]{:S(2)}, u32[]{:S(2)}) collective-permute-start(bf16[48,16384]{1,0:T(8,128)(2,1)} %collective-permute-done.4.refs_0_), channel_id=1, source_target_pairs={{0,1},{1,0},{2,3},{3,2},{4,5},{5,4},{6,7},{7,6},{8,9},{9,8},{10,11... | collective-permute-start | bytes 4718600 | tf_op jit(solution)/shard_map/ppermute | solution.py:423
  71.6 3.8 %collective-permute-start.9 = (bf16[48,16384]{1,0:T(8,128)(2,1)}, bf16[48,16384]{1,0:T(8,128)(2,1)S(1)}, u32[]{:S(2)}, u32[]{:S(2)}) collective-permute-start(bf16[48,16384]{1,0:T(8,128)(2,1)} %collective-permute-done.8.refs_2_), channel_id=1, source_target_pairs={{0,1},{1,0},{2,3},{3,2},{4,5},{5,4},{6,7},{7,6},{8,9},{9,8},{10,11... | collective-permute-start | bytes 4718600 | tf_op jit(solution)/shard_map/ppermute | solution.py:423
  71.6 37.0 %collective-permute-start.10 = (bf16[48,16384]{1,0:T(8,128)(2,1)}, bf16[48,16384]{1,0:T(8,128)(2,1)S(1)}, u32[]{:S(2)}, u32[]{:S(2)}) collective-permute-start(bf16[48,16384]{1,0:T(8,128)(2,1)} %collective-permute-done.8.refs_2_), channel_id=1, source_target_pairs={{0,4},{1,3},{4,8},{5,1},{8,12},{9,5},{12,14},{13,9},{14,10},{15,13... | collective-permute-start | bytes 4718600 | tf_op jit(solution)/shard_map/ppermute | solution.py:423
  74.1 36.9 %collective-permute-start.6 = (bf16[48,16384]{1,0:T(8,128)(2,1)}, bf16[48,16384]{1,0:T(8,128)(2,1)S(1)}, u32[]{:S(2)}, u32[]{:S(2)}) collective-permute-start(bf16[48,16384]{1,0:T(8,128)(2,1)} %collective-permute-done.5.refs_0_), channel_id=1, source_target_pairs={{0,2},{1,5},{4,0},{5,9},{8,4},{9,13},{12,8},{13,15},{14,12},{15,11... | collective-permute-start | bytes 4718600 | tf_op jit(solution)/shard_map/ppermute | solution.py:423
  74.1 36.9 %collective-permute-start.12 = (bf16[48,16384]{1,0:T(8,128)(2,1)}, bf16[48,16384]{1,0:T(8,128)(2,1)S(1)}, u32[]{:S(2)}, u32[]{:S(2)}) collective-permute-start(bf16[48,16384]{1,0:T(8,128)(2,1)} %collective-permute-done.5.refs_0_), channel_id=1, source_target_pairs={{0,1},{1,0},{2,3},{3,2},{4,5},{5,4},{6,7},{7,6},{8,9},{9,8},{10,11... | collective-permute-start | bytes 4718600 | tf_op jit(solution)/shard_map/ppermute | solution.py:423
  108.7 3.4 %collective-permute-start.13 = (bf16[48,16384]{1,0:T(8,128)(2,1)S(1)}, bf16[48,16384]{1,0:T(8,128)(2,1)S(1)}, u32[]{:S(2)}, u32[]{:S(2)}) collective-permute-start(bf16[48,16384]{1,0:T(8,128)(2,1)S(1)} %collective-permute-done.10.refs_2_), channel_id=1, source_target_pairs={{0,1},{1,0},{2,3},{3,2},{4,5},{5,4},{6,7},{7,6},{8,9},{9,8},{10,11... | collective-permute-start | bytes 4718600 | tf_op jit(solution)/shard_map/ppermute | solution.py:423
  108.7 20.4 %collective-permute-start.11 = (bf16[48,16384]{1,0:T(8,128)(2,1)S(1)}, bf16[48,16384]{1,0:T(8,128)(2,1)S(1)}, u32[]{:S(2)}, u32[]{:S(2)}) collective-permute-start(bf16[48,16384]{1,0:T(8,128)(2,1)S(1)} %collective-permute-done.10.refs_2_), channel_id=1, source_target_pairs={{0,4},{1,3},{4,8},{5,1},{8,12},{9,5},{12,14},{13,9},{14,10},{15,13... | collective-permute-start | bytes 4718600 | tf_op jit(solution)/shard_map/ppermute | solution.py:423
  111.0 24.5 %collective-permute-start.17 = (bf16[48,16384]{1,0:T(8,128)(2,1)S(1)}, bf16[48,16384]{1,0:T(8,128)(2,1)S(1)}, u32[]{:S(2)}, u32[]{:S(2)}) collective-permute-start(bf16[48,16384]{1,0:T(8,128)(2,1)S(1)} %collective-permute-done.6.refs_0_), channel_id=1, source_target_pairs={{0,1},{1,0},{2,3},{3,2},{4,5},{5,4},{6,7},{7,6},{8,9},{9,8},{10,11... | collective-permute-start | bytes 4718600 | tf_op jit(solution)/shard_map/ppermute | solution.py:423
  129.1 6.5 %collective-permute-start.18 = (bf16[48,16384]{1,0:T(8,128)(2,1)S(1)}, bf16[48,16384]{1,0:T(8,128)(2,1)S(1)}, u32[]{:S(2)}, u32[]{:S(2)}) collective-permute-start(bf16[48,16384]{1,0:T(8,128)(2,1)S(1)} %collective-permute-done.11.refs_1_.refs_2_), channel_id=1, source_target_pairs={{0,1},{1,0},{2,3},{3,2},{4,5},{5,4},{6,7},{7,6},{8,9},{9,8},{10,11... | collective-permute-start | bytes 4718600 | tf_op jit(solution)/shard_map/ppermute | solution.py:423
  131.7 11.0 %collective-permute-start.14 = (bf16[192,128]{1,0:T(8,128)(2,1)S(1)}, bf16[192,128]{1,0:T(8,128)(2,1)S(1)}, u32[]{:S(2)}, u32[]{:S(2)}) collective-permute-start(bf16[192,128]{1,0:T(8,128)(2,1)S(1)} %ranks.1), channel_id=1, source_target_pairs={{0,2},{1,3},{2,0},{3,1},{4,6},{5,7},{6,4},{7,5},{8,10},{9,11},{10,... | collective-permute-start | bytes 147464 | tf_op jit(solution)/shard_map/ppermute | solution.py:423
  131.8 10.9 %collective-permute-start.15 = (bf16[192,128]{1,0:T(8,128)(2,1)S(1)}, bf16[192,128]{1,0:T(8,128)(2,1)S(1)}, u32[]{:S(2)}, u32[]{:S(2)}) collective-permute-start(bf16[192,128]{1,0:T(8,128)(2,1)S(1)} %ranks.1), channel_id=1, source_target_pairs={{0,4},{1,5},{2,6},{3,7},{4,0},{5,1},{6,2},{7,3},{8,12},{9,13},{10,... | collective-permute-start | bytes 147464 | tf_op jit(solution)/shard_map/ppermute | solution.py:423
  134.1 8.6 %collective-permute-start.16 = (bf16[192,128]{1,0:T(8,128)(2,1)S(1)}, bf16[192,128]{1,0:T(8,128)(2,1)S(1)}, u32[]{:S(2)}, u32[]{:S(2)}) collective-permute-start(bf16[192,128]{1,0:T(8,128)(2,1)S(1)} %ranks.1), channel_id=1, source_target_pairs={{0,6},{1,7},{2,4},{3,5},{4,2},{5,3},{6,0},{7,1},{8,14},{9,15},{10,... | collective-permute-start | bytes 147464 | tf_op jit(solution)/shard_map/ppermute | solution.py:423
  142.7 10.5 %collective-permute-start.19 = (bf16[192,128]{1,0:T(8,128)(2,1)S(1)}, bf16[192,128]{1,0:T(8,128)(2,1)S(1)}, u32[]{:S(2)}, u32[]{:S(2)}) collective-permute-start(bf16[192,128]{1,0:T(8,128)(2,1)S(1)} %add_add_fusion), channel_id=1, source_target_pairs={{0,8},{1,9},{2,10},{3,11},{4,12},{5,13},{6,14},{7,15},{8,0},{9,1},... | collective-permute-start | bytes 147464 | tf_op jit(solution)/shard_map/ppermute | solution.py:423
  145.3 7.9 %collective-permute-start.20 = (bf16[192,128]{1,0:T(8,128)(2,1)S(1)}, bf16[192,128]{1,0:T(8,128)(2,1)S(1)}, u32[]{:S(2)}, u32[]{:S(2)}) collective-permute-start(bf16[192,128]{1,0:T(8,128)(2,1)S(1)} %add_add_fusion), channel_id=1, source_target_pairs={{0,1},{1,0},{2,3},{3,2},{4,5},{5,4},{6,7},{7,6},{8,9},{9,8},{10,11... | collective-permute-start | bytes 147464 | tf_op jit(solution)/shard_map/ppermute | solution.py:423
  145.3 8.0 %collective-permute-start.21 = (bf16[192,128]{1,0:T(8,128)(2,1)S(1)}, bf16[192,128]{1,0:T(8,128)(2,1)S(1)}, u32[]{:S(2)}, u32[]{:S(2)}) collective-permute-start(bf16[192,128]{1,0:T(8,128)(2,1)S(1)} %add_add_fusion), channel_id=1, source_target_pairs={{0,9},{1,8},{2,11},{3,10},{4,13},{5,12},{6,15},{7,14},{8,1},{9,0},... | collective-permute-start | bytes 147464 | tf_op jit(solution)/shard_map/ppermute | solution.py:423
  (10 other events, 67.2 us)

commit v11 on v10

--- a/solution.py
+++ b/solution.py
@@ -10,13 +10,14 @@
 
 HD = 128
 SEG = 128
-VMEM = 20 * 1024 * 1024
+VMEM = 16 * 1024 * 1024
 F32 = jnp.float32
 BF16 = jnp.bfloat16
 NT = (((1,), (1,)), ((), ()))
 SLOTS = 4
 CHUNK = 256
-BIG_VMEM = 24 * 1024 * 1024
+KEEP = 6
+BIG_VMEM = 16 * 1024 * 1024
 PARAMS = pltpu.CompilerParams(vmem_limit_bytes=VMEM)
 SNAKE = (0, 2, 4, 6, 7, 5, 3, 1)
 ROUNDS = len(SNAKE) // 2
@@ -174,39 +175,84 @@
     return pairs
 
 
-def block_kernel(count, low, tile, steps, first, base, fresh, ranked, *refs):
+def block_kernel(count, low, tile, steps, keep, kept, first, base, fresh, ranked, *refs):
     xs, w_ref, refs = refs[:count], refs[count], refs[count + 1 :]
     if ranked:
         s_refs, refs = refs[:2], refs[2:]
+    if kept:
+        w_kept, refs = refs[0], refs[1:]
     if not first:
         total_in, refs = refs[0], refs[1:]
     total_out, refs = refs[0], refs[1:]
     if ranked:
         h_out, refs = refs[0], refs[1:]
-    acc, before, x_slots, w_slots, s_slots, sems, total_sems = refs
+    if keep:
+        w_keep, refs = refs[0], refs[1:]
+    acc, before, x_slots, w_slots, s_slots, sems, w_sems, total_sems = refs
     rows = xs[0].shape[0]
-
-    def copies(step):
+    streamed = steps - kept
+    to_slots = streamed - keep
+
+    def other_copies(step):
         slot = lax.rem(step, SLOTS)
-        at = pl.multiple_of(step * tile, tile)
-        sem = lambda i: sems.at[slot, i]
-        out = [pltpu.make_async_copy(w_ref.at[pl.ds(low + at, tile)], w_slots.at[slot], sem(count))]
+        at = low + (step - kept) * tile
+        if kept:
+            at = jnp.where(step < kept, w_ref.shape[0] + (step - kept) * tile, at)
+        at = pl.multiple_of(at, tile)
+        out = []
         for i in range(count):
-            cut = xs[i].at[:, pl.ds(low + at, tile)]
-            out.append(pltpu.make_async_copy(cut, x_slots.at[slot, pl.ds(i * rows, rows)], sem(i)))
+            cut = xs[i].at[:, pl.ds(at, tile)]
+            out.append(pltpu.make_async_copy(cut, x_slots.at[slot, pl.ds(i * rows, rows)], sems.at[slot, i]))
         if ranked:
             for i, s_ref in enumerate(s_refs):
-                cut, rank = s_ref.at[:, pl.ds(low + at, tile)], s_ref.shape[0]
+                cut, rank = s_ref.at[:, pl.ds(at, tile)], s_ref.shape[0]
                 to = s_slots.at[slot, pl.ds(i * rank, rank)]
-                out.append(pltpu.make_async_copy(cut, to, sem(count + 1 + i)))
+                out.append(pltpu.make_async_copy(cut, to, sems.at[slot, count + i]))
         return out
 
-    def start(step):
-        for copy in copies(step):
+    def weight_copy(index, to):
+        source = w_ref.at[pl.ds(pl.multiple_of(low + index * tile, tile), tile)]
+        return pltpu.make_async_copy(source, to, w_sems.at[lax.rem(index, SLOTS)])
+
+    def slot_copy(index):
+        return weight_copy(index, w_slots.at[lax.rem(index, SLOTS)])
+
+    def kept_rows(index):
+        return pl.ds(pl.multiple_of((index - to_slots) * tile, tile), tile)
+
+    def start_other(step):
+        for copy in other_copies(step):
             copy.start()
 
+    def start_weights(index):
+        @pl.when(index < to_slots)
+        def _():
+            slot_copy(index).start()
+
+        if keep:
+            @pl.when(index >= to_slots)
+            def _():
+                weight_copy(index, w_keep.at[kept_rows(index)]).start()
+
+    def take(step, weight):
+        slot = lax.rem(step, SLOTS)
+        x = x_slots[slot]
+        for left in range(0, acc.shape[2], CHUNK):
+            cut = slice(left, left + CHUNK)
+            product = jnp.dot(x, weight(cut), preferred_element_type=F32)
+            acc[:, :, cut] += product.reshape(count, rows, CHUNK)
+        if ranked:
+            mine = jnp.concatenate([x[i * rows : (i + 1) * rows] for i in range(0, count, 2)], 0)
+            h_out[...] += lax.dot_general(mine, s_slots[slot], NT, preferred_element_type=F32)
+
+        @pl.when(step + SLOTS < steps)
+        def _():
+            start_other(step + SLOTS)
+
+    for index in range(min(SLOTS, streamed)):
+        start_weights(jnp.int32(index))
     for step in range(min(SLOTS, steps)):
-        start(jnp.int32(step))
+        start_other(jnp.int32(step))
     if not fresh:
         load = pltpu.make_async_copy(total_in.at[pl.ds(base, count)], before, total_sems.at[0])
         load.start()
@@ -214,23 +260,33 @@
     if ranked:
         h_out[...] = jnp.zeros_like(h_out)
 
-    @pl.loop(0, steps)
-    def _(step):
-        for copy in copies(step):
+    if kept:
+        @pl.loop(0, kept)
+        def _(step):
+            for copy in other_copies(step):
+                copy.wait()
+            take(step, lambda cut: w_kept[pl.ds(pl.multiple_of(step * tile, tile), tile), cut])
+
+    @pl.loop(0, to_slots)
+    def _(index):
+        for copy in other_copies(index + kept) + [slot_copy(index)]:
             copy.wait()
-        slot = lax.rem(step, SLOTS)
-        x = x_slots[slot]
-        for left in range(0, acc.shape[2], CHUNK):
-            cut = slice(left, left + CHUNK)
-            product = jnp.dot(x, w_slots[slot, :, cut], preferred_element_type=F32)
-            acc[:, :, cut] += product.reshape(count, rows, CHUNK)
-        if ranked:
-            mine = jnp.concatenate([x[i * rows : (i + 1) * rows] for i in range(0, count, 2)], 0)
-            h_out[...] += lax.dot_general(mine, s_slots[slot], NT, preferred_element_type=F32)
-
-        @pl.when(step + SLOTS < steps)
+        take(index + kept, lambda cut: w_slots[lax.rem(index, SLOTS), :, cut])
+
+        @pl.when(index + SLOTS < streamed)
         def _():
-            start(step + SLOTS)
+            start_weights(index + SLOTS)
+
+    if keep:
+        @pl.loop(to_slots, streamed)
+        def _(index):
+            for copy in other_copies(index + kept) + [weight_copy(index, w_keep.at[kept_rows(index)])]:
+                copy.wait()
+            take(index + kept, lambda cut: w_keep[kept_rows(index), cut])
+
+            @pl.when(index + SLOTS < streamed)
+            def _():
+                start_weights(index + SLOTS)
 
     if not fresh:
         load.wait()
@@ -240,18 +296,23 @@
     store.wait()
 
 
-def block_product(xs, weights, factors, low, high, tile, total, base, ranked):
+def block_product(xs, weights, factors, low, high, tile, total, base, ranked=False, fresh=None, keep=0, kept=None):
     count = len(xs)
     rows = xs[0].shape[0]
     cols = weights.shape[1]
     rank = 2 * factors[0].shape[0]
-    fresh, first = low == 0, total is None
+    fresh, first = low == 0 if fresh is None else fresh, total is None
     anywhere, whole = pl.BlockSpec(memory_space=pl.ANY), pl.BlockSpec(memory_space=pltpu.VMEM)
     operands = list(xs) + [weights]
     specs = [anywhere] * (count + 1)
     if ranked:
         operands += factors
         specs += [anywhere] * 2
+    kept_steps = 0
+    if kept is not None:
+        operands.append(kept)
+        specs.append(whole)
+        kept_steps = kept.shape[0] // tile
     aliases = {}
     if not first:
         aliases = {len(operands): 0}
@@ -261,9 +322,12 @@
     if ranked:
         outs.append(jax.ShapeDtypeStruct((count // 2 * rows, rank), F32))
         out_specs.append(whole)
-    steps = (high - low) // tile
+    if keep:
+        outs.append(jax.ShapeDtypeStruct((keep * tile, cols), weights.dtype))
+        out_specs.append(whole)
+    steps = (high - low) // tile + kept_steps
     result = pl.pallas_call(
-        functools.partial(block_kernel, count, low, tile, steps, first, base, fresh, ranked),
+        functools.partial(block_kernel, count, low, tile, steps, keep, kept_steps, first, base, fresh, ranked),
         in_specs=specs,
         out_specs=out_specs,
         out_shape=outs,
@@ -273,7 +337,8 @@
             pltpu.VMEM((SLOTS, count * rows, tile), BF16),
             pltpu.VMEM((SLOTS, tile, cols), BF16),
             pltpu.VMEM((SLOTS, rank, tile), BF16),
-            pltpu.SemaphoreType.DMA((SLOTS, count + 3)),
+            pltpu.SemaphoreType.DMA((SLOTS, count + 2)),
+            pltpu.SemaphoreType.DMA((SLOTS,)),
             pltpu.SemaphoreType.DMA((2,)),
         ],
         input_output_aliases=aliases,
@@ -292,22 +357,24 @@
     return (2 * len(SNAKE), rows, cols)
 
 
-def some_ranks_kernel(x_ref, s_ref, out_ref):
-    out_ref[...] = lax.dot_general(x_ref[...], s_ref[...], NT, preferred_element_type=F32)
-
-
-def some_ranks(x, factor):
+def some_ranks_kernel(x_ref, *refs):
+    factors, out_ref = refs[:-1], refs[-1]
+    terms = [lax.dot_general(x_ref[...], ref[...], NT, preferred_element_type=F32) for ref in factors]
+    out_ref[...] = jnp.concatenate(terms, 1)
+
+
+def some_ranks(x, factors):
     whole = lambda shape: pl.BlockSpec(shape, lambda _: (0, 0))
-    shape = (x.shape[0], factor.shape[0])
+    shape = (x.shape[0], 2 * factors[0].shape[0])
     return pl.pallas_call(
         some_ranks_kernel,
         grid=(1,),
-        in_specs=[whole(x.shape), whole(factor.shape)],
+        in_specs=[whole(value.shape) for value in (x, *factors)],
         out_specs=whole(shape),
         out_shape=jax.ShapeDtypeStruct(shape, F32),
         compiler_params=PARAMS,
         name="some_ranks",
-    )(x, factor)
+    )(x, *factors)
 
 
 def rank_kernel(count, owners_ref, slot_ref, *refs):
@@ -424,23 +491,22 @@
     swap = lambda value: send(value, [(i, i ^ 1) for i in range(parts)])
     out, home = ring_pairs((1, -1)), ring_pairs((-1, 1))
 
-    half = depth // 2
     hs, counts = [], []
 
-    def multiply(xs, total):
-        total, h = block_product(xs, weights, factors, 0, depth, tile, total, sum(counts), True)
-        hs.extend(h)
+    def multiply(xs, total, keep=0):
+        total, more = block_product(xs, weights, factors, 0, depth, tile, total, sum(counts), True, keep=keep)
+        hs.append(more[0])
         counts.append(len(xs))
-        return total
+        return total, more[1:]
 
     streams = [send(tokens, out), None]
     own, factors = [tokens, swap(tokens)], [shrinks[0], swap(shrinks[0])]
-    mine = some_ranks(tokens, factors[0])
-    second, mine = lax.optimization_barrier((tokens, mine))
+    part = 2 * tile
+    total, _ = block_product(own, weights, factors, 0, part, tile, None, 0)
+    second, total = lax.optimization_barrier((tokens, total))
     streams[1] = send(second, home)
-    total, _ = block_product(own, weights, factors, 0, depth, tile, None, 0, False)
-    mine = jnp.concatenate([mine, some_ranks(tokens, factors[1])], 1)
-    hs, total = lax.optimization_barrier(([mine], total))
+    total, _ = block_product(own, weights, factors, part, depth, tile, total, 0)
+    hs, total = lax.optimization_barrier(([some_ranks(tokens, factors)], total))
     counts.append(len(own))
 
     def make_tables(me, indices):
@@ -459,7 +525,7 @@
             streams[hop % 2] = send(arrived, home if hop % 2 else out)
         if hop % 2:
             late = [arrived, swap(arrived)]
-            total = multiply(blocks, total)
+            total, kept = multiply(blocks, total, KEEP if hop == hops - 2 else 0)
             blocks = late
         else:
             blocks += [arrived, swap(arrived)]
@@ -472,15 +538,17 @@
     h = rank_terms(owners, slots, blocks[::2], factors, hs)
     beside = lambda step: send(h, [(i, i ^ step) for i in range(parts)])
 
-    def last_product(low, high, total):
+    def last_product(low, high, total, **more):
         xs, _ = lax.optimization_barrier((blocks, h))
-        return block_product(xs, weights, factors, low, high, tile, total, held, False)[0]
-
+        return block_product(xs, weights, factors, low, high, tile, total, held, **more)[0]
+
+    streamed = depth - KEEP * tile
+    middle = (16 - KEEP) // 2 * tile
     near = [beside(step) for step in (2, 4, 6)]
-    near, total = lax.optimization_barrier((near, last_product(0, half, total)))
+    near, total = lax.optimization_barrier((near, last_product(0, middle, total, kept=kept[0])))
     h = h + near[0] + near[1] + near[2]
     far = [beside(step) for step in (8, 1, 9)]
-    far, total = lax.optimization_barrier((far, last_product(half, depth, total)))
+    far, total = lax.optimization_barrier((far, last_product(middle, streamed, total)))
     mine, other = h + far[0], far[1] + far[2]
     return block_finish(places, segment_slot, core, total, expands, scale, mine, other, cosine, sine)
 

time: 157 us -> 151 us (0.962)
  waiting for transfers between devices: 46.4 us -> 30.4 us
  Pallas kernels: 77.4 us -> 83.6 us
  starting transfers between devices: 21.5 us -> 27.2 us
  local copies, waits for them, and re-layouts: 8.52 us -> 6.94 us
    ppermute x22, waiting for transfers between devices: 46.4 us -> 30.4 us  [ring_plan(): send = lambda value, pairs: lax.ppermute(value, 'tensor', pairs)]
    pallas_call x8, Pallas kernels: 71.9 us -> 78.1 us  [the longest x7 74.6 us: block_product(): pl.pallas_call(functools.partial(block_kernel, count, low, tile, steps, k...]
    ppermute x22, starting transfers between devices: 21.5 us -> 27.2 us  [ring_plan(): send = lambda value, pairs: lax.ppermute(value, 'tensor', pairs)]
    unnamed x24 -> x22, local copies, waits for them, and re-layouts: 6.4 us -> 4.81 us
  transfers between devices with their start and end apart: 22 -> 22, of which waited for: 6 -> 6; matrix products, arithmetic and copies ran while one was open for 3% -> 3% of each run, Pallas kernels for 48% -> 54%
where the time goes in v11:
time: 151 us
  Pallas kernels  83.6 us (55%)
  waiting for transfers between devices  30.4 us (20%)
  starting transfers between devices  27.2 us (18%)
  local copies, waits for them, and re-layouts  6.94 us (5%)
  other arithmetic  2.14 us (1%)
    pallas_call x7, Pallas kernels, block_product(): pl.pallas_call(functools.partial(block_kernel, count, low, tile, steps, k...  74.6 us
    ppermute x22, waiting for transfers between devices, ring_plan(): send = lambda value, pairs: lax.ppermute(value, 'tensor', pairs)  30.4 us
    ppermute x22, starting transfers between devices, ring_plan(): send = lambda value, pairs: lax.ppermute(value, 'tensor', pairs)  27.2 us
    unnamed x22, local copies, waits for them, and re-layouts  4.81 us
    pallas_call x1, Pallas kernels, some_ranks(): pl.pallas_call(some_ranks_kernel, grid=(1,), in_specs=[whole(value.shape)...  3.49 us
  transfers between devices with their start and end apart: 22, of which 6 were waited for; matrix products, arithmetic and copies ran while one was open for 3% of the time, Pallas kernels for 54%

profile of v11, /device:TPU:0, one launch (start us, length us, event | category | flops | bytes accessed | tf_op | source)
XLA Modules:
  0.0 150.5 jit_solution(8356869037415992651)
XLA Ops:
  0.5 3.0 %collective-permute-start = (bf16[48,16384]{1,0:T(8,128)(2,1)}, bf16[48,16384]{1,0:T(8,128)(2,1)}, u32[]{:S(2)}, u32[]{:S(2)}) collective-permute-start(bf16[48,16384]{1,0:T(8,128)(2,1)} %refs_0_.3), channel_id=1, source_target_pairs={{0,4},{1,3},{4,8},{5,1},{8,12},{9,5},{12,14},{13,9},{14,10},{15,13... | collective-permute-start | bytes 4718600 | tf_op jit(solution)/shard_map/ppermute | solution.py:490
  3.5 3.2 %collective-permute-done.2.refs_1_ = bf16[48,16384]{1,0:T(8,128)(2,1)S(1)} collective-permute-done((bf16[48,16384]{1,0:T(8,128)(2,1)}, bf16[48,16384]{1,0:T(8,128)(2,1)S(1)}, u32[]{:S(2)}, u32[]{:S(2)}) %collective-permute-start.2) | collective-permute-done | bytes 1572896 | tf_op jit(solution)/shard_map/ppermute | solution.py:490
  6.7 3.5 %blocks.7.refs_3_ = f32[16,48,1024]{2,1,0:T(8,128)S(1)} custom-call(bf16[48,16384]{1,0:T(8,128)(2,1)} %refs_0_.3, bf16[48,16384]{1,0:T(8,128)(2,1)S(1)} %collective-permute-done.2.refs_1_, bf16[16384,1024]{1,0:T(8,128)(2,1)} %refs_4_.7), custom_call_target="tpu_custom_call" | custom-call | flops 402653184 | bytes 4194304 | tf_op jit(solution)/shard_map/blocks/pallas_call | solution.py:329
  10.2 2.9 %collective-permute-start.4 = (bf16[48,16384]{1,0:T(8,128)(2,1)}, bf16[48,16384]{1,0:T(8,128)(2,1)}, u32[]{:S(2)}, u32[]{:S(2)}) collective-permute-start(bf16[48,16384]{1,0:T(8,128)(2,1)} %refs_0_.3), channel_id=1, source_target_pairs={{0,2},{1,5},{4,0},{5,9},{8,4},{9,13},{12,8},{13,15},{14,12},{15,11... | collective-permute-start | bytes 4718600 | tf_op jit(solution)/shard_map/ppermute | solution.py:490
  13.2 12.3 %blocks.8.refs_5_ = f32[16,48,1024]{2,1,0:T(8,128)S(1)} custom-call(bf16[48,16384]{1,0:T(8,128)(2,1)} %refs_0_.3, bf16[48,16384]{1,0:T(8,128)(2,1)S(1)} %collective-permute-done.2.refs_1_, bf16[16384,1024]{1,0:T(8,128)(2,1)} %refs_4_.7, f32[16,48,1024]{2,1,0:T(8,128)S(1)} %blocks.7.refs_3_), custom_call_target="tpu_custom_call", output_to_operand_aliasing={{}: (3, {})} | custom-call | flops 2818572288 | bytes 29360128 | tf_op jit(solution)/shard_map/blocks/pallas_call | solution.py:329
  25.5 3.5 %some_ranks.1.refs_4_ = f32[48,128]{1,0:T(8,128)S(1)} custom-call(bf16[48,16384]{1,0:T(8,128)(2,1)} %refs_0_.3, bf16[64,16384]{1,0:T(8,128)(2,1)S(1)} %bitcast.15, bf16[64,16384]{1,0:T(8,128)(2,1)S(1)} %collective-permute-done.1.refs_1_.refs_4_.refs_6_.refs_3_), custom_call_target="tpu_custom_call" | custom-call | tf_op jit(solution)/shard_map/some_ranks/pallas_call | solution.py:369
  29.9 2.4 %collective-permute-start.8 = (bf16[48,16384]{1,0:T(8,128)(2,1)}, bf16[48,16384]{1,0:T(8,128)(2,1)}, u32[]{:S(2)}, u32[]{:S(2)}) collective-permute-start(bf16[48,16384]{1,0:T(8,128)(2,1)} %collective-permute-done.refs_0_), channel_id=1, source_target_pairs={{0,4},{1,3},{4,8},{5,1},{8,12},{9,5},{12,14},{13,9},{14,10},{15,13... | collective-permute-start | bytes 4718600 | tf_op jit(solution)/shard_map/ppermute | solution.py:490
  32.3 10.6 %collective-permute-done.4.refs_0_ = bf16[48,16384]{1,0:T(8,128)(2,1)} collective-permute-done((bf16[48,16384]{1,0:T(8,128)(2,1)}, bf16[48,16384]{1,0:T(8,128)(2,1)}, u32[]{:S(2)}, u32[]{:S(2)}) %collective-permute-start.4) | collective-permute-done | bytes 1572896 | tf_op jit(solution)/shard_map/ppermute | solution.py:490
  42.9 1.7 %collective-permute-start.5 = (bf16[48,16384]{1,0:T(8,128)(2,1)}, bf16[48,16384]{1,0:T(8,128)(2,1)}, u32[]{:S(2)}, u32[]{:S(2)}) collective-permute-start(bf16[48,16384]{1,0:T(8,128)(2,1)} %collective-permute-done.4.refs_0_), channel_id=1, source_target_pairs={{0,2},{1,5},{4,0},{5,9},{8,4},{9,13},{12,8},{13,15},{14,12},{15,11... | collective-permute-start | bytes 4718600 | tf_op jit(solution)/shard_map/ppermute | solution.py:490
  49.0 14.0 %blocks.9 = (f32[16,48,1024]{2,1,0:T(8,128)S(1)}, f32[48,128]{1,0:T(8,128)S(1)}) custom-call(bf16[48,16384]{1,0:T(8,128)(2,1)} %collective-permute-done.refs_0_, bf16[48,16384]{1,0:T(8,128)(2,1)} %collective-permute-done.3.refs_1_, bf16[16384,1024]{1,0:T(8,128)(2,1)} %refs_4_.7, bf16[64,16384]{1,0:T(8,128)(2,1)S(1)} %bitcast.16, ...), custom_call_target="tpu_custom_call", output_to_operand_aliasing={{0}: (5, {})} | custom-call | flops 3221225472 | bytes 33554432 | tf_op jit(solution)/shard_map/blocks/pallas_call | solution.py:329
  69.1 4.9 %collective-permute-done.5.refs_0_ = bf16[48,16384]{1,0:T(8,128)(2,1)} collective-permute-done((bf16[48,16384]{1,0:T(8,128)(2,1)}, bf16[48,16384]{1,0:T(8,128)(2,1)}, u32[]{:S(2)}, u32[]{:S(2)}) %collective-permute-start.5) | collective-permute-done | bytes 1572896 | tf_op jit(solution)/shard_map/ppermute | solution.py:490
  73.9 2.5 %collective-permute-start.6 = (bf16[48,16384]{1,0:T(8,128)(2,1)}, bf16[48,16384]{1,0:T(8,128)(2,1)S(1)}, u32[]{:S(2)}, u32[]{:S(2)}) collective-permute-start(bf16[48,16384]{1,0:T(8,128)(2,1)} %collective-permute-done.5.refs_0_), channel_id=1, source_target_pairs={{0,2},{1,5},{4,0},{5,9},{8,4},{9,13},{12,8},{13,15},{14,12},{15,11... | collective-permute-start | bytes 4718600 | tf_op jit(solution)/shard_map/ppermute | solution.py:490
  78.0 15.4 %blocks.10 = (f32[16,48,1024]{2,1,0:T(8,128)S(1)}, f32[96,128]{1,0:T(8,128)S(1)}) custom-call(bf16[48,16384]{1,0:T(8,128)(2,1)} %collective-permute-done.4.refs_0_, bf16[48,16384]{1,0:T(8,128)(2,1)} %collective-permute-done.7.refs_1_, bf16[48,16384]{1,0:T(8,128)(2,1)} %collective-permute-done.8.refs_2_, ...), custom_call_target="tpu_custom_call", output_to_operand_aliasing={{0}: (7, {})} | custom-call | flops 6442450944 | bytes 33554432 | tf_op jit(solution)/shard_map/blocks/pallas_call | solution.py:329
  93.4 7.8 %collective-permute-done.10.refs_2_ = bf16[48,16384]{1,0:T(8,128)(2,1)S(1)} collective-permute-done((bf16[48,16384]{1,0:T(8,128)(2,1)}, bf16[48,16384]{1,0:T(8,128)(2,1)S(1)}, u32[]{:S(2)}, u32[]{:S(2)}) %collective-permute-start.10) | collective-permute-done | bytes 1572896 | tf_op jit(solution)/shard_map/ppermute | solution.py:490
  101.2 2.4 %collective-permute-start.11 = (bf16[48,16384]{1,0:T(8,128)(2,1)S(1)}, bf16[48,16384]{1,0:T(8,128)(2,1)S(1)}, u32[]{:S(2)}, u32[]{:S(2)}) collective-permute-start(bf16[48,16384]{1,0:T(8,128)(2,1)S(1)} %collective-permute-done.10.refs_2_), channel_id=1, source_target_pairs={{0,4},{1,3},{4,8},{5,1},{8,12},{9,5},{12,14},{13,9},{14,10},{15,13... | collective-permute-start | bytes 4718600 | tf_op jit(solution)/shard_map/ppermute | solution.py:490
  103.6 2.9 %collective-permute-done.6.refs_0_ = bf16[48,16384]{1,0:T(8,128)(2,1)S(1)} collective-permute-done((bf16[48,16384]{1,0:T(8,128)(2,1)}, bf16[48,16384]{1,0:T(8,128)(2,1)S(1)}, u32[]{:S(2)}, u32[]{:S(2)}) %collective-permute-start.6) | collective-permute-done | bytes 1572896 | tf_op jit(solution)/shard_map/ppermute | solution.py:490
  107.9 15.9 %blocks.11 = (f32[16,48,1024]{2,1,0:T(8,128)S(1)}, f32[96,128]{1,0:T(8,128)S(1)}, bf16[6144,1024]{1,0:T(8,128)(2,1)S(1)}) custom-call(bf16[48,16384]{1,0:T(8,128)(2,1)} %collective-permute-done.5.refs_0_, bf16[48,16384]{1,0:T(8,128)(2,1)S(1)} %collective-permute-done.12.refs_1_, ...), custom_call_target="tpu_custom_call", output_to_operand_aliasing={{0}: (7, {})} | custom-call | flops 6442450944 | bytes 33554432 | tf_op jit(solution)/shard_map/blocks/pallas_call | solution.py:329
  124.0 2.5 %ranks.1 = bf16[192,128]{1,0:T(8,128)(2,1)S(1)} custom-call(s32[16]{0:T(128)S(1)} %get-tuple-element.64.owners_ref, s32[8]{0:T(128)S(1)} %pad_add_fusion.slot_ref, bf16[48,16384]{1,0:T(8,128)(2,1)S(1)} %collective-permute-done.6.refs_0_, bf16[48,16384]{1,0:T(8,128)(2,1)S(1)} %collective-permute-done.11.refs_1_.refs_2_, bf16[64,16384]{1,0:T(8,128)(2,1)S(1)} %bitcast.19, ...), custom_call_target="tpu_custom_call" | custom-call | tf_op jit(solution)/shard_map/ranks/pallas_call | solution.py:408
  126.5 2.5 %collective-permute-start.14 = (bf16[192,128]{1,0:T(8,128)(2,1)S(1)}, bf16[192,128]{1,0:T(8,128)(2,1)S(1)}, u32[]{:S(2)}, u32[]{:S(2)}) collective-permute-start(bf16[192,128]{1,0:T(8,128)(2,1)S(1)} %ranks.1), channel_id=1, source_target_pairs={{0,2},{1,3},{2,0},{3,1},{4,6},{5,7},{6,4},{7,5},{8,10},{9,11},{10,... | collective-permute-start | bytes 147464 | tf_op jit(solution)/shard_map/ppermute | solution.py:490
  129.0 1.6 %collective-permute-start.15 = (bf16[192,128]{1,0:T(8,128)(2,1)S(1)}, bf16[192,128]{1,0:T(8,128)(2,1)S(1)}, u32[]{:S(2)}, u32[]{:S(2)}) collective-permute-start(bf16[192,128]{1,0:T(8,128)(2,1)S(1)} %ranks.1), channel_id=1, source_target_pairs={{0,4},{1,5},{2,6},{3,7},{4,0},{5,1},{6,2},{7,3},{8,12},{9,13},{10,... | collective-permute-start | bytes 147464 | tf_op jit(solution)/shard_map/ppermute | solution.py:490
  130.6 8.0 %blocks.12.refs_5_ = f32[16,48,1024]{2,1,0:T(8,128)S(1)} custom-call(bf16[48,16384]{1,0:T(8,128)(2,1)S(1)} %collective-permute-done.6.refs_0_, bf16[48,16384]{1,0:T(8,128)(2,1)S(1)} %collective-permute-done.17.refs_1_, bf16[48,16384]{1,0:T(8,128)(2,1)S(1)} %collective-permute-done.11.refs_1_.refs_2_, ...), custom_call_target="tpu_custom_call", output_to_operand_aliasing={{}: (6, {})} | custom-call | flops 2013265920 | bytes 10485760 | tf_op jit(solution)/shard_map/blocks/pallas_call | solution.py:329
  138.7 3.0 %collective-permute-start.19 = (bf16[192,128]{1,0:T(8,128)(2,1)S(1)}, bf16[192,128]{1,0:T(8,128)(2,1)S(1)}, u32[]{:S(2)}, u32[]{:S(2)}) collective-permute-start(bf16[192,128]{1,0:T(8,128)(2,1)S(1)} %add_add_fusion), channel_id=1, source_target_pairs={{0,8},{1,9},{2,10},{3,11},{4,12},{5,13},{6,14},{7,15},{8,0},{9,1},... | collective-permute-start | bytes 147464 | tf_op jit(solution)/shard_map/ppermute | solution.py:490
  142.0 5.4 %blocks.13.refs_0_.refs_1_.refs_2_.refs_3_.refs_4_.refs_5_.refs_6_.refs_7_ = f32[16,48,1024]{2,1,0:T(8,128)S(1)} custom-call(bf16[48,16384]{1,0:T(8,128)(2,1)S(1)} %collective-permute-done.6.refs_0_, bf16[48,16384]{1,0:T(8,128)(2,1)S(1)} %collective-permute-done.17.refs_1_, ...), custom_call_target="tpu_custom_call", output_to_operand_aliasing={{}: (5, {})} | custom-call | flops 2013265920 | bytes 10485760 | tf_op jit(solution)/shard_map/blocks/pallas_call | solution.py:329
  147.5 3.0 %finish.1 = bf16[768,1024]{1,0:T(8,128)(2,1)} custom-call(s32[16]{0:T(128)S(1)} %get-tuple-element.61.places_ref, s32[6]{0:T(128)S(1)} %gather_fusion, s32[1]{0:T(128)} %bitcast.7.core_ref, f32[16,48,1024]{2,1,0:T(8,128)S(1)} %blocks.13.refs_0_.refs_1_.refs_2_.refs_3_.refs_4_.refs_5_.refs_6_.refs_7_, ...), custom_call_target="tpu_custom_call" | custom-call | tf_op jit(solution)/shard_map/finish/pallas_call | solution.py:462
  (67 shorter events, 15.1 us)
Async XLA Ops:
  0.0 64.1 %copy-start = (s32[16]{0:T(128)S(1)}, s32[16]{0:T(128)}, u32[]{:S(2)}) copy-start(s32[16]{0:T(128)} %param.16) | copy-start | bytes 196
  0.0 25.5 %collective-permute-start.1 = (bf16[64,16384]{1,0:T(8,128)(2,1)}, bf16[64,16384]{1,0:T(8,128)(2,1)S(1)}, u32[]{:S(2)}, u32[]{:S(2)}) collective-permute-start(bf16[64,16384]{1,0:T(8,128)(2,1)} %bitcast.14), channel_id=1, source_target_pairs={{0,1},{1,0},{2,3},{3,2},{4,5},{5,4},{6,7},{7,6},{8,9},{9,8},{10,11... | collective-permute-start | bytes 6291464 | tf_op jit(solution)/shard_map/ppermute | solution.py:490
  0.5 6.2 %collective-permute-start.2 = (bf16[48,16384]{1,0:T(8,128)(2,1)}, bf16[48,16384]{1,0:T(8,128)(2,1)S(1)}, u32[]{:S(2)}, u32[]{:S(2)}) collective-permute-start(bf16[48,16384]{1,0:T(8,128)(2,1)} %refs_0_.3), channel_id=1, source_target_pairs={{0,1},{1,0},{2,3},{3,2},{4,5},{5,4},{6,7},{7,6},{8,9},{9,8},{10,11... | collective-permute-start | bytes 4718600 | tf_op jit(solution)/shard_map/ppermute | solution.py:490
  0.5 29.3 %collective-permute-start = (bf16[48,16384]{1,0:T(8,128)(2,1)}, bf16[48,16384]{1,0:T(8,128)(2,1)}, u32[]{:S(2)}, u32[]{:S(2)}) collective-permute-start(bf16[48,16384]{1,0:T(8,128)(2,1)} %refs_0_.3), channel_id=1, source_target_pairs={{0,4},{1,3},{4,8},{5,1},{8,12},{9,5},{12,14},{13,9},{14,10},{15,13... | collective-permute-start | bytes 4718600 | tf_op jit(solution)/shard_map/ppermute | solution.py:490
  10.2 32.7 %collective-permute-start.4 = (bf16[48,16384]{1,0:T(8,128)(2,1)}, bf16[48,16384]{1,0:T(8,128)(2,1)}, u32[]{:S(2)}, u32[]{:S(2)}) collective-permute-start(bf16[48,16384]{1,0:T(8,128)(2,1)} %refs_0_.3), channel_id=1, source_target_pairs={{0,2},{1,5},{4,0},{5,9},{8,4},{9,13},{12,8},{13,15},{14,12},{15,11... | collective-permute-start | bytes 4718600 | tf_op jit(solution)/shard_map/ppermute | solution.py:490
  29.9 16.0 %collective-permute-start.3 = (bf16[48,16384]{1,0:T(8,128)(2,1)}, bf16[48,16384]{1,0:T(8,128)(2,1)}, u32[]{:S(2)}, u32[]{:S(2)}) collective-permute-start(bf16[48,16384]{1,0:T(8,128)(2,1)} %collective-permute-done.refs_0_), channel_id=1, source_target_pairs={{0,1},{1,0},{2,3},{3,2},{4,5},{5,4},{6,7},{7,6},{8,9},{9,8},{10,11... | collective-permute-start | bytes 4718600 | tf_op jit(solution)/shard_map/ppermute | solution.py:490
  29.9 33.2 %copy-start.10 = (s32[8]{0:T(128)S(1)}, s32[8]{0:T(128)}, u32[]{:S(2)}) copy-start(s32[8]{0:T(128)} %param.17) | copy-start | bytes 100
  29.9 37.5 %collective-permute-start.8 = (bf16[48,16384]{1,0:T(8,128)(2,1)}, bf16[48,16384]{1,0:T(8,128)(2,1)}, u32[]{:S(2)}, u32[]{:S(2)}) collective-permute-start(bf16[48,16384]{1,0:T(8,128)(2,1)} %collective-permute-done.refs_0_), channel_id=1, source_target_pairs={{0,4},{1,3},{4,8},{5,1},{8,12},{9,5},{12,14},{13,9},{14,10},{15,13... | collective-permute-start | bytes 4718600 | tf_op jit(solution)/shard_map/ppermute | solution.py:490
  42.9 31.0 %collective-permute-start.5 = (bf16[48,16384]{1,0:T(8,128)(2,1)}, bf16[48,16384]{1,0:T(8,128)(2,1)}, u32[]{:S(2)}, u32[]{:S(2)}) collective-permute-start(bf16[48,16384]{1,0:T(8,128)(2,1)} %collective-permute-done.4.refs_0_), channel_id=1, source_target_pairs={{0,2},{1,5},{4,0},{5,9},{8,4},{9,13},{12,8},{13,15},{14,12},{15,11... | collective-permute-start | bytes 4718600 | tf_op jit(solution)/shard_map/ppermute | solution.py:490
  44.6 31.8 %collective-permute-start.7 = (bf16[48,16384]{1,0:T(8,128)(2,1)}, bf16[48,16384]{1,0:T(8,128)(2,1)}, u32[]{:S(2)}, u32[]{:S(2)}) collective-permute-start(bf16[48,16384]{1,0:T(8,128)(2,1)} %collective-permute-done.4.refs_0_), channel_id=1, source_target_pairs={{0,1},{1,0},{2,3},{3,2},{4,5},{5,4},{6,7},{7,6},{8,9},{9,8},{10,11... | collective-permute-start | bytes 4718600 | tf_op jit(solution)/shard_map/ppermute | solution.py:490
  67.4 9.1 %collective-permute-start.9 = (bf16[48,16384]{1,0:T(8,128)(2,1)}, bf16[48,16384]{1,0:T(8,128)(2,1)S(1)}, u32[]{:S(2)}, u32[]{:S(2)}) collective-permute-start(bf16[48,16384]{1,0:T(8,128)(2,1)} %collective-permute-done.8.refs_2_), channel_id=1, source_target_pairs={{0,1},{1,0},{2,3},{3,2},{4,5},{5,4},{6,7},{7,6},{8,9},{9,8},{10,11... | collective-permute-start | bytes 4718600 | tf_op jit(solution)/shard_map/ppermute | solution.py:490
  67.4 33.8 %collective-permute-start.10 = (bf16[48,16384]{1,0:T(8,128)(2,1)}, bf16[48,16384]{1,0:T(8,128)(2,1)S(1)}, u32[]{:S(2)}, u32[]{:S(2)}) collective-permute-start(bf16[48,16384]{1,0:T(8,128)(2,1)} %collective-permute-done.8.refs_2_), channel_id=1, source_target_pairs={{0,4},{1,3},{4,8},{5,1},{8,12},{9,5},{12,14},{13,9},{14,10},{15,13... | collective-permute-start | bytes 4718600 | tf_op jit(solution)/shard_map/ppermute | solution.py:490
  73.9 32.6 %collective-permute-start.6 = (bf16[48,16384]{1,0:T(8,128)(2,1)}, bf16[48,16384]{1,0:T(8,128)(2,1)S(1)}, u32[]{:S(2)}, u32[]{:S(2)}) collective-permute-start(bf16[48,16384]{1,0:T(8,128)(2,1)} %collective-permute-done.5.refs_0_), channel_id=1, source_target_pairs={{0,2},{1,5},{4,0},{5,9},{8,4},{9,13},{12,8},{13,15},{14,12},{15,11... | collective-permute-start | bytes 4718600 | tf_op jit(solution)/shard_map/ppermute | solution.py:490
  76.4 31.5 %collective-permute-start.12 = (bf16[48,16384]{1,0:T(8,128)(2,1)}, bf16[48,16384]{1,0:T(8,128)(2,1)S(1)}, u32[]{:S(2)}, u32[]{:S(2)}) collective-permute-start(bf16[48,16384]{1,0:T(8,128)(2,1)} %collective-permute-done.5.refs_0_), channel_id=1, source_target_pairs={{0,1},{1,0},{2,3},{3,2},{4,5},{5,4},{6,7},{7,6},{8,9},{9,8},{10,11... | collective-permute-start | bytes 4718600 | tf_op jit(solution)/shard_map/ppermute | solution.py:490
  101.2 6.7 %collective-permute-start.13 = (bf16[48,16384]{1,0:T(8,128)(2,1)S(1)}, bf16[48,16384]{1,0:T(8,128)(2,1)S(1)}, u32[]{:S(2)}, u32[]{:S(2)}) collective-permute-start(bf16[48,16384]{1,0:T(8,128)(2,1)S(1)} %collective-permute-done.10.refs_2_), channel_id=1, source_target_pairs={{0,1},{1,0},{2,3},{3,2},{4,5},{5,4},{6,7},{7,6},{8,9},{9,8},{10,11... | collective-permute-start | bytes 4718600 | tf_op jit(solution)/shard_map/ppermute | solution.py:490
  101.2 22.6 %collective-permute-start.11 = (bf16[48,16384]{1,0:T(8,128)(2,1)S(1)}, bf16[48,16384]{1,0:T(8,128)(2,1)S(1)}, u32[]{:S(2)}, u32[]{:S(2)}) collective-permute-start(bf16[48,16384]{1,0:T(8,128)(2,1)S(1)} %collective-permute-done.10.refs_2_), channel_id=1, source_target_pairs={{0,4},{1,3},{4,8},{5,1},{8,12},{9,5},{12,14},{13,9},{14,10},{15,13... | collective-permute-start | bytes 4718600 | tf_op jit(solution)/shard_map/ppermute | solution.py:490
  106.6 24.0 %collective-permute-start.17 = (bf16[48,16384]{1,0:T(8,128)(2,1)S(1)}, bf16[48,16384]{1,0:T(8,128)(2,1)S(1)}, u32[]{:S(2)}, u32[]{:S(2)}) collective-permute-start(bf16[48,16384]{1,0:T(8,128)(2,1)S(1)} %collective-permute-done.6.refs_0_), channel_id=1, source_target_pairs={{0,1},{1,0},{2,3},{3,2},{4,5},{5,4},{6,7},{7,6},{8,9},{9,8},{10,11... | collective-permute-start | bytes 4718600 | tf_op jit(solution)/shard_map/ppermute | solution.py:490
  123.9 6.7 %collective-permute-start.18 = (bf16[48,16384]{1,0:T(8,128)(2,1)S(1)}, bf16[48,16384]{1,0:T(8,128)(2,1)S(1)}, u32[]{:S(2)}, u32[]{:S(2)}) collective-permute-start(bf16[48,16384]{1,0:T(8,128)(2,1)S(1)} %collective-permute-done.11.refs_1_.refs_2_), channel_id=1, source_target_pairs={{0,1},{1,0},{2,3},{3,2},{4,5},{5,4},{6,7},{7,6},{8,9},{9,8},{10,11... | collective-permute-start | bytes 4718600 | tf_op jit(solution)/shard_map/ppermute | solution.py:490
  126.5 12.2 %collective-permute-start.14 = (bf16[192,128]{1,0:T(8,128)(2,1)S(1)}, bf16[192,128]{1,0:T(8,128)(2,1)S(1)}, u32[]{:S(2)}, u32[]{:S(2)}) collective-permute-start(bf16[192,128]{1,0:T(8,128)(2,1)S(1)} %ranks.1), channel_id=1, source_target_pairs={{0,2},{1,3},{2,0},{3,1},{4,6},{5,7},{6,4},{7,5},{8,10},{9,11},{10,... | collective-permute-start | bytes 147464 | tf_op jit(solution)/shard_map/ppermute | solution.py:490
  129.0 9.7 %collective-permute-start.15 = (bf16[192,128]{1,0:T(8,128)(2,1)S(1)}, bf16[192,128]{1,0:T(8,128)(2,1)S(1)}, u32[]{:S(2)}, u32[]{:S(2)}) collective-permute-start(bf16[192,128]{1,0:T(8,128)(2,1)S(1)} %ranks.1), channel_id=1, source_target_pairs={{0,4},{1,5},{2,6},{3,7},{4,0},{5,1},{6,2},{7,3},{8,12},{9,13},{10,... | collective-permute-start | bytes 147464 | tf_op jit(solution)/shard_map/ppermute | solution.py:490
  130.6 8.1 %collective-permute-start.16 = (bf16[192,128]{1,0:T(8,128)(2,1)S(1)}, bf16[192,128]{1,0:T(8,128)(2,1)S(1)}, u32[]{:S(2)}, u32[]{:S(2)}) collective-permute-start(bf16[192,128]{1,0:T(8,128)(2,1)S(1)} %ranks.1), channel_id=1, source_target_pairs={{0,6},{1,7},{2,4},{3,5},{4,2},{5,3},{6,0},{7,1},{8,14},{9,15},{10,... | collective-permute-start | bytes 147464 | tf_op jit(solution)/shard_map/ppermute | solution.py:490
  138.7 8.7 %collective-permute-start.19 = (bf16[192,128]{1,0:T(8,128)(2,1)S(1)}, bf16[192,128]{1,0:T(8,128)(2,1)S(1)}, u32[]{:S(2)}, u32[]{:S(2)}) collective-permute-start(bf16[192,128]{1,0:T(8,128)(2,1)S(1)} %add_add_fusion), channel_id=1, source_target_pairs={{0,8},{1,9},{2,10},{3,11},{4,12},{5,13},{6,14},{7,15},{8,0},{9,1},... | collective-permute-start | bytes 147464 | tf_op jit(solution)/shard_map/ppermute | solution.py:490
  141.8 5.7 %collective-permute-start.20 = (bf16[192,128]{1,0:T(8,128)(2,1)S(1)}, bf16[192,128]{1,0:T(8,128)(2,1)S(1)}, u32[]{:S(2)}, u32[]{:S(2)}) collective-permute-start(bf16[192,128]{1,0:T(8,128)(2,1)S(1)} %add_add_fusion), channel_id=1, source_target_pairs={{0,1},{1,0},{2,3},{3,2},{4,5},{5,4},{6,7},{7,6},{8,9},{9,8},{10,11... | collective-permute-start | bytes 147464 | tf_op jit(solution)/shard_map/ppermute | solution.py:490
  141.8 5.7 %collective-permute-start.21 = (bf16[192,128]{1,0:T(8,128)(2,1)S(1)}, bf16[192,128]{1,0:T(8,128)(2,1)S(1)}, u32[]{:S(2)}, u32[]{:S(2)}) collective-permute-start(bf16[192,128]{1,0:T(8,128)(2,1)S(1)} %add_add_fusion), channel_id=1, source_target_pairs={{0,9},{1,8},{2,11},{3,10},{4,13},{5,12},{6,15},{7,14},{8,1},{9,0},... | collective-permute-start | bytes 147464 | tf_op jit(solution)/shard_map/ppermute | solution.py:490
  (9 other events, 51.7 us)

commit v12 on v10

--- a/solution.py
+++ b/solution.py
@@ -292,22 +292,24 @@
     return (2 * len(SNAKE), rows, cols)
 
 
-def some_ranks_kernel(x_ref, s_ref, out_ref):
-    out_ref[...] = lax.dot_general(x_ref[...], s_ref[...], NT, preferred_element_type=F32)
-
-
-def some_ranks(x, factor):
+def some_ranks_kernel(x_ref, *refs):
+    factors, out_ref = refs[:-1], refs[-1]
+    terms = [lax.dot_general(x_ref[...], ref[...], NT, preferred_element_type=F32) for ref in factors]
+    out_ref[...] = jnp.concatenate(terms, 1)
+
+
+def some_ranks(x, factors):
     whole = lambda shape: pl.BlockSpec(shape, lambda _: (0, 0))
-    shape = (x.shape[0], factor.shape[0])
+    shape = (x.shape[0], 2 * factors[0].shape[0])
     return pl.pallas_call(
         some_ranks_kernel,
         grid=(1,),
-        in_specs=[whole(x.shape), whole(factor.shape)],
+        in_specs=[whole(value.shape) for value in (x, *factors)],
         out_specs=whole(shape),
         out_shape=jax.ShapeDtypeStruct(shape, F32),
         compiler_params=PARAMS,
         name="some_ranks",
-    )(x, factor)
+    )(x, *factors)
 
 
 def rank_kernel(count, owners_ref, slot_ref, *refs):
@@ -337,82 +339,68 @@
 def rank_terms(owners, slots, xs, factors, hs):
     rank = factors[0].shape[0]
     core_rows = owners.shape[0] // 2 * xs[0].shape[0]
-    whole = lambda shape: pl.BlockSpec(shape, lambda _, *rest: (0, 0))
+    scalars, whole = pl.BlockSpec(memory_space=pltpu.SMEM), pl.BlockSpec(memory_space=pltpu.VMEM)
     return pl.pallas_call(
         functools.partial(rank_kernel, len(xs)),
-        grid_spec=pltpu.PrefetchScalarGridSpec(
-            num_scalar_prefetch=2,
-            grid=(1,),
-            in_specs=[whole(value.shape) for value in (*xs, *factors, *hs)],
-            out_specs=whole((core_rows // 2, 2 * rank)),
-            scratch_shapes=[pltpu.VMEM((core_rows, rank), F32)],
-        ),
+        in_specs=[scalars] * 2 + [whole] * (len(xs) + len(factors) + len(hs)),
+        out_specs=whole,
+        scratch_shapes=[pltpu.VMEM((core_rows, rank), F32)],
         out_shape=jax.ShapeDtypeStruct((core_rows // 2, 2 * rank), BF16),
         compiler_params=PARAMS,
         name="ranks",
     )(owners, slots, *xs, *factors, *hs)
 
 
-def block_finish_kernel(blocks, segments, places_ref, slot_ref, core_ref, *refs):
-    accs, refs = refs[:blocks], refs[blocks:]
-    expands, refs = refs[:segments], refs[segments:]
-    scale_ref, mine_ref, other_ref, cos_ref, sin_ref, out_ref, h, update = refs
+def block_finish_kernel(places_ref, slot_ref, core_ref, total_ref, expand_ref, scale_ref, mine_ref, other_ref, *refs):
+    cos_ref, sin_ref, out_ref, h, update, done, sems = refs
+    blocks, rows, cols = total_ref.shape
     rank = mine_ref.shape[1] // 2
-    rows = accs[0].shape[1]
-    first = pl.program_id(0) == 0
     even = core_ref[0] == 0
-    mine, other = (jnp.where(first, ref[:, :rank], ref[:, rank:]) for ref in (mine_ref, other_ref))
+    mine, other = mine_ref[...], other_ref[...]
     for core, terms in enumerate((jnp.where(even, mine, other), jnp.where(even, other, mine))):
-        for i in range(blocks // 2):
-            at = (2 * i + core) * rows
-            h[at : at + rows, :] = terms[i * rows : (i + 1) * rows]
-    for segment in range(segments):
+        for chip in range(blocks // 2):
+            side, at = divmod(chip * rows, terms.shape[0])
+            to = (2 * chip + core) * rows
+            h[to : to + rows, :] = terms[at : at + rows, side * rank : (side + 1) * rank]
+    for segment in range(h.shape[0] // SEG):
         cut = slice(segment * SEG, (segment + 1) * SEG)
-        update[cut, :] = jnp.dot(h[cut, :], expands[segment][0], preferred_element_type=F32)
+        expand = expand_ref[slot_ref[segment]]
+        update[cut, :] = jnp.dot(h[cut, :], expand, preferred_element_type=F32)
+    copies = []
     for block in range(blocks):
         at = slice(block * rows, (block + 1) * rows)
         cosine, sine = cos_ref[at, :], sin_ref[at, :]
-        for head in range(out_ref.shape[1] // HD):
-            cut = slice(head * HD, (head + 1) * HD)
-            value = accs[block][0, :, cut] * scale_ref[:, cut] + update[at, cut]
-            out_ref[at, cut] = rotate(value, cosine, sine).astype(out_ref.dtype)
+        place = places_ref[block]
+        for left in range(0, cols, HD):
+            cut = slice(left, left + HD)
+            value = total_ref[place, :, cut] * scale_ref[:, cut] + update[at, cut]
+            done[at, cut] = rotate(value, cosine, sine).astype(done.dtype)
+        if block % 2:
+            strip = pl.ds((block - 1) * rows, 2 * rows)
+            copies.append(pltpu.make_async_copy(done.at[strip], out_ref.at[strip], sems.at[block // 2]))
+            copies[-1].start()
+    for copy in copies:
+        copy.wait()
 
 
 def block_finish(places, slots, core, total, expands, scale, mine, other, cosine, sine):
     blocks, rows, cols = total.shape
-    half = blocks // 2
-    half_rows = half * rows
-    segments = half_rows // SEG
     rank = expands.shape[1]
-
-    def acc_at(i):
-        return pl.BlockSpec((1, rows, cols), lambda g, places, *_: (places[g * half + i], 0, 0))
-
-    def expand_at(i):
-        return pl.BlockSpec((1, rank, cols), lambda g, places, slots, _: (slots[g * segments + i], 0, 0))
-
-    half_of = lambda width: pl.BlockSpec((half_rows, width), lambda g, *_: (g, 0))
+    scalars, whole = pl.BlockSpec(memory_space=pltpu.SMEM), pl.BlockSpec(memory_space=pltpu.VMEM)
     return pl.pallas_call(
-        functools.partial(block_finish_kernel, half, segments),
-        grid_spec=pltpu.PrefetchScalarGridSpec(
-            num_scalar_prefetch=3,
-            grid=(2,),
-            in_specs=[acc_at(i) for i in range(half)]
-            + [expand_at(i) for i in range(segments)]
-            + [
-                pl.BlockSpec((1, cols), lambda g, *_: (0, 0)),
-                pl.BlockSpec(mine.shape, lambda g, *_: (0, 0)),
-                pl.BlockSpec(other.shape, lambda g, *_: (0, 0)),
-                half_of(HD),
-                half_of(HD),
-            ],
-            out_specs=half_of(cols),
-            scratch_shapes=[pltpu.VMEM((half_rows, rank), BF16), pltpu.VMEM((half_rows, cols), F32)],
-        ),
+        block_finish_kernel,
+        in_specs=[scalars] * 3 + [whole] * 7,
+        out_specs=pl.BlockSpec(memory_space=pl.ANY),
+        scratch_shapes=[
+            pltpu.VMEM((blocks * rows, rank), BF16),
+            pltpu.VMEM((blocks * rows, cols), F32),
+            pltpu.VMEM((blocks * rows, cols), BF16),
+            pltpu.SemaphoreType.DMA((blocks // 2,)),
+        ],
         out_shape=jax.ShapeDtypeStruct((blocks * rows, cols), BF16),
         compiler_params=PARAMS,
         name="finish",
-    )(places, slots, core, *([total] * half), *([expands] * segments), scale, mine, other, cosine, sine)
+    )(places, slots, core, total, expands, scale, mine, other, cosine, sine)
 
 
 def ring_plan(parts, tokens, weights, scale, shrinks, expands, indices):
@@ -435,12 +423,12 @@
 
     streams = [send(tokens, out), None]
     own, factors = [tokens, swap(tokens)], [shrinks[0], swap(shrinks[0])]
-    mine = some_ranks(tokens, factors[0])
-    second, mine = lax.optimization_barrier((tokens, mine))
+    part = 2 * tile
+    total, _ = block_product(own, weights, factors, 0, part, tile, None, 0, False)
+    second, total = lax.optimization_barrier((tokens, total))
     streams[1] = send(second, home)
-    total, _ = block_product(own, weights, factors, 0, depth, tile, None, 0, False)
-    mine = jnp.concatenate([mine, some_ranks(tokens, factors[1])], 1)
-    hs, total = lax.optimization_barrier(([mine], total))
+    total, _ = block_product(own, weights, factors, part, depth, tile, total, 0, False)
+    hs, total = lax.optimization_barrier(([some_ranks(tokens, factors)], total))
     counts.append(len(own))
 
     def make_tables(me, indices):

time: 157 us -> 151 us (0.962)
  waiting for transfers between devices: 46.4 us -> 36.6 us
  starting transfers between devices: 21.5 us -> 26.9 us
  local copies, waits for them, and re-layouts: 8.52 us -> 6.94 us
    ppermute x22, waiting for transfers between devices: 46.4 us -> 36.6 us  [ring_plan(): send = lambda value, pairs: lax.ppermute(value, 'tensor', pairs)]
    ppermute x22, starting transfers between devices: 21.5 us -> 26.9 us  [ring_plan(): send = lambda value, pairs: lax.ppermute(value, 'tensor', pairs)]
    pallas_call x4 -> x3, Pallas kernels: 10.4 us -> 8.54 us  [the longest x1 3.45 us: some_ranks(): pl.pallas_call(some_ranks_kernel, grid=(1,), in_specs=[whole(value.shape)...]
    pallas_call x6 -> x7, Pallas kernels: 66.9 us -> 68.7 us  [block_product(): pl.pallas_call(functools.partial(block_kernel, count, low, tile, steps, f...]
    unnamed x24, local copies, waits for them, and re-layouts: 6.4 us -> 4.81 us
  transfers between devices with their start and end apart: 22 -> 22, of which waited for: 6 -> 6; matrix products, arithmetic and copies ran while one was open for 3% -> 3% of each run, Pallas kernels for 48% -> 50%
where the time goes in v12:
time: 151 us; the launch traced here: 150 us
  Pallas kernels  77.3 us (51%)
  waiting for transfers between devices  36.6 us (24%)
  starting transfers between devices  26.9 us (18%)
  local copies, waits for them, and re-layouts  6.94 us (5%)
  other arithmetic  2.14 us (1%)
    pallas_call x7, Pallas kernels, block_product(): pl.pallas_call(functools.partial(block_kernel, count, low, tile, steps, f...  68.7 us
    ppermute x22, waiting for transfers between devices, ring_plan(): send = lambda value, pairs: lax.ppermute(value, 'tensor', pairs)  36.6 us
    ppermute x22, starting transfers between devices, ring_plan(): send = lambda value, pairs: lax.ppermute(value, 'tensor', pairs)  26.9 us
    unnamed x24, local copies, waits for them, and re-layouts  4.81 us
    pallas_call x1, Pallas kernels, some_ranks(): pl.pallas_call(some_ranks_kernel, grid=(1,), in_specs=[whole(value.shape)...  3.45 us
  transfers between devices with their start and end apart: 22, of which 6 were waited for; matrix products, arithmetic and copies ran while one was open for 3% of the time, Pallas kernels for 50%

profile of v12, /device:TPU:0, one launch (start us, length us, event | category | flops | bytes accessed | tf_op | source)
XLA Modules:
  0.0 150.4 jit_solution(6354766944941740242)
XLA Ops:
  0.5 3.0 %collective-permute-start = (bf16[48,16384]{1,0:T(8,128)(2,1)}, bf16[48,16384]{1,0:T(8,128)(2,1)}, u32[]{:S(2)}, u32[]{:S(2)}) collective-permute-start(bf16[48,16384]{1,0:T(8,128)(2,1)} %refs_0_.3), channel_id=1, source_target_pairs={{0,4},{1,3},{4,8},{5,1},{8,12},{9,5},{12,14},{13,9},{14,10},{15,13... | collective-permute-start | bytes 4718600 | tf_op jit(solution)/shard_map/ppermute | solution.py:411
  3.5 3.2 %collective-permute-done.2.refs_1_ = bf16[48,16384]{1,0:T(8,128)(2,1)S(1)} collective-permute-done((bf16[48,16384]{1,0:T(8,128)(2,1)}, bf16[48,16384]{1,0:T(8,128)(2,1)S(1)}, u32[]{:S(2)}, u32[]{:S(2)}) %collective-permute-start.2) | collective-permute-done | bytes 1572896 | tf_op jit(solution)/shard_map/ppermute | solution.py:411
  6.7 3.1 %blocks.7.refs_3_ = f32[16,48,1024]{2,1,0:T(8,128)S(1)} custom-call(bf16[48,16384]{1,0:T(8,128)(2,1)} %refs_0_.3, bf16[48,16384]{1,0:T(8,128)(2,1)S(1)} %collective-permute-done.2.refs_1_, bf16[16384,1024]{1,0:T(8,128)(2,1)} %refs_4_.7), custom_call_target="tpu_custom_call" | custom-call | flops 402653184 | bytes 4194304 | tf_op jit(solution)/shard_map/blocks/pallas_call | solution.py:265
  9.8 2.9 %collective-permute-start.4 = (bf16[48,16384]{1,0:T(8,128)(2,1)}, bf16[48,16384]{1,0:T(8,128)(2,1)}, u32[]{:S(2)}, u32[]{:S(2)}) collective-permute-start(bf16[48,16384]{1,0:T(8,128)(2,1)} %refs_0_.3), channel_id=1, source_target_pairs={{0,2},{1,5},{4,0},{5,9},{8,4},{9,13},{12,8},{13,15},{14,12},{15,11... | collective-permute-start | bytes 4718600 | tf_op jit(solution)/shard_map/ppermute | solution.py:411
  12.8 10.9 %blocks.8.refs_5_ = f32[16,48,1024]{2,1,0:T(8,128)S(1)} custom-call(bf16[48,16384]{1,0:T(8,128)(2,1)} %refs_0_.3, bf16[48,16384]{1,0:T(8,128)(2,1)S(1)} %collective-permute-done.2.refs_1_, bf16[16384,1024]{1,0:T(8,128)(2,1)} %refs_4_.7, f32[16,48,1024]{2,1,0:T(8,128)S(1)} %blocks.7.refs_3_), custom_call_target="tpu_custom_call", output_to_operand_aliasing={{}: (3, {})} | custom-call | flops 2818572288 | bytes 29360128 | tf_op jit(solution)/shard_map/blocks/pallas_call | solution.py:265
  23.7 3.5 %some_ranks.1.refs_4_ = f32[48,128]{1,0:T(8,128)S(1)} custom-call(bf16[48,16384]{1,0:T(8,128)(2,1)} %refs_0_.3, bf16[64,16384]{1,0:T(8,128)(2,1)S(1)} %bitcast.15, bf16[64,16384]{1,0:T(8,128)(2,1)S(1)} %collective-permute-done.1.refs_1_.refs_4_.refs_6_.refs_3_), custom_call_target="tpu_custom_call" | custom-call | tf_op jit(solution)/shard_map/some_ranks/pallas_call | solution.py:304
  27.2 3.0 %collective-permute-done.refs_0_ = bf16[48,16384]{1,0:T(8,128)(2,1)} collective-permute-done((bf16[48,16384]{1,0:T(8,128)(2,1)}, bf16[48,16384]{1,0:T(8,128)(2,1)}, u32[]{:S(2)}, u32[]{:S(2)}) %collective-permute-start) | collective-permute-done | bytes 1572896 | tf_op jit(solution)/shard_map/ppermute | solution.py:411
  30.2 2.4 %collective-permute-start.8 = (bf16[48,16384]{1,0:T(8,128)(2,1)}, bf16[48,16384]{1,0:T(8,128)(2,1)}, u32[]{:S(2)}, u32[]{:S(2)}) collective-permute-start(bf16[48,16384]{1,0:T(8,128)(2,1)} %collective-permute-done.refs_0_), channel_id=1, source_target_pairs={{0,4},{1,3},{4,8},{5,1},{8,12},{9,5},{12,14},{13,9},{14,10},{15,13... | collective-permute-start | bytes 4718600 | tf_op jit(solution)/shard_map/ppermute | solution.py:411
  32.7 9.9 %collective-permute-done.4.refs_0_ = bf16[48,16384]{1,0:T(8,128)(2,1)} collective-permute-done((bf16[48,16384]{1,0:T(8,128)(2,1)}, bf16[48,16384]{1,0:T(8,128)(2,1)}, u32[]{:S(2)}, u32[]{:S(2)}) %collective-permute-start.4) | collective-permute-done | bytes 1572896 | tf_op jit(solution)/shard_map/ppermute | solution.py:411
  42.6 1.7 %collective-permute-start.5 = (bf16[48,16384]{1,0:T(8,128)(2,1)}, bf16[48,16384]{1,0:T(8,128)(2,1)}, u32[]{:S(2)}, u32[]{:S(2)}) collective-permute-start(bf16[48,16384]{1,0:T(8,128)(2,1)} %collective-permute-done.4.refs_0_), channel_id=1, source_target_pairs={{0,2},{1,5},{4,0},{5,9},{8,4},{9,13},{12,8},{13,15},{14,12},{15,11... | collective-permute-start | bytes 4718600 | tf_op jit(solution)/shard_map/ppermute | solution.py:411
  48.7 12.6 %blocks.9 = (f32[16,48,1024]{2,1,0:T(8,128)S(1)}, f32[48,128]{1,0:T(8,128)S(1)}) custom-call(bf16[48,16384]{1,0:T(8,128)(2,1)} %collective-permute-done.refs_0_, bf16[48,16384]{1,0:T(8,128)(2,1)} %collective-permute-done.3.refs_1_, bf16[16384,1024]{1,0:T(8,128)(2,1)} %refs_4_.7, bf16[64,16384]{1,0:T(8,128)(2,1)S(1)} %bitcast.16, ...), custom_call_target="tpu_custom_call", output_to_operand_aliasing={{0}: (5, {})} | custom-call | flops 3221225472 | bytes 33554432 | tf_op jit(solution)/shard_map/blocks/pallas_call | solution.py:265
  67.3 8.0 %collective-permute-done.5.refs_0_ = bf16[48,16384]{1,0:T(8,128)(2,1)} collective-permute-done((bf16[48,16384]{1,0:T(8,128)(2,1)}, bf16[48,16384]{1,0:T(8,128)(2,1)}, u32[]{:S(2)}, u32[]{:S(2)}) %collective-permute-start.5) | collective-permute-done | bytes 1572896 | tf_op jit(solution)/shard_map/ppermute | solution.py:411
  75.2 1.8 %collective-permute-start.6 = (bf16[48,16384]{1,0:T(8,128)(2,1)}, bf16[48,16384]{1,0:T(8,128)(2,1)S(1)}, u32[]{:S(2)}, u32[]{:S(2)}) collective-permute-start(bf16[48,16384]{1,0:T(8,128)(2,1)} %collective-permute-done.5.refs_0_), channel_id=1, source_target_pairs={{0,2},{1,5},{4,0},{5,9},{8,4},{9,13},{12,8},{13,15},{14,12},{15,11... | collective-permute-start | bytes 4718600 | tf_op jit(solution)/shard_map/ppermute | solution.py:411
  79.8 13.6 %blocks.10 = (f32[16,48,1024]{2,1,0:T(8,128)S(1)}, f32[96,128]{1,0:T(8,128)S(1)}) custom-call(bf16[48,16384]{1,0:T(8,128)(2,1)} %collective-permute-done.4.refs_0_, bf16[48,16384]{1,0:T(8,128)(2,1)} %collective-permute-done.7.refs_1_, bf16[48,16384]{1,0:T(8,128)(2,1)} %collective-permute-done.8.refs_2_, ...), custom_call_target="tpu_custom_call", output_to_operand_aliasing={{0}: (7, {})} | custom-call | flops 6442450944 | bytes 33554432 | tf_op jit(solution)/shard_map/blocks/pallas_call | solution.py:265
  93.4 6.1 %collective-permute-done.10.refs_2_ = bf16[48,16384]{1,0:T(8,128)(2,1)S(1)} collective-permute-done((bf16[48,16384]{1,0:T(8,128)(2,1)}, bf16[48,16384]{1,0:T(8,128)(2,1)S(1)}, u32[]{:S(2)}, u32[]{:S(2)}) %collective-permute-start.10) | collective-permute-done | bytes 1572896 | tf_op jit(solution)/shard_map/ppermute | solution.py:411
  99.5 2.4 %collective-permute-start.11 = (bf16[48,16384]{1,0:T(8,128)(2,1)S(1)}, bf16[48,16384]{1,0:T(8,128)(2,1)S(1)}, u32[]{:S(2)}, u32[]{:S(2)}) collective-permute-start(bf16[48,16384]{1,0:T(8,128)(2,1)S(1)} %collective-permute-done.10.refs_2_), channel_id=1, source_target_pairs={{0,4},{1,3},{4,8},{5,1},{8,12},{9,5},{12,14},{13,9},{14,10},{15,13... | collective-permute-start | bytes 4718600 | tf_op jit(solution)/shard_map/ppermute | solution.py:411
  101.8 6.5 %collective-permute-done.6.refs_0_ = bf16[48,16384]{1,0:T(8,128)(2,1)S(1)} collective-permute-done((bf16[48,16384]{1,0:T(8,128)(2,1)}, bf16[48,16384]{1,0:T(8,128)(2,1)S(1)}, u32[]{:S(2)}, u32[]{:S(2)}) %collective-permute-start.6) | collective-permute-done | bytes 1572896 | tf_op jit(solution)/shard_map/ppermute | solution.py:411
  109.5 14.0 %blocks.11 = (f32[16,48,1024]{2,1,0:T(8,128)S(1)}, f32[96,128]{1,0:T(8,128)S(1)}) custom-call(bf16[48,16384]{1,0:T(8,128)(2,1)} %collective-permute-done.5.refs_0_, bf16[48,16384]{1,0:T(8,128)(2,1)S(1)} %collective-permute-done.12.refs_1_, bf16[48,16384]{1,0:T(8,128)(2,1)S(1)} %collective-permute-done.10.refs_2_, ...), custom_call_target="tpu_custom_call", output_to_operand_aliasing={{0}: (7, {})} | custom-call | flops 6442450944 | bytes 33554432 | tf_op jit(solution)/shard_map/blocks/pallas_call | solution.py:265
  123.6 2.5 %ranks.1 = bf16[192,128]{1,0:T(8,128)(2,1)S(1)} custom-call(s32[16]{0:T(128)S(1)} %get-tuple-element.63.owners_ref, s32[8]{0:T(128)S(1)} %pad_add_fusion.slot_ref, bf16[48,16384]{1,0:T(8,128)(2,1)S(1)} %collective-permute-done.6.refs_0_, bf16[48,16384]{1,0:T(8,128)(2,1)S(1)} %collective-permute-done.11.refs_1_.refs_2_, bf16[64,16384]{1,0:T(8,128)(2,1)S(1)} %bitcast.19, ...), custom_call_target="tpu_custom_call" | custom-call | tf_op jit(solution)/shard_map/ranks/pallas_call | solution.py:343
  126.1 2.1 %collective-permute-start.14 = (bf16[192,128]{1,0:T(8,128)(2,1)S(1)}, bf16[192,128]{1,0:T(8,128)(2,1)S(1)}, u32[]{:S(2)}, u32[]{:S(2)}) collective-permute-start(bf16[192,128]{1,0:T(8,128)(2,1)S(1)} %ranks.1), channel_id=1, source_target_pairs={{0,2},{1,3},{2,0},{3,1},{4,6},{5,7},{6,4},{7,5},{8,10},{9,11},{10,... | collective-permute-start | bytes 147464 | tf_op jit(solution)/shard_map/ppermute | solution.py:411
  129.8 7.1 %blocks.12.refs_5_ = f32[16,48,1024]{2,1,0:T(8,128)S(1)} custom-call(bf16[48,16384]{1,0:T(8,128)(2,1)S(1)} %collective-permute-done.6.refs_0_, bf16[48,16384]{1,0:T(8,128)(2,1)S(1)} %collective-permute-done.17.refs_1_, bf16[48,16384]{1,0:T(8,128)(2,1)S(1)} %collective-permute-done.11.refs_1_.refs_2_, ...), custom_call_target="tpu_custom_call", output_to_operand_aliasing={{}: (5, {})} | custom-call | flops 3221225472 | bytes 16777216 | tf_op jit(solution)/shard_map/blocks/pallas_call | solution.py:265
  137.0 3.0 %collective-permute-start.19 = (bf16[192,128]{1,0:T(8,128)(2,1)S(1)}, bf16[192,128]{1,0:T(8,128)(2,1)S(1)}, u32[]{:S(2)}, u32[]{:S(2)}) collective-permute-start(bf16[192,128]{1,0:T(8,128)(2,1)S(1)} %add_add_fusion), channel_id=1, source_target_pairs={{0,8},{1,9},{2,10},{3,11},{4,12},{5,13},{6,14},{7,15},{8,0},{9,1},... | collective-permute-start | bytes 147464 | tf_op jit(solution)/shard_map/ppermute | solution.py:411
  140.2 7.3 %blocks.13.total_ref = f32[16,48,1024]{2,1,0:T(8,128)S(1)} custom-call(bf16[48,16384]{1,0:T(8,128)(2,1)S(1)} %collective-permute-done.6.refs_0_, bf16[48,16384]{1,0:T(8,128)(2,1)S(1)} %collective-permute-done.17.refs_1_, bf16[48,16384]{1,0:T(8,128)(2,1)S(1)} %collective-permute-done.11.refs_1_.refs_2_, ...), custom_call_target="tpu_custom_call", output_to_operand_aliasing={{}: (5, {})} | custom-call | flops 3221225472 | bytes 16777216 | tf_op jit(solution)/shard_map/blocks/pallas_call | solution.py:265
  147.7 2.6 %finish.1 = bf16[768,1024]{1,0:T(8,128)(2,1)} custom-call(s32[16]{0:T(128)S(1)} %get-tuple-element.60.places_ref, s32[6]{0:T(128)S(1)} %gather_fusion, s32[1]{0:T(128)} %bitcast.7.core_ref, f32[16,48,1024]{2,1,0:T(8,128)S(1)} %blocks.13.total_ref, bf16[16,64,1024]{2,1,0:T(8,128)(2,1)S(1)} %bitcast.20, f32[1,1024]{1,0:T(1,128)S(1)} %bitcast.21, ...), custom_call_target="tpu_custom_call" | custom-call | tf_op jit(solution)/shard_map/finish/pallas_call | solution.py:390
  (69 shorter events, 16.8 us)
Async XLA Ops:
  0.0 62.3 %copy-start = (s32[16]{0:T(128)S(1)}, s32[16]{0:T(128)}, u32[]{:S(2)}) copy-start(s32[16]{0:T(128)} %param.16) | copy-start | bytes 196
  0.0 23.7 %collective-permute-start.1 = (bf16[64,16384]{1,0:T(8,128)(2,1)}, bf16[64,16384]{1,0:T(8,128)(2,1)S(1)}, u32[]{:S(2)}, u32[]{:S(2)}) collective-permute-start(bf16[64,16384]{1,0:T(8,128)(2,1)} %bitcast.14), channel_id=1, source_target_pairs={{0,1},{1,0},{2,3},{3,2},{4,5},{5,4},{6,7},{7,6},{8,9},{9,8},{10,11... | collective-permute-start | bytes 6291464 | tf_op jit(solution)/shard_map/ppermute | solution.py:411
  0.5 6.2 %collective-permute-start.2 = (bf16[48,16384]{1,0:T(8,128)(2,1)}, bf16[48,16384]{1,0:T(8,128)(2,1)S(1)}, u32[]{:S(2)}, u32[]{:S(2)}) collective-permute-start(bf16[48,16384]{1,0:T(8,128)(2,1)} %refs_0_.3), channel_id=1, source_target_pairs={{0,1},{1,0},{2,3},{3,2},{4,5},{5,4},{6,7},{7,6},{8,9},{9,8},{10,11... | collective-permute-start | bytes 4718600 | tf_op jit(solution)/shard_map/ppermute | solution.py:411
  0.5 29.7 %collective-permute-start = (bf16[48,16384]{1,0:T(8,128)(2,1)}, bf16[48,16384]{1,0:T(8,128)(2,1)}, u32[]{:S(2)}, u32[]{:S(2)}) collective-permute-start(bf16[48,16384]{1,0:T(8,128)(2,1)} %refs_0_.3), channel_id=1, source_target_pairs={{0,4},{1,3},{4,8},{5,1},{8,12},{9,5},{12,14},{13,9},{14,10},{15,13... | collective-permute-start | bytes 4718600 | tf_op jit(solution)/shard_map/ppermute | solution.py:411
  9.8 32.7 %collective-permute-start.4 = (bf16[48,16384]{1,0:T(8,128)(2,1)}, bf16[48,16384]{1,0:T(8,128)(2,1)}, u32[]{:S(2)}, u32[]{:S(2)}) collective-permute-start(bf16[48,16384]{1,0:T(8,128)(2,1)} %refs_0_.3), channel_id=1, source_target_pairs={{0,2},{1,5},{4,0},{5,9},{8,4},{9,13},{12,8},{13,15},{14,12},{15,11... | collective-permute-start | bytes 4718600 | tf_op jit(solution)/shard_map/ppermute | solution.py:411
  30.2 15.2 %collective-permute-start.3 = (bf16[48,16384]{1,0:T(8,128)(2,1)}, bf16[48,16384]{1,0:T(8,128)(2,1)}, u32[]{:S(2)}, u32[]{:S(2)}) collective-permute-start(bf16[48,16384]{1,0:T(8,128)(2,1)} %collective-permute-done.refs_0_), channel_id=1, source_target_pairs={{0,1},{1,0},{2,3},{3,2},{4,5},{5,4},{6,7},{7,6},{8,9},{9,8},{10,11... | collective-permute-start | bytes 4718600 | tf_op jit(solution)/shard_map/ppermute | solution.py:411
  30.2 31.1 %copy-start.11 = (s32[8]{0:T(128)S(1)}, s32[8]{0:T(128)}, u32[]{:S(2)}) copy-start(s32[8]{0:T(128)} %param.17) | copy-start | bytes 100
  30.2 35.3 %collective-permute-start.8 = (bf16[48,16384]{1,0:T(8,128)(2,1)}, bf16[48,16384]{1,0:T(8,128)(2,1)}, u32[]{:S(2)}, u32[]{:S(2)}) collective-permute-start(bf16[48,16384]{1,0:T(8,128)(2,1)} %collective-permute-done.refs_0_), channel_id=1, source_target_pairs={{0,4},{1,3},{4,8},{5,1},{8,12},{9,5},{12,14},{13,9},{14,10},{15,13... | collective-permute-start | bytes 4718600 | tf_op jit(solution)/shard_map/ppermute | solution.py:411
  42.6 32.7 %collective-permute-start.5 = (bf16[48,16384]{1,0:T(8,128)(2,1)}, bf16[48,16384]{1,0:T(8,128)(2,1)}, u32[]{:S(2)}, u32[]{:S(2)}) collective-permute-start(bf16[48,16384]{1,0:T(8,128)(2,1)} %collective-permute-done.4.refs_0_), channel_id=1, source_target_pairs={{0,2},{1,5},{4,0},{5,9},{8,4},{9,13},{12,8},{13,15},{14,12},{15,11... | collective-permute-start | bytes 4718600 | tf_op jit(solution)/shard_map/ppermute | solution.py:411
  44.2 33.9 %collective-permute-start.7 = (bf16[48,16384]{1,0:T(8,128)(2,1)}, bf16[48,16384]{1,0:T(8,128)(2,1)}, u32[]{:S(2)}, u32[]{:S(2)}) collective-permute-start(bf16[48,16384]{1,0:T(8,128)(2,1)} %collective-permute-done.4.refs_0_), channel_id=1, source_target_pairs={{0,1},{1,0},{2,3},{3,2},{4,5},{5,4},{6,7},{7,6},{8,9},{9,8},{10,11... | collective-permute-start | bytes 4718600 | tf_op jit(solution)/shard_map/ppermute | solution.py:411
  65.6 12.6 %collective-permute-start.9 = (bf16[48,16384]{1,0:T(8,128)(2,1)}, bf16[48,16384]{1,0:T(8,128)(2,1)S(1)}, u32[]{:S(2)}, u32[]{:S(2)}) collective-permute-start(bf16[48,16384]{1,0:T(8,128)(2,1)} %collective-permute-done.8.refs_2_), channel_id=1, source_target_pairs={{0,1},{1,0},{2,3},{3,2},{4,5},{5,4},{6,7},{7,6},{8,9},{9,8},{10,11... | collective-permute-start | bytes 4718600 | tf_op jit(solution)/shard_map/ppermute | solution.py:411
  65.7 33.8 %collective-permute-start.10 = (bf16[48,16384]{1,0:T(8,128)(2,1)}, bf16[48,16384]{1,0:T(8,128)(2,1)S(1)}, u32[]{:S(2)}, u32[]{:S(2)}) collective-permute-start(bf16[48,16384]{1,0:T(8,128)(2,1)} %collective-permute-done.8.refs_2_), channel_id=1, source_target_pairs={{0,4},{1,3},{4,8},{5,1},{8,12},{9,5},{12,14},{13,9},{14,10},{15,13... | collective-permute-start | bytes 4718600 | tf_op jit(solution)/shard_map/ppermute | solution.py:411
  75.2 33.1 %collective-permute-start.6 = (bf16[48,16384]{1,0:T(8,128)(2,1)}, bf16[48,16384]{1,0:T(8,128)(2,1)S(1)}, u32[]{:S(2)}, u32[]{:S(2)}) collective-permute-start(bf16[48,16384]{1,0:T(8,128)(2,1)} %collective-permute-done.5.refs_0_), channel_id=1, source_target_pairs={{0,2},{1,5},{4,0},{5,9},{8,4},{9,13},{12,8},{13,15},{14,12},{15,11... | collective-permute-start | bytes 4718600 | tf_op jit(solution)/shard_map/ppermute | solution.py:411
  77.1 32.4 %collective-permute-start.12 = (bf16[48,16384]{1,0:T(8,128)(2,1)}, bf16[48,16384]{1,0:T(8,128)(2,1)S(1)}, u32[]{:S(2)}, u32[]{:S(2)}) collective-permute-start(bf16[48,16384]{1,0:T(8,128)(2,1)} %collective-permute-done.5.refs_0_), channel_id=1, source_target_pairs={{0,1},{1,0},{2,3},{3,2},{4,5},{5,4},{6,7},{7,6},{8,9},{9,8},{10,11... | collective-permute-start | bytes 4718600 | tf_op jit(solution)/shard_map/ppermute | solution.py:411
  99.5 10.0 %collective-permute-start.13 = (bf16[48,16384]{1,0:T(8,128)(2,1)S(1)}, bf16[48,16384]{1,0:T(8,128)(2,1)S(1)}, u32[]{:S(2)}, u32[]{:S(2)}) collective-permute-start(bf16[48,16384]{1,0:T(8,128)(2,1)S(1)} %collective-permute-done.10.refs_2_), channel_id=1, source_target_pairs={{0,1},{1,0},{2,3},{3,2},{4,5},{5,4},{6,7},{7,6},{8,9},{9,8},{10,11... | collective-permute-start | bytes 4718600 | tf_op jit(solution)/shard_map/ppermute | solution.py:411
  99.5 24.0 %collective-permute-start.11 = (bf16[48,16384]{1,0:T(8,128)(2,1)S(1)}, bf16[48,16384]{1,0:T(8,128)(2,1)S(1)}, u32[]{:S(2)}, u32[]{:S(2)}) collective-permute-start(bf16[48,16384]{1,0:T(8,128)(2,1)S(1)} %collective-permute-done.10.refs_2_), channel_id=1, source_target_pairs={{0,4},{1,3},{4,8},{5,1},{8,12},{9,5},{12,14},{13,9},{14,10},{15,13... | collective-permute-start | bytes 4718600 | tf_op jit(solution)/shard_map/ppermute | solution.py:411
  108.3 21.5 %collective-permute-start.17 = (bf16[48,16384]{1,0:T(8,128)(2,1)S(1)}, bf16[48,16384]{1,0:T(8,128)(2,1)S(1)}, u32[]{:S(2)}, u32[]{:S(2)}) collective-permute-start(bf16[48,16384]{1,0:T(8,128)(2,1)S(1)} %collective-permute-done.6.refs_0_), channel_id=1, source_target_pairs={{0,1},{1,0},{2,3},{3,2},{4,5},{5,4},{6,7},{7,6},{8,9},{9,8},{10,11... | collective-permute-start | bytes 4718600 | tf_op jit(solution)/shard_map/ppermute | solution.py:411
  123.5 6.3 %collective-permute-start.18 = (bf16[48,16384]{1,0:T(8,128)(2,1)S(1)}, bf16[48,16384]{1,0:T(8,128)(2,1)S(1)}, u32[]{:S(2)}, u32[]{:S(2)}) collective-permute-start(bf16[48,16384]{1,0:T(8,128)(2,1)S(1)} %collective-permute-done.11.refs_1_.refs_2_), channel_id=1, source_target_pairs={{0,1},{1,0},{2,3},{3,2},{4,5},{5,4},{6,7},{7,6},{8,9},{9,8},{10,11... | collective-permute-start | bytes 4718600 | tf_op jit(solution)/shard_map/ppermute | solution.py:411
  126.1 10.8 %collective-permute-start.14 = (bf16[192,128]{1,0:T(8,128)(2,1)S(1)}, bf16[192,128]{1,0:T(8,128)(2,1)S(1)}, u32[]{:S(2)}, u32[]{:S(2)}) collective-permute-start(bf16[192,128]{1,0:T(8,128)(2,1)S(1)} %ranks.1), channel_id=1, source_target_pairs={{0,2},{1,3},{2,0},{3,1},{4,6},{5,7},{6,4},{7,5},{8,10},{9,11},{10,... | collective-permute-start | bytes 147464 | tf_op jit(solution)/shard_map/ppermute | solution.py:411
  128.2 8.8 %collective-permute-start.15 = (bf16[192,128]{1,0:T(8,128)(2,1)S(1)}, bf16[192,128]{1,0:T(8,128)(2,1)S(1)}, u32[]{:S(2)}, u32[]{:S(2)}) collective-permute-start(bf16[192,128]{1,0:T(8,128)(2,1)S(1)} %ranks.1), channel_id=1, source_target_pairs={{0,4},{1,5},{2,6},{3,7},{4,0},{5,1},{6,2},{7,3},{8,12},{9,13},{10,... | collective-permute-start | bytes 147464 | tf_op jit(solution)/shard_map/ppermute | solution.py:411
  129.8 7.2 %collective-permute-start.16 = (bf16[192,128]{1,0:T(8,128)(2,1)S(1)}, bf16[192,128]{1,0:T(8,128)(2,1)S(1)}, u32[]{:S(2)}, u32[]{:S(2)}) collective-permute-start(bf16[192,128]{1,0:T(8,128)(2,1)S(1)} %ranks.1), channel_id=1, source_target_pairs={{0,6},{1,7},{2,4},{3,5},{4,2},{5,3},{6,0},{7,1},{8,14},{9,15},{10,... | collective-permute-start | bytes 147464 | tf_op jit(solution)/shard_map/ppermute | solution.py:411
  137.0 10.5 %collective-permute-start.19 = (bf16[192,128]{1,0:T(8,128)(2,1)S(1)}, bf16[192,128]{1,0:T(8,128)(2,1)S(1)}, u32[]{:S(2)}, u32[]{:S(2)}) collective-permute-start(bf16[192,128]{1,0:T(8,128)(2,1)S(1)} %add_add_fusion), channel_id=1, source_target_pairs={{0,8},{1,9},{2,10},{3,11},{4,12},{5,13},{6,14},{7,15},{8,0},{9,1},... | collective-permute-start | bytes 147464 | tf_op jit(solution)/shard_map/ppermute | solution.py:411
  140.0 7.6 %collective-permute-start.20 = (bf16[192,128]{1,0:T(8,128)(2,1)S(1)}, bf16[192,128]{1,0:T(8,128)(2,1)S(1)}, u32[]{:S(2)}, u32[]{:S(2)}) collective-permute-start(bf16[192,128]{1,0:T(8,128)(2,1)S(1)} %add_add_fusion), channel_id=1, source_target_pairs={{0,1},{1,0},{2,3},{3,2},{4,5},{5,4},{6,7},{7,6},{8,9},{9,8},{10,11... | collective-permute-start | bytes 147464 | tf_op jit(solution)/shard_map/ppermute | solution.py:411
  140.0 7.6 %collective-permute-start.21 = (bf16[192,128]{1,0:T(8,128)(2,1)S(1)}, bf16[192,128]{1,0:T(8,128)(2,1)S(1)}, u32[]{:S(2)}, u32[]{:S(2)}) collective-permute-start(bf16[192,128]{1,0:T(8,128)(2,1)S(1)} %add_add_fusion), channel_id=1, source_target_pairs={{0,9},{1,8},{2,11},{3,10},{4,13},{5,12},{6,15},{7,14},{8,1},{9,0},... | collective-permute-start | bytes 147464 | tf_op jit(solution)/shard_map/ppermute | solution.py:411
  (10 other events, 81.3 us)

commit v13 on v12

--- a/solution.py
+++ b/solution.py
@@ -177,7 +177,7 @@
 def block_kernel(count, low, tile, steps, first, base, fresh, ranked, *refs):
     xs, w_ref, refs = refs[:count], refs[count], refs[count + 1 :]
     if ranked:
-        s_refs, refs = refs[:2], refs[2:]
+        s_ref, refs = refs[0], refs[1:]
     if not first:
         total_in, refs = refs[0], refs[1:]
     total_out, refs = refs[0], refs[1:]
@@ -195,10 +195,8 @@
             cut = xs[i].at[:, pl.ds(low + at, tile)]
             out.append(pltpu.make_async_copy(cut, x_slots.at[slot, pl.ds(i * rows, rows)], sem(i)))
         if ranked:
-            for i, s_ref in enumerate(s_refs):
-                cut, rank = s_ref.at[:, pl.ds(low + at, tile)], s_ref.shape[0]
-                to = s_slots.at[slot, pl.ds(i * rank, rank)]
-                out.append(pltpu.make_async_copy(cut, to, sem(count + 1 + i)))
+            cut = s_ref.at[:, pl.ds(low + at, tile)]
+            out.append(pltpu.make_async_copy(cut, s_slots.at[slot], sem(count + 1)))
         return out
 
     def start(step):
@@ -244,14 +242,14 @@
     count = len(xs)
     rows = xs[0].shape[0]
     cols = weights.shape[1]
-    rank = 2 * factors[0].shape[0]
+    rank = factors.shape[0]
     fresh, first = low == 0, total is None
     anywhere, whole = pl.BlockSpec(memory_space=pl.ANY), pl.BlockSpec(memory_space=pltpu.VMEM)
     operands = list(xs) + [weights]
     specs = [anywhere] * (count + 1)
     if ranked:
-        operands += factors
-        specs += [anywhere] * 2
+        operands.append(factors)
+        specs.append(anywhere)
     aliases = {}
     if not first:
         aliases = {len(operands): 0}
@@ -273,7 +271,7 @@
             pltpu.VMEM((SLOTS, count * rows, tile), BF16),
             pltpu.VMEM((SLOTS, tile, cols), BF16),
             pltpu.VMEM((SLOTS, rank, tile), BF16),
-            pltpu.SemaphoreType.DMA((SLOTS, count + 3)),
+            pltpu.SemaphoreType.DMA((SLOTS, count + 2)),
             pltpu.SemaphoreType.DMA((2,)),
         ],
         input_output_aliases=aliases,
@@ -292,33 +290,28 @@
     return (2 * len(SNAKE), rows, cols)
 
 
-def some_ranks_kernel(x_ref, *refs):
-    factors, out_ref = refs[:-1], refs[-1]
-    terms = [lax.dot_general(x_ref[...], ref[...], NT, preferred_element_type=F32) for ref in factors]
-    out_ref[...] = jnp.concatenate(terms, 1)
+def some_ranks_kernel(x_ref, s_ref, out_ref):
+    out_ref[...] = lax.dot_general(x_ref[...], s_ref[...], NT, preferred_element_type=F32)
 
 
 def some_ranks(x, factors):
-    whole = lambda shape: pl.BlockSpec(shape, lambda _: (0, 0))
-    shape = (x.shape[0], 2 * factors[0].shape[0])
+    whole = pl.BlockSpec(memory_space=pltpu.VMEM)
     return pl.pallas_call(
         some_ranks_kernel,
-        grid=(1,),
-        in_specs=[whole(value.shape) for value in (x, *factors)],
-        out_specs=whole(shape),
-        out_shape=jax.ShapeDtypeStruct(shape, F32),
+        in_specs=[whole] * 2,
+        out_specs=whole,
+        out_shape=jax.ShapeDtypeStruct((x.shape[0], factors.shape[0]), F32),
         compiler_params=PARAMS,
         name="some_ranks",
-    )(x, *factors)
+    )(x, factors)
 
 
 def rank_kernel(count, owners_ref, slot_ref, *refs):
     xs, refs = refs[:count], refs[count:]
-    sa_ref, sb_ref, h_refs, out_ref, placed = refs[0], refs[1], refs[2:-2], refs[-2], refs[-1]
-    rows, rank = xs[0].shape[0], sa_ref.shape[0]
+    s_ref, h_refs, out_ref, placed = refs[0], refs[1:-2], refs[-2], refs[-1]
+    rows, rank = xs[0].shape[0], s_ref.shape[0] // 2
     x = jnp.concatenate([ref[...] for ref in xs], 0)
-    last = [lax.dot_general(x, ref[...], NT, preferred_element_type=F32) for ref in (sa_ref, sb_ref)]
-    last = jnp.concatenate(last, 1)
+    last = lax.dot_general(x, s_ref[...], NT, preferred_element_type=F32)
     segments = slot_ref.shape[0] - 2
     block = 0
     for source in h_refs + (last,):
@@ -337,18 +330,18 @@
 
 
 def rank_terms(owners, slots, xs, factors, hs):
-    rank = factors[0].shape[0]
+    rank = factors.shape[0] // 2
     core_rows = owners.shape[0] // 2 * xs[0].shape[0]
     scalars, whole = pl.BlockSpec(memory_space=pltpu.SMEM), pl.BlockSpec(memory_space=pltpu.VMEM)
     return pl.pallas_call(
         functools.partial(rank_kernel, len(xs)),
-        in_specs=[scalars] * 2 + [whole] * (len(xs) + len(factors) + len(hs)),
+        in_specs=[scalars] * 2 + [whole] * (len(xs) + 1 + len(hs)),
         out_specs=whole,
         scratch_shapes=[pltpu.VMEM((core_rows, rank), F32)],
         out_shape=jax.ShapeDtypeStruct((core_rows // 2, 2 * rank), BF16),
         compiler_params=PARAMS,
         name="ranks",
-    )(owners, slots, *xs, *factors, *hs)
+    )(owners, slots, *xs, factors, *hs)
 
 
 def block_finish_kernel(places_ref, slot_ref, core_ref, total_ref, expand_ref, scale_ref, mine_ref, other_ref, *refs):
@@ -415,14 +408,14 @@
     half = depth // 2
     hs, counts = [], []
 
-    def multiply(xs, total):
-        total, h = block_product(xs, weights, factors, 0, depth, tile, total, sum(counts), True)
+    def multiply(xs, total, ranked):
+        total, h = block_product(xs, weights, factors, 0, depth, tile, total, sum(counts), ranked)
         hs.extend(h)
         counts.append(len(xs))
         return total
 
     streams = [send(tokens, out), None]
-    own, factors = [tokens, swap(tokens)], [shrinks[0], swap(shrinks[0])]
+    own, factors = [tokens, swap(tokens)], jnp.concatenate([shrinks[0], swap(shrinks[0])], 0)
     part = 2 * tile
     total, _ = block_product(own, weights, factors, 0, part, tile, None, 0, False)
     second, total = lax.optimization_barrier((tokens, total))
@@ -447,7 +440,8 @@
             streams[hop % 2] = send(arrived, home if hop % 2 else out)
         if hop % 2:
             late = [arrived, swap(arrived)]
-            total = multiply(blocks, total)
+            total = multiply(blocks, total, hop < hops - 2)
+            unranked = blocks if hop == hops - 2 else []
             blocks = late
         else:
             blocks += [arrived, swap(arrived)]
@@ -457,7 +451,7 @@
         totals.append(total)
     held = sum(counts)
     owners, places, slots, core, segment_slot, cosine, sine = tables
-    h = rank_terms(owners, slots, blocks[::2], factors, hs)
+    h = rank_terms(owners, slots, (unranked + blocks)[::2], factors, hs)
     beside = lambda step: send(h, [(i, i ^ step) for i in range(parts)])
 
     def last_product(low, high, total):

time: 151 us -> 151 us (level)
    pallas_call x7, Pallas kernels: 68.7 us -> 66.8 us  [block_product(): pl.pallas_call(functools.partial(block_kernel, count, low, tile, steps, f...]
    unnamed x24 -> x20, local copies, waits for them, and re-layouts: 4.81 us -> 4.42 us
  transfers between devices with their start and end apart: 22 -> 22, of which waited for: 6 -> 8; matrix products, arithmetic and copies ran while one was open for 3% -> 3% of each run, Pallas kernels for 50% -> 49%
where the time goes in v13:
time: 151 us
  Pallas kernels  76.9 us (51%)
  waiting for transfers between devices  36.9 us (24%)
  starting transfers between devices  27.4 us (18%)
  local copies, waits for them, and re-layouts  6.55 us (4%)
  other arithmetic  2.52 us (2%)
    pallas_call x7, Pallas kernels, block_product(): pl.pallas_call(functools.partial(block_kernel, count, low, tile, steps, f...  66.8 us
    ppermute x22, waiting for transfers between devices, ring_plan(): send = lambda value, pairs: lax.ppermute(value, 'tensor', pairs)  36.9 us
    ppermute x22, starting transfers between devices, ring_plan(): send = lambda value, pairs: lax.ppermute(value, 'tensor', pairs)  27.4 us
    unnamed x20, local copies, waits for them, and re-layouts  4.42 us
    pallas_call x1, Pallas kernels, some_ranks(): pl.pallas_call(some_ranks_kernel, in_specs=[whole] * 2, out_specs=whole,...  4.11 us
    pallas_call x1, Pallas kernels, rank_terms(): pl.pallas_call(functools.partial(rank_kernel, len(xs)), in_specs=[scalars...  3.35 us
  transfers between devices with their start and end apart: 22, of which 8 were waited for; matrix products, arithmetic and copies ran while one was open for 3% of the time, Pallas kernels for 49%

profile of v13, /device:TPU:0, one launch (start us, length us, event | category | flops | bytes accessed | tf_op | source)
XLA Modules:
  0.0 150.7 jit_solution(13202343759670236503)
XLA Ops:
  0.5 3.0 %collective-permute-start = (bf16[48,16384]{1,0:T(8,128)(2,1)}, bf16[48,16384]{1,0:T(8,128)(2,1)}, u32[]{:S(2)}, u32[]{:S(2)}) collective-permute-start(bf16[48,16384]{1,0:T(8,128)(2,1)} %refs_0_.3), channel_id=1, source_target_pairs={{0,4},{1,3},{4,8},{5,1},{8,12},{9,5},{12,14},{13,9},{14,10},{15,13... | collective-permute-start | bytes 4718600 | tf_op jit(solution)/shard_map/ppermute | solution.py:404
  3.5 3.2 %collective-permute-done.2.refs_1_ = bf16[48,16384]{1,0:T(8,128)(2,1)S(1)} collective-permute-done((bf16[48,16384]{1,0:T(8,128)(2,1)}, bf16[48,16384]{1,0:T(8,128)(2,1)S(1)}, u32[]{:S(2)}, u32[]{:S(2)}) %collective-permute-start.2) | collective-permute-done | bytes 1572896 | tf_op jit(solution)/shard_map/ppermute | solution.py:404
  6.7 3.1 %blocks.7.refs_3_ = f32[16,48,1024]{2,1,0:T(8,128)S(1)} custom-call(bf16[48,16384]{1,0:T(8,128)(2,1)} %refs_0_.3, bf16[48,16384]{1,0:T(8,128)(2,1)S(1)} %collective-permute-done.2.refs_1_, bf16[16384,1024]{1,0:T(8,128)(2,1)} %refs_4_.7), custom_call_target="tpu_custom_call" | custom-call | flops 402653184 | bytes 4194304 | tf_op jit(solution)/shard_map/blocks/pallas_call | solution.py:263
  9.8 2.9 %collective-permute-start.4 = (bf16[48,16384]{1,0:T(8,128)(2,1)}, bf16[48,16384]{1,0:T(8,128)(2,1)}, u32[]{:S(2)}, u32[]{:S(2)}) collective-permute-start(bf16[48,16384]{1,0:T(8,128)(2,1)} %refs_0_.3), channel_id=1, source_target_pairs={{0,2},{1,5},{4,0},{5,9},{8,4},{9,13},{12,8},{13,15},{14,12},{15,11... | collective-permute-start | bytes 4718600 | tf_op jit(solution)/shard_map/ppermute | solution.py:404
  12.7 10.9 %blocks.8.refs_4_ = f32[16,48,1024]{2,1,0:T(8,128)S(1)} custom-call(bf16[48,16384]{1,0:T(8,128)(2,1)} %refs_0_.3, bf16[48,16384]{1,0:T(8,128)(2,1)S(1)} %collective-permute-done.2.refs_1_, bf16[16384,1024]{1,0:T(8,128)(2,1)} %refs_4_.7, f32[16,48,1024]{2,1,0:T(8,128)S(1)} %blocks.7.refs_3_), custom_call_target="tpu_custom_call", output_to_operand_aliasing={{}: (3, {})} | custom-call | flops 2818572288 | bytes 29360128 | tf_op jit(solution)/shard_map/blocks/pallas_call | solution.py:263
  24.1 4.1 %some_ranks.1.refs_5_ = f32[48,128]{1,0:T(8,128)S(1)} custom-call(bf16[48,16384]{1,0:T(8,128)(2,1)} %refs_0_.3, bf16[128,16384]{1,0:T(8,128)(2,1)S(1)} %pad_maximum_fusion.s_ref.refs_3_.refs_5_.refs_4_), custom_call_target="tpu_custom_call" | custom-call | tf_op jit(solution)/shard_map/some_ranks/pallas_call | solution.py:299
  30.3 2.4 %collective-permute-start.6 = (bf16[48,16384]{1,0:T(8,128)(2,1)}, bf16[48,16384]{1,0:T(8,128)(2,1)}, u32[]{:S(2)}, u32[]{:S(2)}) collective-permute-start(bf16[48,16384]{1,0:T(8,128)(2,1)} %collective-permute-done.refs_0_), channel_id=1, source_target_pairs={{0,4},{1,3},{4,8},{5,1},{8,12},{9,5},{12,14},{13,9},{14,10},{15,13... | collective-permute-start | bytes 4718600 | tf_op jit(solution)/shard_map/ppermute | solution.py:404
  32.7 9.8 %collective-permute-done.4.refs_0_ = bf16[48,16384]{1,0:T(8,128)(2,1)} collective-permute-done((bf16[48,16384]{1,0:T(8,128)(2,1)}, bf16[48,16384]{1,0:T(8,128)(2,1)}, u32[]{:S(2)}, u32[]{:S(2)}) %collective-permute-start.4) | collective-permute-done | bytes 1572896 | tf_op jit(solution)/shard_map/ppermute | solution.py:404
  45.4 2.2 %copy-done.3 = bf16[128,16384]{1,0:T(8,128)(2,1)S(1)} copy-done((bf16[128,16384]{1,0:T(8,128)(2,1)S(1)}, bf16[128,16384]{1,0:T(8,128)(2,1)}, u32[]{:S(2)}) %copy-start.3) | copy-done | bytes 4194328
  47.6 12.6 %blocks.9 = (f32[16,48,1024]{2,1,0:T(8,128)S(1)}, f32[48,128]{1,0:T(8,128)S(1)}) custom-call(bf16[48,16384]{1,0:T(8,128)(2,1)} %collective-permute-done.refs_0_, bf16[48,16384]{1,0:T(8,128)(2,1)} %collective-permute-done.3.refs_1_, bf16[16384,1024]{1,0:T(8,128)(2,1)} %refs_4_.7, bf16[128,16384]{1,0:T(8,128)(2,1)S(1)} %copy-done.3, ...), custom_call_target="tpu_custom_call", output_to_operand_aliasing={{0}: (4, {})} | custom-call | flops 3221225472 | bytes 33554432 | tf_op jit(solution)/shard_map/blocks/pallas_call | solution.py:263
  64.9 2.4 %collective-permute-start.7 = (bf16[48,16384]{1,0:T(8,128)(2,1)}, bf16[48,16384]{1,0:T(8,128)(2,1)S(1)}, u32[]{:S(2)}, u32[]{:S(2)}) collective-permute-start(bf16[48,16384]{1,0:T(8,128)(2,1)} %collective-permute-done.6.refs_2_), channel_id=1, source_target_pairs={{0,4},{1,3},{4,8},{5,1},{8,12},{9,5},{12,14},{13,9},{14,10},{15,13... | collective-permute-start | bytes 4718600 | tf_op jit(solution)/shard_map/ppermute | solution.py:404
  67.3 8.1 %collective-permute-done.5.refs_0_ = bf16[48,16384]{1,0:T(8,128)(2,1)} collective-permute-done((bf16[48,16384]{1,0:T(8,128)(2,1)}, bf16[48,16384]{1,0:T(8,128)(2,1)}, u32[]{:S(2)}, u32[]{:S(2)}) %collective-permute-start.5) | collective-permute-done | bytes 1572896 | tf_op jit(solution)/shard_map/ppermute | solution.py:404
  78.2 2.2 %copy-done.4 = bf16[128,16384]{1,0:T(8,128)(2,1)S(1)} copy-done((bf16[128,16384]{1,0:T(8,128)(2,1)S(1)}, bf16[128,16384]{1,0:T(8,128)(2,1)}, u32[]{:S(2)}) %copy-start.4) | copy-done | bytes 4194328
  80.4 13.3 %blocks.10 = (f32[16,48,1024]{2,1,0:T(8,128)S(1)}, f32[96,128]{1,0:T(8,128)S(1)}) custom-call(bf16[48,16384]{1,0:T(8,128)(2,1)} %collective-permute-done.4.refs_0_, bf16[48,16384]{1,0:T(8,128)(2,1)} %collective-permute-done.8.refs_1_, bf16[48,16384]{1,0:T(8,128)(2,1)} %collective-permute-done.6.refs_2_, ...), custom_call_target="tpu_custom_call", output_to_operand_aliasing={{0}: (6, {})} | custom-call | flops 6442450944 | bytes 33554432 | tf_op jit(solution)/shard_map/blocks/pallas_call | solution.py:263
  93.7 5.7 %collective-permute-done.7.refs_2_.refs_1_ = bf16[48,16384]{1,0:T(8,128)(2,1)S(1)} collective-permute-done((bf16[48,16384]{1,0:T(8,128)(2,1)}, bf16[48,16384]{1,0:T(8,128)(2,1)S(1)}, u32[]{:S(2)}, u32[]{:S(2)}) %collective-permute-start.7) | collective-permute-done | bytes 1572896 | tf_op jit(solution)/shard_map/ppermute | solution.py:404
  99.5 2.4 %collective-permute-start.11 = (bf16[48,16384]{1,0:T(8,128)(2,1)S(1)}, bf16[48,16384]{1,0:T(8,128)(2,1)S(1)}, u32[]{:S(2)}, u32[]{:S(2)}) collective-permute-start(bf16[48,16384]{1,0:T(8,128)(2,1)S(1)} %collective-permute-done.7.refs_2_.refs_1_), channel_id=1, source_target_pairs={{0,4},{1,3},{4,8},{5,1},{8,12},{9,5},{12,14},{13,9},{14,10},{15,13... | collective-permute-start | bytes 4718600 | tf_op jit(solution)/shard_map/ppermute | solution.py:404
  101.8 6.5 %collective-permute-done.10.refs_2_.refs_0_ = bf16[48,16384]{1,0:T(8,128)(2,1)S(1)} collective-permute-done((bf16[48,16384]{1,0:T(8,128)(2,1)}, bf16[48,16384]{1,0:T(8,128)(2,1)S(1)}, u32[]{:S(2)}, u32[]{:S(2)}) %collective-permute-start.10) | collective-permute-done | bytes 1572896 | tf_op jit(solution)/shard_map/ppermute | solution.py:404
  109.4 12.7 %blocks.11.refs_5_ = f32[16,48,1024]{2,1,0:T(8,128)S(1)} custom-call(bf16[48,16384]{1,0:T(8,128)(2,1)} %collective-permute-done.5.refs_0_, bf16[48,16384]{1,0:T(8,128)(2,1)S(1)} %collective-permute-done.12.refs_1_, bf16[48,16384]{1,0:T(8,128)(2,1)S(1)} %collective-permute-done.7.refs_2_.refs_1_, ...), custom_call_target="tpu_custom_call", output_to_operand_aliasing={{}: (5, {})} | custom-call | flops 6442450944 | bytes 33554432 | tf_op jit(solution)/shard_map/blocks/pallas_call | solution.py:263
  123.2 3.4 %ranks.1 = bf16[192,128]{1,0:T(8,128)(2,1)S(1)} custom-call(s32[16]{0:T(128)S(1)} %get-tuple-element.61.owners_ref, s32[8]{0:T(128)S(1)} %pad_add_fusion.slot_ref, bf16[48,16384]{1,0:T(8,128)(2,1)} %collective-permute-done.5.refs_0_, bf16[48,16384]{1,0:T(8,128)(2,1)S(1)} %collective-permute-done.7.refs_2_.refs_1_, ...), custom_call_target="tpu_custom_call" | custom-call | tf_op jit(solution)/shard_map/ranks/pallas_call | solution.py:336
  126.6 2.1 %collective-permute-start.14 = (bf16[192,128]{1,0:T(8,128)(2,1)S(1)}, bf16[192,128]{1,0:T(8,128)(2,1)S(1)}, u32[]{:S(2)}, u32[]{:S(2)}) collective-permute-start(bf16[192,128]{1,0:T(8,128)(2,1)S(1)} %ranks.1), channel_id=1, source_target_pairs={{0,2},{1,3},{2,0},{3,1},{4,6},{5,7},{6,4},{7,5},{8,10},{9,11},{10,... | collective-permute-start | bytes 147464 | tf_op jit(solution)/shard_map/ppermute | solution.py:404
  130.2 7.1 %blocks.12.refs_5_ = f32[16,48,1024]{2,1,0:T(8,128)S(1)} custom-call(bf16[48,16384]{1,0:T(8,128)(2,1)S(1)} %collective-permute-done.10.refs_2_.refs_0_, bf16[48,16384]{1,0:T(8,128)(2,1)S(1)} %collective-permute-done.17.refs_1_, bf16[48,16384]{1,0:T(8,128)(2,1)S(1)} %collective-permute-done.11.refs_3_.refs_2_, ...), custom_call_target="tpu_custom_call", output_to_operand_aliasing={{}: (5, {})} | custom-call | flops 3221225472 | bytes 16777216 | tf_op jit(solution)/shard_map/blocks/pallas_call | solution.py:263
  137.4 3.1 %collective-permute-start.19 = (bf16[192,128]{1,0:T(8,128)(2,1)S(1)}, bf16[192,128]{1,0:T(8,128)(2,1)S(1)}, u32[]{:S(2)}, u32[]{:S(2)}) collective-permute-start(bf16[192,128]{1,0:T(8,128)(2,1)S(1)} %add_add_fusion), channel_id=1, source_target_pairs={{0,8},{1,9},{2,10},{3,11},{4,12},{5,13},{6,14},{7,15},{8,0},{9,1},... | collective-permute-start | bytes 147464 | tf_op jit(solution)/shard_map/ppermute | solution.py:404
  140.7 7.2 %blocks.13.total_ref = f32[16,48,1024]{2,1,0:T(8,128)S(1)} custom-call(bf16[48,16384]{1,0:T(8,128)(2,1)S(1)} %collective-permute-done.10.refs_2_.refs_0_, bf16[48,16384]{1,0:T(8,128)(2,1)S(1)} %collective-permute-done.17.refs_1_, bf16[48,16384]{1,0:T(8,128)(2,1)S(1)} %collective-permute-done.11.refs_3_.refs_2_, ...), custom_call_target="tpu_custom_call", output_to_operand_aliasing={{}: (5, {})} | custom-call | flops 3221225472 | bytes 16777216 | tf_op jit(solution)/shard_map/blocks/pallas_call | solution.py:263
  148.0 2.6 %finish.1 = bf16[768,1024]{1,0:T(8,128)(2,1)} custom-call(s32[16]{0:T(128)S(1)} %get-tuple-element.58.places_ref, s32[6]{0:T(128)S(1)} %gather_fusion, s32[1]{0:T(128)} %bitcast.7.core_ref, f32[16,48,1024]{2,1,0:T(8,128)S(1)} %blocks.13.total_ref, bf16[16,64,1024]{2,1,0:T(8,128)(2,1)S(1)} %bitcast.14, f32[1,1024]{1,0:T(1,128)S(1)} %bitcast.15, ...), custom_call_target="tpu_custom_call" | custom-call | tf_op jit(solution)/shard_map/finish/pallas_call | solution.py:383
  (66 shorter events, 17.5 us)
Async XLA Ops:
  0.0 61.2 %copy-start = (s32[16]{0:T(128)S(1)}, s32[16]{0:T(128)}, u32[]{:S(2)}) copy-start(s32[16]{0:T(128)} %param.16) | copy-start | bytes 196
  0.0 23.6 %collective-permute-start.1 = (bf16[64,16384]{1,0:T(8,128)(2,1)}, bf16[64,16384]{1,0:T(8,128)(2,1)S(1)}, u32[]{:S(2)}, u32[]{:S(2)}) collective-permute-start(bf16[64,16384]{1,0:T(8,128)(2,1)} %bitcast.16), channel_id=1, source_target_pairs={{0,1},{1,0},{2,3},{3,2},{4,5},{5,4},{6,7},{7,6},{8,9},{9,8},{10,11... | collective-permute-start | bytes 6291464 | tf_op jit(solution)/shard_map/ppermute | solution.py:404
  0.5 6.2 %collective-permute-start.2 = (bf16[48,16384]{1,0:T(8,128)(2,1)}, bf16[48,16384]{1,0:T(8,128)(2,1)S(1)}, u32[]{:S(2)}, u32[]{:S(2)}) collective-permute-start(bf16[48,16384]{1,0:T(8,128)(2,1)} %refs_0_.3), channel_id=1, source_target_pairs={{0,1},{1,0},{2,3},{3,2},{4,5},{5,4},{6,7},{7,6},{8,9},{9,8},{10,11... | collective-permute-start | bytes 4718600 | tf_op jit(solution)/shard_map/ppermute | solution.py:404
  0.5 29.7 %collective-permute-start = (bf16[48,16384]{1,0:T(8,128)(2,1)}, bf16[48,16384]{1,0:T(8,128)(2,1)}, u32[]{:S(2)}, u32[]{:S(2)}) collective-permute-start(bf16[48,16384]{1,0:T(8,128)(2,1)} %refs_0_.3), channel_id=1, source_target_pairs={{0,4},{1,3},{4,8},{5,1},{8,12},{9,5},{12,14},{13,9},{14,10},{15,13... | collective-permute-start | bytes 4718600 | tf_op jit(solution)/shard_map/ppermute | solution.py:404
  9.8 32.7 %collective-permute-start.4 = (bf16[48,16384]{1,0:T(8,128)(2,1)}, bf16[48,16384]{1,0:T(8,128)(2,1)}, u32[]{:S(2)}, u32[]{:S(2)}) collective-permute-start(bf16[48,16384]{1,0:T(8,128)(2,1)} %refs_0_.3), channel_id=1, source_target_pairs={{0,2},{1,5},{4,0},{5,9},{8,4},{9,13},{12,8},{13,15},{14,12},{15,11... | collective-permute-start | bytes 4718600 | tf_op jit(solution)/shard_map/ppermute | solution.py:404
  30.3 15.2 %collective-permute-start.3 = (bf16[48,16384]{1,0:T(8,128)(2,1)}, bf16[48,16384]{1,0:T(8,128)(2,1)}, u32[]{:S(2)}, u32[]{:S(2)}) collective-permute-start(bf16[48,16384]{1,0:T(8,128)(2,1)} %collective-permute-done.refs_0_), channel_id=1, source_target_pairs={{0,1},{1,0},{2,3},{3,2},{4,5},{5,4},{6,7},{7,6},{8,9},{9,8},{10,11... | collective-permute-start | bytes 4718600 | tf_op jit(solution)/shard_map/ppermute | solution.py:404
  30.3 30.0 %copy-start.9 = (s32[8]{0:T(128)S(1)}, s32[8]{0:T(128)}, u32[]{:S(2)}) copy-start(s32[8]{0:T(128)} %param.17) | copy-start | bytes 100
  30.3 34.6 %collective-permute-start.6 = (bf16[48,16384]{1,0:T(8,128)(2,1)}, bf16[48,16384]{1,0:T(8,128)(2,1)}, u32[]{:S(2)}, u32[]{:S(2)}) collective-permute-start(bf16[48,16384]{1,0:T(8,128)(2,1)} %collective-permute-done.refs_0_), channel_id=1, source_target_pairs={{0,4},{1,3},{4,8},{5,1},{8,12},{9,5},{12,14},{13,9},{14,10},{15,13... | collective-permute-start | bytes 4718600 | tf_op jit(solution)/shard_map/ppermute | solution.py:404
  42.5 32.9 %collective-permute-start.5 = (bf16[48,16384]{1,0:T(8,128)(2,1)}, bf16[48,16384]{1,0:T(8,128)(2,1)}, u32[]{:S(2)}, u32[]{:S(2)}) collective-permute-start(bf16[48,16384]{1,0:T(8,128)(2,1)} %collective-permute-done.4.refs_0_), channel_id=1, source_target_pairs={{0,2},{1,5},{4,0},{5,9},{8,4},{9,13},{12,8},{13,15},{14,12},{15,11... | collective-permute-start | bytes 4718600 | tf_op jit(solution)/shard_map/ppermute | solution.py:404
  44.2 34.0 %collective-permute-start.8 = (bf16[48,16384]{1,0:T(8,128)(2,1)}, bf16[48,16384]{1,0:T(8,128)(2,1)}, u32[]{:S(2)}, u32[]{:S(2)}) collective-permute-start(bf16[48,16384]{1,0:T(8,128)(2,1)} %collective-permute-done.4.refs_0_), channel_id=1, source_target_pairs={{0,1},{1,0},{2,3},{3,2},{4,5},{5,4},{6,7},{7,6},{8,9},{9,8},{10,11... | collective-permute-start | bytes 4718600 | tf_op jit(solution)/shard_map/ppermute | solution.py:404
  64.9 13.3 %collective-permute-start.9 = (bf16[48,16384]{1,0:T(8,128)(2,1)}, bf16[48,16384]{1,0:T(8,128)(2,1)S(1)}, u32[]{:S(2)}, u32[]{:S(2)}) collective-permute-start(bf16[48,16384]{1,0:T(8,128)(2,1)} %collective-permute-done.6.refs_2_), channel_id=1, source_target_pairs={{0,1},{1,0},{2,3},{3,2},{4,5},{5,4},{6,7},{7,6},{8,9},{9,8},{10,11... | collective-permute-start | bytes 4718600 | tf_op jit(solution)/shard_map/ppermute | solution.py:404
  64.9 34.6 %collective-permute-start.7 = (bf16[48,16384]{1,0:T(8,128)(2,1)}, bf16[48,16384]{1,0:T(8,128)(2,1)S(1)}, u32[]{:S(2)}, u32[]{:S(2)}) collective-permute-start(bf16[48,16384]{1,0:T(8,128)(2,1)} %collective-permute-done.6.refs_2_), channel_id=1, source_target_pairs={{0,4},{1,3},{4,8},{5,1},{8,12},{9,5},{12,14},{13,9},{14,10},{15,13... | collective-permute-start | bytes 4718600 | tf_op jit(solution)/shard_map/ppermute | solution.py:404
  75.4 33.0 %collective-permute-start.10 = (bf16[48,16384]{1,0:T(8,128)(2,1)}, bf16[48,16384]{1,0:T(8,128)(2,1)S(1)}, u32[]{:S(2)}, u32[]{:S(2)}) collective-permute-start(bf16[48,16384]{1,0:T(8,128)(2,1)} %collective-permute-done.5.refs_0_), channel_id=1, source_target_pairs={{0,2},{1,5},{4,0},{5,9},{8,4},{9,13},{12,8},{13,15},{14,12},{15,11... | collective-permute-start | bytes 4718600 | tf_op jit(solution)/shard_map/ppermute | solution.py:404
  77.1 32.4 %collective-permute-start.12 = (bf16[48,16384]{1,0:T(8,128)(2,1)}, bf16[48,16384]{1,0:T(8,128)(2,1)S(1)}, u32[]{:S(2)}, u32[]{:S(2)}) collective-permute-start(bf16[48,16384]{1,0:T(8,128)(2,1)} %collective-permute-done.5.refs_0_), channel_id=1, source_target_pairs={{0,1},{1,0},{2,3},{3,2},{4,5},{5,4},{6,7},{7,6},{8,9},{9,8},{10,11... | collective-permute-start | bytes 4718600 | tf_op jit(solution)/shard_map/ppermute | solution.py:404
  99.5 10.0 %collective-permute-start.13 = (bf16[48,16384]{1,0:T(8,128)(2,1)S(1)}, bf16[48,16384]{1,0:T(8,128)(2,1)S(1)}, u32[]{:S(2)}, u32[]{:S(2)}) collective-permute-start(bf16[48,16384]{1,0:T(8,128)(2,1)S(1)} %collective-permute-done.7.refs_2_.refs_1_), channel_id=1, source_target_pairs={{0,1},{1,0},{2,3},{3,2},{4,5},{5,4},{6,7},{7,6},{8,9},{9,8},{10,11... | collective-permute-start | bytes 4718600 | tf_op jit(solution)/shard_map/ppermute | solution.py:404
  99.5 23.7 %collective-permute-start.11 = (bf16[48,16384]{1,0:T(8,128)(2,1)S(1)}, bf16[48,16384]{1,0:T(8,128)(2,1)S(1)}, u32[]{:S(2)}, u32[]{:S(2)}) collective-permute-start(bf16[48,16384]{1,0:T(8,128)(2,1)S(1)} %collective-permute-done.7.refs_2_.refs_1_), channel_id=1, source_target_pairs={{0,4},{1,3},{4,8},{5,1},{8,12},{9,5},{12,14},{13,9},{14,10},{15,13... | collective-permute-start | bytes 4718600 | tf_op jit(solution)/shard_map/ppermute | solution.py:404
  108.3 21.9 %collective-permute-start.17 = (bf16[48,16384]{1,0:T(8,128)(2,1)S(1)}, bf16[48,16384]{1,0:T(8,128)(2,1)S(1)}, u32[]{:S(2)}, u32[]{:S(2)}) collective-permute-start(bf16[48,16384]{1,0:T(8,128)(2,1)S(1)} %collective-permute-done.10.refs_2_.refs_0_), channel_id=1, source_target_pairs={{0,1},{1,0},{2,3},{3,2},{4,5},{5,4},{6,7},{7,6},{8,9},{9,8},{10,11... | collective-permute-start | bytes 4718600 | tf_op jit(solution)/shard_map/ppermute | solution.py:404
  123.2 7.0 %collective-permute-start.18 = (bf16[48,16384]{1,0:T(8,128)(2,1)S(1)}, bf16[48,16384]{1,0:T(8,128)(2,1)S(1)}, u32[]{:S(2)}, u32[]{:S(2)}) collective-permute-start(bf16[48,16384]{1,0:T(8,128)(2,1)S(1)} %collective-permute-done.11.refs_3_.refs_2_), channel_id=1, source_target_pairs={{0,1},{1,0},{2,3},{3,2},{4,5},{5,4},{6,7},{7,6},{8,9},{9,8},{10,11... | collective-permute-start | bytes 4718600 | tf_op jit(solution)/shard_map/ppermute | solution.py:404
  126.6 10.8 %collective-permute-start.14 = (bf16[192,128]{1,0:T(8,128)(2,1)S(1)}, bf16[192,128]{1,0:T(8,128)(2,1)S(1)}, u32[]{:S(2)}, u32[]{:S(2)}) collective-permute-start(bf16[192,128]{1,0:T(8,128)(2,1)S(1)} %ranks.1), channel_id=1, source_target_pairs={{0,2},{1,3},{2,0},{3,1},{4,6},{5,7},{6,4},{7,5},{8,10},{9,11},{10,... | collective-permute-start | bytes 147464 | tf_op jit(solution)/shard_map/ppermute | solution.py:404
  128.7 8.7 %collective-permute-start.15 = (bf16[192,128]{1,0:T(8,128)(2,1)S(1)}, bf16[192,128]{1,0:T(8,128)(2,1)S(1)}, u32[]{:S(2)}, u32[]{:S(2)}) collective-permute-start(bf16[192,128]{1,0:T(8,128)(2,1)S(1)} %ranks.1), channel_id=1, source_target_pairs={{0,4},{1,5},{2,6},{3,7},{4,0},{5,1},{6,2},{7,3},{8,12},{9,13},{10,... | collective-permute-start | bytes 147464 | tf_op jit(solution)/shard_map/ppermute | solution.py:404
  130.2 7.1 %collective-permute-start.16 = (bf16[192,128]{1,0:T(8,128)(2,1)S(1)}, bf16[192,128]{1,0:T(8,128)(2,1)S(1)}, u32[]{:S(2)}, u32[]{:S(2)}) collective-permute-start(bf16[192,128]{1,0:T(8,128)(2,1)S(1)} %ranks.1), channel_id=1, source_target_pairs={{0,6},{1,7},{2,4},{3,5},{4,2},{5,3},{6,0},{7,1},{8,14},{9,15},{10,... | collective-permute-start | bytes 147464 | tf_op jit(solution)/shard_map/ppermute | solution.py:404
  137.4 10.4 %collective-permute-start.19 = (bf16[192,128]{1,0:T(8,128)(2,1)S(1)}, bf16[192,128]{1,0:T(8,128)(2,1)S(1)}, u32[]{:S(2)}, u32[]{:S(2)}) collective-permute-start(bf16[192,128]{1,0:T(8,128)(2,1)S(1)} %add_add_fusion), channel_id=1, source_target_pairs={{0,8},{1,9},{2,10},{3,11},{4,12},{5,13},{6,14},{7,15},{8,0},{9,1},... | collective-permute-start | bytes 147464 | tf_op jit(solution)/shard_map/ppermute | solution.py:404
  140.5 7.4 %collective-permute-start.20 = (bf16[192,128]{1,0:T(8,128)(2,1)S(1)}, bf16[192,128]{1,0:T(8,128)(2,1)S(1)}, u32[]{:S(2)}, u32[]{:S(2)}) collective-permute-start(bf16[192,128]{1,0:T(8,128)(2,1)S(1)} %add_add_fusion), channel_id=1, source_target_pairs={{0,1},{1,0},{2,3},{3,2},{4,5},{5,4},{6,7},{7,6},{8,9},{9,8},{10,11... | collective-permute-start | bytes 147464 | tf_op jit(solution)/shard_map/ppermute | solution.py:404
  140.5 7.4 %collective-permute-start.21 = (bf16[192,128]{1,0:T(8,128)(2,1)S(1)}, bf16[192,128]{1,0:T(8,128)(2,1)S(1)}, u32[]{:S(2)}, u32[]{:S(2)}) collective-permute-start(bf16[192,128]{1,0:T(8,128)(2,1)S(1)} %add_add_fusion), channel_id=1, source_target_pairs={{0,9},{1,8},{2,11},{3,10},{4,13},{5,12},{6,15},{7,14},{8,1},{9,0},... | collective-permute-start | bytes 147464 | tf_op jit(solution)/shard_map/ppermute | solution.py:404
  (8 other events, 59.9 us)

commit v14 on v13

--- a/solution.py
+++ b/solution.py
@@ -441,17 +441,24 @@
         if hop % 2:
             late = [arrived, swap(arrived)]
             total = multiply(blocks, total, hop < hops - 2)
-            unranked = blocks if hop == hops - 2 else []
             blocks = late
         else:
             blocks += [arrived, swap(arrived)]
+        if hop == hops - 3:
+            early = [some_ranks(part, factors) for part in blocks[::2]]
+            early, total = lax.optimization_barrier((early, total))
+        if hop == hops - 2:
+            hs += early
+            last, _ = lax.optimization_barrier((arrived, total))
+            hs.append(some_ranks(last, factors))
+            hs, total = lax.optimization_barrier((hs, total))
         if hop == 1:
             known, total = lax.optimization_barrier(((me, indices), total))
             tables, total = lax.optimization_barrier((make_tables(*known), total))
         totals.append(total)
     held = sum(counts)
     owners, places, slots, core, segment_slot, cosine, sine = tables
-    h = rank_terms(owners, slots, (unranked + blocks)[::2], factors, hs)
+    h = rank_terms(owners, slots, blocks[2:3], factors, hs)
     beside = lambda step: send(h, [(i, i ^ step) for i in range(parts)])
 
     def last_product(low, high, total):

time: 151 us -> 150 us (level)
  waiting for transfers between devices: 36.9 us -> 31.3 us
  Pallas kernels: 76.9 us -> 81.7 us
    pallas_call x1 -> x4, Pallas kernels: 4.11 us -> 10.1 us  [some_ranks(): pl.pallas_call(some_ranks_kernel, in_specs=[whole] * 2, out_specs=whole,...]
    ppermute x22, waiting for transfers between devices: 36.9 us -> 31.3 us  [ring_plan(): send = lambda value, pairs: lax.ppermute(value, 'tensor', pairs)]
  transfers between devices with their start and end apart: 22 -> 22, of which waited for: 8 -> 7; matrix products, arithmetic and copies ran while one was open for 3% -> 3% of each run, Pallas kernels for 49% -> 53%
where the time goes in v14:
time: 150 us
  Pallas kernels  81.7 us (54%)
  waiting for transfers between devices  31.3 us (21%)
  starting transfers between devices  27.5 us (18%)
  local copies, waits for them, and re-layouts  6.55 us (4%)
  other arithmetic  2.52 us (2%)
    pallas_call x7, Pallas kernels, block_product(): pl.pallas_call(functools.partial(block_kernel, count, low, tile, steps, f...  66.8 us
    ppermute x22, waiting for transfers between devices, ring_plan(): send = lambda value, pairs: lax.ppermute(value, 'tensor', pairs)  31.3 us
    ppermute x22, starting transfers between devices, ring_plan(): send = lambda value, pairs: lax.ppermute(value, 'tensor', pairs)  27.5 us
    pallas_call x4, Pallas kernels, some_ranks(): pl.pallas_call(some_ranks_kernel, in_specs=[whole] * 2, out_specs=whole,...  10.1 us
    unnamed x20, local copies, waits for them, and re-layouts  4.42 us
  transfers between devices with their start and end apart: 22, of which 7 were waited for; matrix products, arithmetic and copies ran while one was open for 3% of the time, Pallas kernels for 53%

profile of v14, /device:TPU:0, one launch (start us, length us, event | category | flops | bytes accessed | tf_op | source)
XLA Modules:
  0.0 150.1 jit_solution(6033730504216030086)
XLA Ops:
  0.5 3.0 %collective-permute-start = (bf16[48,16384]{1,0:T(8,128)(2,1)}, bf16[48,16384]{1,0:T(8,128)(2,1)}, u32[]{:S(2)}, u32[]{:S(2)}) collective-permute-start(bf16[48,16384]{1,0:T(8,128)(2,1)} %refs_0_.3), channel_id=1, source_target_pairs={{0,4},{1,3},{4,8},{5,1},{8,12},{9,5},{12,14},{13,9},{14,10},{15,13... | collective-permute-start | bytes 4718600 | tf_op jit(solution)/shard_map/ppermute | solution.py:404
  3.5 3.2 %collective-permute-done.2.refs_1_ = bf16[48,16384]{1,0:T(8,128)(2,1)S(1)} collective-permute-done((bf16[48,16384]{1,0:T(8,128)(2,1)}, bf16[48,16384]{1,0:T(8,128)(2,1)S(1)}, u32[]{:S(2)}, u32[]{:S(2)}) %collective-permute-start.2) | collective-permute-done | bytes 1572896 | tf_op jit(solution)/shard_map/ppermute | solution.py:404
  6.7 3.1 %blocks.7.refs_3_ = f32[16,48,1024]{2,1,0:T(8,128)S(1)} custom-call(bf16[48,16384]{1,0:T(8,128)(2,1)} %refs_0_.3, bf16[48,16384]{1,0:T(8,128)(2,1)S(1)} %collective-permute-done.2.refs_1_, bf16[16384,1024]{1,0:T(8,128)(2,1)} %refs_4_.7), custom_call_target="tpu_custom_call" | custom-call | flops 402653184 | bytes 4194304 | tf_op jit(solution)/shard_map/blocks/pallas_call | solution.py:263
  9.8 2.9 %collective-permute-start.6 = (bf16[48,16384]{1,0:T(8,128)(2,1)}, bf16[48,16384]{1,0:T(8,128)(2,1)}, u32[]{:S(2)}, u32[]{:S(2)}) collective-permute-start(bf16[48,16384]{1,0:T(8,128)(2,1)} %refs_0_.3), channel_id=1, source_target_pairs={{0,2},{1,5},{4,0},{5,9},{8,4},{9,13},{12,8},{13,15},{14,12},{15,11... | collective-permute-start | bytes 4718600 | tf_op jit(solution)/shard_map/ppermute | solution.py:404
  12.7 10.9 %blocks.8.refs_4_ = f32[16,48,1024]{2,1,0:T(8,128)S(1)} custom-call(bf16[48,16384]{1,0:T(8,128)(2,1)} %refs_0_.3, bf16[48,16384]{1,0:T(8,128)(2,1)S(1)} %collective-permute-done.2.refs_1_, bf16[16384,1024]{1,0:T(8,128)(2,1)} %refs_4_.7, f32[16,48,1024]{2,1,0:T(8,128)S(1)} %blocks.7.refs_3_), custom_call_target="tpu_custom_call", output_to_operand_aliasing={{}: (3, {})} | custom-call | flops 2818572288 | bytes 29360128 | tf_op jit(solution)/shard_map/blocks/pallas_call | solution.py:263
  24.1 4.1 %some_ranks.4.refs_2_ = f32[48,128]{1,0:T(8,128)S(1)} custom-call(bf16[48,16384]{1,0:T(8,128)(2,1)} %refs_0_.3, bf16[128,16384]{1,0:T(8,128)(2,1)S(1)} %pad_maximum_fusion.s_ref.refs_3_.refs_5_.refs_1_), custom_call_target="tpu_custom_call" | custom-call | tf_op jit(solution)/shard_map/some_ranks/pallas_call | solution.py:299
  30.3 2.4 %collective-permute-start.4 = (bf16[48,16384]{1,0:T(8,128)(2,1)}, bf16[48,16384]{1,0:T(8,128)(2,1)}, u32[]{:S(2)}, u32[]{:S(2)}) collective-permute-start(bf16[48,16384]{1,0:T(8,128)(2,1)} %collective-permute-done.refs_0_), channel_id=1, source_target_pairs={{0,4},{1,3},{4,8},{5,1},{8,12},{9,5},{12,14},{13,9},{14,10},{15,13... | collective-permute-start | bytes 4718600 | tf_op jit(solution)/shard_map/ppermute | solution.py:404
  32.7 9.8 %collective-permute-done.6.refs_0_ = bf16[48,16384]{1,0:T(8,128)(2,1)} collective-permute-done((bf16[48,16384]{1,0:T(8,128)(2,1)}, bf16[48,16384]{1,0:T(8,128)(2,1)}, u32[]{:S(2)}, u32[]{:S(2)}) %collective-permute-start.6) | collective-permute-done | bytes 1572896 | tf_op jit(solution)/shard_map/ppermute | solution.py:404
  45.4 2.2 %copy-done.3 = bf16[128,16384]{1,0:T(8,128)(2,1)S(1)} copy-done((bf16[128,16384]{1,0:T(8,128)(2,1)S(1)}, bf16[128,16384]{1,0:T(8,128)(2,1)}, u32[]{:S(2)}) %copy-start.3) | copy-done | bytes 4194328
  47.6 12.6 %blocks.9 = (f32[16,48,1024]{2,1,0:T(8,128)S(1)}, f32[48,128]{1,0:T(8,128)S(1)}) custom-call(bf16[48,16384]{1,0:T(8,128)(2,1)} %collective-permute-done.refs_0_, bf16[48,16384]{1,0:T(8,128)(2,1)} %collective-permute-done.3.refs_1_, bf16[16384,1024]{1,0:T(8,128)(2,1)} %refs_4_.7, bf16[128,16384]{1,0:T(8,128)(2,1)S(1)} %copy-done.3, ...), custom_call_target="tpu_custom_call", output_to_operand_aliasing={{0}: (4, {})} | custom-call | flops 3221225472 | bytes 33554432 | tf_op jit(solution)/shard_map/blocks/pallas_call | solution.py:263
  64.9 2.4 %collective-permute-start.5 = (bf16[48,16384]{1,0:T(8,128)(2,1)}, bf16[48,16384]{1,0:T(8,128)(2,1)S(1)}, u32[]{:S(2)}, u32[]{:S(2)}) collective-permute-start(bf16[48,16384]{1,0:T(8,128)(2,1)} %collective-permute-done.4.refs_2_), channel_id=1, source_target_pairs={{0,4},{1,3},{4,8},{5,1},{8,12},{9,5},{12,14},{13,9},{14,10},{15,13... | collective-permute-start | bytes 4718600 | tf_op jit(solution)/shard_map/ppermute | solution.py:404
  67.3 8.1 %collective-permute-done.10.x_ref.refs_0_ = bf16[48,16384]{1,0:T(8,128)(2,1)} collective-permute-done((bf16[48,16384]{1,0:T(8,128)(2,1)}, bf16[48,16384]{1,0:T(8,128)(2,1)}, u32[]{:S(2)}, u32[]{:S(2)}) %collective-permute-start.10) | collective-permute-done | bytes 1572896 | tf_op jit(solution)/shard_map/ppermute | solution.py:404
  78.2 2.2 %copy-done.4 = bf16[128,16384]{1,0:T(8,128)(2,1)S(1)} copy-done((bf16[128,16384]{1,0:T(8,128)(2,1)S(1)}, bf16[128,16384]{1,0:T(8,128)(2,1)}, u32[]{:S(2)}) %copy-start.4) | copy-done | bytes 4194328
  80.4 13.3 %blocks.10 = (f32[16,48,1024]{2,1,0:T(8,128)S(1)}, f32[96,128]{1,0:T(8,128)S(1)}) custom-call(bf16[48,16384]{1,0:T(8,128)(2,1)} %collective-permute-done.6.refs_0_, bf16[48,16384]{1,0:T(8,128)(2,1)} %collective-permute-done.7.refs_1_, bf16[48,16384]{1,0:T(8,128)(2,1)} %collective-permute-done.4.refs_2_, ...), custom_call_target="tpu_custom_call", output_to_operand_aliasing={{0}: (6, {})} | custom-call | flops 6442450944 | bytes 33554432 | tf_op jit(solution)/shard_map/blocks/pallas_call | solution.py:263
  93.7 5.7 %collective-permute-done.5.x_ref.refs_2_ = bf16[48,16384]{1,0:T(8,128)(2,1)S(1)} collective-permute-done((bf16[48,16384]{1,0:T(8,128)(2,1)}, bf16[48,16384]{1,0:T(8,128)(2,1)S(1)}, u32[]{:S(2)}, u32[]{:S(2)}) %collective-permute-start.5) | collective-permute-done | bytes 1572896 | tf_op jit(solution)/shard_map/ppermute | solution.py:404
  99.5 2.4 %collective-permute-start.9 = (bf16[48,16384]{1,0:T(8,128)(2,1)S(1)}, bf16[48,16384]{1,0:T(8,128)(2,1)S(1)}, u32[]{:S(2)}, u32[]{:S(2)}) collective-permute-start(bf16[48,16384]{1,0:T(8,128)(2,1)S(1)} %collective-permute-done.5.x_ref.refs_2_), channel_id=1, source_target_pairs={{0,4},{1,3},{4,8},{5,1},{8,12},{9,5},{12,14},{13,9},{14,10},{15,13... | collective-permute-start | bytes 4718600 | tf_op jit(solution)/shard_map/ppermute | solution.py:404
  101.8 2.9 %some_ranks.5.refs_5_ = f32[48,128]{1,0:T(8,128)S(1)} custom-call(bf16[48,16384]{1,0:T(8,128)(2,1)} %collective-permute-done.10.x_ref.refs_0_, bf16[128,16384]{1,0:T(8,128)(2,1)S(1)} %copy-done.4), custom_call_target="tpu_custom_call" | custom-call | tf_op jit(solution)/shard_map/some_ranks/pallas_call | solution.py:299
  109.4 12.7 %blocks.11.refs_5_ = f32[16,48,1024]{2,1,0:T(8,128)S(1)} custom-call(bf16[48,16384]{1,0:T(8,128)(2,1)} %collective-permute-done.10.x_ref.refs_0_, bf16[48,16384]{1,0:T(8,128)(2,1)S(1)} %collective-permute-done.12.refs_1_, bf16[48,16384]{1,0:T(8,128)(2,1)S(1)} %collective-permute-done.5.x_ref.refs_2_, ...), custom_call_target="tpu_custom_call", output_to_operand_aliasing={{}: (5, {})} | custom-call | flops 6442450944 | bytes 33554432 | tf_op jit(solution)/shard_map/blocks/pallas_call | solution.py:263
  123.8 2.2 %ranks.1 = bf16[192,128]{1,0:T(8,128)(2,1)S(1)} custom-call(s32[16]{0:T(128)S(1)} %get-tuple-element.72.owners_ref, s32[8]{0:T(128)S(1)} %pad_add_fusion.slot_ref, bf16[48,16384]{1,0:T(8,128)(2,1)S(1)} %collective-permute-done.9.refs_0_.refs_2_, bf16[128,16384]{1,0:T(8,128)(2,1)S(1)} %copy-done.5, f32[48,128]{1,0:T(8,128)S(1)} %some_ranks.4.refs_2_, ...), custom_call_target="tpu_custom_call" | custom-call | tf_op jit(solution)/shard_map/ranks/pallas_call | solution.py:336
  126.0 2.1 %collective-permute-start.14 = (bf16[192,128]{1,0:T(8,128)(2,1)S(1)}, bf16[192,128]{1,0:T(8,128)(2,1)S(1)}, u32[]{:S(2)}, u32[]{:S(2)}) collective-permute-start(bf16[192,128]{1,0:T(8,128)(2,1)S(1)} %ranks.1), channel_id=1, source_target_pairs={{0,2},{1,3},{2,0},{3,1},{4,6},{5,7},{6,4},{7,5},{8,10},{9,11},{10,... | collective-permute-start | bytes 147464 | tf_op jit(solution)/shard_map/ppermute | solution.py:404
  129.7 7.1 %blocks.12.refs_5_ = f32[16,48,1024]{2,1,0:T(8,128)S(1)} custom-call(bf16[48,16384]{1,0:T(8,128)(2,1)S(1)} %collective-permute-done.11.x_ref.refs_0_, bf16[48,16384]{1,0:T(8,128)(2,1)S(1)} %collective-permute-done.17.refs_1_, bf16[48,16384]{1,0:T(8,128)(2,1)S(1)} %collective-permute-done.9.refs_0_.refs_2_, ...), custom_call_target="tpu_custom_call", output_to_operand_aliasing={{}: (5, {})} | custom-call | flops 3221225472 | bytes 16777216 | tf_op jit(solution)/shard_map/blocks/pallas_call | solution.py:263
  136.9 3.0 %collective-permute-start.19 = (bf16[192,128]{1,0:T(8,128)(2,1)S(1)}, bf16[192,128]{1,0:T(8,128)(2,1)S(1)}, u32[]{:S(2)}, u32[]{:S(2)}) collective-permute-start(bf16[192,128]{1,0:T(8,128)(2,1)S(1)} %add_add_fusion), channel_id=1, source_target_pairs={{0,8},{1,9},{2,10},{3,11},{4,12},{5,13},{6,14},{7,15},{8,0},{9,1},... | collective-permute-start | bytes 147464 | tf_op jit(solution)/shard_map/ppermute | solution.py:404
  140.1 7.2 %blocks.13.total_ref = f32[16,48,1024]{2,1,0:T(8,128)S(1)} custom-call(bf16[48,16384]{1,0:T(8,128)(2,1)S(1)} %collective-permute-done.11.x_ref.refs_0_, bf16[48,16384]{1,0:T(8,128)(2,1)S(1)} %collective-permute-done.17.refs_1_, bf16[48,16384]{1,0:T(8,128)(2,1)S(1)} %collective-permute-done.9.refs_0_.refs_2_, ...), custom_call_target="tpu_custom_call", output_to_operand_aliasing={{}: (5, {})} | custom-call | flops 3221225472 | bytes 16777216 | tf_op jit(solution)/shard_map/blocks/pallas_call | solution.py:263
  147.4 2.6 %finish.1 = bf16[768,1024]{1,0:T(8,128)(2,1)} custom-call(s32[16]{0:T(128)S(1)} %get-tuple-element.69.places_ref, s32[6]{0:T(128)S(1)} %gather_fusion, s32[1]{0:T(128)} %bitcast.7.core_ref, f32[16,48,1024]{2,1,0:T(8,128)S(1)} %blocks.13.total_ref, bf16[16,64,1024]{2,1,0:T(8,128)(2,1)S(1)} %bitcast.14, f32[1,1024]{1,0:T(1,128)S(1)} %bitcast.15, ...), custom_call_target="tpu_custom_call" | custom-call | tf_op jit(solution)/shard_map/finish/pallas_call | solution.py:383
  (69 shorter events, 21.5 us)
Async XLA Ops:
  0.0 61.2 %copy-start = (s32[16]{0:T(128)S(1)}, s32[16]{0:T(128)}, u32[]{:S(2)}) copy-start(s32[16]{0:T(128)} %param.16) | copy-start | bytes 196
  0.0 23.6 %collective-permute-start.1 = (bf16[64,16384]{1,0:T(8,128)(2,1)}, bf16[64,16384]{1,0:T(8,128)(2,1)S(1)}, u32[]{:S(2)}, u32[]{:S(2)}) collective-permute-start(bf16[64,16384]{1,0:T(8,128)(2,1)} %bitcast.16), channel_id=1, source_target_pairs={{0,1},{1,0},{2,3},{3,2},{4,5},{5,4},{6,7},{7,6},{8,9},{9,8},{10,11... | collective-permute-start | bytes 6291464 | tf_op jit(solution)/shard_map/ppermute | solution.py:404
  0.5 6.2 %collective-permute-start.2 = (bf16[48,16384]{1,0:T(8,128)(2,1)}, bf16[48,16384]{1,0:T(8,128)(2,1)S(1)}, u32[]{:S(2)}, u32[]{:S(2)}) collective-permute-start(bf16[48,16384]{1,0:T(8,128)(2,1)} %refs_0_.3), channel_id=1, source_target_pairs={{0,1},{1,0},{2,3},{3,2},{4,5},{5,4},{6,7},{7,6},{8,9},{9,8},{10,11... | collective-permute-start | bytes 4718600 | tf_op jit(solution)/shard_map/ppermute | solution.py:404
  0.5 29.7 %collective-permute-start = (bf16[48,16384]{1,0:T(8,128)(2,1)}, bf16[48,16384]{1,0:T(8,128)(2,1)}, u32[]{:S(2)}, u32[]{:S(2)}) collective-permute-start(bf16[48,16384]{1,0:T(8,128)(2,1)} %refs_0_.3), channel_id=1, source_target_pairs={{0,4},{1,3},{4,8},{5,1},{8,12},{9,5},{12,14},{13,9},{14,10},{15,13... | collective-permute-start | bytes 4718600 | tf_op jit(solution)/shard_map/ppermute | solution.py:404
  9.8 32.7 %collective-permute-start.6 = (bf16[48,16384]{1,0:T(8,128)(2,1)}, bf16[48,16384]{1,0:T(8,128)(2,1)}, u32[]{:S(2)}, u32[]{:S(2)}) collective-permute-start(bf16[48,16384]{1,0:T(8,128)(2,1)} %refs_0_.3), channel_id=1, source_target_pairs={{0,2},{1,5},{4,0},{5,9},{8,4},{9,13},{12,8},{13,15},{14,12},{15,11... | collective-permute-start | bytes 4718600 | tf_op jit(solution)/shard_map/ppermute | solution.py:404
  30.3 15.2 %collective-permute-start.3 = (bf16[48,16384]{1,0:T(8,128)(2,1)}, bf16[48,16384]{1,0:T(8,128)(2,1)}, u32[]{:S(2)}, u32[]{:S(2)}) collective-permute-start(bf16[48,16384]{1,0:T(8,128)(2,1)} %collective-permute-done.refs_0_), channel_id=1, source_target_pairs={{0,1},{1,0},{2,3},{3,2},{4,5},{5,4},{6,7},{7,6},{8,9},{9,8},{10,11... | collective-permute-start | bytes 4718600 | tf_op jit(solution)/shard_map/ppermute | solution.py:404
  30.3 30.0 %copy-start.9 = (s32[8]{0:T(128)S(1)}, s32[8]{0:T(128)}, u32[]{:S(2)}) copy-start(s32[8]{0:T(128)} %param.17) | copy-start | bytes 100
  30.3 34.6 %collective-permute-start.4 = (bf16[48,16384]{1,0:T(8,128)(2,1)}, bf16[48,16384]{1,0:T(8,128)(2,1)}, u32[]{:S(2)}, u32[]{:S(2)}) collective-permute-start(bf16[48,16384]{1,0:T(8,128)(2,1)} %collective-permute-done.refs_0_), channel_id=1, source_target_pairs={{0,4},{1,3},{4,8},{5,1},{8,12},{9,5},{12,14},{13,9},{14,10},{15,13... | collective-permute-start | bytes 4718600 | tf_op jit(solution)/shard_map/ppermute | solution.py:404
  42.5 32.9 %collective-permute-start.10 = (bf16[48,16384]{1,0:T(8,128)(2,1)}, bf16[48,16384]{1,0:T(8,128)(2,1)}, u32[]{:S(2)}, u32[]{:S(2)}) collective-permute-start(bf16[48,16384]{1,0:T(8,128)(2,1)} %collective-permute-done.6.refs_0_), channel_id=1, source_target_pairs={{0,2},{1,5},{4,0},{5,9},{8,4},{9,13},{12,8},{13,15},{14,12},{15,11... | collective-permute-start | bytes 4718600 | tf_op jit(solution)/shard_map/ppermute | solution.py:404
  44.2 34.0 %collective-permute-start.7 = (bf16[48,16384]{1,0:T(8,128)(2,1)}, bf16[48,16384]{1,0:T(8,128)(2,1)}, u32[]{:S(2)}, u32[]{:S(2)}) collective-permute-start(bf16[48,16384]{1,0:T(8,128)(2,1)} %collective-permute-done.6.refs_0_), channel_id=1, source_target_pairs={{0,1},{1,0},{2,3},{3,2},{4,5},{5,4},{6,7},{7,6},{8,9},{9,8},{10,11... | collective-permute-start | bytes 4718600 | tf_op jit(solution)/shard_map/ppermute | solution.py:404
  64.9 13.3 %collective-permute-start.8 = (bf16[48,16384]{1,0:T(8,128)(2,1)}, bf16[48,16384]{1,0:T(8,128)(2,1)S(1)}, u32[]{:S(2)}, u32[]{:S(2)}) collective-permute-start(bf16[48,16384]{1,0:T(8,128)(2,1)} %collective-permute-done.4.refs_2_), channel_id=1, source_target_pairs={{0,1},{1,0},{2,3},{3,2},{4,5},{5,4},{6,7},{7,6},{8,9},{9,8},{10,11... | collective-permute-start | bytes 4718600 | tf_op jit(solution)/shard_map/ppermute | solution.py:404
  64.9 34.6 %collective-permute-start.5 = (bf16[48,16384]{1,0:T(8,128)(2,1)}, bf16[48,16384]{1,0:T(8,128)(2,1)S(1)}, u32[]{:S(2)}, u32[]{:S(2)}) collective-permute-start(bf16[48,16384]{1,0:T(8,128)(2,1)} %collective-permute-done.4.refs_2_), channel_id=1, source_target_pairs={{0,4},{1,3},{4,8},{5,1},{8,12},{9,5},{12,14},{13,9},{14,10},{15,13... | collective-permute-start | bytes 4718600 | tf_op jit(solution)/shard_map/ppermute | solution.py:404
  75.4 33.0 %collective-permute-start.11 = (bf16[48,16384]{1,0:T(8,128)(2,1)}, bf16[48,16384]{1,0:T(8,128)(2,1)S(1)}, u32[]{:S(2)}, u32[]{:S(2)}) collective-permute-start(bf16[48,16384]{1,0:T(8,128)(2,1)} %collective-permute-done.10.x_ref.refs_0_), channel_id=1, source_target_pairs={{0,2},{1,5},{4,0},{5,9},{8,4},{9,13},{12,8},{13,15},{14,12},{15,11... | collective-permute-start | bytes 4718600 | tf_op jit(solution)/shard_map/ppermute | solution.py:404
  77.1 32.4 %collective-permute-start.12 = (bf16[48,16384]{1,0:T(8,128)(2,1)}, bf16[48,16384]{1,0:T(8,128)(2,1)S(1)}, u32[]{:S(2)}, u32[]{:S(2)}) collective-permute-start(bf16[48,16384]{1,0:T(8,128)(2,1)} %collective-permute-done.10.x_ref.refs_0_), channel_id=1, source_target_pairs={{0,1},{1,0},{2,3},{3,2},{4,5},{5,4},{6,7},{7,6},{8,9},{9,8},{10,11... | collective-permute-start | bytes 4718600 | tf_op jit(solution)/shard_map/ppermute | solution.py:404
  99.5 10.0 %collective-permute-start.13 = (bf16[48,16384]{1,0:T(8,128)(2,1)S(1)}, bf16[48,16384]{1,0:T(8,128)(2,1)S(1)}, u32[]{:S(2)}, u32[]{:S(2)}) collective-permute-start(bf16[48,16384]{1,0:T(8,128)(2,1)S(1)} %collective-permute-done.5.x_ref.refs_2_), channel_id=1, source_target_pairs={{0,1},{1,0},{2,3},{3,2},{4,5},{5,4},{6,7},{7,6},{8,9},{9,8},{10,11... | collective-permute-start | bytes 4718600 | tf_op jit(solution)/shard_map/ppermute | solution.py:404
  99.5 24.2 %collective-permute-start.9 = (bf16[48,16384]{1,0:T(8,128)(2,1)S(1)}, bf16[48,16384]{1,0:T(8,128)(2,1)S(1)}, u32[]{:S(2)}, u32[]{:S(2)}) collective-permute-start(bf16[48,16384]{1,0:T(8,128)(2,1)S(1)} %collective-permute-done.5.x_ref.refs_2_), channel_id=1, source_target_pairs={{0,4},{1,3},{4,8},{5,1},{8,12},{9,5},{12,14},{13,9},{14,10},{15,13... | collective-permute-start | bytes 4718600 | tf_op jit(solution)/shard_map/ppermute | solution.py:404
  108.3 21.4 %collective-permute-start.17 = (bf16[48,16384]{1,0:T(8,128)(2,1)S(1)}, bf16[48,16384]{1,0:T(8,128)(2,1)S(1)}, u32[]{:S(2)}, u32[]{:S(2)}) collective-permute-start(bf16[48,16384]{1,0:T(8,128)(2,1)S(1)} %collective-permute-done.11.x_ref.refs_0_), channel_id=1, source_target_pairs={{0,1},{1,0},{2,3},{3,2},{4,5},{5,4},{6,7},{7,6},{8,9},{9,8},{10,11... | collective-permute-start | bytes 4718600 | tf_op jit(solution)/shard_map/ppermute | solution.py:404
  123.7 6.0 %collective-permute-start.18 = (bf16[48,16384]{1,0:T(8,128)(2,1)S(1)}, bf16[48,16384]{1,0:T(8,128)(2,1)S(1)}, u32[]{:S(2)}, u32[]{:S(2)}) collective-permute-start(bf16[48,16384]{1,0:T(8,128)(2,1)S(1)} %collective-permute-done.9.refs_0_.refs_2_), channel_id=1, source_target_pairs={{0,1},{1,0},{2,3},{3,2},{4,5},{5,4},{6,7},{7,6},{8,9},{9,8},{10,11... | collective-permute-start | bytes 4718600 | tf_op jit(solution)/shard_map/ppermute | solution.py:404
  126.0 10.8 %collective-permute-start.14 = (bf16[192,128]{1,0:T(8,128)(2,1)S(1)}, bf16[192,128]{1,0:T(8,128)(2,1)S(1)}, u32[]{:S(2)}, u32[]{:S(2)}) collective-permute-start(bf16[192,128]{1,0:T(8,128)(2,1)S(1)} %ranks.1), channel_id=1, source_target_pairs={{0,2},{1,3},{2,0},{3,1},{4,6},{5,7},{6,4},{7,5},{8,10},{9,11},{10,... | collective-permute-start | bytes 147464 | tf_op jit(solution)/shard_map/ppermute | solution.py:404
  128.1 8.7 %collective-permute-start.15 = (bf16[192,128]{1,0:T(8,128)(2,1)S(1)}, bf16[192,128]{1,0:T(8,128)(2,1)S(1)}, u32[]{:S(2)}, u32[]{:S(2)}) collective-permute-start(bf16[192,128]{1,0:T(8,128)(2,1)S(1)} %ranks.1), channel_id=1, source_target_pairs={{0,4},{1,5},{2,6},{3,7},{4,0},{5,1},{6,2},{7,3},{8,12},{9,13},{10,... | collective-permute-start | bytes 147464 | tf_op jit(solution)/shard_map/ppermute | solution.py:404
  129.7 7.1 %collective-permute-start.16 = (bf16[192,128]{1,0:T(8,128)(2,1)S(1)}, bf16[192,128]{1,0:T(8,128)(2,1)S(1)}, u32[]{:S(2)}, u32[]{:S(2)}) collective-permute-start(bf16[192,128]{1,0:T(8,128)(2,1)S(1)} %ranks.1), channel_id=1, source_target_pairs={{0,6},{1,7},{2,4},{3,5},{4,2},{5,3},{6,0},{7,1},{8,14},{9,15},{10,... | collective-permute-start | bytes 147464 | tf_op jit(solution)/shard_map/ppermute | solution.py:404
  136.9 10.4 %collective-permute-start.19 = (bf16[192,128]{1,0:T(8,128)(2,1)S(1)}, bf16[192,128]{1,0:T(8,128)(2,1)S(1)}, u32[]{:S(2)}, u32[]{:S(2)}) collective-permute-start(bf16[192,128]{1,0:T(8,128)(2,1)S(1)} %add_add_fusion), channel_id=1, source_target_pairs={{0,8},{1,9},{2,10},{3,11},{4,12},{5,13},{6,14},{7,15},{8,0},{9,1},... | collective-permute-start | bytes 147464 | tf_op jit(solution)/shard_map/ppermute | solution.py:404
  139.9 7.4 %collective-permute-start.20 = (bf16[192,128]{1,0:T(8,128)(2,1)S(1)}, bf16[192,128]{1,0:T(8,128)(2,1)S(1)}, u32[]{:S(2)}, u32[]{:S(2)}) collective-permute-start(bf16[192,128]{1,0:T(8,128)(2,1)S(1)} %add_add_fusion), channel_id=1, source_target_pairs={{0,1},{1,0},{2,3},{3,2},{4,5},{5,4},{6,7},{7,6},{8,9},{9,8},{10,11... | collective-permute-start | bytes 147464 | tf_op jit(solution)/shard_map/ppermute | solution.py:404
  139.9 7.4 %collective-permute-start.21 = (bf16[192,128]{1,0:T(8,128)(2,1)S(1)}, bf16[192,128]{1,0:T(8,128)(2,1)S(1)}, u32[]{:S(2)}, u32[]{:S(2)}) collective-permute-start(bf16[192,128]{1,0:T(8,128)(2,1)S(1)} %add_add_fusion), channel_id=1, source_target_pairs={{0,9},{1,8},{2,11},{3,10},{4,13},{5,12},{6,15},{7,14},{8,1},{9,0},... | collective-permute-start | bytes 147464 | tf_op jit(solution)/shard_map/ppermute | solution.py:404
  (8 other events, 58.7 us)

commit v15 on v14

--- a/solution.py
+++ b/solution.py
@@ -195,7 +195,7 @@
             cut = xs[i].at[:, pl.ds(low + at, tile)]
             out.append(pltpu.make_async_copy(cut, x_slots.at[slot, pl.ds(i * rows, rows)], sem(i)))
         if ranked:
-            cut = s_ref.at[:, pl.ds(low + at, tile)]
+            cut = s_ref.at[pl.ds(low + at, tile)]
             out.append(pltpu.make_async_copy(cut, s_slots.at[slot], sem(count + 1)))
         return out
 
@@ -224,7 +224,7 @@
             acc[:, :, cut] += product.reshape(count, rows, CHUNK)
         if ranked:
             mine = jnp.concatenate([x[i * rows : (i + 1) * rows] for i in range(0, count, 2)], 0)
-            h_out[...] += lax.dot_general(mine, s_slots[slot], NT, preferred_element_type=F32)
+            h_out[...] += jnp.dot(mine, s_slots[slot], preferred_element_type=F32)
 
         @pl.when(step + SLOTS < steps)
         def _():
@@ -242,7 +242,7 @@
     count = len(xs)
     rows = xs[0].shape[0]
     cols = weights.shape[1]
-    rank = factors.shape[0]
+    rank = factors.shape[1]
     fresh, first = low == 0, total is None
     anywhere, whole = pl.BlockSpec(memory_space=pl.ANY), pl.BlockSpec(memory_space=pltpu.VMEM)
     operands = list(xs) + [weights]
@@ -270,7 +270,7 @@
             pltpu.VMEM((1, 8, 128) if fresh else (count, rows, cols), F32),
             pltpu.VMEM((SLOTS, count * rows, tile), BF16),
             pltpu.VMEM((SLOTS, tile, cols), BF16),
-            pltpu.VMEM((SLOTS, rank, tile), BF16),
+            pltpu.VMEM((SLOTS, tile, rank), BF16),
             pltpu.SemaphoreType.DMA((SLOTS, count + 2)),
             pltpu.SemaphoreType.DMA((2,)),
         ],
@@ -291,7 +291,7 @@
 
 
 def some_ranks_kernel(x_ref, s_ref, out_ref):
-    out_ref[...] = lax.dot_general(x_ref[...], s_ref[...], NT, preferred_element_type=F32)
+    out_ref[...] = jnp.dot(x_ref[...], s_ref[...], preferred_element_type=F32)
 
 
 def some_ranks(x, factors):
@@ -300,7 +300,7 @@
         some_ranks_kernel,
         in_specs=[whole] * 2,
         out_specs=whole,
-        out_shape=jax.ShapeDtypeStruct((x.shape[0], factors.shape[0]), F32),
+        out_shape=jax.ShapeDtypeStruct((x.shape[0], factors.shape[1]), F32),
         compiler_params=PARAMS,
         name="some_ranks",
     )(x, factors)
@@ -309,9 +309,9 @@
 def rank_kernel(count, owners_ref, slot_ref, *refs):
     xs, refs = refs[:count], refs[count:]
     s_ref, h_refs, out_ref, placed = refs[0], refs[1:-2], refs[-2], refs[-1]
-    rows, rank = xs[0].shape[0], s_ref.shape[0] // 2
+    rows, rank = xs[0].shape[0], s_ref.shape[1] // 2
     x = jnp.concatenate([ref[...] for ref in xs], 0)
-    last = lax.dot_general(x, s_ref[...], NT, preferred_element_type=F32)
+    last = jnp.dot(x, s_ref[...], preferred_element_type=F32)
     segments = slot_ref.shape[0] - 2
     block = 0
     for source in h_refs + (last,):
@@ -330,7 +330,7 @@
 
 
 def rank_terms(owners, slots, xs, factors, hs):
-    rank = factors.shape[0] // 2
+    rank = factors.shape[1] // 2
     core_rows = owners.shape[0] // 2 * xs[0].shape[0]
     scalars, whole = pl.BlockSpec(memory_space=pltpu.SMEM), pl.BlockSpec(memory_space=pltpu.VMEM)
     return pl.pallas_call(
@@ -415,7 +415,7 @@
         return total
 
     streams = [send(tokens, out), None]
-    own, factors = [tokens, swap(tokens)], jnp.concatenate([shrinks[0], swap(shrinks[0])], 0)
+    own, factors = [tokens, swap(tokens)], jnp.concatenate([shrinks[0], swap(shrinks[0])], 0).T
     part = 2 * tile
     total, _ = block_product(own, weights, factors, 0, part, tile, None, 0, False)
     second, total = lax.optimization_barrier((tokens, total))

time: 150 us -> 160 us (1.067)
  local copies, waits for them, and re-layouts: 6.55 us -> 18.7 us
  starting transfers between devices: 27.5 us -> 19.3 us
  waiting for transfers between devices: 31.3 us -> 36.3 us
  other arithmetic: 2.52 us -> 6.78 us
  Pallas kernels: 81.7 us -> 77.7 us
    ppermute x22, starting transfers between devices: 27.5 us -> 19.3 us  [ring_plan(): send = lambda value, pairs: lax.ppermute(value, 'tensor', pairs)]
    unnamed x20 -> x23, local copies, waits for them, and re-layouts: 4.42 us -> 11.7 us
    ppermute x22, waiting for transfers between devices: 31.3 us -> 36.3 us  [ring_plan(): send = lambda value, pairs: lax.ppermute(value, 'tensor', pairs)]
    ppermute x0 -> x1, local copies, waits for them, and re-layouts: none -> 4.9 us  [ring_plan(): send = lambda value, pairs: lax.ppermute(value, 'tensor', pairs)]
    transpose x0 -> x1, other arithmetic: none -> 4.64 us  [ring_plan(): jnp.concatenate([shrinks[0], swap(shrinks[0])], 0)]
    pallas_call x4, Pallas kernels: 10.1 us -> 6.93 us  [some_ranks(): pl.pallas_call(some_ranks_kernel, in_specs=[whole] * 2, out_specs=whole,...]
  transfers between devices with their start and end apart: 22 -> 22, of which waited for: 7 -> 5; matrix products, arithmetic and copies ran while one was open for 3% -> 12% of each run, Pallas kernels for 53% -> 47%
where the time goes in v15:
time: 160 us; the launch traced here: 159 us
  Pallas kernels  77.7 us (49%)
  waiting for transfers between devices  36.3 us (23%)
  starting transfers between devices  19.3 us (12%)
  local copies, waits for them, and re-layouts  18.7 us (12%)
  other arithmetic  6.78 us (4%)
    pallas_call x7, Pallas kernels, block_product(): pl.pallas_call(functools.partial(block_kernel, count, low, tile, steps, f...  66.8 us
    ppermute x22, waiting for transfers between devices, ring_plan(): send = lambda value, pairs: lax.ppermute(value, 'tensor', pairs)  36.3 us
    ppermute x22, starting transfers between devices, ring_plan(): send = lambda value, pairs: lax.ppermute(value, 'tensor', pairs)  19.3 us
    unnamed x23, local copies, waits for them, and re-layouts  11.7 us
    pallas_call x4, Pallas kernels, some_ranks(): pl.pallas_call(some_ranks_kernel, in_specs=[whole] * 2, out_specs=whole,...  6.93 us
    ppermute x1, local copies, waits for them, and re-layouts, ring_plan(): send = lambda value, pairs: lax.ppermute(value, 'tensor', pairs)  4.9 us
    transpose x1, other arithmetic, ring_plan(): jnp.concatenate([shrinks[0], swap(shrinks[0])], 0)  4.64 us
  transfers between devices with their start and end apart: 22, of which 5 were waited for; matrix products, arithmetic and copies ran while one was open for 12% of the time, Pallas kernels for 47%

profile of v15, /device:TPU:0, one launch (start us, length us, event | category | flops | bytes accessed | tf_op | source)
XLA Modules:
  0.0 159.3 jit_solution(13332085823884121643)
XLA Ops:
  0.5 3.0 %collective-permute-start = (bf16[48,16384]{1,0:T(8,128)(2,1)}, bf16[48,16384]{1,0:T(8,128)(2,1)}, u32[]{:S(2)}, u32[]{:S(2)}) collective-permute-start(bf16[48,16384]{1,0:T(8,128)(2,1)} %refs_0_.3), channel_id=1, source_target_pairs={{0,4},{1,3},{4,8},{5,1},{8,12},{9,5},{12,14},{13,9},{14,10},{15,13... | collective-permute-start | bytes 4718600 | tf_op jit(solution)/shard_map/ppermute | solution.py:404
  3.5 4.8 %copy.22 = bf16[1,16384,64]{2,1,0:T(8,128)(2,1)} copy(bf16[1,16384,64]{1,2,0:T(8,128)(2,1)} %param.13) | data formatting | bytes 4194304 | tf_op args[3]
  10.9 3.1 %blocks.7.refs_3_ = f32[16,48,1024]{2,1,0:T(8,128)S(1)} custom-call(bf16[48,16384]{1,0:T(8,128)(2,1)} %refs_0_.3, bf16[48,16384]{1,0:T(8,128)(2,1)S(1)} %copy-done.7, bf16[16384,1024]{1,0:T(8,128)(2,1)} %refs_4_.7), custom_call_target="tpu_custom_call" | custom-call | flops 402653184 | bytes 4194304 | tf_op jit(solution)/shard_map/blocks/pallas_call | solution.py:263
  15.2 10.9 %blocks.8.refs_4_ = f32[16,48,1024]{2,1,0:T(8,128)S(1)} custom-call(bf16[48,16384]{1,0:T(8,128)(2,1)} %refs_0_.3, bf16[48,16384]{1,0:T(8,128)(2,1)S(1)} %copy-done.7, bf16[16384,1024]{1,0:T(8,128)(2,1)} %refs_4_.7, f32[16,48,1024]{2,1,0:T(8,128)S(1)} %blocks.7.refs_3_), custom_call_target="tpu_custom_call", output_to_operand_aliasing={{}: (3, {})} | custom-call | flops 2818572288 | bytes 29360128 | tf_op jit(solution)/shard_map/blocks/pallas_call | solution.py:263
  26.2 4.9 %copy.24 = bf16[64,16384]{0,1:T(8,128)(2,1)} copy(bf16[64,16384]{1,0:T(8,128)(2,1)} %collective-permute-done.1) | data formatting | bytes 4194304 | tf_op jit(solution)/shard_map/ppermute | solution.py:404
  31.1 4.6 %maximum_bitcast_fusion.s_ref.refs_3_.refs_5_.refs_1_ = bf16[16384,128]{1,0:T(8,128)(2,1)S(1)} fusion(bf16[64,16384]{0,1:T(8,128)(2,1)} %copy.24, bf16[64,16384]{0,1:T(8,128)(2,1)} %bitcast.19), kind=kLoop, calls=%fused_computation.1 | loop fusion | flops 8388608 | bytes 8388608 | tf_op jit(solution)/shard_map/transpose | solution.py:418
  35.7 3.3 %some_ranks.4.refs_2_ = f32[48,128]{1,0:T(8,128)S(1)} custom-call(bf16[48,16384]{1,0:T(8,128)(2,1)} %refs_0_.3, bf16[16384,128]{1,0:T(8,128)(2,1)S(1)} %maximum_bitcast_fusion.s_ref.refs_3_.refs_5_.refs_1_), custom_call_target="tpu_custom_call" | custom-call | tf_op jit(solution)/shard_map/some_ranks/pallas_call | solution.py:299
  41.2 1.6 %collective-permute-done.3.refs_1_ = bf16[48,16384]{1,0:T(8,128)(2,1)} collective-permute-done((bf16[48,16384]{1,0:T(8,128)(2,1)}, bf16[48,16384]{1,0:T(8,128)(2,1)}, u32[]{:S(2)}, u32[]{:S(2)}) %collective-permute-start.3) | collective-permute-done | bytes 1572896 | tf_op jit(solution)/shard_map/ppermute | solution.py:404
  42.9 2.2 %copy-done.3 = bf16[16384,128]{1,0:T(8,128)(2,1)S(1)} copy-done((bf16[16384,128]{1,0:T(8,128)(2,1)S(1)}, bf16[16384,128]{1,0:T(8,128)(2,1)}, u32[]{:S(2)}) %copy-start.3) | copy-done | bytes 4194328
  45.1 12.6 %blocks.9 = (f32[16,48,1024]{2,1,0:T(8,128)S(1)}, f32[48,128]{1,0:T(8,128)S(1)}) custom-call(bf16[48,16384]{1,0:T(8,128)(2,1)} %collective-permute-done.refs_0_, bf16[48,16384]{1,0:T(8,128)(2,1)} %collective-permute-done.3.refs_1_, bf16[16384,1024]{1,0:T(8,128)(2,1)} %refs_4_.7, bf16[16384,128]{1,0:T(8,128)(2,1)S(1)} %copy-done.3, ...), custom_call_target="tpu_custom_call", output_to_operand_aliasing={{0}: (4, {})} | custom-call | flops 3221225472 | bytes 33554432 | tf_op jit(solution)/shard_map/blocks/pallas_call | solution.py:263
  61.9 14.1 %collective-permute-done.4.refs_2_ = bf16[48,16384]{1,0:T(8,128)(2,1)} collective-permute-done((bf16[48,16384]{1,0:T(8,128)(2,1)}, bf16[48,16384]{1,0:T(8,128)(2,1)}, u32[]{:S(2)}, u32[]{:S(2)}) %collective-permute-start.4) | collective-permute-done | bytes 1572896 | tf_op jit(solution)/shard_map/ppermute | solution.py:404
  76.0 2.0 %collective-permute-start.5 = (bf16[48,16384]{1,0:T(8,128)(2,1)}, bf16[48,16384]{1,0:T(8,128)(2,1)S(1)}, u32[]{:S(2)}, u32[]{:S(2)}) collective-permute-start(bf16[48,16384]{1,0:T(8,128)(2,1)} %collective-permute-done.4.refs_2_), channel_id=1, source_target_pairs={{0,4},{1,3},{4,8},{5,1},{8,12},{9,5},{12,14},{13,9},{14,10},{15,13... | collective-permute-start | bytes 4718600 | tf_op jit(solution)/shard_map/ppermute | solution.py:404
  79.6 2.2 %copy-done.4 = bf16[16384,128]{1,0:T(8,128)(2,1)S(1)} copy-done((bf16[16384,128]{1,0:T(8,128)(2,1)S(1)}, bf16[16384,128]{1,0:T(8,128)(2,1)}, u32[]{:S(2)}) %copy-start.4) | copy-done | bytes 4194328
  81.8 13.3 %blocks.10 = (f32[16,48,1024]{2,1,0:T(8,128)S(1)}, f32[96,128]{1,0:T(8,128)S(1)}) custom-call(bf16[48,16384]{1,0:T(8,128)(2,1)} %collective-permute-done.6.refs_0_, bf16[48,16384]{1,0:T(8,128)(2,1)} %collective-permute-done.7.refs_1_, bf16[48,16384]{1,0:T(8,128)(2,1)} %collective-permute-done.4.refs_2_, ...), custom_call_target="tpu_custom_call", output_to_operand_aliasing={{0}: (6, {})} | custom-call | flops 6442450944 | bytes 33554432 | tf_op jit(solution)/shard_map/blocks/pallas_call | solution.py:263
  95.1 17.6 %collective-permute-done.5.x_ref.refs_2_ = bf16[48,16384]{1,0:T(8,128)(2,1)S(1)} collective-permute-done((bf16[48,16384]{1,0:T(8,128)(2,1)}, bf16[48,16384]{1,0:T(8,128)(2,1)S(1)}, u32[]{:S(2)}, u32[]{:S(2)}) %collective-permute-start.5) | collective-permute-done | bytes 1572896 | tf_op jit(solution)/shard_map/ppermute | solution.py:404
  112.7 2.4 %collective-permute-start.9 = (bf16[48,16384]{1,0:T(8,128)(2,1)S(1)}, bf16[48,16384]{1,0:T(8,128)(2,1)S(1)}, u32[]{:S(2)}, u32[]{:S(2)}) collective-permute-start(bf16[48,16384]{1,0:T(8,128)(2,1)S(1)} %collective-permute-done.5.x_ref.refs_2_), channel_id=1, source_target_pairs={{0,4},{1,3},{4,8},{5,1},{8,12},{9,5},{12,14},{13,9},{14,10},{15,13... | collective-permute-start | bytes 4718600 | tf_op jit(solution)/shard_map/ppermute | solution.py:404
  115.1 2.1 %some_ranks.5.refs_5_ = f32[48,128]{1,0:T(8,128)S(1)} custom-call(bf16[48,16384]{1,0:T(8,128)(2,1)} %collective-permute-done.10.x_ref.refs_0_, bf16[16384,128]{1,0:T(8,128)(2,1)S(1)} %copy-done.4), custom_call_target="tpu_custom_call" | custom-call | tf_op jit(solution)/shard_map/some_ranks/pallas_call | solution.py:299
  118.1 12.7 %blocks.11.refs_5_ = f32[16,48,1024]{2,1,0:T(8,128)S(1)} custom-call(bf16[48,16384]{1,0:T(8,128)(2,1)} %collective-permute-done.10.x_ref.refs_0_, bf16[48,16384]{1,0:T(8,128)(2,1)S(1)} %collective-permute-done.12.refs_1_, bf16[48,16384]{1,0:T(8,128)(2,1)S(1)} %collective-permute-done.5.x_ref.refs_2_, ...), custom_call_target="tpu_custom_call", output_to_operand_aliasing={{}: (5, {})} | custom-call | flops 6442450944 | bytes 33554432 | tf_op jit(solution)/shard_map/blocks/pallas_call | solution.py:263
  131.5 1.6 collective-permute-done.9.refs_0_.refs_2_
  135.7 3.1 %collective-permute-start.15 = (bf16[192,128]{1,0:T(8,128)(2,1)S(1)}, bf16[192,128]{1,0:T(8,128)(2,1)S(1)}, u32[]{:S(2)}, u32[]{:S(2)}) collective-permute-start(bf16[192,128]{1,0:T(8,128)(2,1)S(1)} %ranks.1), channel_id=1, source_target_pairs={{0,4},{1,5},{2,6},{3,7},{4,0},{5,1},{6,2},{7,3},{8,12},{9,13},{10,... | collective-permute-start | bytes 147464 | tf_op jit(solution)/shard_map/ppermute | solution.py:404
  138.9 7.1 %blocks.12.refs_5_ = f32[16,48,1024]{2,1,0:T(8,128)S(1)} custom-call(bf16[48,16384]{1,0:T(8,128)(2,1)S(1)} %collective-permute-done.11.x_ref.refs_0_, bf16[48,16384]{1,0:T(8,128)(2,1)S(1)} %collective-permute-done.17.refs_1_, bf16[48,16384]{1,0:T(8,128)(2,1)S(1)} %collective-permute-done.9.refs_0_.refs_2_, ...), custom_call_target="tpu_custom_call", output_to_operand_aliasing={{}: (5, {})} | custom-call | flops 3221225472 | bytes 16777216 | tf_op jit(solution)/shard_map/blocks/pallas_call | solution.py:263
  146.0 3.1 %collective-permute-start.19 = (bf16[192,128]{1,0:T(8,128)(2,1)S(1)}, bf16[192,128]{1,0:T(8,128)(2,1)S(1)}, u32[]{:S(2)}, u32[]{:S(2)}) collective-permute-start(bf16[192,128]{1,0:T(8,128)(2,1)S(1)} %add_add_fusion), channel_id=1, source_target_pairs={{0,8},{1,9},{2,10},{3,11},{4,12},{5,13},{6,14},{7,15},{8,0},{9,1},... | collective-permute-start | bytes 147464 | tf_op jit(solution)/shard_map/ppermute | solution.py:404
  149.3 7.2 %blocks.13.total_ref = f32[16,48,1024]{2,1,0:T(8,128)S(1)} custom-call(bf16[48,16384]{1,0:T(8,128)(2,1)S(1)} %collective-permute-done.11.x_ref.refs_0_, bf16[48,16384]{1,0:T(8,128)(2,1)S(1)} %collective-permute-done.17.refs_1_, bf16[48,16384]{1,0:T(8,128)(2,1)S(1)} %collective-permute-done.9.refs_0_.refs_2_, ...), custom_call_target="tpu_custom_call", output_to_operand_aliasing={{}: (5, {})} | custom-call | flops 3221225472 | bytes 16777216 | tf_op jit(solution)/shard_map/blocks/pallas_call | solution.py:263
  156.6 2.6 %finish.1 = bf16[768,1024]{1,0:T(8,128)(2,1)} custom-call(s32[16]{0:T(128)S(1)} %get-tuple-element.69.places_ref, s32[6]{0:T(128)S(1)} %gather_fusion, s32[1]{0:T(128)} %bitcast.9.core_ref, f32[16,48,1024]{2,1,0:T(8,128)S(1)} %blocks.13.total_ref, bf16[16,64,1024]{2,1,0:T(8,128)(2,1)S(1)} %bitcast.17, f32[1,1024]{1,0:T(1,128)S(1)} %bitcast.18, ...), custom_call_target="tpu_custom_call" | custom-call | tf_op jit(solution)/shard_map/finish/pallas_call | solution.py:383
  (73 shorter events, 16.8 us)
Async XLA Ops:
  0.0 58.6 %copy-start = (s32[16]{0:T(128)S(1)}, s32[16]{0:T(128)}, u32[]{:S(2)}) copy-start(s32[16]{0:T(128)} %param.16) | copy-start | bytes 196
  0.0 26.1 %collective-permute-start.1 = (bf16[64,16384]{1,0:T(8,128)(2,1)}, bf16[64,16384]{1,0:T(8,128)(2,1)}, u32[]{:S(2)}, u32[]{:S(2)}) collective-permute-start(bf16[64,16384]{1,0:T(8,128)(2,1)} %bitcast.20), channel_id=1, source_target_pairs={{0,1},{1,0},{2,3},{3,2},{4,5},{5,4},{6,7},{7,6},{8,9},{9,8},{10,11... | collective-permute-start | bytes 6291464 | tf_op jit(solution)/shard_map/ppermute | solution.py:404
  0.5 7.8 %collective-permute-start.2 = (bf16[48,16384]{1,0:T(8,128)(2,1)}, bf16[48,16384]{1,0:T(8,128)(2,1)S(1)}, u32[]{:S(2)}, u32[]{:S(2)}) collective-permute-start(bf16[48,16384]{1,0:T(8,128)(2,1)} %refs_0_.3), channel_id=1, source_target_pairs={{0,1},{1,0},{2,3},{3,2},{4,5},{5,4},{6,7},{7,6},{8,9},{9,8},{10,11... | collective-permute-start | bytes 4718600 | tf_op jit(solution)/shard_map/ppermute | solution.py:404
  0.5 38.5 %collective-permute-start = (bf16[48,16384]{1,0:T(8,128)(2,1)}, bf16[48,16384]{1,0:T(8,128)(2,1)}, u32[]{:S(2)}, u32[]{:S(2)}) collective-permute-start(bf16[48,16384]{1,0:T(8,128)(2,1)} %refs_0_.3), channel_id=1, source_target_pairs={{0,4},{1,3},{4,8},{5,1},{8,12},{9,5},{12,14},{13,9},{14,10},{15,13... | collective-permute-start | bytes 4718600 | tf_op jit(solution)/shard_map/ppermute | solution.py:404
  13.9 26.7 %collective-permute-start.6 = (bf16[48,16384]{1,0:T(8,128)(2,1)}, bf16[48,16384]{1,0:T(8,128)(2,1)}, u32[]{:S(2)}, u32[]{:S(2)}) collective-permute-start(bf16[48,16384]{1,0:T(8,128)(2,1)} %refs_0_.3), channel_id=1, source_target_pairs={{0,2},{1,5},{4,0},{5,9},{8,4},{9,13},{12,8},{13,15},{14,12},{15,11... | collective-permute-start | bytes 4718600 | tf_op jit(solution)/shard_map/ppermute | solution.py:404
  39.0 3.8 %collective-permute-start.3 = (bf16[48,16384]{1,0:T(8,128)(2,1)}, bf16[48,16384]{1,0:T(8,128)(2,1)}, u32[]{:S(2)}, u32[]{:S(2)}) collective-permute-start(bf16[48,16384]{1,0:T(8,128)(2,1)} %collective-permute-done.refs_0_), channel_id=1, source_target_pairs={{0,1},{1,0},{2,3},{3,2},{4,5},{5,4},{6,7},{7,6},{8,9},{9,8},{10,11... | collective-permute-start | bytes 4718600 | tf_op jit(solution)/shard_map/ppermute | solution.py:404
  39.1 18.5 %copy-start.10 = (s32[8]{0:T(128)S(1)}, s32[8]{0:T(128)}, u32[]{:S(2)}) copy-start(s32[8]{0:T(128)} %param.17) | copy-start | bytes 100
  39.2 36.9 %collective-permute-start.4 = (bf16[48,16384]{1,0:T(8,128)(2,1)}, bf16[48,16384]{1,0:T(8,128)(2,1)}, u32[]{:S(2)}, u32[]{:S(2)}) collective-permute-start(bf16[48,16384]{1,0:T(8,128)(2,1)} %collective-permute-done.refs_0_), channel_id=1, source_target_pairs={{0,4},{1,3},{4,8},{5,1},{8,12},{9,5},{12,14},{13,9},{14,10},{15,13... | collective-permute-start | bytes 4718600 | tf_op jit(solution)/shard_map/ppermute | solution.py:404
  40.7 37.4 %collective-permute-start.10 = (bf16[48,16384]{1,0:T(8,128)(2,1)}, bf16[48,16384]{1,0:T(8,128)(2,1)}, u32[]{:S(2)}, u32[]{:S(2)}) collective-permute-start(bf16[48,16384]{1,0:T(8,128)(2,1)} %collective-permute-done.6.refs_0_), channel_id=1, source_target_pairs={{0,2},{1,5},{4,0},{5,9},{8,4},{9,13},{12,8},{13,15},{14,12},{15,11... | collective-permute-start | bytes 4718600 | tf_op jit(solution)/shard_map/ppermute | solution.py:404
  41.2 37.1 %collective-permute-start.7 = (bf16[48,16384]{1,0:T(8,128)(2,1)}, bf16[48,16384]{1,0:T(8,128)(2,1)}, u32[]{:S(2)}, u32[]{:S(2)}) collective-permute-start(bf16[48,16384]{1,0:T(8,128)(2,1)} %collective-permute-done.6.refs_0_), channel_id=1, source_target_pairs={{0,1},{1,0},{2,3},{3,2},{4,5},{5,4},{6,7},{7,6},{8,9},{9,8},{10,11... | collective-permute-start | bytes 4718600 | tf_op jit(solution)/shard_map/ppermute | solution.py:404
  76.0 3.6 %collective-permute-start.8 = (bf16[48,16384]{1,0:T(8,128)(2,1)}, bf16[48,16384]{1,0:T(8,128)(2,1)S(1)}, u32[]{:S(2)}, u32[]{:S(2)}) collective-permute-start(bf16[48,16384]{1,0:T(8,128)(2,1)} %collective-permute-done.4.refs_2_), channel_id=1, source_target_pairs={{0,1},{1,0},{2,3},{3,2},{4,5},{5,4},{6,7},{7,6},{8,9},{9,8},{10,11... | collective-permute-start | bytes 4718600 | tf_op jit(solution)/shard_map/ppermute | solution.py:404
  76.0 36.7 %collective-permute-start.5 = (bf16[48,16384]{1,0:T(8,128)(2,1)}, bf16[48,16384]{1,0:T(8,128)(2,1)S(1)}, u32[]{:S(2)}, u32[]{:S(2)}) collective-permute-start(bf16[48,16384]{1,0:T(8,128)(2,1)} %collective-permute-done.4.refs_2_), channel_id=1, source_target_pairs={{0,4},{1,3},{4,8},{5,1},{8,12},{9,5},{12,14},{13,9},{14,10},{15,13... | collective-permute-start | bytes 4718600 | tf_op jit(solution)/shard_map/ppermute | solution.py:404
  78.1 39.9 %collective-permute-start.11 = (bf16[48,16384]{1,0:T(8,128)(2,1)}, bf16[48,16384]{1,0:T(8,128)(2,1)S(1)}, u32[]{:S(2)}, u32[]{:S(2)}) collective-permute-start(bf16[48,16384]{1,0:T(8,128)(2,1)} %collective-permute-done.10.x_ref.refs_0_), channel_id=1, source_target_pairs={{0,2},{1,5},{4,0},{5,9},{8,4},{9,13},{12,8},{13,15},{14,12},{15,11... | collective-permute-start | bytes 4718600 | tf_op jit(solution)/shard_map/ppermute | solution.py:404
  78.1 40.0 %collective-permute-start.12 = (bf16[48,16384]{1,0:T(8,128)(2,1)}, bf16[48,16384]{1,0:T(8,128)(2,1)S(1)}, u32[]{:S(2)}, u32[]{:S(2)}) collective-permute-start(bf16[48,16384]{1,0:T(8,128)(2,1)} %collective-permute-done.10.x_ref.refs_0_), channel_id=1, source_target_pairs={{0,1},{1,0},{2,3},{3,2},{4,5},{5,4},{6,7},{7,6},{8,9},{9,8},{10,11... | collective-permute-start | bytes 4718600 | tf_op jit(solution)/shard_map/ppermute | solution.py:404
  112.7 5.4 %collective-permute-start.13 = (bf16[48,16384]{1,0:T(8,128)(2,1)S(1)}, bf16[48,16384]{1,0:T(8,128)(2,1)S(1)}, u32[]{:S(2)}, u32[]{:S(2)}) collective-permute-start(bf16[48,16384]{1,0:T(8,128)(2,1)S(1)} %collective-permute-done.5.x_ref.refs_2_), channel_id=1, source_target_pairs={{0,1},{1,0},{2,3},{3,2},{4,5},{5,4},{6,7},{7,6},{8,9},{9,8},{10,11... | collective-permute-start | bytes 4718600 | tf_op jit(solution)/shard_map/ppermute | solution.py:404
  112.7 20.4 %collective-permute-start.9 = (bf16[48,16384]{1,0:T(8,128)(2,1)S(1)}, bf16[48,16384]{1,0:T(8,128)(2,1)S(1)}, u32[]{:S(2)}, u32[]{:S(2)}) collective-permute-start(bf16[48,16384]{1,0:T(8,128)(2,1)S(1)} %collective-permute-done.5.x_ref.refs_2_), channel_id=1, source_target_pairs={{0,4},{1,3},{4,8},{5,1},{8,12},{9,5},{12,14},{13,9},{14,10},{15,13... | collective-permute-start | bytes 4718600 | tf_op jit(solution)/shard_map/ppermute | solution.py:404
  118.0 20.9 %collective-permute-start.17 = (bf16[48,16384]{1,0:T(8,128)(2,1)S(1)}, bf16[48,16384]{1,0:T(8,128)(2,1)S(1)}, u32[]{:S(2)}, u32[]{:S(2)}) collective-permute-start(bf16[48,16384]{1,0:T(8,128)(2,1)S(1)} %collective-permute-done.11.x_ref.refs_0_), channel_id=1, source_target_pairs={{0,1},{1,0},{2,3},{3,2},{4,5},{5,4},{6,7},{7,6},{8,9},{9,8},{10,11... | collective-permute-start | bytes 4718600 | tf_op jit(solution)/shard_map/ppermute | solution.py:404
  133.1 5.7 %collective-permute-start.18 = (bf16[48,16384]{1,0:T(8,128)(2,1)S(1)}, bf16[48,16384]{1,0:T(8,128)(2,1)S(1)}, u32[]{:S(2)}, u32[]{:S(2)}) collective-permute-start(bf16[48,16384]{1,0:T(8,128)(2,1)S(1)} %collective-permute-done.9.refs_0_.refs_2_), channel_id=1, source_target_pairs={{0,1},{1,0},{2,3},{3,2},{4,5},{5,4},{6,7},{7,6},{8,9},{9,8},{10,11... | collective-permute-start | bytes 4718600 | tf_op jit(solution)/shard_map/ppermute | solution.py:404
  134.7 11.3 %collective-permute-start.14 = (bf16[192,128]{1,0:T(8,128)(2,1)S(1)}, bf16[192,128]{1,0:T(8,128)(2,1)S(1)}, u32[]{:S(2)}, u32[]{:S(2)}) collective-permute-start(bf16[192,128]{1,0:T(8,128)(2,1)S(1)} %ranks.1), channel_id=1, source_target_pairs={{0,2},{1,3},{2,0},{3,1},{4,6},{5,7},{6,4},{7,5},{8,10},{9,11},{10,... | collective-permute-start | bytes 147464 | tf_op jit(solution)/shard_map/ppermute | solution.py:404
  135.7 10.3 %collective-permute-start.15 = (bf16[192,128]{1,0:T(8,128)(2,1)S(1)}, bf16[192,128]{1,0:T(8,128)(2,1)S(1)}, u32[]{:S(2)}, u32[]{:S(2)}) collective-permute-start(bf16[192,128]{1,0:T(8,128)(2,1)S(1)} %ranks.1), channel_id=1, source_target_pairs={{0,4},{1,5},{2,6},{3,7},{4,0},{5,1},{6,2},{7,3},{8,12},{9,13},{10,... | collective-permute-start | bytes 147464 | tf_op jit(solution)/shard_map/ppermute | solution.py:404
  138.9 7.1 %collective-permute-start.16 = (bf16[192,128]{1,0:T(8,128)(2,1)S(1)}, bf16[192,128]{1,0:T(8,128)(2,1)S(1)}, u32[]{:S(2)}, u32[]{:S(2)}) collective-permute-start(bf16[192,128]{1,0:T(8,128)(2,1)S(1)} %ranks.1), channel_id=1, source_target_pairs={{0,6},{1,7},{2,4},{3,5},{4,2},{5,3},{6,0},{7,1},{8,14},{9,15},{10,... | collective-permute-start | bytes 147464 | tf_op jit(solution)/shard_map/ppermute | solution.py:404
  146.0 10.4 %collective-permute-start.19 = (bf16[192,128]{1,0:T(8,128)(2,1)S(1)}, bf16[192,128]{1,0:T(8,128)(2,1)S(1)}, u32[]{:S(2)}, u32[]{:S(2)}) collective-permute-start(bf16[192,128]{1,0:T(8,128)(2,1)S(1)} %add_add_fusion), channel_id=1, source_target_pairs={{0,8},{1,9},{2,10},{3,11},{4,12},{5,13},{6,14},{7,15},{8,0},{9,1},... | collective-permute-start | bytes 147464 | tf_op jit(solution)/shard_map/ppermute | solution.py:404
  149.1 7.4 %collective-permute-start.20 = (bf16[192,128]{1,0:T(8,128)(2,1)S(1)}, bf16[192,128]{1,0:T(8,128)(2,1)S(1)}, u32[]{:S(2)}, u32[]{:S(2)}) collective-permute-start(bf16[192,128]{1,0:T(8,128)(2,1)S(1)} %add_add_fusion), channel_id=1, source_target_pairs={{0,1},{1,0},{2,3},{3,2},{4,5},{5,4},{6,7},{7,6},{8,9},{9,8},{10,11... | collective-permute-start | bytes 147464 | tf_op jit(solution)/shard_map/ppermute | solution.py:404
  149.1 7.4 %collective-permute-start.21 = (bf16[192,128]{1,0:T(8,128)(2,1)S(1)}, bf16[192,128]{1,0:T(8,128)(2,1)S(1)}, u32[]{:S(2)}, u32[]{:S(2)}) collective-permute-start(bf16[192,128]{1,0:T(8,128)(2,1)S(1)} %add_add_fusion), channel_id=1, source_target_pairs={{0,9},{1,8},{2,11},{3,10},{4,13},{5,12},{6,15},{7,14},{8,1},{9,0},... | collective-permute-start | bytes 147464 | tf_op jit(solution)/shard_map/ppermute | solution.py:404
  (9 other events, 46.7 us)

commit v16 on v15

--- a/solution.py
+++ b/solution.py
@@ -242,7 +242,7 @@
     count = len(xs)
     rows = xs[0].shape[0]
     cols = weights.shape[1]
-    rank = factors.shape[1]
+    rank = factors.shape[1] if ranked else 128
     fresh, first = low == 0, total is None
     anywhere, whole = pl.BlockSpec(memory_space=pl.ANY), pl.BlockSpec(memory_space=pltpu.VMEM)
     operands = list(xs) + [weights]
@@ -290,6 +290,29 @@
     return (2 * len(SNAKE), rows, cols)
 
 
+def turn_kernel(a_ref, b_ref, out_ref):
+    width = 2 * a_ref.shape[0]
+
+    @pl.loop(0, a_ref.shape[1] // width)
+    def _(step):
+        cut = pl.ds(pl.multiple_of(step * width, width), width)
+        both = jnp.concatenate([a_ref[:, cut], b_ref[:, cut]], 0)
+        out_ref[cut, :] = both.astype(F32).T.astype(out_ref.dtype)
+
+
+def turn(factors):
+    rank, depth = factors[0].shape
+    whole = pl.BlockSpec(memory_space=pltpu.VMEM)
+    return pl.pallas_call(
+        turn_kernel,
+        in_specs=[whole] * 2,
+        out_specs=whole,
+        out_shape=jax.ShapeDtypeStruct((depth, 2 * rank), BF16),
+        compiler_params=PARAMS,
+        name="turn",
+    )(*factors)
+
+
 def some_ranks_kernel(x_ref, s_ref, out_ref):
     out_ref[...] = jnp.dot(x_ref[...], s_ref[...], preferred_element_type=F32)
 
@@ -415,12 +438,13 @@
         return total
 
     streams = [send(tokens, out), None]
-    own, factors = [tokens, swap(tokens)], jnp.concatenate([shrinks[0], swap(shrinks[0])], 0).T
+    own, raw = [tokens, swap(tokens)], [shrinks[0], swap(shrinks[0])]
     part = 2 * tile
-    total, _ = block_product(own, weights, factors, 0, part, tile, None, 0, False)
+    total, _ = block_product(own, weights, None, 0, part, tile, None, 0, False)
     second, total = lax.optimization_barrier((tokens, total))
     streams[1] = send(second, home)
-    total, _ = block_product(own, weights, factors, part, depth, tile, total, 0, False)
+    total, _ = block_product(own, weights, None, part, depth, tile, total, 0, False)
+    factors = turn(raw)
     hs, total = lax.optimization_barrier(([some_ranks(tokens, factors)], total))
     counts.append(len(own))
 

time: 160 us -> 161 us (level)
  Pallas kernels: 77.7 us -> 91.1 us
  local copies, waits for them, and re-layouts: 18.7 us -> 6.55 us
  other arithmetic: 6.78 us -> 2.14 us
  waiting for transfers between devices: 36.3 us -> 39.5 us
    pallas_call x0 -> x1, Pallas kernels: none -> 13.3 us  [turn(): pl.pallas_call(turn_kernel, in_specs=[whole] * 2, out_specs=whole, out_sh...]
    unnamed x23 -> x20, local copies, waits for them, and re-layouts: 11.7 us -> 4.42 us
    ppermute x1 -> x0, local copies, waits for them, and re-layouts: 4.9 us -> none  [ring_plan(): send = lambda value, pairs: lax.ppermute(value, 'tensor', pairs)]
    transpose x1 -> x0, other arithmetic: 4.64 us -> none  [ring_plan(): jnp.concatenate([shrinks[0], swap(shrinks[0])], 0)]
    ppermute x22, waiting for transfers between devices: 36.3 us -> 39.5 us  [ring_plan(): send = lambda value, pairs: lax.ppermute(value, 'tensor', pairs)]
  transfers between devices with their start and end apart: 22 -> 22, of which waited for: 5 -> 6; matrix products, arithmetic and copies ran while one was open for 12% -> 3% of each run, Pallas kernels for 47% -> 55%
where the time goes in v16:
time: 161 us
  Pallas kernels  91.1 us (57%)
  waiting for transfers between devices  39.5 us (25%)
  starting transfers between devices  20.7 us (13%)
  local copies, waits for them, and re-layouts  6.55 us (4%)
  other arithmetic  2.14 us (1%)
    pallas_call x7, Pallas kernels, block_product(): pl.pallas_call(functools.partial(block_kernel, count, low, tile, steps, f...  66.9 us
    ppermute x22, waiting for transfers between devices, ring_plan(): send = lambda value, pairs: lax.ppermute(value, 'tensor', pairs)  39.5 us
    ppermute x22, starting transfers between devices, ring_plan(): send = lambda value, pairs: lax.ppermute(value, 'tensor', pairs)  20.7 us
    pallas_call x1, Pallas kernels, turn(): pl.pallas_call(turn_kernel, in_specs=[whole] * 2, out_specs=whole, out_sh...  13.3 us
    pallas_call x4, Pallas kernels, some_ranks(): pl.pallas_call(some_ranks_kernel, in_specs=[whole] * 2, out_specs=whole,...  6.98 us
    unnamed x20, local copies, waits for them, and re-layouts  4.42 us
  transfers between devices with their start and end apart: 22, of which 6 were waited for; matrix products, arithmetic and copies ran while one was open for 3% of the time, Pallas kernels for 55%

profile of v16, /device:TPU:0, one launch (start us, length us, event | category | flops | bytes accessed | tf_op | source)
XLA Modules:
  0.0 160.6 jit_solution(3159584115426760607)
XLA Ops:
  0.5 3.0 %collective-permute-start = (bf16[48,16384]{1,0:T(8,128)(2,1)}, bf16[48,16384]{1,0:T(8,128)(2,1)}, u32[]{:S(2)}, u32[]{:S(2)}) collective-permute-start(bf16[48,16384]{1,0:T(8,128)(2,1)} %refs_0_.3), channel_id=1, source_target_pairs={{0,4},{1,3},{4,8},{5,1},{8,12},{9,5},{12,14},{13,9},{14,10},{15,13... | collective-permute-start | bytes 4718600 | tf_op jit(solution)/shard_map/ppermute | solution.py:427
  3.5 3.2 %collective-permute-done.2.refs_1_ = bf16[48,16384]{1,0:T(8,128)(2,1)S(1)} collective-permute-done((bf16[48,16384]{1,0:T(8,128)(2,1)}, bf16[48,16384]{1,0:T(8,128)(2,1)S(1)}, u32[]{:S(2)}, u32[]{:S(2)}) %collective-permute-start.2) | collective-permute-done | bytes 1572896 | tf_op jit(solution)/shard_map/ppermute | solution.py:427
  6.7 3.1 %blocks.7.refs_3_ = f32[16,48,1024]{2,1,0:T(8,128)S(1)} custom-call(bf16[48,16384]{1,0:T(8,128)(2,1)} %refs_0_.3, bf16[48,16384]{1,0:T(8,128)(2,1)S(1)} %collective-permute-done.2.refs_1_, bf16[16384,1024]{1,0:T(8,128)(2,1)} %refs_4_.7), custom_call_target="tpu_custom_call" | custom-call | flops 402653184 | bytes 4194304 | tf_op jit(solution)/shard_map/blocks/pallas_call | solution.py:263
  9.8 2.9 %collective-permute-start.6 = (bf16[48,16384]{1,0:T(8,128)(2,1)}, bf16[48,16384]{1,0:T(8,128)(2,1)}, u32[]{:S(2)}, u32[]{:S(2)}) collective-permute-start(bf16[48,16384]{1,0:T(8,128)(2,1)} %refs_0_.3), channel_id=1, source_target_pairs={{0,2},{1,5},{4,0},{5,9},{8,4},{9,13},{12,8},{13,15},{14,12},{15,11... | collective-permute-start | bytes 4718600 | tf_op jit(solution)/shard_map/ppermute | solution.py:427
  12.7 10.9 %blocks.8.refs_4_ = f32[16,48,1024]{2,1,0:T(8,128)S(1)} custom-call(bf16[48,16384]{1,0:T(8,128)(2,1)} %refs_0_.3, bf16[48,16384]{1,0:T(8,128)(2,1)S(1)} %collective-permute-done.2.refs_1_, bf16[16384,1024]{1,0:T(8,128)(2,1)} %refs_4_.7, f32[16,48,1024]{2,1,0:T(8,128)S(1)} %blocks.7.refs_3_), custom_call_target="tpu_custom_call", output_to_operand_aliasing={{}: (3, {})} | custom-call | flops 2818572288 | bytes 29360128 | tf_op jit(solution)/shard_map/blocks/pallas_call | solution.py:263
  23.7 13.3 %turn.1.s_ref.refs_3_.refs_5_.refs_1_ = bf16[16384,128]{1,0:T(8,128)(2,1)S(1)} custom-call(bf16[64,16384]{1,0:T(8,128)(2,1)S(1)} %bitcast.15, bf16[64,16384]{1,0:T(8,128)(2,1)S(1)} %collective-permute-done.1.b_ref), custom_call_target="tpu_custom_call" | custom-call | tf_op jit(solution)/shard_map/turn/pallas_call | solution.py:306
  36.9 3.4 %some_ranks.4.refs_2_ = f32[48,128]{1,0:T(8,128)S(1)} custom-call(bf16[48,16384]{1,0:T(8,128)(2,1)} %refs_0_.3, bf16[16384,128]{1,0:T(8,128)(2,1)S(1)} %turn.1.s_ref.refs_3_.refs_5_.refs_1_), custom_call_target="tpu_custom_call" | custom-call | tf_op jit(solution)/shard_map/some_ranks/pallas_call | solution.py:322
  42.5 1.6 %collective-permute-done.3.refs_1_ = bf16[48,16384]{1,0:T(8,128)(2,1)} collective-permute-done((bf16[48,16384]{1,0:T(8,128)(2,1)}, bf16[48,16384]{1,0:T(8,128)(2,1)}, u32[]{:S(2)}, u32[]{:S(2)}) %collective-permute-start.3) | collective-permute-done | bytes 1572896 | tf_op jit(solution)/shard_map/ppermute | solution.py:427
  44.2 2.2 %copy-done.3 = bf16[16384,128]{1,0:T(8,128)(2,1)S(1)} copy-done((bf16[16384,128]{1,0:T(8,128)(2,1)S(1)}, bf16[16384,128]{1,0:T(8,128)(2,1)}, u32[]{:S(2)}) %copy-start.3) | copy-done | bytes 4194328
  46.3 12.6 %blocks.9 = (f32[16,48,1024]{2,1,0:T(8,128)S(1)}, f32[48,128]{1,0:T(8,128)S(1)}) custom-call(bf16[48,16384]{1,0:T(8,128)(2,1)} %collective-permute-done.refs_0_, bf16[48,16384]{1,0:T(8,128)(2,1)} %collective-permute-done.3.refs_1_, bf16[16384,1024]{1,0:T(8,128)(2,1)} %refs_4_.7, bf16[16384,128]{1,0:T(8,128)(2,1)S(1)} %copy-done.3, ...), custom_call_target="tpu_custom_call", output_to_operand_aliasing={{0}: (4, {})} | custom-call | flops 3221225472 | bytes 33554432 | tf_op jit(solution)/shard_map/blocks/pallas_call | solution.py:263
  63.2 14.1 %collective-permute-done.4.refs_2_ = bf16[48,16384]{1,0:T(8,128)(2,1)} collective-permute-done((bf16[48,16384]{1,0:T(8,128)(2,1)}, bf16[48,16384]{1,0:T(8,128)(2,1)}, u32[]{:S(2)}, u32[]{:S(2)}) %collective-permute-start.4) | collective-permute-done | bytes 1572896 | tf_op jit(solution)/shard_map/ppermute | solution.py:427
  77.3 2.0 %collective-permute-start.5 = (bf16[48,16384]{1,0:T(8,128)(2,1)}, bf16[48,16384]{1,0:T(8,128)(2,1)S(1)}, u32[]{:S(2)}, u32[]{:S(2)}) collective-permute-start(bf16[48,16384]{1,0:T(8,128)(2,1)} %collective-permute-done.4.refs_2_), channel_id=1, source_target_pairs={{0,4},{1,3},{4,8},{5,1},{8,12},{9,5},{12,14},{13,9},{14,10},{15,13... | collective-permute-start | bytes 4718600 | tf_op jit(solution)/shard_map/ppermute | solution.py:427
  80.9 2.2 %copy-done.4 = bf16[16384,128]{1,0:T(8,128)(2,1)S(1)} copy-done((bf16[16384,128]{1,0:T(8,128)(2,1)S(1)}, bf16[16384,128]{1,0:T(8,128)(2,1)}, u32[]{:S(2)}) %copy-start.4) | copy-done | bytes 4194328
  83.1 13.4 %blocks.10 = (f32[16,48,1024]{2,1,0:T(8,128)S(1)}, f32[96,128]{1,0:T(8,128)S(1)}) custom-call(bf16[48,16384]{1,0:T(8,128)(2,1)} %collective-permute-done.6.refs_0_, bf16[48,16384]{1,0:T(8,128)(2,1)} %collective-permute-done.7.refs_1_, bf16[48,16384]{1,0:T(8,128)(2,1)} %collective-permute-done.4.refs_2_, ...), custom_call_target="tpu_custom_call", output_to_operand_aliasing={{0}: (6, {})} | custom-call | flops 6442450944 | bytes 33554432 | tf_op jit(solution)/shard_map/blocks/pallas_call | solution.py:263
  96.6 17.4 %collective-permute-done.5.x_ref.refs_2_ = bf16[48,16384]{1,0:T(8,128)(2,1)S(1)} collective-permute-done((bf16[48,16384]{1,0:T(8,128)(2,1)}, bf16[48,16384]{1,0:T(8,128)(2,1)S(1)}, u32[]{:S(2)}, u32[]{:S(2)}) %collective-permute-start.5) | collective-permute-done | bytes 1572896 | tf_op jit(solution)/shard_map/ppermute | solution.py:427
  114.0 2.4 %collective-permute-start.9 = (bf16[48,16384]{1,0:T(8,128)(2,1)S(1)}, bf16[48,16384]{1,0:T(8,128)(2,1)S(1)}, u32[]{:S(2)}, u32[]{:S(2)}) collective-permute-start(bf16[48,16384]{1,0:T(8,128)(2,1)S(1)} %collective-permute-done.5.x_ref.refs_2_), channel_id=1, source_target_pairs={{0,4},{1,3},{4,8},{5,1},{8,12},{9,5},{12,14},{13,9},{14,10},{15,13... | collective-permute-start | bytes 4718600 | tf_op jit(solution)/shard_map/ppermute | solution.py:427
  116.4 2.1 %some_ranks.5.refs_5_ = f32[48,128]{1,0:T(8,128)S(1)} custom-call(bf16[48,16384]{1,0:T(8,128)(2,1)} %collective-permute-done.10.x_ref.refs_0_, bf16[16384,128]{1,0:T(8,128)(2,1)S(1)} %copy-done.5), custom_call_target="tpu_custom_call" | custom-call | tf_op jit(solution)/shard_map/some_ranks/pallas_call | solution.py:322
  119.4 12.5 %blocks.11.refs_5_ = f32[16,48,1024]{2,1,0:T(8,128)S(1)} custom-call(bf16[48,16384]{1,0:T(8,128)(2,1)} %collective-permute-done.10.x_ref.refs_0_, bf16[48,16384]{1,0:T(8,128)(2,1)S(1)} %collective-permute-done.12.refs_1_, bf16[48,16384]{1,0:T(8,128)(2,1)S(1)} %collective-permute-done.5.x_ref.refs_2_, ...), custom_call_target="tpu_custom_call", output_to_operand_aliasing={{}: (5, {})} | custom-call | flops 6442450944 | bytes 33554432 | tf_op jit(solution)/shard_map/blocks/pallas_call | solution.py:263
  132.6 1.8 %collective-permute-done.9.refs_0_.refs_2_ = bf16[48,16384]{1,0:T(8,128)(2,1)S(1)} collective-permute-done((bf16[48,16384]{1,0:T(8,128)(2,1)S(1)}, bf16[48,16384]{1,0:T(8,128)(2,1)S(1)}, u32[]{:S(2)}, u32[]{:S(2)}) %collective-permute-start.9) | collective-permute-done | bytes 1572896 | tf_op jit(solution)/shard_map/ppermute | solution.py:427
  137.0 3.0 %collective-permute-start.15 = (bf16[192,128]{1,0:T(8,128)(2,1)S(1)}, bf16[192,128]{1,0:T(8,128)(2,1)S(1)}, u32[]{:S(2)}, u32[]{:S(2)}) collective-permute-start(bf16[192,128]{1,0:T(8,128)(2,1)S(1)} %ranks.1), channel_id=1, source_target_pairs={{0,4},{1,5},{2,6},{3,7},{4,0},{5,1},{6,2},{7,3},{8,12},{9,13},{10,... | collective-permute-start | bytes 147464 | tf_op jit(solution)/shard_map/ppermute | solution.py:427
  140.0 7.1 %blocks.12.refs_5_ = f32[16,48,1024]{2,1,0:T(8,128)S(1)} custom-call(bf16[48,16384]{1,0:T(8,128)(2,1)S(1)} %collective-permute-done.11.x_ref.refs_0_, bf16[48,16384]{1,0:T(8,128)(2,1)S(1)} %collective-permute-done.17.refs_1_, bf16[48,16384]{1,0:T(8,128)(2,1)S(1)} %collective-permute-done.9.refs_0_.refs_2_, ...), custom_call_target="tpu_custom_call", output_to_operand_aliasing={{}: (5, {})} | custom-call | flops 3221225472 | bytes 16777216 | tf_op jit(solution)/shard_map/blocks/pallas_call | solution.py:263
  147.1 3.0 %collective-permute-start.19 = (bf16[192,128]{1,0:T(8,128)(2,1)S(1)}, bf16[192,128]{1,0:T(8,128)(2,1)S(1)}, u32[]{:S(2)}, u32[]{:S(2)}) collective-permute-start(bf16[192,128]{1,0:T(8,128)(2,1)S(1)} %add_add_fusion), channel_id=1, source_target_pairs={{0,8},{1,9},{2,10},{3,11},{4,12},{5,13},{6,14},{7,15},{8,0},{9,1},... | collective-permute-start | bytes 147464 | tf_op jit(solution)/shard_map/ppermute | solution.py:427
  150.4 7.3 %blocks.13.total_ref = f32[16,48,1024]{2,1,0:T(8,128)S(1)} custom-call(bf16[48,16384]{1,0:T(8,128)(2,1)S(1)} %collective-permute-done.11.x_ref.refs_0_, bf16[48,16384]{1,0:T(8,128)(2,1)S(1)} %collective-permute-done.17.refs_1_, bf16[48,16384]{1,0:T(8,128)(2,1)S(1)} %collective-permute-done.9.refs_0_.refs_2_, ...), custom_call_target="tpu_custom_call", output_to_operand_aliasing={{}: (5, {})} | custom-call | flops 3221225472 | bytes 16777216 | tf_op jit(solution)/shard_map/blocks/pallas_call | solution.py:263
  157.8 2.6 %finish.1 = bf16[768,1024]{1,0:T(8,128)(2,1)} custom-call(s32[16]{0:T(128)S(1)} %get-tuple-element.69.places_ref, s32[6]{0:T(128)S(1)} %gather_fusion, s32[1]{0:T(128)} %bitcast.7.core_ref, f32[16,48,1024]{2,1,0:T(8,128)S(1)} %blocks.13.total_ref, bf16[16,64,1024]{2,1,0:T(8,128)(2,1)S(1)} %bitcast.16, f32[1,1024]{1,0:T(1,128)S(1)} %bitcast.17, ...), custom_call_target="tpu_custom_call" | custom-call | tf_op jit(solution)/shard_map/finish/pallas_call | solution.py:406
  (69 shorter events, 13.0 us)
Async XLA Ops:
  0.0 59.9 %copy-start = (s32[16]{0:T(128)S(1)}, s32[16]{0:T(128)}, u32[]{:S(2)}) copy-start(s32[16]{0:T(128)} %param.16) | copy-start | bytes 196
  0.0 23.6 %collective-permute-start.1 = (bf16[64,16384]{1,0:T(8,128)(2,1)}, bf16[64,16384]{1,0:T(8,128)(2,1)S(1)}, u32[]{:S(2)}, u32[]{:S(2)}) collective-permute-start(bf16[64,16384]{1,0:T(8,128)(2,1)} %bitcast.14), channel_id=1, source_target_pairs={{0,1},{1,0},{2,3},{3,2},{4,5},{5,4},{6,7},{7,6},{8,9},{9,8},{10,11... | collective-permute-start | bytes 6291464 | tf_op jit(solution)/shard_map/ppermute | solution.py:427
  0.5 6.2 %collective-permute-start.2 = (bf16[48,16384]{1,0:T(8,128)(2,1)}, bf16[48,16384]{1,0:T(8,128)(2,1)S(1)}, u32[]{:S(2)}, u32[]{:S(2)}) collective-permute-start(bf16[48,16384]{1,0:T(8,128)(2,1)} %refs_0_.3), channel_id=1, source_target_pairs={{0,1},{1,0},{2,3},{3,2},{4,5},{5,4},{6,7},{7,6},{8,9},{9,8},{10,11... | collective-permute-start | bytes 4718600 | tf_op jit(solution)/shard_map/ppermute | solution.py:427
  0.5 39.8 %collective-permute-start = (bf16[48,16384]{1,0:T(8,128)(2,1)}, bf16[48,16384]{1,0:T(8,128)(2,1)}, u32[]{:S(2)}, u32[]{:S(2)}) collective-permute-start(bf16[48,16384]{1,0:T(8,128)(2,1)} %refs_0_.3), channel_id=1, source_target_pairs={{0,4},{1,3},{4,8},{5,1},{8,12},{9,5},{12,14},{13,9},{14,10},{15,13... | collective-permute-start | bytes 4718600 | tf_op jit(solution)/shard_map/ppermute | solution.py:427
  9.8 32.2 %collective-permute-start.6 = (bf16[48,16384]{1,0:T(8,128)(2,1)}, bf16[48,16384]{1,0:T(8,128)(2,1)}, u32[]{:S(2)}, u32[]{:S(2)}) collective-permute-start(bf16[48,16384]{1,0:T(8,128)(2,1)} %refs_0_.3), channel_id=1, source_target_pairs={{0,2},{1,5},{4,0},{5,9},{8,4},{9,13},{12,8},{13,15},{14,12},{15,11... | collective-permute-start | bytes 4718600 | tf_op jit(solution)/shard_map/ppermute | solution.py:427
  40.3 3.8 %collective-permute-start.3 = (bf16[48,16384]{1,0:T(8,128)(2,1)}, bf16[48,16384]{1,0:T(8,128)(2,1)}, u32[]{:S(2)}, u32[]{:S(2)}) collective-permute-start(bf16[48,16384]{1,0:T(8,128)(2,1)} %collective-permute-done.refs_0_), channel_id=1, source_target_pairs={{0,1},{1,0},{2,3},{3,2},{4,5},{5,4},{6,7},{7,6},{8,9},{9,8},{10,11... | collective-permute-start | bytes 4718600 | tf_op jit(solution)/shard_map/ppermute | solution.py:427
  40.4 36.9 %collective-permute-start.4 = (bf16[48,16384]{1,0:T(8,128)(2,1)}, bf16[48,16384]{1,0:T(8,128)(2,1)}, u32[]{:S(2)}, u32[]{:S(2)}) collective-permute-start(bf16[48,16384]{1,0:T(8,128)(2,1)} %collective-permute-done.refs_0_), channel_id=1, source_target_pairs={{0,4},{1,3},{4,8},{5,1},{8,12},{9,5},{12,14},{13,9},{14,10},{15,13... | collective-permute-start | bytes 4718600 | tf_op jit(solution)/shard_map/ppermute | solution.py:427
  42.0 37.4 %collective-permute-start.10 = (bf16[48,16384]{1,0:T(8,128)(2,1)}, bf16[48,16384]{1,0:T(8,128)(2,1)}, u32[]{:S(2)}, u32[]{:S(2)}) collective-permute-start(bf16[48,16384]{1,0:T(8,128)(2,1)} %collective-permute-done.6.refs_0_), channel_id=1, source_target_pairs={{0,2},{1,5},{4,0},{5,9},{8,4},{9,13},{12,8},{13,15},{14,12},{15,11... | collective-permute-start | bytes 4718600 | tf_op jit(solution)/shard_map/ppermute | solution.py:427
  42.5 37.1 %collective-permute-start.7 = (bf16[48,16384]{1,0:T(8,128)(2,1)}, bf16[48,16384]{1,0:T(8,128)(2,1)}, u32[]{:S(2)}, u32[]{:S(2)}) collective-permute-start(bf16[48,16384]{1,0:T(8,128)(2,1)} %collective-permute-done.6.refs_0_), channel_id=1, source_target_pairs={{0,1},{1,0},{2,3},{3,2},{4,5},{5,4},{6,7},{7,6},{8,9},{9,8},{10,11... | collective-permute-start | bytes 4718600 | tf_op jit(solution)/shard_map/ppermute | solution.py:427
  77.3 3.6 %collective-permute-start.8 = (bf16[48,16384]{1,0:T(8,128)(2,1)}, bf16[48,16384]{1,0:T(8,128)(2,1)S(1)}, u32[]{:S(2)}, u32[]{:S(2)}) collective-permute-start(bf16[48,16384]{1,0:T(8,128)(2,1)} %collective-permute-done.4.refs_2_), channel_id=1, source_target_pairs={{0,1},{1,0},{2,3},{3,2},{4,5},{5,4},{6,7},{7,6},{8,9},{9,8},{10,11... | collective-permute-start | bytes 4718600 | tf_op jit(solution)/shard_map/ppermute | solution.py:427
  77.3 36.7 %collective-permute-start.5 = (bf16[48,16384]{1,0:T(8,128)(2,1)}, bf16[48,16384]{1,0:T(8,128)(2,1)S(1)}, u32[]{:S(2)}, u32[]{:S(2)}) collective-permute-start(bf16[48,16384]{1,0:T(8,128)(2,1)} %collective-permute-done.4.refs_2_), channel_id=1, source_target_pairs={{0,4},{1,3},{4,8},{5,1},{8,12},{9,5},{12,14},{13,9},{14,10},{15,13... | collective-permute-start | bytes 4718600 | tf_op jit(solution)/shard_map/ppermute | solution.py:427
  79.3 39.9 %collective-permute-start.11 = (bf16[48,16384]{1,0:T(8,128)(2,1)}, bf16[48,16384]{1,0:T(8,128)(2,1)S(1)}, u32[]{:S(2)}, u32[]{:S(2)}) collective-permute-start(bf16[48,16384]{1,0:T(8,128)(2,1)} %collective-permute-done.10.x_ref.refs_0_), channel_id=1, source_target_pairs={{0,2},{1,5},{4,0},{5,9},{8,4},{9,13},{12,8},{13,15},{14,12},{15,11... | collective-permute-start | bytes 4718600 | tf_op jit(solution)/shard_map/ppermute | solution.py:427
  79.3 40.0 %collective-permute-start.12 = (bf16[48,16384]{1,0:T(8,128)(2,1)}, bf16[48,16384]{1,0:T(8,128)(2,1)S(1)}, u32[]{:S(2)}, u32[]{:S(2)}) collective-permute-start(bf16[48,16384]{1,0:T(8,128)(2,1)} %collective-permute-done.10.x_ref.refs_0_), channel_id=1, source_target_pairs={{0,1},{1,0},{2,3},{3,2},{4,5},{5,4},{6,7},{7,6},{8,9},{9,8},{10,11... | collective-permute-start | bytes 4718600 | tf_op jit(solution)/shard_map/ppermute | solution.py:427
  83.1 33.3 %copy-start.5 = (bf16[16384,128]{1,0:T(8,128)(2,1)S(1)}, bf16[16384,128]{1,0:T(8,128)(2,1)}, u32[]{:S(2)}) copy-start(bf16[16384,128]{1,0:T(8,128)(2,1)} %copy-done.2) | copy-start | bytes 12582916
  114.0 5.4 %collective-permute-start.13 = (bf16[48,16384]{1,0:T(8,128)(2,1)S(1)}, bf16[48,16384]{1,0:T(8,128)(2,1)S(1)}, u32[]{:S(2)}, u32[]{:S(2)}) collective-permute-start(bf16[48,16384]{1,0:T(8,128)(2,1)S(1)} %collective-permute-done.5.x_ref.refs_2_), channel_id=1, source_target_pairs={{0,1},{1,0},{2,3},{3,2},{4,5},{5,4},{6,7},{7,6},{8,9},{9,8},{10,11... | collective-permute-start | bytes 4718600 | tf_op jit(solution)/shard_map/ppermute | solution.py:427
  114.0 20.4 %collective-permute-start.9 = (bf16[48,16384]{1,0:T(8,128)(2,1)S(1)}, bf16[48,16384]{1,0:T(8,128)(2,1)S(1)}, u32[]{:S(2)}, u32[]{:S(2)}) collective-permute-start(bf16[48,16384]{1,0:T(8,128)(2,1)S(1)} %collective-permute-done.5.x_ref.refs_2_), channel_id=1, source_target_pairs={{0,4},{1,3},{4,8},{5,1},{8,12},{9,5},{12,14},{13,9},{14,10},{15,13... | collective-permute-start | bytes 4718600 | tf_op jit(solution)/shard_map/ppermute | solution.py:427
  119.3 20.7 %collective-permute-start.17 = (bf16[48,16384]{1,0:T(8,128)(2,1)S(1)}, bf16[48,16384]{1,0:T(8,128)(2,1)S(1)}, u32[]{:S(2)}, u32[]{:S(2)}) collective-permute-start(bf16[48,16384]{1,0:T(8,128)(2,1)S(1)} %collective-permute-done.11.x_ref.refs_0_), channel_id=1, source_target_pairs={{0,1},{1,0},{2,3},{3,2},{4,5},{5,4},{6,7},{7,6},{8,9},{9,8},{10,11... | collective-permute-start | bytes 4718600 | tf_op jit(solution)/shard_map/ppermute | solution.py:427
  134.4 5.6 %collective-permute-start.18 = (bf16[48,16384]{1,0:T(8,128)(2,1)S(1)}, bf16[48,16384]{1,0:T(8,128)(2,1)S(1)}, u32[]{:S(2)}, u32[]{:S(2)}) collective-permute-start(bf16[48,16384]{1,0:T(8,128)(2,1)S(1)} %collective-permute-done.9.refs_0_.refs_2_), channel_id=1, source_target_pairs={{0,1},{1,0},{2,3},{3,2},{4,5},{5,4},{6,7},{7,6},{8,9},{9,8},{10,11... | collective-permute-start | bytes 4718600 | tf_op jit(solution)/shard_map/ppermute | solution.py:427
  136.0 11.1 %collective-permute-start.14 = (bf16[192,128]{1,0:T(8,128)(2,1)S(1)}, bf16[192,128]{1,0:T(8,128)(2,1)S(1)}, u32[]{:S(2)}, u32[]{:S(2)}) collective-permute-start(bf16[192,128]{1,0:T(8,128)(2,1)S(1)} %ranks.1), channel_id=1, source_target_pairs={{0,2},{1,3},{2,0},{3,1},{4,6},{5,7},{6,4},{7,5},{8,10},{9,11},{10,... | collective-permute-start | bytes 147464 | tf_op jit(solution)/shard_map/ppermute | solution.py:427
  137.0 10.1 %collective-permute-start.15 = (bf16[192,128]{1,0:T(8,128)(2,1)S(1)}, bf16[192,128]{1,0:T(8,128)(2,1)S(1)}, u32[]{:S(2)}, u32[]{:S(2)}) collective-permute-start(bf16[192,128]{1,0:T(8,128)(2,1)S(1)} %ranks.1), channel_id=1, source_target_pairs={{0,4},{1,5},{2,6},{3,7},{4,0},{5,1},{6,2},{7,3},{8,12},{9,13},{10,... | collective-permute-start | bytes 147464 | tf_op jit(solution)/shard_map/ppermute | solution.py:427
  140.0 7.1 %collective-permute-start.16 = (bf16[192,128]{1,0:T(8,128)(2,1)S(1)}, bf16[192,128]{1,0:T(8,128)(2,1)S(1)}, u32[]{:S(2)}, u32[]{:S(2)}) collective-permute-start(bf16[192,128]{1,0:T(8,128)(2,1)S(1)} %ranks.1), channel_id=1, source_target_pairs={{0,6},{1,7},{2,4},{3,5},{4,2},{5,3},{6,0},{7,1},{8,14},{9,15},{10,... | collective-permute-start | bytes 147464 | tf_op jit(solution)/shard_map/ppermute | solution.py:427
  147.1 10.6 %collective-permute-start.19 = (bf16[192,128]{1,0:T(8,128)(2,1)S(1)}, bf16[192,128]{1,0:T(8,128)(2,1)S(1)}, u32[]{:S(2)}, u32[]{:S(2)}) collective-permute-start(bf16[192,128]{1,0:T(8,128)(2,1)S(1)} %add_add_fusion), channel_id=1, source_target_pairs={{0,8},{1,9},{2,10},{3,11},{4,12},{5,13},{6,14},{7,15},{8,0},{9,1},... | collective-permute-start | bytes 147464 | tf_op jit(solution)/shard_map/ppermute | solution.py:427
  150.2 7.5 %collective-permute-start.20 = (bf16[192,128]{1,0:T(8,128)(2,1)S(1)}, bf16[192,128]{1,0:T(8,128)(2,1)S(1)}, u32[]{:S(2)}, u32[]{:S(2)}) collective-permute-start(bf16[192,128]{1,0:T(8,128)(2,1)S(1)} %add_add_fusion), channel_id=1, source_target_pairs={{0,1},{1,0},{2,3},{3,2},{4,5},{5,4},{6,7},{7,6},{8,9},{9,8},{10,11... | collective-permute-start | bytes 147464 | tf_op jit(solution)/shard_map/ppermute | solution.py:427
  150.2 7.5 %collective-permute-start.21 = (bf16[192,128]{1,0:T(8,128)(2,1)S(1)}, bf16[192,128]{1,0:T(8,128)(2,1)S(1)}, u32[]{:S(2)}, u32[]{:S(2)}) collective-permute-start(bf16[192,128]{1,0:T(8,128)(2,1)S(1)} %add_add_fusion), channel_id=1, source_target_pairs={{0,9},{1,8},{2,11},{3,10},{4,13},{5,12},{6,15},{7,14},{8,1},{9,0},... | collective-permute-start | bytes 147464 | tf_op jit(solution)/shard_map/ppermute | solution.py:427
  (8 other events, 60.8 us)

commit v17 on v16

--- a/solution.py
+++ b/solution.py
@@ -292,12 +292,14 @@
 
 def turn_kernel(a_ref, b_ref, out_ref):
     width = 2 * a_ref.shape[0]
-
-    @pl.loop(0, a_ref.shape[1] // width)
+    together = 16
+
+    @pl.loop(0, a_ref.shape[1] // (width * together))
     def _(step):
-        cut = pl.ds(pl.multiple_of(step * width, width), width)
-        both = jnp.concatenate([a_ref[:, cut], b_ref[:, cut]], 0)
-        out_ref[cut, :] = both.astype(F32).T.astype(out_ref.dtype)
+        for i in range(together):
+            cut = pl.ds(pl.multiple_of((step * together + i) * width, width), width)
+            both = jnp.concatenate([a_ref[:, cut], b_ref[:, cut]], 0)
+            out_ref[cut, :] = both.T
 
 
 def turn(factors):
@@ -504,6 +506,7 @@
     shrinks = jnp.swapaxes(shrink_store, 1, 2)
     expands = jnp.swapaxes(expand_store, 1, 2)
     ring = parts == 2 * len(SNAKE) and rows % 16 == 0 and shrinks.shape[0] == 1 and total_rows % (2 * SEG) == 0
+    ring = ring and shrinks.shape[1] == 64 and tokens.shape[1] % 2048 == 0
     plan = ring_plan if ring else gather_plan
     indices = (row_adapter, placement, document_lengths)
     return plan(parts, tokens, weight_codes, column_scale[None, :], shrinks, expands, indices)

time: 161 us -> 149 us (0.925)
  Pallas kernels: 91.1 us -> 79.4 us
  starting transfers between devices: 20.7 us -> 27.4 us
  waiting for transfers between devices: 39.5 us -> 32.9 us
    pallas_call x1, Pallas kernels: 13.3 us -> 1.56 us  [turn(): pl.pallas_call(turn_kernel, in_specs=[whole] * 2, out_specs=whole, out_sh...]
    ppermute x22, starting transfers between devices: 20.7 us -> 27.4 us  [ring_plan(): send = lambda value, pairs: lax.ppermute(value, 'tensor', pairs)]
    ppermute x22, waiting for transfers between devices: 39.5 us -> 32.9 us  [ring_plan(): send = lambda value, pairs: lax.ppermute(value, 'tensor', pairs)]
  transfers between devices with their start and end apart: 22 -> 22, of which waited for: 6 -> 8; matrix products, arithmetic and copies ran while one was open for 3% -> 3% of each run, Pallas kernels for 55% -> 52%
where the time goes in v17:
time: 149 us
  Pallas kernels  79.4 us (53%)
  waiting for transfers between devices  32.9 us (22%)
  starting transfers between devices  27.4 us (18%)
  local copies, waits for them, and re-layouts  6.54 us (4%)
  other arithmetic  2.14 us (1%)
    pallas_call x7, Pallas kernels, block_product(): pl.pallas_call(functools.partial(block_kernel, count, low, tile, steps, f...  66.9 us
    ppermute x22, waiting for transfers between devices, ring_plan(): send = lambda value, pairs: lax.ppermute(value, 'tensor', pairs)  32.9 us
    ppermute x22, starting transfers between devices, ring_plan(): send = lambda value, pairs: lax.ppermute(value, 'tensor', pairs)  27.4 us
    pallas_call x4, Pallas kernels, some_ranks(): pl.pallas_call(some_ranks_kernel, in_specs=[whole] * 2, out_specs=whole,...  6.98 us
    unnamed x20, local copies, waits for them, and re-layouts  4.41 us
  transfers between devices with their start and end apart: 22, of which 8 were waited for; matrix products, arithmetic and copies ran while one was open for 3% of the time, Pallas kernels for 52%

profile of v17, /device:TPU:0, one launch (start us, length us, event | category | flops | bytes accessed | tf_op | source)
XLA Modules:
  0.0 148.9 jit_solution(11975201235143020376)
XLA Ops:
  0.5 3.0 %collective-permute-start = (bf16[48,16384]{1,0:T(8,128)(2,1)}, bf16[48,16384]{1,0:T(8,128)(2,1)}, u32[]{:S(2)}, u32[]{:S(2)}) collective-permute-start(bf16[48,16384]{1,0:T(8,128)(2,1)} %refs_0_.3), channel_id=1, source_target_pairs={{0,4},{1,3},{4,8},{5,1},{8,12},{9,5},{12,14},{13,9},{14,10},{15,13... | collective-permute-start | bytes 4718600 | tf_op jit(solution)/shard_map/ppermute | solution.py:429
  3.5 3.2 %collective-permute-done.2.refs_1_ = bf16[48,16384]{1,0:T(8,128)(2,1)S(1)} collective-permute-done((bf16[48,16384]{1,0:T(8,128)(2,1)}, bf16[48,16384]{1,0:T(8,128)(2,1)S(1)}, u32[]{:S(2)}, u32[]{:S(2)}) %collective-permute-start.2) | collective-permute-done | bytes 1572896 | tf_op jit(solution)/shard_map/ppermute | solution.py:429
  6.7 3.1 %blocks.7.refs_3_ = f32[16,48,1024]{2,1,0:T(8,128)S(1)} custom-call(bf16[48,16384]{1,0:T(8,128)(2,1)} %refs_0_.3, bf16[48,16384]{1,0:T(8,128)(2,1)S(1)} %collective-permute-done.2.refs_1_, bf16[16384,1024]{1,0:T(8,128)(2,1)} %refs_4_.7), custom_call_target="tpu_custom_call" | custom-call | flops 402653184 | bytes 4194304 | tf_op jit(solution)/shard_map/blocks/pallas_call | solution.py:263
  9.8 2.9 %collective-permute-start.6 = (bf16[48,16384]{1,0:T(8,128)(2,1)}, bf16[48,16384]{1,0:T(8,128)(2,1)}, u32[]{:S(2)}, u32[]{:S(2)}) collective-permute-start(bf16[48,16384]{1,0:T(8,128)(2,1)} %refs_0_.3), channel_id=1, source_target_pairs={{0,2},{1,5},{4,0},{5,9},{8,4},{9,13},{12,8},{13,15},{14,12},{15,11... | collective-permute-start | bytes 4718600 | tf_op jit(solution)/shard_map/ppermute | solution.py:429
  12.7 10.9 %blocks.8.refs_4_ = f32[16,48,1024]{2,1,0:T(8,128)S(1)} custom-call(bf16[48,16384]{1,0:T(8,128)(2,1)} %refs_0_.3, bf16[48,16384]{1,0:T(8,128)(2,1)S(1)} %collective-permute-done.2.refs_1_, bf16[16384,1024]{1,0:T(8,128)(2,1)} %refs_4_.7, f32[16,48,1024]{2,1,0:T(8,128)S(1)} %blocks.7.refs_3_), custom_call_target="tpu_custom_call", output_to_operand_aliasing={{}: (3, {})} | custom-call | flops 2818572288 | bytes 29360128 | tf_op jit(solution)/shard_map/blocks/pallas_call | solution.py:263
  25.2 3.4 %some_ranks.4.refs_2_ = f32[48,128]{1,0:T(8,128)S(1)} custom-call(bf16[48,16384]{1,0:T(8,128)(2,1)} %refs_0_.3, bf16[16384,128]{1,0:T(8,128)(2,1)S(1)} %turn.1.s_ref.refs_3_.refs_5_.refs_1_), custom_call_target="tpu_custom_call" | custom-call | tf_op jit(solution)/shard_map/some_ranks/pallas_call | solution.py:324
  30.3 2.4 %collective-permute-start.4 = (bf16[48,16384]{1,0:T(8,128)(2,1)}, bf16[48,16384]{1,0:T(8,128)(2,1)}, u32[]{:S(2)}, u32[]{:S(2)}) collective-permute-start(bf16[48,16384]{1,0:T(8,128)(2,1)} %collective-permute-done.refs_0_), channel_id=1, source_target_pairs={{0,4},{1,3},{4,8},{5,1},{8,12},{9,5},{12,14},{13,9},{14,10},{15,13... | collective-permute-start | bytes 4718600 | tf_op jit(solution)/shard_map/ppermute | solution.py:429
  32.7 9.8 %collective-permute-done.6.refs_0_ = bf16[48,16384]{1,0:T(8,128)(2,1)} collective-permute-done((bf16[48,16384]{1,0:T(8,128)(2,1)}, bf16[48,16384]{1,0:T(8,128)(2,1)}, u32[]{:S(2)}, u32[]{:S(2)}) %collective-permute-start.6) | collective-permute-done | bytes 1572896 | tf_op jit(solution)/shard_map/ppermute | solution.py:429
  45.4 2.2 %copy-done.3 = bf16[16384,128]{1,0:T(8,128)(2,1)S(1)} copy-done((bf16[16384,128]{1,0:T(8,128)(2,1)S(1)}, bf16[16384,128]{1,0:T(8,128)(2,1)}, u32[]{:S(2)}) %copy-start.3) | copy-done | bytes 4194328
  47.6 12.6 %blocks.9 = (f32[16,48,1024]{2,1,0:T(8,128)S(1)}, f32[48,128]{1,0:T(8,128)S(1)}) custom-call(bf16[48,16384]{1,0:T(8,128)(2,1)} %collective-permute-done.refs_0_, bf16[48,16384]{1,0:T(8,128)(2,1)} %collective-permute-done.3.refs_1_, bf16[16384,1024]{1,0:T(8,128)(2,1)} %refs_4_.7, bf16[16384,128]{1,0:T(8,128)(2,1)S(1)} %copy-done.3, ...), custom_call_target="tpu_custom_call", output_to_operand_aliasing={{0}: (4, {})} | custom-call | flops 3221225472 | bytes 33554432 | tf_op jit(solution)/shard_map/blocks/pallas_call | solution.py:263
  64.9 2.4 %collective-permute-start.5 = (bf16[48,16384]{1,0:T(8,128)(2,1)}, bf16[48,16384]{1,0:T(8,128)(2,1)S(1)}, u32[]{:S(2)}, u32[]{:S(2)}) collective-permute-start(bf16[48,16384]{1,0:T(8,128)(2,1)} %collective-permute-done.4.refs_2_), channel_id=1, source_target_pairs={{0,4},{1,3},{4,8},{5,1},{8,12},{9,5},{12,14},{13,9},{14,10},{15,13... | collective-permute-start | bytes 4718600 | tf_op jit(solution)/shard_map/ppermute | solution.py:429
  67.3 8.1 %collective-permute-done.10.x_ref.refs_0_ = bf16[48,16384]{1,0:T(8,128)(2,1)} collective-permute-done((bf16[48,16384]{1,0:T(8,128)(2,1)}, bf16[48,16384]{1,0:T(8,128)(2,1)}, u32[]{:S(2)}, u32[]{:S(2)}) %collective-permute-start.10) | collective-permute-done | bytes 1572896 | tf_op jit(solution)/shard_map/ppermute | solution.py:429
  78.2 2.2 %copy-done.4 = bf16[16384,128]{1,0:T(8,128)(2,1)S(1)} copy-done((bf16[16384,128]{1,0:T(8,128)(2,1)S(1)}, bf16[16384,128]{1,0:T(8,128)(2,1)}, u32[]{:S(2)}) %copy-start.4) | copy-done | bytes 4194328
  80.4 13.4 %blocks.10 = (f32[16,48,1024]{2,1,0:T(8,128)S(1)}, f32[96,128]{1,0:T(8,128)S(1)}) custom-call(bf16[48,16384]{1,0:T(8,128)(2,1)} %collective-permute-done.6.refs_0_, bf16[48,16384]{1,0:T(8,128)(2,1)} %collective-permute-done.7.refs_1_, bf16[48,16384]{1,0:T(8,128)(2,1)} %collective-permute-done.4.refs_2_, ...), custom_call_target="tpu_custom_call", output_to_operand_aliasing={{0}: (6, {})} | custom-call | flops 6442450944 | bytes 33554432 | tf_op jit(solution)/shard_map/blocks/pallas_call | solution.py:263
  93.8 5.6 %collective-permute-done.5.x_ref.refs_2_ = bf16[48,16384]{1,0:T(8,128)(2,1)S(1)} collective-permute-done((bf16[48,16384]{1,0:T(8,128)(2,1)}, bf16[48,16384]{1,0:T(8,128)(2,1)S(1)}, u32[]{:S(2)}, u32[]{:S(2)}) %collective-permute-start.5) | collective-permute-done | bytes 1572896 | tf_op jit(solution)/shard_map/ppermute | solution.py:429
  99.5 2.4 %collective-permute-start.9 = (bf16[48,16384]{1,0:T(8,128)(2,1)S(1)}, bf16[48,16384]{1,0:T(8,128)(2,1)S(1)}, u32[]{:S(2)}, u32[]{:S(2)}) collective-permute-start(bf16[48,16384]{1,0:T(8,128)(2,1)S(1)} %collective-permute-done.5.x_ref.refs_2_), channel_id=1, source_target_pairs={{0,4},{1,3},{4,8},{5,1},{8,12},{9,5},{12,14},{13,9},{14,10},{15,13... | collective-permute-start | bytes 4718600 | tf_op jit(solution)/shard_map/ppermute | solution.py:429
  101.8 2.1 %some_ranks.5.refs_5_ = f32[48,128]{1,0:T(8,128)S(1)} custom-call(bf16[48,16384]{1,0:T(8,128)(2,1)} %collective-permute-done.10.x_ref.refs_0_, bf16[16384,128]{1,0:T(8,128)(2,1)S(1)} %copy-done.5), custom_call_target="tpu_custom_call" | custom-call | tf_op jit(solution)/shard_map/some_ranks/pallas_call | solution.py:324
  104.7 3.6 %collective-permute-done.11.x_ref.refs_0_ = bf16[48,16384]{1,0:T(8,128)(2,1)S(1)} collective-permute-done((bf16[48,16384]{1,0:T(8,128)(2,1)}, bf16[48,16384]{1,0:T(8,128)(2,1)S(1)}, u32[]{:S(2)}, u32[]{:S(2)}) %collective-permute-start.11) | collective-permute-done | bytes 1572896 | tf_op jit(solution)/shard_map/ppermute | solution.py:429
  109.4 12.5 %blocks.11.refs_5_ = f32[16,48,1024]{2,1,0:T(8,128)S(1)} custom-call(bf16[48,16384]{1,0:T(8,128)(2,1)} %collective-permute-done.10.x_ref.refs_0_, bf16[48,16384]{1,0:T(8,128)(2,1)S(1)} %collective-permute-done.12.refs_1_, bf16[48,16384]{1,0:T(8,128)(2,1)S(1)} %collective-permute-done.5.x_ref.refs_2_, ...), custom_call_target="tpu_custom_call", output_to_operand_aliasing={{}: (5, {})} | custom-call | flops 6442450944 | bytes 33554432 | tf_op jit(solution)/shard_map/blocks/pallas_call | solution.py:263
  124.7 2.1 %collective-permute-start.14 = (bf16[192,128]{1,0:T(8,128)(2,1)S(1)}, bf16[192,128]{1,0:T(8,128)(2,1)S(1)}, u32[]{:S(2)}, u32[]{:S(2)}) collective-permute-start(bf16[192,128]{1,0:T(8,128)(2,1)S(1)} %ranks.1), channel_id=1, source_target_pairs={{0,2},{1,3},{2,0},{3,1},{4,6},{5,7},{6,4},{7,5},{8,10},{9,11},{10,... | collective-permute-start | bytes 147464 | tf_op jit(solution)/shard_map/ppermute | solution.py:429
  128.3 7.1 %blocks.12.refs_5_ = f32[16,48,1024]{2,1,0:T(8,128)S(1)} custom-call(bf16[48,16384]{1,0:T(8,128)(2,1)S(1)} %collective-permute-done.11.x_ref.refs_0_, bf16[48,16384]{1,0:T(8,128)(2,1)S(1)} %collective-permute-done.17.refs_1_, bf16[48,16384]{1,0:T(8,128)(2,1)S(1)} %collective-permute-done.9.refs_0_.refs_2_, ...), custom_call_target="tpu_custom_call", output_to_operand_aliasing={{}: (5, {})} | custom-call | flops 3221225472 | bytes 16777216 | tf_op jit(solution)/shard_map/blocks/pallas_call | solution.py:263
  135.5 3.1 %collective-permute-start.19 = (bf16[192,128]{1,0:T(8,128)(2,1)S(1)}, bf16[192,128]{1,0:T(8,128)(2,1)S(1)}, u32[]{:S(2)}, u32[]{:S(2)}) collective-permute-start(bf16[192,128]{1,0:T(8,128)(2,1)S(1)} %add_add_fusion), channel_id=1, source_target_pairs={{0,8},{1,9},{2,10},{3,11},{4,12},{5,13},{6,14},{7,15},{8,0},{9,1},... | collective-permute-start | bytes 147464 | tf_op jit(solution)/shard_map/ppermute | solution.py:429
  138.7 7.3 %blocks.13.total_ref = f32[16,48,1024]{2,1,0:T(8,128)S(1)} custom-call(bf16[48,16384]{1,0:T(8,128)(2,1)S(1)} %collective-permute-done.11.x_ref.refs_0_, bf16[48,16384]{1,0:T(8,128)(2,1)S(1)} %collective-permute-done.17.refs_1_, bf16[48,16384]{1,0:T(8,128)(2,1)S(1)} %collective-permute-done.9.refs_0_.refs_2_, ...), custom_call_target="tpu_custom_call", output_to_operand_aliasing={{}: (5, {})} | custom-call | flops 3221225472 | bytes 16777216 | tf_op jit(solution)/shard_map/blocks/pallas_call | solution.py:263
  146.2 2.6 %finish.1 = bf16[768,1024]{1,0:T(8,128)(2,1)} custom-call(s32[16]{0:T(128)S(1)} %get-tuple-element.69.places_ref, s32[6]{0:T(128)S(1)} %gather_fusion, s32[1]{0:T(128)} %bitcast.7.core_ref, f32[16,48,1024]{2,1,0:T(8,128)S(1)} %blocks.13.total_ref, bf16[16,64,1024]{2,1,0:T(8,128)(2,1)S(1)} %bitcast.16, f32[1,1024]{1,0:T(1,128)S(1)} %bitcast.17, ...), custom_call_target="tpu_custom_call" | custom-call | tf_op jit(solution)/shard_map/finish/pallas_call | solution.py:408
  (69 shorter events, 20.6 us)
Async XLA Ops:
  0.0 61.2 %copy-start = (s32[16]{0:T(128)S(1)}, s32[16]{0:T(128)}, u32[]{:S(2)}) copy-start(s32[16]{0:T(128)} %param.16) | copy-start | bytes 196
  0.0 23.6 %collective-permute-start.1 = (bf16[64,16384]{1,0:T(8,128)(2,1)}, bf16[64,16384]{1,0:T(8,128)(2,1)S(1)}, u32[]{:S(2)}, u32[]{:S(2)}) collective-permute-start(bf16[64,16384]{1,0:T(8,128)(2,1)} %bitcast.14), channel_id=1, source_target_pairs={{0,1},{1,0},{2,3},{3,2},{4,5},{5,4},{6,7},{7,6},{8,9},{9,8},{10,11... | collective-permute-start | bytes 6291464 | tf_op jit(solution)/shard_map/ppermute | solution.py:429
  0.5 6.2 %collective-permute-start.2 = (bf16[48,16384]{1,0:T(8,128)(2,1)}, bf16[48,16384]{1,0:T(8,128)(2,1)S(1)}, u32[]{:S(2)}, u32[]{:S(2)}) collective-permute-start(bf16[48,16384]{1,0:T(8,128)(2,1)} %refs_0_.3), channel_id=1, source_target_pairs={{0,1},{1,0},{2,3},{3,2},{4,5},{5,4},{6,7},{7,6},{8,9},{9,8},{10,11... | collective-permute-start | bytes 4718600 | tf_op jit(solution)/shard_map/ppermute | solution.py:429
  0.5 29.7 %collective-permute-start = (bf16[48,16384]{1,0:T(8,128)(2,1)}, bf16[48,16384]{1,0:T(8,128)(2,1)}, u32[]{:S(2)}, u32[]{:S(2)}) collective-permute-start(bf16[48,16384]{1,0:T(8,128)(2,1)} %refs_0_.3), channel_id=1, source_target_pairs={{0,4},{1,3},{4,8},{5,1},{8,12},{9,5},{12,14},{13,9},{14,10},{15,13... | collective-permute-start | bytes 4718600 | tf_op jit(solution)/shard_map/ppermute | solution.py:429
  9.8 32.7 %collective-permute-start.6 = (bf16[48,16384]{1,0:T(8,128)(2,1)}, bf16[48,16384]{1,0:T(8,128)(2,1)}, u32[]{:S(2)}, u32[]{:S(2)}) collective-permute-start(bf16[48,16384]{1,0:T(8,128)(2,1)} %refs_0_.3), channel_id=1, source_target_pairs={{0,2},{1,5},{4,0},{5,9},{8,4},{9,13},{12,8},{13,15},{14,12},{15,11... | collective-permute-start | bytes 4718600 | tf_op jit(solution)/shard_map/ppermute | solution.py:429
  30.3 15.2 %collective-permute-start.3 = (bf16[48,16384]{1,0:T(8,128)(2,1)}, bf16[48,16384]{1,0:T(8,128)(2,1)}, u32[]{:S(2)}, u32[]{:S(2)}) collective-permute-start(bf16[48,16384]{1,0:T(8,128)(2,1)} %collective-permute-done.refs_0_), channel_id=1, source_target_pairs={{0,1},{1,0},{2,3},{3,2},{4,5},{5,4},{6,7},{7,6},{8,9},{9,8},{10,11... | collective-permute-start | bytes 4718600 | tf_op jit(solution)/shard_map/ppermute | solution.py:429
  30.3 29.9 %copy-start.9 = (s32[8]{0:T(128)S(1)}, s32[8]{0:T(128)}, u32[]{:S(2)}) copy-start(s32[8]{0:T(128)} %param.17) | copy-start | bytes 100
  30.3 34.6 %collective-permute-start.4 = (bf16[48,16384]{1,0:T(8,128)(2,1)}, bf16[48,16384]{1,0:T(8,128)(2,1)}, u32[]{:S(2)}, u32[]{:S(2)}) collective-permute-start(bf16[48,16384]{1,0:T(8,128)(2,1)} %collective-permute-done.refs_0_), channel_id=1, source_target_pairs={{0,4},{1,3},{4,8},{5,1},{8,12},{9,5},{12,14},{13,9},{14,10},{15,13... | collective-permute-start | bytes 4718600 | tf_op jit(solution)/shard_map/ppermute | solution.py:429
  42.5 32.9 %collective-permute-start.10 = (bf16[48,16384]{1,0:T(8,128)(2,1)}, bf16[48,16384]{1,0:T(8,128)(2,1)}, u32[]{:S(2)}, u32[]{:S(2)}) collective-permute-start(bf16[48,16384]{1,0:T(8,128)(2,1)} %collective-permute-done.6.refs_0_), channel_id=1, source_target_pairs={{0,2},{1,5},{4,0},{5,9},{8,4},{9,13},{12,8},{13,15},{14,12},{15,11... | collective-permute-start | bytes 4718600 | tf_op jit(solution)/shard_map/ppermute | solution.py:429
  44.2 34.0 %collective-permute-start.7 = (bf16[48,16384]{1,0:T(8,128)(2,1)}, bf16[48,16384]{1,0:T(8,128)(2,1)}, u32[]{:S(2)}, u32[]{:S(2)}) collective-permute-start(bf16[48,16384]{1,0:T(8,128)(2,1)} %collective-permute-done.6.refs_0_), channel_id=1, source_target_pairs={{0,1},{1,0},{2,3},{3,2},{4,5},{5,4},{6,7},{7,6},{8,9},{9,8},{10,11... | collective-permute-start | bytes 4718600 | tf_op jit(solution)/shard_map/ppermute | solution.py:429
  64.9 13.3 %collective-permute-start.8 = (bf16[48,16384]{1,0:T(8,128)(2,1)}, bf16[48,16384]{1,0:T(8,128)(2,1)S(1)}, u32[]{:S(2)}, u32[]{:S(2)}) collective-permute-start(bf16[48,16384]{1,0:T(8,128)(2,1)} %collective-permute-done.4.refs_2_), channel_id=1, source_target_pairs={{0,1},{1,0},{2,3},{3,2},{4,5},{5,4},{6,7},{7,6},{8,9},{9,8},{10,11... | collective-permute-start | bytes 4718600 | tf_op jit(solution)/shard_map/ppermute | solution.py:429
  64.9 34.6 %collective-permute-start.5 = (bf16[48,16384]{1,0:T(8,128)(2,1)}, bf16[48,16384]{1,0:T(8,128)(2,1)S(1)}, u32[]{:S(2)}, u32[]{:S(2)}) collective-permute-start(bf16[48,16384]{1,0:T(8,128)(2,1)} %collective-permute-done.4.refs_2_), channel_id=1, source_target_pairs={{0,4},{1,3},{4,8},{5,1},{8,12},{9,5},{12,14},{13,9},{14,10},{15,13... | collective-permute-start | bytes 4718600 | tf_op jit(solution)/shard_map/ppermute | solution.py:429
  75.4 33.0 %collective-permute-start.11 = (bf16[48,16384]{1,0:T(8,128)(2,1)}, bf16[48,16384]{1,0:T(8,128)(2,1)S(1)}, u32[]{:S(2)}, u32[]{:S(2)}) collective-permute-start(bf16[48,16384]{1,0:T(8,128)(2,1)} %collective-permute-done.10.x_ref.refs_0_), channel_id=1, source_target_pairs={{0,2},{1,5},{4,0},{5,9},{8,4},{9,13},{12,8},{13,15},{14,12},{15,11... | collective-permute-start | bytes 4718600 | tf_op jit(solution)/shard_map/ppermute | solution.py:429
  77.1 32.4 %collective-permute-start.12 = (bf16[48,16384]{1,0:T(8,128)(2,1)}, bf16[48,16384]{1,0:T(8,128)(2,1)S(1)}, u32[]{:S(2)}, u32[]{:S(2)}) collective-permute-start(bf16[48,16384]{1,0:T(8,128)(2,1)} %collective-permute-done.10.x_ref.refs_0_), channel_id=1, source_target_pairs={{0,1},{1,0},{2,3},{3,2},{4,5},{5,4},{6,7},{7,6},{8,9},{9,8},{10,11... | collective-permute-start | bytes 4718600 | tf_op jit(solution)/shard_map/ppermute | solution.py:429
  99.5 10.0 %collective-permute-start.13 = (bf16[48,16384]{1,0:T(8,128)(2,1)S(1)}, bf16[48,16384]{1,0:T(8,128)(2,1)S(1)}, u32[]{:S(2)}, u32[]{:S(2)}) collective-permute-start(bf16[48,16384]{1,0:T(8,128)(2,1)S(1)} %collective-permute-done.5.x_ref.refs_2_), channel_id=1, source_target_pairs={{0,1},{1,0},{2,3},{3,2},{4,5},{5,4},{6,7},{7,6},{8,9},{9,8},{10,11... | collective-permute-start | bytes 4718600 | tf_op jit(solution)/shard_map/ppermute | solution.py:429
  99.5 23.7 %collective-permute-start.9 = (bf16[48,16384]{1,0:T(8,128)(2,1)S(1)}, bf16[48,16384]{1,0:T(8,128)(2,1)S(1)}, u32[]{:S(2)}, u32[]{:S(2)}) collective-permute-start(bf16[48,16384]{1,0:T(8,128)(2,1)S(1)} %collective-permute-done.5.x_ref.refs_2_), channel_id=1, source_target_pairs={{0,4},{1,3},{4,8},{5,1},{8,12},{9,5},{12,14},{13,9},{14,10},{15,13... | collective-permute-start | bytes 4718600 | tf_op jit(solution)/shard_map/ppermute | solution.py:429
  108.3 20.0 %collective-permute-start.17 = (bf16[48,16384]{1,0:T(8,128)(2,1)S(1)}, bf16[48,16384]{1,0:T(8,128)(2,1)S(1)}, u32[]{:S(2)}, u32[]{:S(2)}) collective-permute-start(bf16[48,16384]{1,0:T(8,128)(2,1)S(1)} %collective-permute-done.11.x_ref.refs_0_), channel_id=1, source_target_pairs={{0,1},{1,0},{2,3},{3,2},{4,5},{5,4},{6,7},{7,6},{8,9},{9,8},{10,11... | collective-permute-start | bytes 4718600 | tf_op jit(solution)/shard_map/ppermute | solution.py:429
  123.2 5.1 %collective-permute-start.18 = (bf16[48,16384]{1,0:T(8,128)(2,1)S(1)}, bf16[48,16384]{1,0:T(8,128)(2,1)S(1)}, u32[]{:S(2)}, u32[]{:S(2)}) collective-permute-start(bf16[48,16384]{1,0:T(8,128)(2,1)S(1)} %collective-permute-done.9.refs_0_.refs_2_), channel_id=1, source_target_pairs={{0,1},{1,0},{2,3},{3,2},{4,5},{5,4},{6,7},{7,6},{8,9},{9,8},{10,11... | collective-permute-start | bytes 4718600 | tf_op jit(solution)/shard_map/ppermute | solution.py:429
  124.7 10.8 %collective-permute-start.14 = (bf16[192,128]{1,0:T(8,128)(2,1)S(1)}, bf16[192,128]{1,0:T(8,128)(2,1)S(1)}, u32[]{:S(2)}, u32[]{:S(2)}) collective-permute-start(bf16[192,128]{1,0:T(8,128)(2,1)S(1)} %ranks.1), channel_id=1, source_target_pairs={{0,2},{1,3},{2,0},{3,1},{4,6},{5,7},{6,4},{7,5},{8,10},{9,11},{10,... | collective-permute-start | bytes 147464 | tf_op jit(solution)/shard_map/ppermute | solution.py:429
  126.7 8.7 %collective-permute-start.15 = (bf16[192,128]{1,0:T(8,128)(2,1)S(1)}, bf16[192,128]{1,0:T(8,128)(2,1)S(1)}, u32[]{:S(2)}, u32[]{:S(2)}) collective-permute-start(bf16[192,128]{1,0:T(8,128)(2,1)S(1)} %ranks.1), channel_id=1, source_target_pairs={{0,4},{1,5},{2,6},{3,7},{4,0},{5,1},{6,2},{7,3},{8,12},{9,13},{10,... | collective-permute-start | bytes 147464 | tf_op jit(solution)/shard_map/ppermute | solution.py:429
  128.3 7.1 %collective-permute-start.16 = (bf16[192,128]{1,0:T(8,128)(2,1)S(1)}, bf16[192,128]{1,0:T(8,128)(2,1)S(1)}, u32[]{:S(2)}, u32[]{:S(2)}) collective-permute-start(bf16[192,128]{1,0:T(8,128)(2,1)S(1)} %ranks.1), channel_id=1, source_target_pairs={{0,6},{1,7},{2,4},{3,5},{4,2},{5,3},{6,0},{7,1},{8,14},{9,15},{10,... | collective-permute-start | bytes 147464 | tf_op jit(solution)/shard_map/ppermute | solution.py:429
  135.5 10.6 %collective-permute-start.19 = (bf16[192,128]{1,0:T(8,128)(2,1)S(1)}, bf16[192,128]{1,0:T(8,128)(2,1)S(1)}, u32[]{:S(2)}, u32[]{:S(2)}) collective-permute-start(bf16[192,128]{1,0:T(8,128)(2,1)S(1)} %add_add_fusion), channel_id=1, source_target_pairs={{0,8},{1,9},{2,10},{3,11},{4,12},{5,13},{6,14},{7,15},{8,0},{9,1},... | collective-permute-start | bytes 147464 | tf_op jit(solution)/shard_map/ppermute | solution.py:429
  138.5 7.5 %collective-permute-start.20 = (bf16[192,128]{1,0:T(8,128)(2,1)S(1)}, bf16[192,128]{1,0:T(8,128)(2,1)S(1)}, u32[]{:S(2)}, u32[]{:S(2)}) collective-permute-start(bf16[192,128]{1,0:T(8,128)(2,1)S(1)} %add_add_fusion), channel_id=1, source_target_pairs={{0,1},{1,0},{2,3},{3,2},{4,5},{5,4},{6,7},{7,6},{8,9},{9,8},{10,11... | collective-permute-start | bytes 147464 | tf_op jit(solution)/shard_map/ppermute | solution.py:429
  138.5 7.6 %collective-permute-start.21 = (bf16[192,128]{1,0:T(8,128)(2,1)S(1)}, bf16[192,128]{1,0:T(8,128)(2,1)S(1)}, u32[]{:S(2)}, u32[]{:S(2)}) collective-permute-start(bf16[192,128]{1,0:T(8,128)(2,1)S(1)} %add_add_fusion), channel_id=1, source_target_pairs={{0,9},{1,8},{2,11},{3,10},{4,13},{5,12},{6,15},{7,14},{8,1},{9,0},... | collective-permute-start | bytes 147464 | tf_op jit(solution)/shard_map/ppermute | solution.py:429
  (8 other events, 63.8 us)

commit v18 on v17

--- a/solution.py
+++ b/solution.py
@@ -179,11 +179,12 @@
     if ranked:
         s_ref, refs = refs[0], refs[1:]
     if not first:
-        total_in, refs = refs[0], refs[1:]
-    total_out, refs = refs[0], refs[1:]
+        refs = refs[1:]
+    total, refs = refs[0], refs[1:]
     if ranked:
         h_out, refs = refs[0], refs[1:]
-    acc, before, x_slots, w_slots, s_slots, sems, total_sems = refs
+    x_slots, w_slots, s_slots, sems = refs
+    here = slice(base, base + count)
     rows = xs[0].shape[0]
 
     def copies(step):
@@ -205,10 +206,8 @@
 
     for step in range(min(SLOTS, steps)):
         start(jnp.int32(step))
-    if not fresh:
-        load = pltpu.make_async_copy(total_in.at[pl.ds(base, count)], before, total_sems.at[0])
-        load.start()
-    acc[...] = jnp.zeros_like(acc)
+    if fresh:
+        total[here] = jnp.zeros((count,) + total.shape[1:], F32)
     if ranked:
         h_out[...] = jnp.zeros_like(h_out)
 
@@ -218,10 +217,10 @@
             copy.wait()
         slot = lax.rem(step, SLOTS)
         x = x_slots[slot]
-        for left in range(0, acc.shape[2], CHUNK):
+        for left in range(0, total.shape[2], CHUNK):
             cut = slice(left, left + CHUNK)
             product = jnp.dot(x, w_slots[slot, :, cut], preferred_element_type=F32)
-            acc[:, :, cut] += product.reshape(count, rows, CHUNK)
+            total[here, :, cut] += product.reshape(count, rows, CHUNK)
         if ranked:
             mine = jnp.concatenate([x[i * rows : (i + 1) * rows] for i in range(0, count, 2)], 0)
             h_out[...] += jnp.dot(mine, s_slots[slot], preferred_element_type=F32)
@@ -229,13 +228,6 @@
         @pl.when(step + SLOTS < steps)
         def _():
             start(step + SLOTS)
-
-    if not fresh:
-        load.wait()
-        acc[...] += before[...]
-    store = pltpu.make_async_copy(acc, total_out.at[pl.ds(base, count)], total_sems.at[1])
-    store.start()
-    store.wait()
 
 
 def block_product(xs, weights, factors, low, high, tile, total, base, ranked):
@@ -254,8 +246,8 @@
     if not first:
         aliases = {len(operands): 0}
         operands.append(total)
-        specs.append(anywhere)
-    outs, out_specs = [jax.ShapeDtypeStruct(total_shape(rows, cols), F32)], [anywhere]
+        specs.append(whole)
+    outs, out_specs = [jax.ShapeDtypeStruct(total_shape(rows, cols), F32)], [whole]
     if ranked:
         outs.append(jax.ShapeDtypeStruct((count // 2 * rows, rank), F32))
         out_specs.append(whole)
@@ -266,13 +258,10 @@
         out_specs=out_specs,
         out_shape=outs,
         scratch_shapes=[
-            pltpu.VMEM((count, rows, cols), F32),
-            pltpu.VMEM((1, 8, 128) if fresh else (count, rows, cols), F32),
             pltpu.VMEM((SLOTS, count * rows, tile), BF16),
             pltpu.VMEM((SLOTS, tile, cols), BF16),
             pltpu.VMEM((SLOTS, tile, rank), BF16),
             pltpu.SemaphoreType.DMA((SLOTS, count + 2)),
-            pltpu.SemaphoreType.DMA((2,)),
         ],
         input_output_aliases=aliases,
         compiler_params=pltpu.CompilerParams(vmem_limit_bytes=BIG_VMEM),

time: 149 us -> 149 us (level)
  transfers between devices with their start and end apart: 22 -> 22, of which waited for: 8 -> 8; matrix products, arithmetic and copies ran while one was open for 3% -> 3% of each run, Pallas kernels for 52% -> 51%
where the time goes in v18:
time: 149 us
  Pallas kernels  78.8 us (53%)
  waiting for transfers between devices  33.5 us (22%)
  starting transfers between devices  27.4 us (18%)
  local copies, waits for them, and re-layouts  6.54 us (4%)
  other arithmetic  2.14 us (1%)
    pallas_call x7, Pallas kernels, block_product(): pl.pallas_call(functools.partial(block_kernel, count, low, tile, steps, f...  66.2 us
    ppermute x22, waiting for transfers between devices, ring_plan(): send = lambda value, pairs: lax.ppermute(value, 'tensor', pairs)  33.5 us
    ppermute x22, starting transfers between devices, ring_plan(): send = lambda value, pairs: lax.ppermute(value, 'tensor', pairs)  27.4 us
    pallas_call x4, Pallas kernels, some_ranks(): pl.pallas_call(some_ranks_kernel, in_specs=[whole] * 2, out_specs=whole,...  6.98 us
    unnamed x20, local copies, waits for them, and re-layouts  4.41 us
  transfers between devices with their start and end apart: 22, of which 8 were waited for; matrix products, arithmetic and copies ran while one was open for 3% of the time, Pallas kernels for 51%

profile of v18, /device:TPU:0, one launch (start us, length us, event | category | flops | bytes accessed | tf_op | source)
XLA Modules:
  0.0 148.8 jit_solution(7570528695972681094)
XLA Ops:
  0.5 3.0 %collective-permute-start = (bf16[48,16384]{1,0:T(8,128)(2,1)}, bf16[48,16384]{1,0:T(8,128)(2,1)}, u32[]{:S(2)}, u32[]{:S(2)}) collective-permute-start(bf16[48,16384]{1,0:T(8,128)(2,1)} %refs_0_.3), channel_id=1, source_target_pairs={{0,4},{1,3},{4,8},{5,1},{8,12},{9,5},{12,14},{13,9},{14,10},{15,13... | collective-permute-start | bytes 4718600 | tf_op jit(solution)/shard_map/ppermute | solution.py:418
  3.5 3.2 %collective-permute-done.2.refs_1_ = bf16[48,16384]{1,0:T(8,128)(2,1)S(1)} collective-permute-done((bf16[48,16384]{1,0:T(8,128)(2,1)}, bf16[48,16384]{1,0:T(8,128)(2,1)S(1)}, u32[]{:S(2)}, u32[]{:S(2)}) %collective-permute-start.2) | collective-permute-done | bytes 1572896 | tf_op jit(solution)/shard_map/ppermute | solution.py:418
  6.7 2.9 %blocks.7.refs_3_ = f32[16,48,1024]{2,1,0:T(8,128)S(1)} custom-call(bf16[48,16384]{1,0:T(8,128)(2,1)} %refs_0_.3, bf16[48,16384]{1,0:T(8,128)(2,1)S(1)} %collective-permute-done.2.refs_1_, bf16[16384,1024]{1,0:T(8,128)(2,1)} %refs_4_.7), custom_call_target="tpu_custom_call" | custom-call | flops 402653184 | bytes 4194304 | tf_op jit(solution)/shard_map/blocks/pallas_call | solution.py:255
  9.6 2.9 %collective-permute-start.6 = (bf16[48,16384]{1,0:T(8,128)(2,1)}, bf16[48,16384]{1,0:T(8,128)(2,1)}, u32[]{:S(2)}, u32[]{:S(2)}) collective-permute-start(bf16[48,16384]{1,0:T(8,128)(2,1)} %refs_0_.3), channel_id=1, source_target_pairs={{0,2},{1,5},{4,0},{5,9},{8,4},{9,13},{12,8},{13,15},{14,12},{15,11... | collective-permute-start | bytes 4718600 | tf_op jit(solution)/shard_map/ppermute | solution.py:418
  12.5 10.7 %blocks.8.refs_4_ = f32[16,48,1024]{2,1,0:T(8,128)S(1)} custom-call(bf16[48,16384]{1,0:T(8,128)(2,1)} %refs_0_.3, bf16[48,16384]{1,0:T(8,128)(2,1)S(1)} %collective-permute-done.2.refs_1_, bf16[16384,1024]{1,0:T(8,128)(2,1)} %refs_4_.7, f32[16,48,1024]{2,1,0:T(8,128)S(1)} %blocks.7.refs_3_), custom_call_target="tpu_custom_call", output_to_operand_aliasing={{}: (3, {})} | custom-call | flops 2818572288 | bytes 29360128 | tf_op jit(solution)/shard_map/blocks/pallas_call | solution.py:255
  24.8 3.4 %some_ranks.4.refs_2_ = f32[48,128]{1,0:T(8,128)S(1)} custom-call(bf16[48,16384]{1,0:T(8,128)(2,1)} %refs_0_.3, bf16[16384,128]{1,0:T(8,128)(2,1)S(1)} %turn.1.s_ref.refs_3_.refs_5_.refs_1_), custom_call_target="tpu_custom_call" | custom-call | tf_op jit(solution)/shard_map/some_ranks/pallas_call | solution.py:313
  28.2 2.3 %collective-permute-done.refs_0_ = bf16[48,16384]{1,0:T(8,128)(2,1)} collective-permute-done((bf16[48,16384]{1,0:T(8,128)(2,1)}, bf16[48,16384]{1,0:T(8,128)(2,1)}, u32[]{:S(2)}, u32[]{:S(2)}) %collective-permute-start) | collective-permute-done | bytes 1572896 | tf_op jit(solution)/shard_map/ppermute | solution.py:418
  30.5 2.4 %collective-permute-start.4 = (bf16[48,16384]{1,0:T(8,128)(2,1)}, bf16[48,16384]{1,0:T(8,128)(2,1)}, u32[]{:S(2)}, u32[]{:S(2)}) collective-permute-start(bf16[48,16384]{1,0:T(8,128)(2,1)} %collective-permute-done.refs_0_), channel_id=1, source_target_pairs={{0,4},{1,3},{4,8},{5,1},{8,12},{9,5},{12,14},{13,9},{14,10},{15,13... | collective-permute-start | bytes 4718600 | tf_op jit(solution)/shard_map/ppermute | solution.py:418
  32.9 9.4 %collective-permute-done.6.refs_0_ = bf16[48,16384]{1,0:T(8,128)(2,1)} collective-permute-done((bf16[48,16384]{1,0:T(8,128)(2,1)}, bf16[48,16384]{1,0:T(8,128)(2,1)}, u32[]{:S(2)}, u32[]{:S(2)}) %collective-permute-start.6) | collective-permute-done | bytes 1572896 | tf_op jit(solution)/shard_map/ppermute | solution.py:418
  45.2 2.2 %copy-done.3 = bf16[16384,128]{1,0:T(8,128)(2,1)S(1)} copy-done((bf16[16384,128]{1,0:T(8,128)(2,1)S(1)}, bf16[16384,128]{1,0:T(8,128)(2,1)}, u32[]{:S(2)}) %copy-start.3) | copy-done | bytes 4194328
  47.4 12.4 %blocks.9 = (f32[16,48,1024]{2,1,0:T(8,128)S(1)}, f32[48,128]{1,0:T(8,128)S(1)}) custom-call(bf16[48,16384]{1,0:T(8,128)(2,1)} %collective-permute-done.refs_0_, bf16[48,16384]{1,0:T(8,128)(2,1)} %collective-permute-done.3.refs_1_, bf16[16384,1024]{1,0:T(8,128)(2,1)} %refs_4_.7, bf16[16384,128]{1,0:T(8,128)(2,1)S(1)} %copy-done.3, ...), custom_call_target="tpu_custom_call", output_to_operand_aliasing={{0}: (4, {})} | custom-call | flops 3221225472 | bytes 33554432 | tf_op jit(solution)/shard_map/blocks/pallas_call | solution.py:255
  65.1 2.4 %collective-permute-start.5 = (bf16[48,16384]{1,0:T(8,128)(2,1)}, bf16[48,16384]{1,0:T(8,128)(2,1)S(1)}, u32[]{:S(2)}, u32[]{:S(2)}) collective-permute-start(bf16[48,16384]{1,0:T(8,128)(2,1)} %collective-permute-done.4.refs_2_), channel_id=1, source_target_pairs={{0,4},{1,3},{4,8},{5,1},{8,12},{9,5},{12,14},{13,9},{14,10},{15,13... | collective-permute-start | bytes 4718600 | tf_op jit(solution)/shard_map/ppermute | solution.py:418
  67.5 7.7 %collective-permute-done.10.x_ref.refs_0_ = bf16[48,16384]{1,0:T(8,128)(2,1)} collective-permute-done((bf16[48,16384]{1,0:T(8,128)(2,1)}, bf16[48,16384]{1,0:T(8,128)(2,1)}, u32[]{:S(2)}, u32[]{:S(2)}) %collective-permute-start.10) | collective-permute-done | bytes 1572896 | tf_op jit(solution)/shard_map/ppermute | solution.py:418
  78.0 2.2 %copy-done.4 = bf16[16384,128]{1,0:T(8,128)(2,1)S(1)} copy-done((bf16[16384,128]{1,0:T(8,128)(2,1)S(1)}, bf16[16384,128]{1,0:T(8,128)(2,1)}, u32[]{:S(2)}) %copy-start.4) | copy-done | bytes 4194328
  80.2 13.5 %blocks.10 = (f32[16,48,1024]{2,1,0:T(8,128)S(1)}, f32[96,128]{1,0:T(8,128)S(1)}) custom-call(bf16[48,16384]{1,0:T(8,128)(2,1)} %collective-permute-done.6.refs_0_, bf16[48,16384]{1,0:T(8,128)(2,1)} %collective-permute-done.7.refs_1_, bf16[48,16384]{1,0:T(8,128)(2,1)} %collective-permute-done.4.refs_2_, ...), custom_call_target="tpu_custom_call", output_to_operand_aliasing={{0}: (6, {})} | custom-call | flops 6442450944 | bytes 33554432 | tf_op jit(solution)/shard_map/blocks/pallas_call | solution.py:255
  93.7 6.0 %collective-permute-done.5.x_ref.refs_2_ = bf16[48,16384]{1,0:T(8,128)(2,1)S(1)} collective-permute-done((bf16[48,16384]{1,0:T(8,128)(2,1)}, bf16[48,16384]{1,0:T(8,128)(2,1)S(1)}, u32[]{:S(2)}, u32[]{:S(2)}) %collective-permute-start.5) | collective-permute-done | bytes 1572896 | tf_op jit(solution)/shard_map/ppermute | solution.py:418
  99.7 2.4 %collective-permute-start.9 = (bf16[48,16384]{1,0:T(8,128)(2,1)S(1)}, bf16[48,16384]{1,0:T(8,128)(2,1)S(1)}, u32[]{:S(2)}, u32[]{:S(2)}) collective-permute-start(bf16[48,16384]{1,0:T(8,128)(2,1)S(1)} %collective-permute-done.5.x_ref.refs_2_), channel_id=1, source_target_pairs={{0,4},{1,3},{4,8},{5,1},{8,12},{9,5},{12,14},{13,9},{14,10},{15,13... | collective-permute-start | bytes 4718600 | tf_op jit(solution)/shard_map/ppermute | solution.py:418
  102.0 2.1 %some_ranks.5.refs_5_ = f32[48,128]{1,0:T(8,128)S(1)} custom-call(bf16[48,16384]{1,0:T(8,128)(2,1)} %collective-permute-done.10.x_ref.refs_0_, bf16[16384,128]{1,0:T(8,128)(2,1)S(1)} %copy-done.5), custom_call_target="tpu_custom_call" | custom-call | tf_op jit(solution)/shard_map/some_ranks/pallas_call | solution.py:313
  104.9 3.2 %collective-permute-done.11.x_ref.refs_0_ = bf16[48,16384]{1,0:T(8,128)(2,1)S(1)} collective-permute-done((bf16[48,16384]{1,0:T(8,128)(2,1)}, bf16[48,16384]{1,0:T(8,128)(2,1)S(1)}, u32[]{:S(2)}, u32[]{:S(2)}) %collective-permute-start.11) | collective-permute-done | bytes 1572896 | tf_op jit(solution)/shard_map/ppermute | solution.py:418
  109.2 12.5 %blocks.11.refs_5_ = f32[16,48,1024]{2,1,0:T(8,128)S(1)} custom-call(bf16[48,16384]{1,0:T(8,128)(2,1)} %collective-permute-done.10.x_ref.refs_0_, bf16[48,16384]{1,0:T(8,128)(2,1)S(1)} %collective-permute-done.12.refs_1_, bf16[48,16384]{1,0:T(8,128)(2,1)S(1)} %collective-permute-done.5.x_ref.refs_2_, ...), custom_call_target="tpu_custom_call", output_to_operand_aliasing={{}: (5, {})} | custom-call | flops 6442450944 | bytes 33554432 | tf_op jit(solution)/shard_map/blocks/pallas_call | solution.py:255
  128.3 7.1 %blocks.12.refs_5_ = f32[16,48,1024]{2,1,0:T(8,128)S(1)} custom-call(bf16[48,16384]{1,0:T(8,128)(2,1)S(1)} %collective-permute-done.11.x_ref.refs_0_, bf16[48,16384]{1,0:T(8,128)(2,1)S(1)} %collective-permute-done.17.refs_1_, bf16[48,16384]{1,0:T(8,128)(2,1)S(1)} %collective-permute-done.9.refs_0_.refs_2_, ...), custom_call_target="tpu_custom_call", output_to_operand_aliasing={{}: (5, {})} | custom-call | flops 3221225472 | bytes 16777216 | tf_op jit(solution)/shard_map/blocks/pallas_call | solution.py:255
  135.5 3.0 %collective-permute-start.19 = (bf16[192,128]{1,0:T(8,128)(2,1)S(1)}, bf16[192,128]{1,0:T(8,128)(2,1)S(1)}, u32[]{:S(2)}, u32[]{:S(2)}) collective-permute-start(bf16[192,128]{1,0:T(8,128)(2,1)S(1)} %add_add_fusion), channel_id=1, source_target_pairs={{0,8},{1,9},{2,10},{3,11},{4,12},{5,13},{6,14},{7,15},{8,0},{9,1},... | collective-permute-start | bytes 147464 | tf_op jit(solution)/shard_map/ppermute | solution.py:418
  138.7 7.2 %blocks.13.total_ref = f32[16,48,1024]{2,1,0:T(8,128)S(1)} custom-call(bf16[48,16384]{1,0:T(8,128)(2,1)S(1)} %collective-permute-done.11.x_ref.refs_0_, bf16[48,16384]{1,0:T(8,128)(2,1)S(1)} %collective-permute-done.17.refs_1_, bf16[48,16384]{1,0:T(8,128)(2,1)S(1)} %collective-permute-done.9.refs_0_.refs_2_, ...), custom_call_target="tpu_custom_call", output_to_operand_aliasing={{}: (5, {})} | custom-call | flops 3221225472 | bytes 16777216 | tf_op jit(solution)/shard_map/blocks/pallas_call | solution.py:255
  146.1 2.6 %finish.1 = bf16[768,1024]{1,0:T(8,128)(2,1)} custom-call(s32[16]{0:T(128)S(1)} %get-tuple-element.69.places_ref, s32[6]{0:T(128)S(1)} %gather_fusion, s32[1]{0:T(128)} %bitcast.7.core_ref, f32[16,48,1024]{2,1,0:T(8,128)S(1)} %blocks.13.total_ref, bf16[16,64,1024]{2,1,0:T(8,128)(2,1)S(1)} %bitcast.16, f32[1,1024]{1,0:T(1,128)S(1)} %bitcast.17, ...), custom_call_target="tpu_custom_call" | custom-call | tf_op jit(solution)/shard_map/finish/pallas_call | solution.py:397
  (69 shorter events, 21.8 us)
Async XLA Ops:
  0.0 60.8 %copy-start = (s32[16]{0:T(128)S(1)}, s32[16]{0:T(128)}, u32[]{:S(2)}) copy-start(s32[16]{0:T(128)} %param.16) | copy-start | bytes 196
  0.0 23.2 %collective-permute-start.1 = (bf16[64,16384]{1,0:T(8,128)(2,1)}, bf16[64,16384]{1,0:T(8,128)(2,1)S(1)}, u32[]{:S(2)}, u32[]{:S(2)}) collective-permute-start(bf16[64,16384]{1,0:T(8,128)(2,1)} %bitcast.14), channel_id=1, source_target_pairs={{0,1},{1,0},{2,3},{3,2},{4,5},{5,4},{6,7},{7,6},{8,9},{9,8},{10,11... | collective-permute-start | bytes 6291464 | tf_op jit(solution)/shard_map/ppermute | solution.py:418
  0.5 6.2 %collective-permute-start.2 = (bf16[48,16384]{1,0:T(8,128)(2,1)}, bf16[48,16384]{1,0:T(8,128)(2,1)S(1)}, u32[]{:S(2)}, u32[]{:S(2)}) collective-permute-start(bf16[48,16384]{1,0:T(8,128)(2,1)} %refs_0_.3), channel_id=1, source_target_pairs={{0,1},{1,0},{2,3},{3,2},{4,5},{5,4},{6,7},{7,6},{8,9},{9,8},{10,11... | collective-permute-start | bytes 4718600 | tf_op jit(solution)/shard_map/ppermute | solution.py:418
  0.5 29.9 %collective-permute-start = (bf16[48,16384]{1,0:T(8,128)(2,1)}, bf16[48,16384]{1,0:T(8,128)(2,1)}, u32[]{:S(2)}, u32[]{:S(2)}) collective-permute-start(bf16[48,16384]{1,0:T(8,128)(2,1)} %refs_0_.3), channel_id=1, source_target_pairs={{0,4},{1,3},{4,8},{5,1},{8,12},{9,5},{12,14},{13,9},{14,10},{15,13... | collective-permute-start | bytes 4718600 | tf_op jit(solution)/shard_map/ppermute | solution.py:418
  9.6 32.7 %collective-permute-start.6 = (bf16[48,16384]{1,0:T(8,128)(2,1)}, bf16[48,16384]{1,0:T(8,128)(2,1)}, u32[]{:S(2)}, u32[]{:S(2)}) collective-permute-start(bf16[48,16384]{1,0:T(8,128)(2,1)} %refs_0_.3), channel_id=1, source_target_pairs={{0,2},{1,5},{4,0},{5,9},{8,4},{9,13},{12,8},{13,15},{14,12},{15,11... | collective-permute-start | bytes 4718600 | tf_op jit(solution)/shard_map/ppermute | solution.py:418
  30.5 14.8 %collective-permute-start.3 = (bf16[48,16384]{1,0:T(8,128)(2,1)}, bf16[48,16384]{1,0:T(8,128)(2,1)}, u32[]{:S(2)}, u32[]{:S(2)}) collective-permute-start(bf16[48,16384]{1,0:T(8,128)(2,1)} %collective-permute-done.refs_0_), channel_id=1, source_target_pairs={{0,1},{1,0},{2,3},{3,2},{4,5},{5,4},{6,7},{7,6},{8,9},{9,8},{10,11... | collective-permute-start | bytes 4718600 | tf_op jit(solution)/shard_map/ppermute | solution.py:418
  30.5 29.3 %copy-start.9 = (s32[8]{0:T(128)S(1)}, s32[8]{0:T(128)}, u32[]{:S(2)}) copy-start(s32[8]{0:T(128)} %param.17) | copy-start | bytes 100
  30.5 34.6 %collective-permute-start.4 = (bf16[48,16384]{1,0:T(8,128)(2,1)}, bf16[48,16384]{1,0:T(8,128)(2,1)}, u32[]{:S(2)}, u32[]{:S(2)}) collective-permute-start(bf16[48,16384]{1,0:T(8,128)(2,1)} %collective-permute-done.refs_0_), channel_id=1, source_target_pairs={{0,4},{1,3},{4,8},{5,1},{8,12},{9,5},{12,14},{13,9},{14,10},{15,13... | collective-permute-start | bytes 4718600 | tf_op jit(solution)/shard_map/ppermute | solution.py:418
  42.3 32.8 %collective-permute-start.10 = (bf16[48,16384]{1,0:T(8,128)(2,1)}, bf16[48,16384]{1,0:T(8,128)(2,1)}, u32[]{:S(2)}, u32[]{:S(2)}) collective-permute-start(bf16[48,16384]{1,0:T(8,128)(2,1)} %collective-permute-done.6.refs_0_), channel_id=1, source_target_pairs={{0,2},{1,5},{4,0},{5,9},{8,4},{9,13},{12,8},{13,15},{14,12},{15,11... | collective-permute-start | bytes 4718600 | tf_op jit(solution)/shard_map/ppermute | solution.py:418
  44.0 34.0 %collective-permute-start.7 = (bf16[48,16384]{1,0:T(8,128)(2,1)}, bf16[48,16384]{1,0:T(8,128)(2,1)}, u32[]{:S(2)}, u32[]{:S(2)}) collective-permute-start(bf16[48,16384]{1,0:T(8,128)(2,1)} %collective-permute-done.6.refs_0_), channel_id=1, source_target_pairs={{0,1},{1,0},{2,3},{3,2},{4,5},{5,4},{6,7},{7,6},{8,9},{9,8},{10,11... | collective-permute-start | bytes 4718600 | tf_op jit(solution)/shard_map/ppermute | solution.py:418
  65.1 12.9 %collective-permute-start.8 = (bf16[48,16384]{1,0:T(8,128)(2,1)}, bf16[48,16384]{1,0:T(8,128)(2,1)S(1)}, u32[]{:S(2)}, u32[]{:S(2)}) collective-permute-start(bf16[48,16384]{1,0:T(8,128)(2,1)} %collective-permute-done.4.refs_2_), channel_id=1, source_target_pairs={{0,1},{1,0},{2,3},{3,2},{4,5},{5,4},{6,7},{7,6},{8,9},{9,8},{10,11... | collective-permute-start | bytes 4718600 | tf_op jit(solution)/shard_map/ppermute | solution.py:418
  65.1 34.6 %collective-permute-start.5 = (bf16[48,16384]{1,0:T(8,128)(2,1)}, bf16[48,16384]{1,0:T(8,128)(2,1)S(1)}, u32[]{:S(2)}, u32[]{:S(2)}) collective-permute-start(bf16[48,16384]{1,0:T(8,128)(2,1)} %collective-permute-done.4.refs_2_), channel_id=1, source_target_pairs={{0,4},{1,3},{4,8},{5,1},{8,12},{9,5},{12,14},{13,9},{14,10},{15,13... | collective-permute-start | bytes 4718600 | tf_op jit(solution)/shard_map/ppermute | solution.py:418
  75.2 33.0 %collective-permute-start.11 = (bf16[48,16384]{1,0:T(8,128)(2,1)}, bf16[48,16384]{1,0:T(8,128)(2,1)S(1)}, u32[]{:S(2)}, u32[]{:S(2)}) collective-permute-start(bf16[48,16384]{1,0:T(8,128)(2,1)} %collective-permute-done.10.x_ref.refs_0_), channel_id=1, source_target_pairs={{0,2},{1,5},{4,0},{5,9},{8,4},{9,13},{12,8},{13,15},{14,12},{15,11... | collective-permute-start | bytes 4718600 | tf_op jit(solution)/shard_map/ppermute | solution.py:418
  76.9 32.4 %collective-permute-start.12 = (bf16[48,16384]{1,0:T(8,128)(2,1)}, bf16[48,16384]{1,0:T(8,128)(2,1)S(1)}, u32[]{:S(2)}, u32[]{:S(2)}) collective-permute-start(bf16[48,16384]{1,0:T(8,128)(2,1)} %collective-permute-done.10.x_ref.refs_0_), channel_id=1, source_target_pairs={{0,1},{1,0},{2,3},{3,2},{4,5},{5,4},{6,7},{7,6},{8,9},{9,8},{10,11... | collective-permute-start | bytes 4718600 | tf_op jit(solution)/shard_map/ppermute | solution.py:418
  99.7 9.6 %collective-permute-start.13 = (bf16[48,16384]{1,0:T(8,128)(2,1)S(1)}, bf16[48,16384]{1,0:T(8,128)(2,1)S(1)}, u32[]{:S(2)}, u32[]{:S(2)}) collective-permute-start(bf16[48,16384]{1,0:T(8,128)(2,1)S(1)} %collective-permute-done.5.x_ref.refs_2_), channel_id=1, source_target_pairs={{0,1},{1,0},{2,3},{3,2},{4,5},{5,4},{6,7},{7,6},{8,9},{9,8},{10,11... | collective-permute-start | bytes 4718600 | tf_op jit(solution)/shard_map/ppermute | solution.py:418
  99.7 23.5 %collective-permute-start.9 = (bf16[48,16384]{1,0:T(8,128)(2,1)S(1)}, bf16[48,16384]{1,0:T(8,128)(2,1)S(1)}, u32[]{:S(2)}, u32[]{:S(2)}) collective-permute-start(bf16[48,16384]{1,0:T(8,128)(2,1)S(1)} %collective-permute-done.5.x_ref.refs_2_), channel_id=1, source_target_pairs={{0,4},{1,3},{4,8},{5,1},{8,12},{9,5},{12,14},{13,9},{14,10},{15,13... | collective-permute-start | bytes 4718600 | tf_op jit(solution)/shard_map/ppermute | solution.py:418
  108.1 20.2 %collective-permute-start.17 = (bf16[48,16384]{1,0:T(8,128)(2,1)S(1)}, bf16[48,16384]{1,0:T(8,128)(2,1)S(1)}, u32[]{:S(2)}, u32[]{:S(2)}) collective-permute-start(bf16[48,16384]{1,0:T(8,128)(2,1)S(1)} %collective-permute-done.11.x_ref.refs_0_), channel_id=1, source_target_pairs={{0,1},{1,0},{2,3},{3,2},{4,5},{5,4},{6,7},{7,6},{8,9},{9,8},{10,11... | collective-permute-start | bytes 4718600 | tf_op jit(solution)/shard_map/ppermute | solution.py:418
  123.2 5.1 %collective-permute-start.18 = (bf16[48,16384]{1,0:T(8,128)(2,1)S(1)}, bf16[48,16384]{1,0:T(8,128)(2,1)S(1)}, u32[]{:S(2)}, u32[]{:S(2)}) collective-permute-start(bf16[48,16384]{1,0:T(8,128)(2,1)S(1)} %collective-permute-done.9.refs_0_.refs_2_), channel_id=1, source_target_pairs={{0,1},{1,0},{2,3},{3,2},{4,5},{5,4},{6,7},{7,6},{8,9},{9,8},{10,11... | collective-permute-start | bytes 4718600 | tf_op jit(solution)/shard_map/ppermute | solution.py:418
  124.7 10.8 %collective-permute-start.14 = (bf16[192,128]{1,0:T(8,128)(2,1)S(1)}, bf16[192,128]{1,0:T(8,128)(2,1)S(1)}, u32[]{:S(2)}, u32[]{:S(2)}) collective-permute-start(bf16[192,128]{1,0:T(8,128)(2,1)S(1)} %ranks.1), channel_id=1, source_target_pairs={{0,2},{1,3},{2,0},{3,1},{4,6},{5,7},{6,4},{7,5},{8,10},{9,11},{10,... | collective-permute-start | bytes 147464 | tf_op jit(solution)/shard_map/ppermute | solution.py:418
  126.7 8.7 %collective-permute-start.15 = (bf16[192,128]{1,0:T(8,128)(2,1)S(1)}, bf16[192,128]{1,0:T(8,128)(2,1)S(1)}, u32[]{:S(2)}, u32[]{:S(2)}) collective-permute-start(bf16[192,128]{1,0:T(8,128)(2,1)S(1)} %ranks.1), channel_id=1, source_target_pairs={{0,4},{1,5},{2,6},{3,7},{4,0},{5,1},{6,2},{7,3},{8,12},{9,13},{10,... | collective-permute-start | bytes 147464 | tf_op jit(solution)/shard_map/ppermute | solution.py:418
  128.3 7.1 %collective-permute-start.16 = (bf16[192,128]{1,0:T(8,128)(2,1)S(1)}, bf16[192,128]{1,0:T(8,128)(2,1)S(1)}, u32[]{:S(2)}, u32[]{:S(2)}) collective-permute-start(bf16[192,128]{1,0:T(8,128)(2,1)S(1)} %ranks.1), channel_id=1, source_target_pairs={{0,6},{1,7},{2,4},{3,5},{4,2},{5,3},{6,0},{7,1},{8,14},{9,15},{10,... | collective-permute-start | bytes 147464 | tf_op jit(solution)/shard_map/ppermute | solution.py:418
  135.5 10.5 %collective-permute-start.19 = (bf16[192,128]{1,0:T(8,128)(2,1)S(1)}, bf16[192,128]{1,0:T(8,128)(2,1)S(1)}, u32[]{:S(2)}, u32[]{:S(2)}) collective-permute-start(bf16[192,128]{1,0:T(8,128)(2,1)S(1)} %add_add_fusion), channel_id=1, source_target_pairs={{0,8},{1,9},{2,10},{3,11},{4,12},{5,13},{6,14},{7,15},{8,0},{9,1},... | collective-permute-start | bytes 147464 | tf_op jit(solution)/shard_map/ppermute | solution.py:418
  138.5 7.5 %collective-permute-start.20 = (bf16[192,128]{1,0:T(8,128)(2,1)S(1)}, bf16[192,128]{1,0:T(8,128)(2,1)S(1)}, u32[]{:S(2)}, u32[]{:S(2)}) collective-permute-start(bf16[192,128]{1,0:T(8,128)(2,1)S(1)} %add_add_fusion), channel_id=1, source_target_pairs={{0,1},{1,0},{2,3},{3,2},{4,5},{5,4},{6,7},{7,6},{8,9},{9,8},{10,11... | collective-permute-start | bytes 147464 | tf_op jit(solution)/shard_map/ppermute | solution.py:418
  138.5 7.5 %collective-permute-start.21 = (bf16[192,128]{1,0:T(8,128)(2,1)S(1)}, bf16[192,128]{1,0:T(8,128)(2,1)S(1)}, u32[]{:S(2)}, u32[]{:S(2)}) collective-permute-start(bf16[192,128]{1,0:T(8,128)(2,1)S(1)} %add_add_fusion), channel_id=1, source_target_pairs={{0,9},{1,8},{2,11},{3,10},{4,13},{5,12},{6,15},{7,14},{8,1},{9,0},... | collective-permute-start | bytes 147464 | tf_op jit(solution)/shard_map/ppermute | solution.py:418
  (8 other events, 63.7 us)

commit v19 on v18

--- a/solution.py
+++ b/solution.py
@@ -10,13 +10,14 @@
 
 HD = 128
 SEG = 128
-VMEM = 20 * 1024 * 1024
+VMEM = 16 * 1024 * 1024
 F32 = jnp.float32
 BF16 = jnp.bfloat16
 NT = (((1,), (1,)), ((), ()))
 SLOTS = 4
 CHUNK = 256
-BIG_VMEM = 24 * 1024 * 1024
+KEEP = 6
+BIG_VMEM = 16 * 1024 * 1024
 PARAMS = pltpu.CompilerParams(vmem_limit_bytes=VMEM)
 SNAKE = (0, 2, 4, 6, 7, 5, 3, 1)
 ROUNDS = len(SNAKE) // 2
@@ -174,10 +175,12 @@
     return pairs
 
 
-def block_kernel(count, low, tile, steps, first, base, fresh, ranked, *refs):
+def block_kernel(count, low, tile, steps, kept, first, base, fresh, ranked, *refs):
     xs, w_ref, refs = refs[:count], refs[count], refs[count + 1 :]
     if ranked:
         s_ref, refs = refs[0], refs[1:]
+    if kept:
+        w_kept, refs = refs[0], refs[1:]
     if not first:
         refs = refs[1:]
     total, refs = refs[0], refs[1:]
@@ -189,21 +192,30 @@
 
     def copies(step):
         slot = lax.rem(step, SLOTS)
-        at = pl.multiple_of(step * tile, tile)
-        sem = lambda i: sems.at[slot, i]
-        out = [pltpu.make_async_copy(w_ref.at[pl.ds(low + at, tile)], w_slots.at[slot], sem(count))]
+        at = low + step * tile
+        if kept:
+            at = jnp.where(step < kept, w_ref.shape[0], low) + (step - kept) * tile
+        at = pl.multiple_of(at, tile)
+        out = []
         for i in range(count):
-            cut = xs[i].at[:, pl.ds(low + at, tile)]
-            out.append(pltpu.make_async_copy(cut, x_slots.at[slot, pl.ds(i * rows, rows)], sem(i)))
+            cut = xs[i].at[:, pl.ds(at, tile)]
+            out.append(pltpu.make_async_copy(cut, x_slots.at[slot, pl.ds(i * rows, rows)], sems.at[slot, i]))
         if ranked:
-            cut = s_ref.at[pl.ds(low + at, tile)]
-            out.append(pltpu.make_async_copy(cut, s_slots.at[slot], sem(count + 1)))
+            cut = s_ref.at[pl.ds(at, tile)]
+            out.append(pltpu.make_async_copy(cut, s_slots.at[slot], sems.at[slot, count + 1]))
         return out
+
+    def weights(index):
+        slot = lax.rem(index, SLOTS)
+        cut = w_ref.at[pl.ds(pl.multiple_of(low + index * tile, tile), tile)]
+        return pltpu.make_async_copy(cut, w_slots.at[slot], sems.at[slot, count])
 
     def start(step):
         for copy in copies(step):
             copy.start()
 
+    for index in range(min(SLOTS, steps - kept)):
+        weights(jnp.int32(index)).start()
     for step in range(min(SLOTS, steps)):
         start(jnp.int32(step))
     if fresh:
@@ -211,37 +223,58 @@
     if ranked:
         h_out[...] = jnp.zeros_like(h_out)
 
-    @pl.loop(0, steps)
-    def _(step):
-        for copy in copies(step):
-            copy.wait()
+    def take(step, weight):
         slot = lax.rem(step, SLOTS)
         x = x_slots[slot]
         for left in range(0, total.shape[2], CHUNK):
             cut = slice(left, left + CHUNK)
-            product = jnp.dot(x, w_slots[slot, :, cut], preferred_element_type=F32)
+            product = jnp.dot(x, weight(cut), preferred_element_type=F32)
             total[here, :, cut] += product.reshape(count, rows, CHUNK)
         if ranked:
             mine = jnp.concatenate([x[i * rows : (i + 1) * rows] for i in range(0, count, 2)], 0)
             h_out[...] += jnp.dot(mine, s_slots[slot], preferred_element_type=F32)
 
+    if kept:
+        @pl.loop(0, kept)
+        def _(step):
+            for copy in copies(step):
+                copy.wait()
+            take(step, lambda cut: w_kept[pl.ds(pl.multiple_of(step * tile, tile), tile), cut])
+
+            @pl.when(step + SLOTS < steps)
+            def _():
+                start(step + SLOTS)
+
+    @pl.loop(kept, steps)
+    def _(step):
+        index = step - kept
+        for copy in copies(step) + [weights(index)]:
+            copy.wait()
+        take(step, lambda cut: w_slots[lax.rem(index, SLOTS), :, cut])
+
         @pl.when(step + SLOTS < steps)
         def _():
             start(step + SLOTS)
-
-
-def block_product(xs, weights, factors, low, high, tile, total, base, ranked):
+            weights(index + SLOTS).start()
+
+
+def block_product(xs, weights, factors, low, high, tile, total, base, ranked, fresh=None, kept=None):
     count = len(xs)
     rows = xs[0].shape[0]
     cols = weights.shape[1]
     rank = factors.shape[1] if ranked else 128
-    fresh, first = low == 0, total is None
+    fresh, first = low == 0 if fresh is None else fresh, total is None
     anywhere, whole = pl.BlockSpec(memory_space=pl.ANY), pl.BlockSpec(memory_space=pltpu.VMEM)
     operands = list(xs) + [weights]
     specs = [anywhere] * (count + 1)
     if ranked:
         operands.append(factors)
         specs.append(anywhere)
+    kept_steps = 0
+    if kept is not None:
+        operands.append(kept)
+        specs.append(whole)
+        kept_steps = kept.shape[0] // tile
     aliases = {}
     if not first:
         aliases = {len(operands): 0}
@@ -251,9 +284,9 @@
     if ranked:
         outs.append(jax.ShapeDtypeStruct((count // 2 * rows, rank), F32))
         out_specs.append(whole)
-    steps = (high - low) // tile
+    steps = (high - low) // tile + kept_steps
     result = pl.pallas_call(
-        functools.partial(block_kernel, count, low, tile, steps, first, base, fresh, ranked),
+        functools.partial(block_kernel, count, low, tile, steps, kept_steps, first, base, fresh, ranked),
         in_specs=specs,
         out_specs=out_specs,
         out_shape=outs,
@@ -273,6 +306,25 @@
         name="blocks",
     )(*operands)
     return result[0], result[1:]
+
+
+def keep_kernel(low, w_ref, out_ref, sem):
+    copy = pltpu.make_async_copy(w_ref.at[pl.ds(low, out_ref.shape[0])], out_ref, sem)
+    copy.start()
+    copy.wait()
+
+
+def keep_weights(weights, low):
+    depth, cols = weights.shape
+    return pl.pallas_call(
+        functools.partial(keep_kernel, low),
+        in_specs=[pl.BlockSpec(memory_space=pl.ANY)],
+        out_specs=pl.BlockSpec(memory_space=pltpu.VMEM),
+        out_shape=jax.ShapeDtypeStruct((depth - low, cols), weights.dtype),
+        scratch_shapes=[pltpu.SemaphoreType.DMA],
+        compiler_params=PARAMS,
+        name="keep",
+    )(weights)
 
 
 def total_shape(rows, cols):
@@ -421,6 +473,7 @@
 
     half = depth // 2
     hs, counts = [], []
+    streamed = depth - KEEP * tile
 
     def multiply(xs, total, ranked):
         total, h = block_product(xs, weights, factors, 0, depth, tile, total, sum(counts), ranked)
@@ -467,6 +520,9 @@
             last, _ = lax.optimization_barrier((arrived, total))
             hs.append(some_ranks(last, factors))
             hs, total = lax.optimization_barrier((hs, total))
+        if hop == 3:
+            known, total = lax.optimization_barrier((weights, total))
+            kept, total = lax.optimization_barrier((keep_weights(known, streamed), total))
         if hop == 1:
             known, total = lax.optimization_barrier(((me, indices), total))
             tables, total = lax.optimization_barrier((make_tables(*known), total))
@@ -476,15 +532,16 @@
     h = rank_terms(owners, slots, blocks[2:3], factors, hs)
     beside = lambda step: send(h, [(i, i ^ step) for i in range(parts)])
 
-    def last_product(low, high, total):
+    def last_product(low, high, total, **more):
         xs, _ = lax.optimization_barrier((blocks, h))
-        return block_product(xs, weights, factors, low, high, tile, total, held, False)[0]
-
+        return block_product(xs, weights, factors, low, high, tile, total, held, False, **more)[0]
+
+    middle = streamed // (2 * tile) * tile
     near = [beside(step) for step in (2, 4, 6)]
-    near, total = lax.optimization_barrier((near, last_product(0, half, total)))
+    near, total = lax.optimization_barrier((near, last_product(0, middle, total, kept=kept)))
     h = h + near[0] + near[1] + near[2]
     far = [beside(step) for step in (8, 1, 9)]
-    far, total = lax.optimization_barrier((far, last_product(half, depth, total)))
+    far, total = lax.optimization_barrier((far, last_product(middle, streamed, total, fresh=False)))
     mine, other = h + far[0], far[1] + far[2]
     return block_finish(places, segment_slot, core, total, expands, scale, mine, other, cosine, sine)
 

time: 149 us -> 150 us (level)
  Pallas kernels: 78.8 us -> 88.8 us
  waiting for transfers between devices: 33.5 us -> 24.5 us
    pallas_call x7 -> x8, Pallas kernels: 66.2 us -> 76.3 us  [the longest x7 71.6 us: block_product(): pl.pallas_call(functools.partial(block_kernel, count, low, tile, steps, k...]
    ppermute x22, waiting for transfers between devices: 33.5 us -> 24.5 us  [ring_plan(): send = lambda value, pairs: lax.ppermute(value, 'tensor', pairs)]
  transfers between devices with their start and end apart: 22 -> 22, of which waited for: 8 -> 6; matrix products, arithmetic and copies ran while one was open for 3% -> 3% of each run, Pallas kernels for 51% -> 58%
where the time goes in v19:
time: 150 us
  Pallas kernels  88.8 us (59%)
  starting transfers between devices  27.1 us (18%)
  waiting for transfers between devices  24.5 us (16%)
  local copies, waits for them, and re-layouts  6.55 us (4%)
  other arithmetic  2.13 us (1%)
    pallas_call x7, Pallas kernels, block_product(): pl.pallas_call(functools.partial(block_kernel, count, low, tile, steps, k...  71.6 us
    ppermute x22, starting transfers between devices, ring_plan(): send = lambda value, pairs: lax.ppermute(value, 'tensor', pairs)  27.1 us
    ppermute x22, waiting for transfers between devices, ring_plan(): send = lambda value, pairs: lax.ppermute(value, 'tensor', pairs)  24.5 us
    pallas_call x4, Pallas kernels, some_ranks(): pl.pallas_call(some_ranks_kernel, in_specs=[whole] * 2, out_specs=whole,...  6.98 us
    pallas_call x1, Pallas kernels, keep_weights(): pl.pallas_call(functools.partial(keep_kernel, low), in_specs=[pl.BlockSpe...  4.74 us
    unnamed x20, local copies, waits for them, and re-layouts  4.41 us
  transfers between devices with their start and end apart: 22, of which 6 were waited for; matrix products, arithmetic and copies ran while one was open for 3% of the time, Pallas kernels for 58%

profile of v19, /device:TPU:0, one launch (start us, length us, event | category | flops | bytes accessed | tf_op | source)
XLA Modules:
  0.0 149.6 jit_solution(17208737380447490694)
XLA Ops:
  0.5 3.0 %collective-permute-start = (bf16[48,16384]{1,0:T(8,128)(2,1)}, bf16[48,16384]{1,0:T(8,128)(2,1)}, u32[]{:S(2)}, u32[]{:S(2)}) collective-permute-start(bf16[48,16384]{1,0:T(8,128)(2,1)} %refs_0_.3), channel_id=1, source_target_pairs={{0,4},{1,3},{4,8},{5,1},{8,12},{9,5},{12,14},{13,9},{14,10},{15,13... | collective-permute-start | bytes 4718600 | tf_op jit(solution)/shard_map/ppermute | solution.py:470
  3.5 3.2 %collective-permute-done.2.refs_1_ = bf16[48,16384]{1,0:T(8,128)(2,1)S(1)} collective-permute-done((bf16[48,16384]{1,0:T(8,128)(2,1)}, bf16[48,16384]{1,0:T(8,128)(2,1)S(1)}, u32[]{:S(2)}, u32[]{:S(2)}) %collective-permute-start.2) | collective-permute-done | bytes 1572896 | tf_op jit(solution)/shard_map/ppermute | solution.py:470
  6.7 3.3 %blocks.7.refs_3_ = f32[16,48,1024]{2,1,0:T(8,128)S(1)} custom-call(bf16[48,16384]{1,0:T(8,128)(2,1)} %refs_0_.3, bf16[48,16384]{1,0:T(8,128)(2,1)S(1)} %collective-permute-done.2.refs_1_, bf16[16384,1024]{1,0:T(8,128)(2,1)} %refs_4_.7), custom_call_target="tpu_custom_call" | custom-call | flops 402653184 | bytes 4194304 | tf_op jit(solution)/shard_map/blocks/pallas_call | solution.py:288
  10.0 2.9 %collective-permute-start.6 = (bf16[48,16384]{1,0:T(8,128)(2,1)}, bf16[48,16384]{1,0:T(8,128)(2,1)}, u32[]{:S(2)}, u32[]{:S(2)}) collective-permute-start(bf16[48,16384]{1,0:T(8,128)(2,1)} %refs_0_.3), channel_id=1, source_target_pairs={{0,2},{1,5},{4,0},{5,9},{8,4},{9,13},{12,8},{13,15},{14,12},{15,11... | collective-permute-start | bytes 4718600 | tf_op jit(solution)/shard_map/ppermute | solution.py:470
  12.9 12.0 %blocks.8.refs_4_ = f32[16,48,1024]{2,1,0:T(8,128)S(1)} custom-call(bf16[48,16384]{1,0:T(8,128)(2,1)} %refs_0_.3, bf16[48,16384]{1,0:T(8,128)(2,1)S(1)} %collective-permute-done.2.refs_1_, bf16[16384,1024]{1,0:T(8,128)(2,1)} %refs_4_.7, f32[16,48,1024]{2,1,0:T(8,128)S(1)} %blocks.7.refs_3_), custom_call_target="tpu_custom_call", output_to_operand_aliasing={{}: (3, {})} | custom-call | flops 2818572288 | bytes 29360128 | tf_op jit(solution)/shard_map/blocks/pallas_call | solution.py:288
  26.5 3.4 %some_ranks.4.refs_2_ = f32[48,128]{1,0:T(8,128)S(1)} custom-call(bf16[48,16384]{1,0:T(8,128)(2,1)} %refs_0_.3, bf16[16384,128]{1,0:T(8,128)(2,1)S(1)} %turn.1.s_ref.refs_3_.refs_5_.refs_1_), custom_call_target="tpu_custom_call" | custom-call | tf_op jit(solution)/shard_map/some_ranks/pallas_call | solution.py:365
  30.1 2.4 %collective-permute-start.4 = (bf16[48,16384]{1,0:T(8,128)(2,1)}, bf16[48,16384]{1,0:T(8,128)(2,1)}, u32[]{:S(2)}, u32[]{:S(2)}) collective-permute-start(bf16[48,16384]{1,0:T(8,128)(2,1)} %collective-permute-done.refs_0_), channel_id=1, source_target_pairs={{0,4},{1,3},{4,8},{5,1},{8,12},{9,5},{12,14},{13,9},{14,10},{15,13... | collective-permute-start | bytes 4718600 | tf_op jit(solution)/shard_map/ppermute | solution.py:470
  32.5 10.2 %collective-permute-done.6.refs_0_ = bf16[48,16384]{1,0:T(8,128)(2,1)} collective-permute-done((bf16[48,16384]{1,0:T(8,128)(2,1)}, bf16[48,16384]{1,0:T(8,128)(2,1)}, u32[]{:S(2)}, u32[]{:S(2)}) %collective-permute-start.6) | collective-permute-done | bytes 1572896 | tf_op jit(solution)/shard_map/ppermute | solution.py:470
  42.7 1.7 %collective-permute-start.10 = (bf16[48,16384]{1,0:T(8,128)(2,1)}, bf16[48,16384]{1,0:T(8,128)(2,1)}, u32[]{:S(2)}, u32[]{:S(2)}) collective-permute-start(bf16[48,16384]{1,0:T(8,128)(2,1)} %collective-permute-done.6.refs_0_), channel_id=1, source_target_pairs={{0,2},{1,5},{4,0},{5,9},{8,4},{9,13},{12,8},{13,15},{14,12},{15,11... | collective-permute-start | bytes 4718600 | tf_op jit(solution)/shard_map/ppermute | solution.py:470
  45.6 2.2 %copy-done.3 = bf16[16384,128]{1,0:T(8,128)(2,1)S(1)} copy-done((bf16[16384,128]{1,0:T(8,128)(2,1)S(1)}, bf16[16384,128]{1,0:T(8,128)(2,1)}, u32[]{:S(2)}) %copy-start.3) | copy-done | bytes 4194328
  47.8 13.7 %blocks.9 = (f32[16,48,1024]{2,1,0:T(8,128)S(1)}, f32[48,128]{1,0:T(8,128)S(1)}) custom-call(bf16[48,16384]{1,0:T(8,128)(2,1)} %collective-permute-done.refs_0_, bf16[48,16384]{1,0:T(8,128)(2,1)} %collective-permute-done.3.refs_1_, bf16[16384,1024]{1,0:T(8,128)(2,1)} %refs_4_.7, bf16[16384,128]{1,0:T(8,128)(2,1)S(1)} %copy-done.3, ...), custom_call_target="tpu_custom_call", output_to_operand_aliasing={{0}: (4, {})} | custom-call | flops 3221225472 | bytes 33554432 | tf_op jit(solution)/shard_map/blocks/pallas_call | solution.py:288
  67.5 7.5 %collective-permute-done.10.x_ref.refs_0_ = bf16[48,16384]{1,0:T(8,128)(2,1)} collective-permute-done((bf16[48,16384]{1,0:T(8,128)(2,1)}, bf16[48,16384]{1,0:T(8,128)(2,1)}, u32[]{:S(2)}, u32[]{:S(2)}) %collective-permute-start.10) | collective-permute-done | bytes 1572896 | tf_op jit(solution)/shard_map/ppermute | solution.py:470
  75.8 2.7 %collective-permute-start.11 = (bf16[48,16384]{1,0:T(8,128)(2,1)}, bf16[48,16384]{1,0:T(8,128)(2,1)S(1)}, u32[]{:S(2)}, u32[]{:S(2)}) collective-permute-start(bf16[48,16384]{1,0:T(8,128)(2,1)} %collective-permute-done.10.x_ref.refs_0_), channel_id=1, source_target_pairs={{0,2},{1,5},{4,0},{5,9},{8,4},{9,13},{12,8},{13,15},{14,12},{15,11... | collective-permute-start | bytes 4718600 | tf_op jit(solution)/shard_map/ppermute | solution.py:470
  78.6 2.2 %copy-done.4 = bf16[16384,128]{1,0:T(8,128)(2,1)S(1)} copy-done((bf16[16384,128]{1,0:T(8,128)(2,1)S(1)}, bf16[16384,128]{1,0:T(8,128)(2,1)}, u32[]{:S(2)}) %copy-start.4) | copy-done | bytes 4194328
  80.8 15.0 %blocks.10 = (f32[16,48,1024]{2,1,0:T(8,128)S(1)}, f32[96,128]{1,0:T(8,128)S(1)}) custom-call(bf16[48,16384]{1,0:T(8,128)(2,1)} %collective-permute-done.6.refs_0_, bf16[48,16384]{1,0:T(8,128)(2,1)} %collective-permute-done.7.refs_1_, bf16[48,16384]{1,0:T(8,128)(2,1)} %collective-permute-done.4.refs_2_, ...), custom_call_target="tpu_custom_call", output_to_operand_aliasing={{0}: (6, {})} | custom-call | flops 6442450944 | bytes 33554432 | tf_op jit(solution)/shard_map/blocks/pallas_call | solution.py:288
  95.8 4.7 %keep.1.refs_5_ = bf16[6144,1024]{1,0:T(8,128)(2,1)S(1)} custom-call(bf16[16384,1024]{1,0:T(8,128)(2,1)} %refs_4_.7), custom_call_target="tpu_custom_call" | custom-call | tf_op jit(solution)/shard_map/keep/pallas_call | solution.py:319
  102.1 2.1 %some_ranks.5.refs_5_ = f32[48,128]{1,0:T(8,128)S(1)} custom-call(bf16[48,16384]{1,0:T(8,128)(2,1)} %collective-permute-done.10.x_ref.refs_0_, bf16[16384,128]{1,0:T(8,128)(2,1)S(1)} %copy-done.5), custom_call_target="tpu_custom_call" | custom-call | tf_op jit(solution)/shard_map/some_ranks/pallas_call | solution.py:365
  105.0 2.8 %collective-permute-done.11.x_ref.refs_0_ = bf16[48,16384]{1,0:T(8,128)(2,1)S(1)} collective-permute-done((bf16[48,16384]{1,0:T(8,128)(2,1)}, bf16[48,16384]{1,0:T(8,128)(2,1)S(1)}, u32[]{:S(2)}, u32[]{:S(2)}) %collective-permute-start.11) | collective-permute-done | bytes 1572896 | tf_op jit(solution)/shard_map/ppermute | solution.py:470
  108.9 14.2 %blocks.11.refs_6_ = f32[16,48,1024]{2,1,0:T(8,128)S(1)} custom-call(bf16[48,16384]{1,0:T(8,128)(2,1)} %collective-permute-done.10.x_ref.refs_0_, bf16[48,16384]{1,0:T(8,128)(2,1)S(1)} %collective-permute-done.12.refs_1_, bf16[48,16384]{1,0:T(8,128)(2,1)S(1)} %collective-permute-done.5.x_ref.refs_2_, ...), custom_call_target="tpu_custom_call", output_to_operand_aliasing={{}: (5, {})} | custom-call | flops 6442450944 | bytes 33554432 | tf_op jit(solution)/shard_map/blocks/pallas_call | solution.py:288
  125.4 3.0 %collective-permute-start.16 = (bf16[192,128]{1,0:T(8,128)(2,1)S(1)}, bf16[192,128]{1,0:T(8,128)(2,1)S(1)}, u32[]{:S(2)}, u32[]{:S(2)}) collective-permute-start(bf16[192,128]{1,0:T(8,128)(2,1)S(1)} %ranks.1), channel_id=1, source_target_pairs={{0,6},{1,7},{2,4},{3,5},{4,2},{5,3},{6,0},{7,1},{8,14},{9,15},{10,... | collective-permute-start | bytes 147464 | tf_op jit(solution)/shard_map/ppermute | solution.py:470
  129.4 8.0 %blocks.12.refs_5_ = f32[16,48,1024]{2,1,0:T(8,128)S(1)} custom-call(bf16[48,16384]{1,0:T(8,128)(2,1)S(1)} %collective-permute-done.11.x_ref.refs_0_, bf16[48,16384]{1,0:T(8,128)(2,1)S(1)} %collective-permute-done.17.refs_1_, bf16[48,16384]{1,0:T(8,128)(2,1)S(1)} %collective-permute-done.9.refs_0_.refs_2_, ...), custom_call_target="tpu_custom_call", output_to_operand_aliasing={{}: (6, {})} | custom-call | flops 2013265920 | bytes 10485760 | tf_op jit(solution)/shard_map/blocks/pallas_call | solution.py:288
  137.4 2.7 %collective-permute-start.21 = (bf16[192,128]{1,0:T(8,128)(2,1)S(1)}, bf16[192,128]{1,0:T(8,128)(2,1)S(1)}, u32[]{:S(2)}, u32[]{:S(2)}) collective-permute-start(bf16[192,128]{1,0:T(8,128)(2,1)S(1)} %add_add_fusion), channel_id=1, source_target_pairs={{0,9},{1,8},{2,11},{3,10},{4,13},{5,12},{6,15},{7,14},{8,1},{9,0},... | collective-permute-start | bytes 147464 | tf_op jit(solution)/shard_map/ppermute | solution.py:470
  140.8 5.3 %blocks.13.total_ref = f32[16,48,1024]{2,1,0:T(8,128)S(1)} custom-call(bf16[48,16384]{1,0:T(8,128)(2,1)S(1)} %collective-permute-done.11.x_ref.refs_0_, bf16[48,16384]{1,0:T(8,128)(2,1)S(1)} %collective-permute-done.17.refs_1_, bf16[48,16384]{1,0:T(8,128)(2,1)S(1)} %collective-permute-done.9.refs_0_.refs_2_, ...), custom_call_target="tpu_custom_call", output_to_operand_aliasing={{}: (5, {})} | custom-call | flops 2013265920 | bytes 10485760 | tf_op jit(solution)/shard_map/blocks/pallas_call | solution.py:288
  146.9 2.6 %finish.1 = bf16[768,1024]{1,0:T(8,128)(2,1)} custom-call(s32[16]{0:T(128)S(1)} %get-tuple-element.73.places_ref, s32[6]{0:T(128)S(1)} %gather_fusion, s32[1]{0:T(128)} %bitcast.7.core_ref, f32[16,48,1024]{2,1,0:T(8,128)S(1)} %blocks.13.total_ref, bf16[16,64,1024]{2,1,0:T(8,128)(2,1)S(1)} %bitcast.16, f32[1,1024]{1,0:T(1,128)S(1)} %bitcast.17, ...), custom_call_target="tpu_custom_call" | custom-call | tf_op jit(solution)/shard_map/finish/pallas_call | solution.py:449
  (70 shorter events, 18.2 us)
Async XLA Ops:
  0.0 62.5 %copy-start = (s32[16]{0:T(128)S(1)}, s32[16]{0:T(128)}, u32[]{:S(2)}) copy-start(s32[16]{0:T(128)} %param.16) | copy-start | bytes 196
  0.0 24.9 %collective-permute-start.1 = (bf16[64,16384]{1,0:T(8,128)(2,1)}, bf16[64,16384]{1,0:T(8,128)(2,1)S(1)}, u32[]{:S(2)}, u32[]{:S(2)}) collective-permute-start(bf16[64,16384]{1,0:T(8,128)(2,1)} %bitcast.14), channel_id=1, source_target_pairs={{0,1},{1,0},{2,3},{3,2},{4,5},{5,4},{6,7},{7,6},{8,9},{9,8},{10,11... | collective-permute-start | bytes 6291464 | tf_op jit(solution)/shard_map/ppermute | solution.py:470
  0.5 6.2 %collective-permute-start.2 = (bf16[48,16384]{1,0:T(8,128)(2,1)}, bf16[48,16384]{1,0:T(8,128)(2,1)S(1)}, u32[]{:S(2)}, u32[]{:S(2)}) collective-permute-start(bf16[48,16384]{1,0:T(8,128)(2,1)} %refs_0_.3), channel_id=1, source_target_pairs={{0,1},{1,0},{2,3},{3,2},{4,5},{5,4},{6,7},{7,6},{8,9},{9,8},{10,11... | collective-permute-start | bytes 4718600 | tf_op jit(solution)/shard_map/ppermute | solution.py:470
  0.5 29.6 %collective-permute-start = (bf16[48,16384]{1,0:T(8,128)(2,1)}, bf16[48,16384]{1,0:T(8,128)(2,1)}, u32[]{:S(2)}, u32[]{:S(2)}) collective-permute-start(bf16[48,16384]{1,0:T(8,128)(2,1)} %refs_0_.3), channel_id=1, source_target_pairs={{0,4},{1,3},{4,8},{5,1},{8,12},{9,5},{12,14},{13,9},{14,10},{15,13... | collective-permute-start | bytes 4718600 | tf_op jit(solution)/shard_map/ppermute | solution.py:470
  10.0 32.7 %collective-permute-start.6 = (bf16[48,16384]{1,0:T(8,128)(2,1)}, bf16[48,16384]{1,0:T(8,128)(2,1)}, u32[]{:S(2)}, u32[]{:S(2)}) collective-permute-start(bf16[48,16384]{1,0:T(8,128)(2,1)} %refs_0_.3), channel_id=1, source_target_pairs={{0,2},{1,5},{4,0},{5,9},{8,4},{9,13},{12,8},{13,15},{14,12},{15,11... | collective-permute-start | bytes 4718600 | tf_op jit(solution)/shard_map/ppermute | solution.py:470
  30.1 15.5 %collective-permute-start.3 = (bf16[48,16384]{1,0:T(8,128)(2,1)}, bf16[48,16384]{1,0:T(8,128)(2,1)}, u32[]{:S(2)}, u32[]{:S(2)}) collective-permute-start(bf16[48,16384]{1,0:T(8,128)(2,1)} %collective-permute-done.refs_0_), channel_id=1, source_target_pairs={{0,1},{1,0},{2,3},{3,2},{4,5},{5,4},{6,7},{7,6},{8,9},{9,8},{10,11... | collective-permute-start | bytes 4718600 | tf_op jit(solution)/shard_map/ppermute | solution.py:470
  30.1 32.2 %copy-start.9 = (s32[8]{0:T(128)S(1)}, s32[8]{0:T(128)}, u32[]{:S(2)}) copy-start(s32[8]{0:T(128)} %param.17) | copy-start | bytes 100
  30.1 35.7 %collective-permute-start.4 = (bf16[48,16384]{1,0:T(8,128)(2,1)}, bf16[48,16384]{1,0:T(8,128)(2,1)}, u32[]{:S(2)}, u32[]{:S(2)}) collective-permute-start(bf16[48,16384]{1,0:T(8,128)(2,1)} %collective-permute-done.refs_0_), channel_id=1, source_target_pairs={{0,4},{1,3},{4,8},{5,1},{8,12},{9,5},{12,14},{13,9},{14,10},{15,13... | collective-permute-start | bytes 4718600 | tf_op jit(solution)/shard_map/ppermute | solution.py:470
  42.7 32.3 %collective-permute-start.10 = (bf16[48,16384]{1,0:T(8,128)(2,1)}, bf16[48,16384]{1,0:T(8,128)(2,1)}, u32[]{:S(2)}, u32[]{:S(2)}) collective-permute-start(bf16[48,16384]{1,0:T(8,128)(2,1)} %collective-permute-done.6.refs_0_), channel_id=1, source_target_pairs={{0,2},{1,5},{4,0},{5,9},{8,4},{9,13},{12,8},{13,15},{14,12},{15,11... | collective-permute-start | bytes 4718600 | tf_op jit(solution)/shard_map/ppermute | solution.py:470
  44.4 34.2 %collective-permute-start.7 = (bf16[48,16384]{1,0:T(8,128)(2,1)}, bf16[48,16384]{1,0:T(8,128)(2,1)}, u32[]{:S(2)}, u32[]{:S(2)}) collective-permute-start(bf16[48,16384]{1,0:T(8,128)(2,1)} %collective-permute-done.6.refs_0_), channel_id=1, source_target_pairs={{0,1},{1,0},{2,3},{3,2},{4,5},{5,4},{6,7},{7,6},{8,9},{9,8},{10,11... | collective-permute-start | bytes 4718600 | tf_op jit(solution)/shard_map/ppermute | solution.py:470
  65.8 12.8 %collective-permute-start.8 = (bf16[48,16384]{1,0:T(8,128)(2,1)}, bf16[48,16384]{1,0:T(8,128)(2,1)S(1)}, u32[]{:S(2)}, u32[]{:S(2)}) collective-permute-start(bf16[48,16384]{1,0:T(8,128)(2,1)} %collective-permute-done.4.refs_2_), channel_id=1, source_target_pairs={{0,1},{1,0},{2,3},{3,2},{4,5},{5,4},{6,7},{7,6},{8,9},{9,8},{10,11... | collective-permute-start | bytes 4718600 | tf_op jit(solution)/shard_map/ppermute | solution.py:470
  65.9 34.7 %collective-permute-start.5 = (bf16[48,16384]{1,0:T(8,128)(2,1)}, bf16[48,16384]{1,0:T(8,128)(2,1)S(1)}, u32[]{:S(2)}, u32[]{:S(2)}) collective-permute-start(bf16[48,16384]{1,0:T(8,128)(2,1)} %collective-permute-done.4.refs_2_), channel_id=1, source_target_pairs={{0,4},{1,3},{4,8},{5,1},{8,12},{9,5},{12,14},{13,9},{14,10},{15,13... | collective-permute-start | bytes 4718600 | tf_op jit(solution)/shard_map/ppermute | solution.py:470
  75.0 33.9 %collective-permute-start.12 = (bf16[48,16384]{1,0:T(8,128)(2,1)}, bf16[48,16384]{1,0:T(8,128)(2,1)S(1)}, u32[]{:S(2)}, u32[]{:S(2)}) collective-permute-start(bf16[48,16384]{1,0:T(8,128)(2,1)} %collective-permute-done.10.x_ref.refs_0_), channel_id=1, source_target_pairs={{0,1},{1,0},{2,3},{3,2},{4,5},{5,4},{6,7},{7,6},{8,9},{9,8},{10,11... | collective-permute-start | bytes 4718600 | tf_op jit(solution)/shard_map/ppermute | solution.py:470
  75.8 31.9 %collective-permute-start.11 = (bf16[48,16384]{1,0:T(8,128)(2,1)}, bf16[48,16384]{1,0:T(8,128)(2,1)S(1)}, u32[]{:S(2)}, u32[]{:S(2)}) collective-permute-start(bf16[48,16384]{1,0:T(8,128)(2,1)} %collective-permute-done.10.x_ref.refs_0_), channel_id=1, source_target_pairs={{0,2},{1,5},{4,0},{5,9},{8,4},{9,13},{12,8},{13,15},{14,12},{15,11... | collective-permute-start | bytes 4718600 | tf_op jit(solution)/shard_map/ppermute | solution.py:470
  100.6 8.3 %collective-permute-start.13 = (bf16[48,16384]{1,0:T(8,128)(2,1)S(1)}, bf16[48,16384]{1,0:T(8,128)(2,1)S(1)}, u32[]{:S(2)}, u32[]{:S(2)}) collective-permute-start(bf16[48,16384]{1,0:T(8,128)(2,1)S(1)} %collective-permute-done.5.x_ref.refs_2_), channel_id=1, source_target_pairs={{0,1},{1,0},{2,3},{3,2},{4,5},{5,4},{6,7},{7,6},{8,9},{9,8},{10,11... | collective-permute-start | bytes 4718600 | tf_op jit(solution)/shard_map/ppermute | solution.py:470
  100.7 23.2 %collective-permute-start.9 = (bf16[48,16384]{1,0:T(8,128)(2,1)S(1)}, bf16[48,16384]{1,0:T(8,128)(2,1)S(1)}, u32[]{:S(2)}, u32[]{:S(2)}) collective-permute-start(bf16[48,16384]{1,0:T(8,128)(2,1)S(1)} %collective-permute-done.5.x_ref.refs_2_), channel_id=1, source_target_pairs={{0,4},{1,3},{4,8},{5,1},{8,12},{9,5},{12,14},{13,9},{14,10},{15,13... | collective-permute-start | bytes 4718600 | tf_op jit(solution)/shard_map/ppermute | solution.py:470
  107.7 21.6 %collective-permute-start.17 = (bf16[48,16384]{1,0:T(8,128)(2,1)S(1)}, bf16[48,16384]{1,0:T(8,128)(2,1)S(1)}, u32[]{:S(2)}, u32[]{:S(2)}) collective-permute-start(bf16[48,16384]{1,0:T(8,128)(2,1)S(1)} %collective-permute-done.11.x_ref.refs_0_), channel_id=1, source_target_pairs={{0,1},{1,0},{2,3},{3,2},{4,5},{5,4},{6,7},{7,6},{8,9},{9,8},{10,11... | collective-permute-start | bytes 4718600 | tf_op jit(solution)/shard_map/ppermute | solution.py:470
  123.9 5.5 %collective-permute-start.18 = (bf16[48,16384]{1,0:T(8,128)(2,1)S(1)}, bf16[48,16384]{1,0:T(8,128)(2,1)S(1)}, u32[]{:S(2)}, u32[]{:S(2)}) collective-permute-start(bf16[48,16384]{1,0:T(8,128)(2,1)S(1)} %collective-permute-done.9.refs_0_.refs_2_), channel_id=1, source_target_pairs={{0,1},{1,0},{2,3},{3,2},{4,5},{5,4},{6,7},{7,6},{8,9},{9,8},{10,11... | collective-permute-start | bytes 4718600 | tf_op jit(solution)/shard_map/ppermute | solution.py:470
  125.4 11.9 %collective-permute-start.16 = (bf16[192,128]{1,0:T(8,128)(2,1)S(1)}, bf16[192,128]{1,0:T(8,128)(2,1)S(1)}, u32[]{:S(2)}, u32[]{:S(2)}) collective-permute-start(bf16[192,128]{1,0:T(8,128)(2,1)S(1)} %ranks.1), channel_id=1, source_target_pairs={{0,6},{1,7},{2,4},{3,5},{4,2},{5,3},{6,0},{7,1},{8,14},{9,15},{10,... | collective-permute-start | bytes 147464 | tf_op jit(solution)/shard_map/ppermute | solution.py:470
  128.4 8.9 %collective-permute-start.15 = (bf16[192,128]{1,0:T(8,128)(2,1)S(1)}, bf16[192,128]{1,0:T(8,128)(2,1)S(1)}, u32[]{:S(2)}, u32[]{:S(2)}) collective-permute-start(bf16[192,128]{1,0:T(8,128)(2,1)S(1)} %ranks.1), channel_id=1, source_target_pairs={{0,4},{1,5},{2,6},{3,7},{4,0},{5,1},{6,2},{7,3},{8,12},{9,13},{10,... | collective-permute-start | bytes 147464 | tf_op jit(solution)/shard_map/ppermute | solution.py:470
  128.9 8.5 %collective-permute-start.14 = (bf16[192,128]{1,0:T(8,128)(2,1)S(1)}, bf16[192,128]{1,0:T(8,128)(2,1)S(1)}, u32[]{:S(2)}, u32[]{:S(2)}) collective-permute-start(bf16[192,128]{1,0:T(8,128)(2,1)S(1)} %ranks.1), channel_id=1, source_target_pairs={{0,2},{1,3},{2,0},{3,1},{4,6},{5,7},{6,4},{7,5},{8,10},{9,11},{10,... | collective-permute-start | bytes 147464 | tf_op jit(solution)/shard_map/ppermute | solution.py:470
  137.4 8.6 %collective-permute-start.21 = (bf16[192,128]{1,0:T(8,128)(2,1)S(1)}, bf16[192,128]{1,0:T(8,128)(2,1)S(1)}, u32[]{:S(2)}, u32[]{:S(2)}) collective-permute-start(bf16[192,128]{1,0:T(8,128)(2,1)S(1)} %add_add_fusion), channel_id=1, source_target_pairs={{0,9},{1,8},{2,11},{3,10},{4,13},{5,12},{6,15},{7,14},{8,1},{9,0},... | collective-permute-start | bytes 147464 | tf_op jit(solution)/shard_map/ppermute | solution.py:470
  140.2 5.9 %collective-permute-start.20 = (bf16[192,128]{1,0:T(8,128)(2,1)S(1)}, bf16[192,128]{1,0:T(8,128)(2,1)S(1)}, u32[]{:S(2)}, u32[]{:S(2)}) collective-permute-start(bf16[192,128]{1,0:T(8,128)(2,1)S(1)} %add_add_fusion), channel_id=1, source_target_pairs={{0,1},{1,0},{2,3},{3,2},{4,5},{5,4},{6,7},{7,6},{8,9},{9,8},{10,11... | collective-permute-start | bytes 147464 | tf_op jit(solution)/shard_map/ppermute | solution.py:470
  140.8 6.0 %collective-permute-start.19 = (bf16[192,128]{1,0:T(8,128)(2,1)S(1)}, bf16[192,128]{1,0:T(8,128)(2,1)S(1)}, u32[]{:S(2)}, u32[]{:S(2)}) collective-permute-start(bf16[192,128]{1,0:T(8,128)(2,1)S(1)} %add_add_fusion), channel_id=1, source_target_pairs={{0,8},{1,9},{2,10},{3,11},{4,12},{5,13},{6,14},{7,15},{8,0},{9,1},... | collective-permute-start | bytes 147464 | tf_op jit(solution)/shard_map/ppermute | solution.py:470
  (8 other events, 47.1 us)

commit v20 on v19

--- a/solution.py
+++ b/solution.py
@@ -214,9 +214,9 @@
         for copy in copies(step):
             copy.start()
 
-    for index in range(min(SLOTS, steps - kept)):
-        weights(jnp.int32(index)).start()
     for step in range(min(SLOTS, steps)):
+        if step < steps - kept:
+            weights(jnp.int32(step)).start()
         start(jnp.int32(step))
     if fresh:
         total[here] = jnp.zeros((count,) + total.shape[1:], F32)
@@ -248,14 +248,14 @@
     @pl.loop(kept, steps)
     def _(step):
         index = step - kept
-        for copy in copies(step) + [weights(index)]:
+        for copy in [weights(index)] + copies(step):
             copy.wait()
         take(step, lambda cut: w_slots[lax.rem(index, SLOTS), :, cut])
 
         @pl.when(step + SLOTS < steps)
         def _():
+            weights(index + SLOTS).start()
             start(step + SLOTS)
-            weights(index + SLOTS).start()
 
 
 def block_product(xs, weights, factors, low, high, tile, total, base, ranked, fresh=None, kept=None):

time: 150 us -> 149 us (level)
  Pallas kernels: 88.8 us -> 82.3 us
  waiting for transfers between devices: 24.5 us -> 29.4 us
    pallas_call x7, Pallas kernels: 71.6 us -> 65 us  [block_product(): pl.pallas_call(functools.partial(block_kernel, count, low, tile, steps, k...]
    ppermute x22, waiting for transfers between devices: 24.5 us -> 29.4 us  [ring_plan(): send = lambda value, pairs: lax.ppermute(value, 'tensor', pairs)]
  transfers between devices with their start and end apart: 22 -> 22, of which waited for: 6 -> 9; matrix products, arithmetic and copies ran while one was open for 3% -> 3% of each run, Pallas kernels for 58% -> 54%
where the time goes in v20:
time: 149 us; the launch traced here: 148 us
  Pallas kernels  82.3 us (55%)
  waiting for transfers between devices  29.4 us (20%)
  starting transfers between devices  27.5 us (18%)
  local copies, waits for them, and re-layouts  6.55 us (4%)
  other arithmetic  2.13 us (1%)
    pallas_call x7, Pallas kernels, block_product(): pl.pallas_call(functools.partial(block_kernel, count, low, tile, steps, k...  65 us
    ppermute x22, waiting for transfers between devices, ring_plan(): send = lambda value, pairs: lax.ppermute(value, 'tensor', pairs)  29.4 us
    ppermute x22, starting transfers between devices, ring_plan(): send = lambda value, pairs: lax.ppermute(value, 'tensor', pairs)  27.5 us
    pallas_call x4, Pallas kernels, some_ranks(): pl.pallas_call(some_ranks_kernel, in_specs=[whole] * 2, out_specs=whole,...  6.98 us
    pallas_call x1, Pallas kernels, keep_weights(): pl.pallas_call(functools.partial(keep_kernel, low), in_specs=[pl.BlockSpe...  4.74 us
    unnamed x20, local copies, waits for them, and re-layouts  4.41 us
  transfers between devices with their start and end apart: 22, of which 9 were waited for; matrix products, arithmetic and copies ran while one was open for 3% of the time, Pallas kernels for 54%

profile of v20, /device:TPU:0, one launch (start us, length us, event | category | flops | bytes accessed | tf_op | source)
XLA Modules:
  0.0 148.4 jit_solution(12792767818155823711)
XLA Ops:
  0.5 3.0 %collective-permute-start = (bf16[48,16384]{1,0:T(8,128)(2,1)}, bf16[48,16384]{1,0:T(8,128)(2,1)}, u32[]{:S(2)}, u32[]{:S(2)}) collective-permute-start(bf16[48,16384]{1,0:T(8,128)(2,1)} %refs_0_.3), channel_id=1, source_target_pairs={{0,4},{1,3},{4,8},{5,1},{8,12},{9,5},{12,14},{13,9},{14,10},{15,13... | collective-permute-start | bytes 4718600 | tf_op jit(solution)/shard_map/ppermute | solution.py:470
  3.5 3.2 %collective-permute-done.2.refs_1_ = bf16[48,16384]{1,0:T(8,128)(2,1)S(1)} collective-permute-done((bf16[48,16384]{1,0:T(8,128)(2,1)}, bf16[48,16384]{1,0:T(8,128)(2,1)S(1)}, u32[]{:S(2)}, u32[]{:S(2)}) %collective-permute-start.2) | collective-permute-done | bytes 1572896 | tf_op jit(solution)/shard_map/ppermute | solution.py:470
  6.7 2.9 %blocks.7.refs_3_ = f32[16,48,1024]{2,1,0:T(8,128)S(1)} custom-call(bf16[48,16384]{1,0:T(8,128)(2,1)} %refs_0_.3, bf16[48,16384]{1,0:T(8,128)(2,1)S(1)} %collective-permute-done.2.refs_1_, bf16[16384,1024]{1,0:T(8,128)(2,1)} %refs_4_.7), custom_call_target="tpu_custom_call" | custom-call | flops 402653184 | bytes 4194304 | tf_op jit(solution)/shard_map/blocks/pallas_call | solution.py:288
  9.6 2.9 %collective-permute-start.6 = (bf16[48,16384]{1,0:T(8,128)(2,1)}, bf16[48,16384]{1,0:T(8,128)(2,1)}, u32[]{:S(2)}, u32[]{:S(2)}) collective-permute-start(bf16[48,16384]{1,0:T(8,128)(2,1)} %refs_0_.3), channel_id=1, source_target_pairs={{0,2},{1,5},{4,0},{5,9},{8,4},{9,13},{12,8},{13,15},{14,12},{15,11... | collective-permute-start | bytes 4718600 | tf_op jit(solution)/shard_map/ppermute | solution.py:470
  12.5 10.7 %blocks.8.refs_4_ = f32[16,48,1024]{2,1,0:T(8,128)S(1)} custom-call(bf16[48,16384]{1,0:T(8,128)(2,1)} %refs_0_.3, bf16[48,16384]{1,0:T(8,128)(2,1)S(1)} %collective-permute-done.2.refs_1_, bf16[16384,1024]{1,0:T(8,128)(2,1)} %refs_4_.7, f32[16,48,1024]{2,1,0:T(8,128)S(1)} %blocks.7.refs_3_), custom_call_target="tpu_custom_call", output_to_operand_aliasing={{}: (3, {})} | custom-call | flops 2818572288 | bytes 29360128 | tf_op jit(solution)/shard_map/blocks/pallas_call | solution.py:288
  24.8 3.4 %some_ranks.4.refs_2_ = f32[48,128]{1,0:T(8,128)S(1)} custom-call(bf16[48,16384]{1,0:T(8,128)(2,1)} %refs_0_.3, bf16[16384,128]{1,0:T(8,128)(2,1)S(1)} %turn.1.s_ref.refs_3_.refs_5_.refs_1_), custom_call_target="tpu_custom_call" | custom-call | tf_op jit(solution)/shard_map/some_ranks/pallas_call | solution.py:365
  28.2 2.3 %collective-permute-done.refs_0_ = bf16[48,16384]{1,0:T(8,128)(2,1)} collective-permute-done((bf16[48,16384]{1,0:T(8,128)(2,1)}, bf16[48,16384]{1,0:T(8,128)(2,1)}, u32[]{:S(2)}, u32[]{:S(2)}) %collective-permute-start) | collective-permute-done | bytes 1572896 | tf_op jit(solution)/shard_map/ppermute | solution.py:470
  30.5 2.4 %collective-permute-start.4 = (bf16[48,16384]{1,0:T(8,128)(2,1)}, bf16[48,16384]{1,0:T(8,128)(2,1)}, u32[]{:S(2)}, u32[]{:S(2)}) collective-permute-start(bf16[48,16384]{1,0:T(8,128)(2,1)} %collective-permute-done.refs_0_), channel_id=1, source_target_pairs={{0,4},{1,3},{4,8},{5,1},{8,12},{9,5},{12,14},{13,9},{14,10},{15,13... | collective-permute-start | bytes 4718600 | tf_op jit(solution)/shard_map/ppermute | solution.py:470
  32.9 9.4 %collective-permute-done.6.refs_0_ = bf16[48,16384]{1,0:T(8,128)(2,1)} collective-permute-done((bf16[48,16384]{1,0:T(8,128)(2,1)}, bf16[48,16384]{1,0:T(8,128)(2,1)}, u32[]{:S(2)}, u32[]{:S(2)}) %collective-permute-start.6) | collective-permute-done | bytes 1572896 | tf_op jit(solution)/shard_map/ppermute | solution.py:470
  45.2 2.2 %copy-done.3 = bf16[16384,128]{1,0:T(8,128)(2,1)S(1)} copy-done((bf16[16384,128]{1,0:T(8,128)(2,1)S(1)}, bf16[16384,128]{1,0:T(8,128)(2,1)}, u32[]{:S(2)}) %copy-start.3) | copy-done | bytes 4194328
  47.4 12.4 %blocks.9 = (f32[16,48,1024]{2,1,0:T(8,128)S(1)}, f32[48,128]{1,0:T(8,128)S(1)}) custom-call(bf16[48,16384]{1,0:T(8,128)(2,1)} %collective-permute-done.refs_0_, bf16[48,16384]{1,0:T(8,128)(2,1)} %collective-permute-done.3.refs_1_, bf16[16384,1024]{1,0:T(8,128)(2,1)} %refs_4_.7, bf16[16384,128]{1,0:T(8,128)(2,1)S(1)} %copy-done.3, ...), custom_call_target="tpu_custom_call", output_to_operand_aliasing={{0}: (4, {})} | custom-call | flops 3221225472 | bytes 33554432 | tf_op jit(solution)/shard_map/blocks/pallas_call | solution.py:288
  65.1 2.4 %collective-permute-start.5 = (bf16[48,16384]{1,0:T(8,128)(2,1)}, bf16[48,16384]{1,0:T(8,128)(2,1)S(1)}, u32[]{:S(2)}, u32[]{:S(2)}) collective-permute-start(bf16[48,16384]{1,0:T(8,128)(2,1)} %collective-permute-done.4.refs_2_), channel_id=1, source_target_pairs={{0,4},{1,3},{4,8},{5,1},{8,12},{9,5},{12,14},{13,9},{14,10},{15,13... | collective-permute-start | bytes 4718600 | tf_op jit(solution)/shard_map/ppermute | solution.py:470
  67.5 7.7 %collective-permute-done.10.x_ref.refs_0_ = bf16[48,16384]{1,0:T(8,128)(2,1)} collective-permute-done((bf16[48,16384]{1,0:T(8,128)(2,1)}, bf16[48,16384]{1,0:T(8,128)(2,1)}, u32[]{:S(2)}, u32[]{:S(2)}) %collective-permute-start.10) | collective-permute-done | bytes 1572896 | tf_op jit(solution)/shard_map/ppermute | solution.py:470
  78.2 2.2 %copy-done.4 = bf16[16384,128]{1,0:T(8,128)(2,1)S(1)} copy-done((bf16[16384,128]{1,0:T(8,128)(2,1)S(1)}, bf16[16384,128]{1,0:T(8,128)(2,1)}, u32[]{:S(2)}) %copy-start.4) | copy-done | bytes 4194328
  80.4 13.3 %blocks.10 = (f32[16,48,1024]{2,1,0:T(8,128)S(1)}, f32[96,128]{1,0:T(8,128)S(1)}) custom-call(bf16[48,16384]{1,0:T(8,128)(2,1)} %collective-permute-done.6.refs_0_, bf16[48,16384]{1,0:T(8,128)(2,1)} %collective-permute-done.7.refs_1_, bf16[48,16384]{1,0:T(8,128)(2,1)} %collective-permute-done.4.refs_2_, ...), custom_call_target="tpu_custom_call", output_to_operand_aliasing={{0}: (6, {})} | custom-call | flops 6442450944 | bytes 33554432 | tf_op jit(solution)/shard_map/blocks/pallas_call | solution.py:288
  93.7 4.7 %keep.1.refs_5_ = bf16[6144,1024]{1,0:T(8,128)(2,1)S(1)} custom-call(bf16[16384,1024]{1,0:T(8,128)(2,1)} %refs_4_.7), custom_call_target="tpu_custom_call" | custom-call | tf_op jit(solution)/shard_map/keep/pallas_call | solution.py:319
  99.7 2.4 %collective-permute-start.9 = (bf16[48,16384]{1,0:T(8,128)(2,1)S(1)}, bf16[48,16384]{1,0:T(8,128)(2,1)S(1)}, u32[]{:S(2)}, u32[]{:S(2)}) collective-permute-start(bf16[48,16384]{1,0:T(8,128)(2,1)S(1)} %collective-permute-done.5.x_ref.refs_2_), channel_id=1, source_target_pairs={{0,4},{1,3},{4,8},{5,1},{8,12},{9,5},{12,14},{13,9},{14,10},{15,13... | collective-permute-start | bytes 4718600 | tf_op jit(solution)/shard_map/ppermute | solution.py:470
  104.9 3.2 %collective-permute-done.11.x_ref.refs_0_ = bf16[48,16384]{1,0:T(8,128)(2,1)S(1)} collective-permute-done((bf16[48,16384]{1,0:T(8,128)(2,1)}, bf16[48,16384]{1,0:T(8,128)(2,1)S(1)}, u32[]{:S(2)}, u32[]{:S(2)}) %collective-permute-start.11) | collective-permute-done | bytes 1572896 | tf_op jit(solution)/shard_map/ppermute | solution.py:470
  109.2 12.5 %blocks.11.refs_6_ = f32[16,48,1024]{2,1,0:T(8,128)S(1)} custom-call(bf16[48,16384]{1,0:T(8,128)(2,1)} %collective-permute-done.10.x_ref.refs_0_, bf16[48,16384]{1,0:T(8,128)(2,1)S(1)} %collective-permute-done.12.refs_1_, bf16[48,16384]{1,0:T(8,128)(2,1)S(1)} %collective-permute-done.5.x_ref.refs_2_, ...), custom_call_target="tpu_custom_call", output_to_operand_aliasing={{}: (5, {})} | custom-call | flops 6442450944 | bytes 33554432 | tf_op jit(solution)/shard_map/blocks/pallas_call | solution.py:288
  124.7 3.1 %collective-permute-start.16 = (bf16[192,128]{1,0:T(8,128)(2,1)S(1)}, bf16[192,128]{1,0:T(8,128)(2,1)S(1)}, u32[]{:S(2)}, u32[]{:S(2)}) collective-permute-start(bf16[192,128]{1,0:T(8,128)(2,1)S(1)} %ranks.1), channel_id=1, source_target_pairs={{0,6},{1,7},{2,4},{3,5},{4,2},{5,3},{6,0},{7,1},{8,14},{9,15},{10,... | collective-permute-start | bytes 147464 | tf_op jit(solution)/shard_map/ppermute | solution.py:470
  128.4 8.0 %blocks.12.refs_5_ = f32[16,48,1024]{2,1,0:T(8,128)S(1)} custom-call(bf16[48,16384]{1,0:T(8,128)(2,1)S(1)} %collective-permute-done.11.x_ref.refs_0_, bf16[48,16384]{1,0:T(8,128)(2,1)S(1)} %collective-permute-done.17.refs_1_, bf16[48,16384]{1,0:T(8,128)(2,1)S(1)} %collective-permute-done.9.refs_0_.refs_2_, ...), custom_call_target="tpu_custom_call", output_to_operand_aliasing={{}: (6, {})} | custom-call | flops 2013265920 | bytes 10485760 | tf_op jit(solution)/shard_map/blocks/pallas_call | solution.py:288
  136.5 2.2 %collective-permute-start.21 = (bf16[192,128]{1,0:T(8,128)(2,1)S(1)}, bf16[192,128]{1,0:T(8,128)(2,1)S(1)}, u32[]{:S(2)}, u32[]{:S(2)}) collective-permute-start(bf16[192,128]{1,0:T(8,128)(2,1)S(1)} %add_add_fusion), channel_id=1, source_target_pairs={{0,9},{1,8},{2,11},{3,10},{4,13},{5,12},{6,15},{7,14},{8,1},{9,0},... | collective-permute-start | bytes 147464 | tf_op jit(solution)/shard_map/ppermute | solution.py:470
  139.6 5.3 %blocks.13.total_ref = f32[16,48,1024]{2,1,0:T(8,128)S(1)} custom-call(bf16[48,16384]{1,0:T(8,128)(2,1)S(1)} %collective-permute-done.11.x_ref.refs_0_, bf16[48,16384]{1,0:T(8,128)(2,1)S(1)} %collective-permute-done.17.refs_1_, bf16[48,16384]{1,0:T(8,128)(2,1)S(1)} %collective-permute-done.9.refs_0_.refs_2_, ...), custom_call_target="tpu_custom_call", output_to_operand_aliasing={{}: (5, {})} | custom-call | flops 2013265920 | bytes 10485760 | tf_op jit(solution)/shard_map/blocks/pallas_call | solution.py:288
  145.7 2.6 %finish.1 = bf16[768,1024]{1,0:T(8,128)(2,1)} custom-call(s32[16]{0:T(128)S(1)} %get-tuple-element.73.places_ref, s32[6]{0:T(128)S(1)} %gather_fusion, s32[1]{0:T(128)} %bitcast.7.core_ref, f32[16,48,1024]{2,1,0:T(8,128)S(1)} %blocks.13.total_ref, bf16[16,64,1024]{2,1,0:T(8,128)(2,1)S(1)} %bitcast.16, f32[1,1024]{1,0:T(1,128)S(1)} %bitcast.17, ...), custom_call_target="tpu_custom_call" | custom-call | tf_op jit(solution)/shard_map/finish/pallas_call | solution.py:449
  (70 shorter events, 23.7 us)
Async XLA Ops:
  0.0 60.8 %copy-start = (s32[16]{0:T(128)S(1)}, s32[16]{0:T(128)}, u32[]{:S(2)}) copy-start(s32[16]{0:T(128)} %param.16) | copy-start | bytes 196
  0.0 23.2 %collective-permute-start.1 = (bf16[64,16384]{1,0:T(8,128)(2,1)}, bf16[64,16384]{1,0:T(8,128)(2,1)S(1)}, u32[]{:S(2)}, u32[]{:S(2)}) collective-permute-start(bf16[64,16384]{1,0:T(8,128)(2,1)} %bitcast.14), channel_id=1, source_target_pairs={{0,1},{1,0},{2,3},{3,2},{4,5},{5,4},{6,7},{7,6},{8,9},{9,8},{10,11... | collective-permute-start | bytes 6291464 | tf_op jit(solution)/shard_map/ppermute | solution.py:470
  0.5 6.2 %collective-permute-start.2 = (bf16[48,16384]{1,0:T(8,128)(2,1)}, bf16[48,16384]{1,0:T(8,128)(2,1)S(1)}, u32[]{:S(2)}, u32[]{:S(2)}) collective-permute-start(bf16[48,16384]{1,0:T(8,128)(2,1)} %refs_0_.3), channel_id=1, source_target_pairs={{0,1},{1,0},{2,3},{3,2},{4,5},{5,4},{6,7},{7,6},{8,9},{9,8},{10,11... | collective-permute-start | bytes 4718600 | tf_op jit(solution)/shard_map/ppermute | solution.py:470
  0.5 29.9 %collective-permute-start = (bf16[48,16384]{1,0:T(8,128)(2,1)}, bf16[48,16384]{1,0:T(8,128)(2,1)}, u32[]{:S(2)}, u32[]{:S(2)}) collective-permute-start(bf16[48,16384]{1,0:T(8,128)(2,1)} %refs_0_.3), channel_id=1, source_target_pairs={{0,4},{1,3},{4,8},{5,1},{8,12},{9,5},{12,14},{13,9},{14,10},{15,13... | collective-permute-start | bytes 4718600 | tf_op jit(solution)/shard_map/ppermute | solution.py:470
  9.6 32.7 %collective-permute-start.6 = (bf16[48,16384]{1,0:T(8,128)(2,1)}, bf16[48,16384]{1,0:T(8,128)(2,1)}, u32[]{:S(2)}, u32[]{:S(2)}) collective-permute-start(bf16[48,16384]{1,0:T(8,128)(2,1)} %refs_0_.3), channel_id=1, source_target_pairs={{0,2},{1,5},{4,0},{5,9},{8,4},{9,13},{12,8},{13,15},{14,12},{15,11... | collective-permute-start | bytes 4718600 | tf_op jit(solution)/shard_map/ppermute | solution.py:470
  30.5 14.8 %collective-permute-start.3 = (bf16[48,16384]{1,0:T(8,128)(2,1)}, bf16[48,16384]{1,0:T(8,128)(2,1)}, u32[]{:S(2)}, u32[]{:S(2)}) collective-permute-start(bf16[48,16384]{1,0:T(8,128)(2,1)} %collective-permute-done.refs_0_), channel_id=1, source_target_pairs={{0,1},{1,0},{2,3},{3,2},{4,5},{5,4},{6,7},{7,6},{8,9},{9,8},{10,11... | collective-permute-start | bytes 4718600 | tf_op jit(solution)/shard_map/ppermute | solution.py:470
  30.5 30.1 %copy-start.9 = (s32[8]{0:T(128)S(1)}, s32[8]{0:T(128)}, u32[]{:S(2)}) copy-start(s32[8]{0:T(128)} %param.17) | copy-start | bytes 100
  30.5 34.6 %collective-permute-start.4 = (bf16[48,16384]{1,0:T(8,128)(2,1)}, bf16[48,16384]{1,0:T(8,128)(2,1)}, u32[]{:S(2)}, u32[]{:S(2)}) collective-permute-start(bf16[48,16384]{1,0:T(8,128)(2,1)} %collective-permute-done.refs_0_), channel_id=1, source_target_pairs={{0,4},{1,3},{4,8},{5,1},{8,12},{9,5},{12,14},{13,9},{14,10},{15,13... | collective-permute-start | bytes 4718600 | tf_op jit(solution)/shard_map/ppermute | solution.py:470
  42.3 32.8 %collective-permute-start.10 = (bf16[48,16384]{1,0:T(8,128)(2,1)}, bf16[48,16384]{1,0:T(8,128)(2,1)}, u32[]{:S(2)}, u32[]{:S(2)}) collective-permute-start(bf16[48,16384]{1,0:T(8,128)(2,1)} %collective-permute-done.6.refs_0_), channel_id=1, source_target_pairs={{0,2},{1,5},{4,0},{5,9},{8,4},{9,13},{12,8},{13,15},{14,12},{15,11... | collective-permute-start | bytes 4718600 | tf_op jit(solution)/shard_map/ppermute | solution.py:470
  44.0 34.2 %collective-permute-start.7 = (bf16[48,16384]{1,0:T(8,128)(2,1)}, bf16[48,16384]{1,0:T(8,128)(2,1)}, u32[]{:S(2)}, u32[]{:S(2)}) collective-permute-start(bf16[48,16384]{1,0:T(8,128)(2,1)} %collective-permute-done.6.refs_0_), channel_id=1, source_target_pairs={{0,1},{1,0},{2,3},{3,2},{4,5},{5,4},{6,7},{7,6},{8,9},{9,8},{10,11... | collective-permute-start | bytes 4718600 | tf_op jit(solution)/shard_map/ppermute | solution.py:470
  65.1 13.1 %collective-permute-start.8 = (bf16[48,16384]{1,0:T(8,128)(2,1)}, bf16[48,16384]{1,0:T(8,128)(2,1)S(1)}, u32[]{:S(2)}, u32[]{:S(2)}) collective-permute-start(bf16[48,16384]{1,0:T(8,128)(2,1)} %collective-permute-done.4.refs_2_), channel_id=1, source_target_pairs={{0,1},{1,0},{2,3},{3,2},{4,5},{5,4},{6,7},{7,6},{8,9},{9,8},{10,11... | collective-permute-start | bytes 4718600 | tf_op jit(solution)/shard_map/ppermute | solution.py:470
  65.1 34.6 %collective-permute-start.5 = (bf16[48,16384]{1,0:T(8,128)(2,1)}, bf16[48,16384]{1,0:T(8,128)(2,1)S(1)}, u32[]{:S(2)}, u32[]{:S(2)}) collective-permute-start(bf16[48,16384]{1,0:T(8,128)(2,1)} %collective-permute-done.4.refs_2_), channel_id=1, source_target_pairs={{0,4},{1,3},{4,8},{5,1},{8,12},{9,5},{12,14},{13,9},{14,10},{15,13... | collective-permute-start | bytes 4718600 | tf_op jit(solution)/shard_map/ppermute | solution.py:470
  75.2 34.1 %collective-permute-start.12 = (bf16[48,16384]{1,0:T(8,128)(2,1)}, bf16[48,16384]{1,0:T(8,128)(2,1)S(1)}, u32[]{:S(2)}, u32[]{:S(2)}) collective-permute-start(bf16[48,16384]{1,0:T(8,128)(2,1)} %collective-permute-done.10.x_ref.refs_0_), channel_id=1, source_target_pairs={{0,1},{1,0},{2,3},{3,2},{4,5},{5,4},{6,7},{7,6},{8,9},{9,8},{10,11... | collective-permute-start | bytes 4718600 | tf_op jit(solution)/shard_map/ppermute | solution.py:470
  76.2 32.0 %collective-permute-start.11 = (bf16[48,16384]{1,0:T(8,128)(2,1)}, bf16[48,16384]{1,0:T(8,128)(2,1)S(1)}, u32[]{:S(2)}, u32[]{:S(2)}) collective-permute-start(bf16[48,16384]{1,0:T(8,128)(2,1)} %collective-permute-done.10.x_ref.refs_0_), channel_id=1, source_target_pairs={{0,2},{1,5},{4,0},{5,9},{8,4},{9,13},{12,8},{13,15},{14,12},{15,11... | collective-permute-start | bytes 4718600 | tf_op jit(solution)/shard_map/ppermute | solution.py:470
  99.7 9.6 %collective-permute-start.13 = (bf16[48,16384]{1,0:T(8,128)(2,1)S(1)}, bf16[48,16384]{1,0:T(8,128)(2,1)S(1)}, u32[]{:S(2)}, u32[]{:S(2)}) collective-permute-start(bf16[48,16384]{1,0:T(8,128)(2,1)S(1)} %collective-permute-done.5.x_ref.refs_2_), channel_id=1, source_target_pairs={{0,1},{1,0},{2,3},{3,2},{4,5},{5,4},{6,7},{7,6},{8,9},{9,8},{10,11... | collective-permute-start | bytes 4718600 | tf_op jit(solution)/shard_map/ppermute | solution.py:470
  99.7 23.5 %collective-permute-start.9 = (bf16[48,16384]{1,0:T(8,128)(2,1)S(1)}, bf16[48,16384]{1,0:T(8,128)(2,1)S(1)}, u32[]{:S(2)}, u32[]{:S(2)}) collective-permute-start(bf16[48,16384]{1,0:T(8,128)(2,1)S(1)} %collective-permute-done.5.x_ref.refs_2_), channel_id=1, source_target_pairs={{0,4},{1,3},{4,8},{5,1},{8,12},{9,5},{12,14},{13,9},{14,10},{15,13... | collective-permute-start | bytes 4718600 | tf_op jit(solution)/shard_map/ppermute | solution.py:470
  108.1 20.3 %collective-permute-start.17 = (bf16[48,16384]{1,0:T(8,128)(2,1)S(1)}, bf16[48,16384]{1,0:T(8,128)(2,1)S(1)}, u32[]{:S(2)}, u32[]{:S(2)}) collective-permute-start(bf16[48,16384]{1,0:T(8,128)(2,1)S(1)} %collective-permute-done.11.x_ref.refs_0_), channel_id=1, source_target_pairs={{0,1},{1,0},{2,3},{3,2},{4,5},{5,4},{6,7},{7,6},{8,9},{9,8},{10,11... | collective-permute-start | bytes 4718600 | tf_op jit(solution)/shard_map/ppermute | solution.py:470
  123.2 5.2 %collective-permute-start.18 = (bf16[48,16384]{1,0:T(8,128)(2,1)S(1)}, bf16[48,16384]{1,0:T(8,128)(2,1)S(1)}, u32[]{:S(2)}, u32[]{:S(2)}) collective-permute-start(bf16[48,16384]{1,0:T(8,128)(2,1)S(1)} %collective-permute-done.9.refs_0_.refs_2_), channel_id=1, source_target_pairs={{0,1},{1,0},{2,3},{3,2},{4,5},{5,4},{6,7},{7,6},{8,9},{9,8},{10,11... | collective-permute-start | bytes 4718600 | tf_op jit(solution)/shard_map/ppermute | solution.py:470
  124.7 11.8 %collective-permute-start.16 = (bf16[192,128]{1,0:T(8,128)(2,1)S(1)}, bf16[192,128]{1,0:T(8,128)(2,1)S(1)}, u32[]{:S(2)}, u32[]{:S(2)}) collective-permute-start(bf16[192,128]{1,0:T(8,128)(2,1)S(1)} %ranks.1), channel_id=1, source_target_pairs={{0,6},{1,7},{2,4},{3,5},{4,2},{5,3},{6,0},{7,1},{8,14},{9,15},{10,... | collective-permute-start | bytes 147464 | tf_op jit(solution)/shard_map/ppermute | solution.py:470
  127.8 8.7 %collective-permute-start.15 = (bf16[192,128]{1,0:T(8,128)(2,1)S(1)}, bf16[192,128]{1,0:T(8,128)(2,1)S(1)}, u32[]{:S(2)}, u32[]{:S(2)}) collective-permute-start(bf16[192,128]{1,0:T(8,128)(2,1)S(1)} %ranks.1), channel_id=1, source_target_pairs={{0,4},{1,5},{2,6},{3,7},{4,0},{5,1},{6,2},{7,3},{8,12},{9,13},{10,... | collective-permute-start | bytes 147464 | tf_op jit(solution)/shard_map/ppermute | solution.py:470
  128.2 8.2 %collective-permute-start.14 = (bf16[192,128]{1,0:T(8,128)(2,1)S(1)}, bf16[192,128]{1,0:T(8,128)(2,1)S(1)}, u32[]{:S(2)}, u32[]{:S(2)}) collective-permute-start(bf16[192,128]{1,0:T(8,128)(2,1)S(1)} %ranks.1), channel_id=1, source_target_pairs={{0,2},{1,3},{2,0},{3,1},{4,6},{5,7},{6,4},{7,5},{8,10},{9,11},{10,... | collective-permute-start | bytes 147464 | tf_op jit(solution)/shard_map/ppermute | solution.py:470
  136.5 8.4 %collective-permute-start.21 = (bf16[192,128]{1,0:T(8,128)(2,1)S(1)}, bf16[192,128]{1,0:T(8,128)(2,1)S(1)}, u32[]{:S(2)}, u32[]{:S(2)}) collective-permute-start(bf16[192,128]{1,0:T(8,128)(2,1)S(1)} %add_add_fusion), channel_id=1, source_target_pairs={{0,9},{1,8},{2,11},{3,10},{4,13},{5,12},{6,15},{7,14},{8,1},{9,0},... | collective-permute-start | bytes 147464 | tf_op jit(solution)/shard_map/ppermute | solution.py:470
  138.7 6.2 %collective-permute-start.20 = (bf16[192,128]{1,0:T(8,128)(2,1)S(1)}, bf16[192,128]{1,0:T(8,128)(2,1)S(1)}, u32[]{:S(2)}, u32[]{:S(2)}) collective-permute-start(bf16[192,128]{1,0:T(8,128)(2,1)S(1)} %add_add_fusion), channel_id=1, source_target_pairs={{0,1},{1,0},{2,3},{3,2},{4,5},{5,4},{6,7},{7,6},{8,9},{9,8},{10,11... | collective-permute-start | bytes 147464 | tf_op jit(solution)/shard_map/ppermute | solution.py:470
  139.6 6.0 %collective-permute-start.19 = (bf16[192,128]{1,0:T(8,128)(2,1)S(1)}, bf16[192,128]{1,0:T(8,128)(2,1)S(1)}, u32[]{:S(2)}, u32[]{:S(2)}) collective-permute-start(bf16[192,128]{1,0:T(8,128)(2,1)S(1)} %add_add_fusion), channel_id=1, source_target_pairs={{0,8},{1,9},{2,10},{3,11},{4,12},{5,13},{6,14},{7,15},{8,0},{9,1},... | collective-permute-start | bytes 147464 | tf_op jit(solution)/shard_map/ppermute | solution.py:470
  (8 other events, 47.5 us)

commit v21 on v20

--- a/solution.py
+++ b/solution.py
@@ -16,7 +16,7 @@
 NT = (((1,), (1,)), ((), ()))
 SLOTS = 4
 CHUNK = 256
-KEEP = 6
+KEEP = 8
 BIG_VMEM = 16 * 1024 * 1024
 PARAMS = pltpu.CompilerParams(vmem_limit_bytes=VMEM)
 SNAKE = (0, 2, 4, 6, 7, 5, 3, 1)

time: 149 us -> 149 us (level)
  transfers between devices with their start and end apart: 22 -> 22, of which waited for: 9 -> 8; matrix products, arithmetic and copies ran while one was open for 3% -> 3% of each run, Pallas kernels for 54% -> 54%
where the time goes in v21:
time: 149 us
  Pallas kernels  83.4 us (56%)
  waiting for transfers between devices  29.1 us (20%)
  starting transfers between devices  27.5 us (18%)
  local copies, waits for them, and re-layouts  6.55 us (4%)
  other arithmetic  2.13 us (1%)
    pallas_call x7, Pallas kernels, block_product(): pl.pallas_call(functools.partial(block_kernel, count, low, tile, steps, k...  64.9 us
    ppermute x22, waiting for transfers between devices, ring_plan(): send = lambda value, pairs: lax.ppermute(value, 'tensor', pairs)  29.1 us
    ppermute x22, starting transfers between devices, ring_plan(): send = lambda value, pairs: lax.ppermute(value, 'tensor', pairs)  27.5 us
    pallas_call x4, Pallas kernels, some_ranks(): pl.pallas_call(some_ranks_kernel, in_specs=[whole] * 2, out_specs=whole,...  6.98 us
    pallas_call x1, Pallas kernels, keep_weights(): pl.pallas_call(functools.partial(keep_kernel, low), in_specs=[pl.BlockSpe...  5.93 us
    unnamed x20, local copies, waits for them, and re-layouts  4.41 us
  transfers between devices with their start and end apart: 22, of which 8 were waited for; matrix products, arithmetic and copies ran while one was open for 3% of the time, Pallas kernels for 54%

profile of v21, /device:TPU:0, one launch (start us, length us, event | category | flops | bytes accessed | tf_op | source)
XLA Modules:
  0.0 149.1 jit_solution(11157980697678242307)
XLA Ops:
  0.5 3.0 %collective-permute-start = (bf16[48,16384]{1,0:T(8,128)(2,1)}, bf16[48,16384]{1,0:T(8,128)(2,1)}, u32[]{:S(2)}, u32[]{:S(2)}) collective-permute-start(bf16[48,16384]{1,0:T(8,128)(2,1)} %refs_0_.3), channel_id=1, source_target_pairs={{0,4},{1,3},{4,8},{5,1},{8,12},{9,5},{12,14},{13,9},{14,10},{15,13... | collective-permute-start | bytes 4718600 | tf_op jit(solution)/shard_map/ppermute | solution.py:470
  3.5 3.2 %collective-permute-done.2.refs_1_ = bf16[48,16384]{1,0:T(8,128)(2,1)S(1)} collective-permute-done((bf16[48,16384]{1,0:T(8,128)(2,1)}, bf16[48,16384]{1,0:T(8,128)(2,1)S(1)}, u32[]{:S(2)}, u32[]{:S(2)}) %collective-permute-start.2) | collective-permute-done | bytes 1572896 | tf_op jit(solution)/shard_map/ppermute | solution.py:470
  6.7 2.9 %blocks.7.refs_3_ = f32[16,48,1024]{2,1,0:T(8,128)S(1)} custom-call(bf16[48,16384]{1,0:T(8,128)(2,1)} %refs_0_.3, bf16[48,16384]{1,0:T(8,128)(2,1)S(1)} %collective-permute-done.2.refs_1_, bf16[16384,1024]{1,0:T(8,128)(2,1)} %refs_4_.7), custom_call_target="tpu_custom_call" | custom-call | flops 402653184 | bytes 4194304 | tf_op jit(solution)/shard_map/blocks/pallas_call | solution.py:288
  9.6 2.9 %collective-permute-start.6 = (bf16[48,16384]{1,0:T(8,128)(2,1)}, bf16[48,16384]{1,0:T(8,128)(2,1)}, u32[]{:S(2)}, u32[]{:S(2)}) collective-permute-start(bf16[48,16384]{1,0:T(8,128)(2,1)} %refs_0_.3), channel_id=1, source_target_pairs={{0,2},{1,5},{4,0},{5,9},{8,4},{9,13},{12,8},{13,15},{14,12},{15,11... | collective-permute-start | bytes 4718600 | tf_op jit(solution)/shard_map/ppermute | solution.py:470
  12.5 10.7 %blocks.8.refs_4_ = f32[16,48,1024]{2,1,0:T(8,128)S(1)} custom-call(bf16[48,16384]{1,0:T(8,128)(2,1)} %refs_0_.3, bf16[48,16384]{1,0:T(8,128)(2,1)S(1)} %collective-permute-done.2.refs_1_, bf16[16384,1024]{1,0:T(8,128)(2,1)} %refs_4_.7, f32[16,48,1024]{2,1,0:T(8,128)S(1)} %blocks.7.refs_3_), custom_call_target="tpu_custom_call", output_to_operand_aliasing={{}: (3, {})} | custom-call | flops 2818572288 | bytes 29360128 | tf_op jit(solution)/shard_map/blocks/pallas_call | solution.py:288
  24.8 3.4 %some_ranks.4.refs_2_ = f32[48,128]{1,0:T(8,128)S(1)} custom-call(bf16[48,16384]{1,0:T(8,128)(2,1)} %refs_0_.3, bf16[16384,128]{1,0:T(8,128)(2,1)S(1)} %turn.1.s_ref.refs_3_.refs_5_.refs_1_), custom_call_target="tpu_custom_call" | custom-call | tf_op jit(solution)/shard_map/some_ranks/pallas_call | solution.py:365
  28.2 2.3 %collective-permute-done.refs_0_ = bf16[48,16384]{1,0:T(8,128)(2,1)} collective-permute-done((bf16[48,16384]{1,0:T(8,128)(2,1)}, bf16[48,16384]{1,0:T(8,128)(2,1)}, u32[]{:S(2)}, u32[]{:S(2)}) %collective-permute-start) | collective-permute-done | bytes 1572896 | tf_op jit(solution)/shard_map/ppermute | solution.py:470
  30.5 2.4 %collective-permute-start.4 = (bf16[48,16384]{1,0:T(8,128)(2,1)}, bf16[48,16384]{1,0:T(8,128)(2,1)}, u32[]{:S(2)}, u32[]{:S(2)}) collective-permute-start(bf16[48,16384]{1,0:T(8,128)(2,1)} %collective-permute-done.refs_0_), channel_id=1, source_target_pairs={{0,4},{1,3},{4,8},{5,1},{8,12},{9,5},{12,14},{13,9},{14,10},{15,13... | collective-permute-start | bytes 4718600 | tf_op jit(solution)/shard_map/ppermute | solution.py:470
  32.9 9.4 %collective-permute-done.6.refs_0_ = bf16[48,16384]{1,0:T(8,128)(2,1)} collective-permute-done((bf16[48,16384]{1,0:T(8,128)(2,1)}, bf16[48,16384]{1,0:T(8,128)(2,1)}, u32[]{:S(2)}, u32[]{:S(2)}) %collective-permute-start.6) | collective-permute-done | bytes 1572896 | tf_op jit(solution)/shard_map/ppermute | solution.py:470
  45.2 2.2 %copy-done.3 = bf16[16384,128]{1,0:T(8,128)(2,1)S(1)} copy-done((bf16[16384,128]{1,0:T(8,128)(2,1)S(1)}, bf16[16384,128]{1,0:T(8,128)(2,1)}, u32[]{:S(2)}) %copy-start.3) | copy-done | bytes 4194328
  47.4 12.4 %blocks.9 = (f32[16,48,1024]{2,1,0:T(8,128)S(1)}, f32[48,128]{1,0:T(8,128)S(1)}) custom-call(bf16[48,16384]{1,0:T(8,128)(2,1)} %collective-permute-done.refs_0_, bf16[48,16384]{1,0:T(8,128)(2,1)} %collective-permute-done.3.refs_1_, bf16[16384,1024]{1,0:T(8,128)(2,1)} %refs_4_.7, bf16[16384,128]{1,0:T(8,128)(2,1)S(1)} %copy-done.3, ...), custom_call_target="tpu_custom_call", output_to_operand_aliasing={{0}: (4, {})} | custom-call | flops 3221225472 | bytes 33554432 | tf_op jit(solution)/shard_map/blocks/pallas_call | solution.py:288
  65.1 2.4 %collective-permute-start.5 = (bf16[48,16384]{1,0:T(8,128)(2,1)}, bf16[48,16384]{1,0:T(8,128)(2,1)S(1)}, u32[]{:S(2)}, u32[]{:S(2)}) collective-permute-start(bf16[48,16384]{1,0:T(8,128)(2,1)} %collective-permute-done.4.refs_2_), channel_id=1, source_target_pairs={{0,4},{1,3},{4,8},{5,1},{8,12},{9,5},{12,14},{13,9},{14,10},{15,13... | collective-permute-start | bytes 4718600 | tf_op jit(solution)/shard_map/ppermute | solution.py:470
  67.5 7.7 %collective-permute-done.10.x_ref.refs_0_ = bf16[48,16384]{1,0:T(8,128)(2,1)} collective-permute-done((bf16[48,16384]{1,0:T(8,128)(2,1)}, bf16[48,16384]{1,0:T(8,128)(2,1)}, u32[]{:S(2)}, u32[]{:S(2)}) %collective-permute-start.10) | collective-permute-done | bytes 1572896 | tf_op jit(solution)/shard_map/ppermute | solution.py:470
  78.2 2.2 %copy-done.4 = bf16[16384,128]{1,0:T(8,128)(2,1)S(1)} copy-done((bf16[16384,128]{1,0:T(8,128)(2,1)S(1)}, bf16[16384,128]{1,0:T(8,128)(2,1)}, u32[]{:S(2)}) %copy-start.4) | copy-done | bytes 4194328
  80.4 13.3 %blocks.10 = (f32[16,48,1024]{2,1,0:T(8,128)S(1)}, f32[96,128]{1,0:T(8,128)S(1)}) custom-call(bf16[48,16384]{1,0:T(8,128)(2,1)} %collective-permute-done.6.refs_0_, bf16[48,16384]{1,0:T(8,128)(2,1)} %collective-permute-done.7.refs_1_, bf16[48,16384]{1,0:T(8,128)(2,1)} %collective-permute-done.4.refs_2_, ...), custom_call_target="tpu_custom_call", output_to_operand_aliasing={{0}: (6, {})} | custom-call | flops 6442450944 | bytes 33554432 | tf_op jit(solution)/shard_map/blocks/pallas_call | solution.py:288
  93.7 5.9 %keep.1.refs_5_ = bf16[8192,1024]{1,0:T(8,128)(2,1)S(1)} custom-call(bf16[16384,1024]{1,0:T(8,128)(2,1)} %refs_4_.7), custom_call_target="tpu_custom_call" | custom-call | tf_op jit(solution)/shard_map/keep/pallas_call | solution.py:319
  99.7 2.3 %collective-permute-start.9 = (bf16[48,16384]{1,0:T(8,128)(2,1)S(1)}, bf16[48,16384]{1,0:T(8,128)(2,1)S(1)}, u32[]{:S(2)}, u32[]{:S(2)}) collective-permute-start(bf16[48,16384]{1,0:T(8,128)(2,1)S(1)} %collective-permute-done.5.x_ref.refs_2_), channel_id=1, source_target_pairs={{0,4},{1,3},{4,8},{5,1},{8,12},{9,5},{12,14},{13,9},{14,10},{15,13... | collective-permute-start | bytes 4718600 | tf_op jit(solution)/shard_map/ppermute | solution.py:470
  104.9 3.2 %collective-permute-done.11.x_ref.refs_0_ = bf16[48,16384]{1,0:T(8,128)(2,1)S(1)} collective-permute-done((bf16[48,16384]{1,0:T(8,128)(2,1)}, bf16[48,16384]{1,0:T(8,128)(2,1)S(1)}, u32[]{:S(2)}, u32[]{:S(2)}) %collective-permute-start.11) | collective-permute-done | bytes 1572896 | tf_op jit(solution)/shard_map/ppermute | solution.py:470
  109.2 12.6 %blocks.11.refs_6_ = f32[16,48,1024]{2,1,0:T(8,128)S(1)} custom-call(bf16[48,16384]{1,0:T(8,128)(2,1)} %collective-permute-done.10.x_ref.refs_0_, bf16[48,16384]{1,0:T(8,128)(2,1)S(1)} %collective-permute-done.12.refs_1_, bf16[48,16384]{1,0:T(8,128)(2,1)S(1)} %collective-permute-done.5.x_ref.refs_2_, ...), custom_call_target="tpu_custom_call", output_to_operand_aliasing={{}: (5, {})} | custom-call | flops 6442450944 | bytes 33554432 | tf_op jit(solution)/shard_map/blocks/pallas_call | solution.py:288
  124.7 3.1 %collective-permute-start.16 = (bf16[192,128]{1,0:T(8,128)(2,1)S(1)}, bf16[192,128]{1,0:T(8,128)(2,1)S(1)}, u32[]{:S(2)}, u32[]{:S(2)}) collective-permute-start(bf16[192,128]{1,0:T(8,128)(2,1)S(1)} %ranks.1), channel_id=1, source_target_pairs={{0,6},{1,7},{2,4},{3,5},{4,2},{5,3},{6,0},{7,1},{8,14},{9,15},{10,... | collective-permute-start | bytes 147464 | tf_op jit(solution)/shard_map/ppermute | solution.py:470
  128.4 8.7 %blocks.12.refs_5_ = f32[16,48,1024]{2,1,0:T(8,128)S(1)} custom-call(bf16[48,16384]{1,0:T(8,128)(2,1)S(1)} %collective-permute-done.11.x_ref.refs_0_, bf16[48,16384]{1,0:T(8,128)(2,1)S(1)} %collective-permute-done.17.refs_1_, bf16[48,16384]{1,0:T(8,128)(2,1)S(1)} %collective-permute-done.9.refs_0_.refs_2_, ...), custom_call_target="tpu_custom_call", output_to_operand_aliasing={{}: (6, {})} | custom-call | flops 1610612736 | bytes 8388608 | tf_op jit(solution)/shard_map/blocks/pallas_call | solution.py:288
  137.2 2.2 %collective-permute-start.21 = (bf16[192,128]{1,0:T(8,128)(2,1)S(1)}, bf16[192,128]{1,0:T(8,128)(2,1)S(1)}, u32[]{:S(2)}, u32[]{:S(2)}) collective-permute-start(bf16[192,128]{1,0:T(8,128)(2,1)S(1)} %add_add_fusion), channel_id=1, source_target_pairs={{0,9},{1,8},{2,11},{3,10},{4,13},{5,12},{6,15},{7,14},{8,1},{9,0},... | collective-permute-start | bytes 147464 | tf_op jit(solution)/shard_map/ppermute | solution.py:470
  140.3 4.5 %blocks.13.total_ref = f32[16,48,1024]{2,1,0:T(8,128)S(1)} custom-call(bf16[48,16384]{1,0:T(8,128)(2,1)S(1)} %collective-permute-done.11.x_ref.refs_0_, bf16[48,16384]{1,0:T(8,128)(2,1)S(1)} %collective-permute-done.17.refs_1_, bf16[48,16384]{1,0:T(8,128)(2,1)S(1)} %collective-permute-done.9.refs_0_.refs_2_, ...), custom_call_target="tpu_custom_call", output_to_operand_aliasing={{}: (5, {})} | custom-call | flops 1610612736 | bytes 8388608 | tf_op jit(solution)/shard_map/blocks/pallas_call | solution.py:288
  146.4 2.6 %finish.1 = bf16[768,1024]{1,0:T(8,128)(2,1)} custom-call(s32[16]{0:T(128)S(1)} %get-tuple-element.73.places_ref, s32[6]{0:T(128)S(1)} %gather_fusion, s32[1]{0:T(128)} %bitcast.7.core_ref, f32[16,48,1024]{2,1,0:T(8,128)S(1)} %blocks.13.total_ref, bf16[16,64,1024]{2,1,0:T(8,128)(2,1)S(1)} %bitcast.16, f32[1,1024]{1,0:T(1,128)S(1)} %bitcast.17, ...), custom_call_target="tpu_custom_call" | custom-call | tf_op jit(solution)/shard_map/finish/pallas_call | solution.py:449
  (70 shorter events, 23.4 us)
Async XLA Ops:
  0.0 60.8 %copy-start = (s32[16]{0:T(128)S(1)}, s32[16]{0:T(128)}, u32[]{:S(2)}) copy-start(s32[16]{0:T(128)} %param.16) | copy-start | bytes 196
  0.0 23.2 %collective-permute-start.1 = (bf16[64,16384]{1,0:T(8,128)(2,1)}, bf16[64,16384]{1,0:T(8,128)(2,1)S(1)}, u32[]{:S(2)}, u32[]{:S(2)}) collective-permute-start(bf16[64,16384]{1,0:T(8,128)(2,1)} %bitcast.14), channel_id=1, source_target_pairs={{0,1},{1,0},{2,3},{3,2},{4,5},{5,4},{6,7},{7,6},{8,9},{9,8},{10,11... | collective-permute-start | bytes 6291464 | tf_op jit(solution)/shard_map/ppermute | solution.py:470
  0.5 6.2 %collective-permute-start.2 = (bf16[48,16384]{1,0:T(8,128)(2,1)}, bf16[48,16384]{1,0:T(8,128)(2,1)S(1)}, u32[]{:S(2)}, u32[]{:S(2)}) collective-permute-start(bf16[48,16384]{1,0:T(8,128)(2,1)} %refs_0_.3), channel_id=1, source_target_pairs={{0,1},{1,0},{2,3},{3,2},{4,5},{5,4},{6,7},{7,6},{8,9},{9,8},{10,11... | collective-permute-start | bytes 4718600 | tf_op jit(solution)/shard_map/ppermute | solution.py:470
  0.5 29.9 %collective-permute-start = (bf16[48,16384]{1,0:T(8,128)(2,1)}, bf16[48,16384]{1,0:T(8,128)(2,1)}, u32[]{:S(2)}, u32[]{:S(2)}) collective-permute-start(bf16[48,16384]{1,0:T(8,128)(2,1)} %refs_0_.3), channel_id=1, source_target_pairs={{0,4},{1,3},{4,8},{5,1},{8,12},{9,5},{12,14},{13,9},{14,10},{15,13... | collective-permute-start | bytes 4718600 | tf_op jit(solution)/shard_map/ppermute | solution.py:470
  9.6 32.7 %collective-permute-start.6 = (bf16[48,16384]{1,0:T(8,128)(2,1)}, bf16[48,16384]{1,0:T(8,128)(2,1)}, u32[]{:S(2)}, u32[]{:S(2)}) collective-permute-start(bf16[48,16384]{1,0:T(8,128)(2,1)} %refs_0_.3), channel_id=1, source_target_pairs={{0,2},{1,5},{4,0},{5,9},{8,4},{9,13},{12,8},{13,15},{14,12},{15,11... | collective-permute-start | bytes 4718600 | tf_op jit(solution)/shard_map/ppermute | solution.py:470
  30.5 14.8 %collective-permute-start.3 = (bf16[48,16384]{1,0:T(8,128)(2,1)}, bf16[48,16384]{1,0:T(8,128)(2,1)}, u32[]{:S(2)}, u32[]{:S(2)}) collective-permute-start(bf16[48,16384]{1,0:T(8,128)(2,1)} %collective-permute-done.refs_0_), channel_id=1, source_target_pairs={{0,1},{1,0},{2,3},{3,2},{4,5},{5,4},{6,7},{7,6},{8,9},{9,8},{10,11... | collective-permute-start | bytes 4718600 | tf_op jit(solution)/shard_map/ppermute | solution.py:470
  30.5 30.1 %copy-start.9 = (s32[8]{0:T(128)S(1)}, s32[8]{0:T(128)}, u32[]{:S(2)}) copy-start(s32[8]{0:T(128)} %param.17) | copy-start | bytes 100
  30.5 34.6 %collective-permute-start.4 = (bf16[48,16384]{1,0:T(8,128)(2,1)}, bf16[48,16384]{1,0:T(8,128)(2,1)}, u32[]{:S(2)}, u32[]{:S(2)}) collective-permute-start(bf16[48,16384]{1,0:T(8,128)(2,1)} %collective-permute-done.refs_0_), channel_id=1, source_target_pairs={{0,4},{1,3},{4,8},{5,1},{8,12},{9,5},{12,14},{13,9},{14,10},{15,13... | collective-permute-start | bytes 4718600 | tf_op jit(solution)/shard_map/ppermute | solution.py:470
  42.3 32.8 %collective-permute-start.10 = (bf16[48,16384]{1,0:T(8,128)(2,1)}, bf16[48,16384]{1,0:T(8,128)(2,1)}, u32[]{:S(2)}, u32[]{:S(2)}) collective-permute-start(bf16[48,16384]{1,0:T(8,128)(2,1)} %collective-permute-done.6.refs_0_), channel_id=1, source_target_pairs={{0,2},{1,5},{4,0},{5,9},{8,4},{9,13},{12,8},{13,15},{14,12},{15,11... | collective-permute-start | bytes 4718600 | tf_op jit(solution)/shard_map/ppermute | solution.py:470
  44.0 34.2 %collective-permute-start.7 = (bf16[48,16384]{1,0:T(8,128)(2,1)}, bf16[48,16384]{1,0:T(8,128)(2,1)}, u32[]{:S(2)}, u32[]{:S(2)}) collective-permute-start(bf16[48,16384]{1,0:T(8,128)(2,1)} %collective-permute-done.6.refs_0_), channel_id=1, source_target_pairs={{0,1},{1,0},{2,3},{3,2},{4,5},{5,4},{6,7},{7,6},{8,9},{9,8},{10,11... | collective-permute-start | bytes 4718600 | tf_op jit(solution)/shard_map/ppermute | solution.py:470
  65.1 13.1 %collective-permute-start.8 = (bf16[48,16384]{1,0:T(8,128)(2,1)}, bf16[48,16384]{1,0:T(8,128)(2,1)S(1)}, u32[]{:S(2)}, u32[]{:S(2)}) collective-permute-start(bf16[48,16384]{1,0:T(8,128)(2,1)} %collective-permute-done.4.refs_2_), channel_id=1, source_target_pairs={{0,1},{1,0},{2,3},{3,2},{4,5},{5,4},{6,7},{7,6},{8,9},{9,8},{10,11... | collective-permute-start | bytes 4718600 | tf_op jit(solution)/shard_map/ppermute | solution.py:470
  65.1 34.6 %collective-permute-start.5 = (bf16[48,16384]{1,0:T(8,128)(2,1)}, bf16[48,16384]{1,0:T(8,128)(2,1)S(1)}, u32[]{:S(2)}, u32[]{:S(2)}) collective-permute-start(bf16[48,16384]{1,0:T(8,128)(2,1)} %collective-permute-done.4.refs_2_), channel_id=1, source_target_pairs={{0,4},{1,3},{4,8},{5,1},{8,12},{9,5},{12,14},{13,9},{14,10},{15,13... | collective-permute-start | bytes 4718600 | tf_op jit(solution)/shard_map/ppermute | solution.py:470
  75.2 34.0 %collective-permute-start.12 = (bf16[48,16384]{1,0:T(8,128)(2,1)}, bf16[48,16384]{1,0:T(8,128)(2,1)S(1)}, u32[]{:S(2)}, u32[]{:S(2)}) collective-permute-start(bf16[48,16384]{1,0:T(8,128)(2,1)} %collective-permute-done.10.x_ref.refs_0_), channel_id=1, source_target_pairs={{0,1},{1,0},{2,3},{3,2},{4,5},{5,4},{6,7},{7,6},{8,9},{9,8},{10,11... | collective-permute-start | bytes 4718600 | tf_op jit(solution)/shard_map/ppermute | solution.py:470
  76.2 32.0 %collective-permute-start.11 = (bf16[48,16384]{1,0:T(8,128)(2,1)}, bf16[48,16384]{1,0:T(8,128)(2,1)S(1)}, u32[]{:S(2)}, u32[]{:S(2)}) collective-permute-start(bf16[48,16384]{1,0:T(8,128)(2,1)} %collective-permute-done.10.x_ref.refs_0_), channel_id=1, source_target_pairs={{0,2},{1,5},{4,0},{5,9},{8,4},{9,13},{12,8},{13,15},{14,12},{15,11... | collective-permute-start | bytes 4718600 | tf_op jit(solution)/shard_map/ppermute | solution.py:470
  99.7 9.5 %collective-permute-start.13 = (bf16[48,16384]{1,0:T(8,128)(2,1)S(1)}, bf16[48,16384]{1,0:T(8,128)(2,1)S(1)}, u32[]{:S(2)}, u32[]{:S(2)}) collective-permute-start(bf16[48,16384]{1,0:T(8,128)(2,1)S(1)} %collective-permute-done.5.x_ref.refs_2_), channel_id=1, source_target_pairs={{0,1},{1,0},{2,3},{3,2},{4,5},{5,4},{6,7},{7,6},{8,9},{9,8},{10,11... | collective-permute-start | bytes 4718600 | tf_op jit(solution)/shard_map/ppermute | solution.py:470
  99.7 23.5 %collective-permute-start.9 = (bf16[48,16384]{1,0:T(8,128)(2,1)S(1)}, bf16[48,16384]{1,0:T(8,128)(2,1)S(1)}, u32[]{:S(2)}, u32[]{:S(2)}) collective-permute-start(bf16[48,16384]{1,0:T(8,128)(2,1)S(1)} %collective-permute-done.5.x_ref.refs_2_), channel_id=1, source_target_pairs={{0,4},{1,3},{4,8},{5,1},{8,12},{9,5},{12,14},{13,9},{14,10},{15,13... | collective-permute-start | bytes 4718600 | tf_op jit(solution)/shard_map/ppermute | solution.py:470
  108.1 20.3 %collective-permute-start.17 = (bf16[48,16384]{1,0:T(8,128)(2,1)S(1)}, bf16[48,16384]{1,0:T(8,128)(2,1)S(1)}, u32[]{:S(2)}, u32[]{:S(2)}) collective-permute-start(bf16[48,16384]{1,0:T(8,128)(2,1)S(1)} %collective-permute-done.11.x_ref.refs_0_), channel_id=1, source_target_pairs={{0,1},{1,0},{2,3},{3,2},{4,5},{5,4},{6,7},{7,6},{8,9},{9,8},{10,11... | collective-permute-start | bytes 4718600 | tf_op jit(solution)/shard_map/ppermute | solution.py:470
  123.2 5.2 %collective-permute-start.18 = (bf16[48,16384]{1,0:T(8,128)(2,1)S(1)}, bf16[48,16384]{1,0:T(8,128)(2,1)S(1)}, u32[]{:S(2)}, u32[]{:S(2)}) collective-permute-start(bf16[48,16384]{1,0:T(8,128)(2,1)S(1)} %collective-permute-done.9.refs_0_.refs_2_), channel_id=1, source_target_pairs={{0,1},{1,0},{2,3},{3,2},{4,5},{5,4},{6,7},{7,6},{8,9},{9,8},{10,11... | collective-permute-start | bytes 4718600 | tf_op jit(solution)/shard_map/ppermute | solution.py:470
  124.7 12.5 %collective-permute-start.16 = (bf16[192,128]{1,0:T(8,128)(2,1)S(1)}, bf16[192,128]{1,0:T(8,128)(2,1)S(1)}, u32[]{:S(2)}, u32[]{:S(2)}) collective-permute-start(bf16[192,128]{1,0:T(8,128)(2,1)S(1)} %ranks.1), channel_id=1, source_target_pairs={{0,6},{1,7},{2,4},{3,5},{4,2},{5,3},{6,0},{7,1},{8,14},{9,15},{10,... | collective-permute-start | bytes 147464 | tf_op jit(solution)/shard_map/ppermute | solution.py:470
  127.8 9.4 %collective-permute-start.15 = (bf16[192,128]{1,0:T(8,128)(2,1)S(1)}, bf16[192,128]{1,0:T(8,128)(2,1)S(1)}, u32[]{:S(2)}, u32[]{:S(2)}) collective-permute-start(bf16[192,128]{1,0:T(8,128)(2,1)S(1)} %ranks.1), channel_id=1, source_target_pairs={{0,4},{1,5},{2,6},{3,7},{4,0},{5,1},{6,2},{7,3},{8,12},{9,13},{10,... | collective-permute-start | bytes 147464 | tf_op jit(solution)/shard_map/ppermute | solution.py:470
  128.2 8.9 %collective-permute-start.14 = (bf16[192,128]{1,0:T(8,128)(2,1)S(1)}, bf16[192,128]{1,0:T(8,128)(2,1)S(1)}, u32[]{:S(2)}, u32[]{:S(2)}) collective-permute-start(bf16[192,128]{1,0:T(8,128)(2,1)S(1)} %ranks.1), channel_id=1, source_target_pairs={{0,2},{1,3},{2,0},{3,1},{4,6},{5,7},{6,4},{7,5},{8,10},{9,11},{10,... | collective-permute-start | bytes 147464 | tf_op jit(solution)/shard_map/ppermute | solution.py:470
  137.2 7.6 %collective-permute-start.21 = (bf16[192,128]{1,0:T(8,128)(2,1)S(1)}, bf16[192,128]{1,0:T(8,128)(2,1)S(1)}, u32[]{:S(2)}, u32[]{:S(2)}) collective-permute-start(bf16[192,128]{1,0:T(8,128)(2,1)S(1)} %add_add_fusion), channel_id=1, source_target_pairs={{0,9},{1,8},{2,11},{3,10},{4,13},{5,12},{6,15},{7,14},{8,1},{9,0},... | collective-permute-start | bytes 147464 | tf_op jit(solution)/shard_map/ppermute | solution.py:470
  139.4 5.4 %collective-permute-start.20 = (bf16[192,128]{1,0:T(8,128)(2,1)S(1)}, bf16[192,128]{1,0:T(8,128)(2,1)S(1)}, u32[]{:S(2)}, u32[]{:S(2)}) collective-permute-start(bf16[192,128]{1,0:T(8,128)(2,1)S(1)} %add_add_fusion), channel_id=1, source_target_pairs={{0,1},{1,0},{2,3},{3,2},{4,5},{5,4},{6,7},{7,6},{8,9},{9,8},{10,11... | collective-permute-start | bytes 147464 | tf_op jit(solution)/shard_map/ppermute | solution.py:470
  140.3 6.0 %collective-permute-start.19 = (bf16[192,128]{1,0:T(8,128)(2,1)S(1)}, bf16[192,128]{1,0:T(8,128)(2,1)S(1)}, u32[]{:S(2)}, u32[]{:S(2)}) collective-permute-start(bf16[192,128]{1,0:T(8,128)(2,1)S(1)} %add_add_fusion), channel_id=1, source_target_pairs={{0,8},{1,9},{2,10},{3,11},{4,12},{5,13},{6,14},{7,15},{8,0},{9,1},... | collective-permute-start | bytes 147464 | tf_op jit(solution)/shard_map/ppermute | solution.py:470
  (8 other events, 47.5 us)
